TPU v7x, 32 devices: a whole 2x2x4 slice. The times are simulated.
32 devices in a mesh: replica: 2 (over core), seq: 4 (over z), tensor: 4 (over y, x).
Axes of the slice: x: 2, y: 2, z: 4, core: 2. Of those that a mesh axis runs over, the one named last changes fastest.
Arguments:
- values: bfloat16 [2, 1024, 4096], P('replica', 'seq', 'tensor'), may hold values from -6 to 6
- gate_in: bfloat16 [2, 1024, 4096], P('replica', 'seq', 'tensor'), may hold values from -6 to 6
- in_b: bfloat16 [2, 1024, 128], P('replica', 'seq'), may hold values from -0.03125 to 0.03125
- in_c: bfloat16 [2, 1024, 128], P('replica', 'seq'), may hold values from -6 to 6
- step_sizes: float32 [2, 64, 1024], P('replica', 'tensor', 'seq'), may hold values from 0.2 to 1028
- log_rates: float32 [64], P('tensor'), as said below
- skip_gain: float32 [64], P('tensor'), may hold values from 0.5 to 1.5
- grad_out: bfloat16 [2, 1024, 4096], P('replica', 'seq', 'tensor'), may hold values from -6 to 6
Outputs:
- grad_values: bfloat16 [2, 1024, 4096], P('replica', 'seq', 'tensor')
- grad_gate: bfloat16 [2, 1024, 4096], P('replica', 'seq', 'tensor')
- grad_b: float32 [2, 1024, 128], P('replica', 'seq')
- grad_c: float32 [2, 1024, 128], P('replica', 'seq')
- grad_step_sizes: float32 [2, 64, 1024], P('replica', 'tensor', 'seq')
- grad_log_rates: float32 [64], P('tensor')
- derivative_bypass_weight: float32 [64], P('tensor')
Inputs may be any that keep to these rules, and one draw needn't show every extreme that they name: `log_rates`: each entry is at least log(0.1 / 1024).
All inputs are finite; a program needn't handle non-finite values.
Results may differ from a plain program's by a relative error of at most 0.0047.
Values sent between devices are 32-bit elements; how exact they have to be, the bound alone decides.
No kernel may reach another device: no remote copies, remote signals or barrier semaphores. Data moves between devices by JAX's collectives and lax.ppermute only.
A program may use at most 64 MiB of HBM per device.

v0:
```python
import functools

import jax
import jax.numpy as jnp
from jax import lax
from jax.experimental import pallas as pl
from jax.experimental.pallas import tpu as pltpu
from jax.sharding import PartitionSpec as P

F32 = jnp.float32
BF16 = jnp.bfloat16
VMEM_LIMIT = 24 * 1024 * 1024
LANES = 256
CHUNKS = 4
PARTS = 2
LAG = 2


def split(x, parts):
    terms = []
    for _ in range(parts - 1):
        term = x.astype(BF16)
        terms.append(term)
        x = x - term.astype(F32)
    terms.append(x.astype(BF16))
    return terms


def mm(a, b):
    return lax.dot_general(a, b, (((1,), (0,)), ((), ())), preferred_element_type=F32)


def mm_nt(a, b):
    return lax.dot_general(a, b, (((1,), (1,)), ((), ())), preferred_element_type=F32)


def mm_tn(a, b):
    return lax.dot_general(a, b, (((0,), (0,)), ((), ())), preferred_element_type=F32)


def iota(shape, dim):
    return lax.broadcasted_iota(jnp.int32, shape, dim)


def to_column(row):
    n = row.shape[1]
    eye = iota((n, n), 0) == iota((n, n), 1)
    return jnp.sum(jnp.where(eye, row, 0.0), axis=1, keepdims=True)


def to_row(column):
    n = column.shape[0]
    eye = iota((n, n), 0) == iota((n, n), 1)
    return jnp.sum(jnp.where(eye, column, 0.0), axis=0, keepdims=True)


def head_map(heads, width, first, lanes):
    low = iota((heads, lanes), 0) * width
    channel = iota((heads, lanes), 1) + first
    return (channel >= low) & (channel < low + width)


def spread_map(heads, width, first, lanes):
    one = jnp.where(head_map(heads, width, first, lanes), 1.0, 0.0).astype(BF16)
    return jnp.concatenate([one, one, one], axis=0)


def rows_of_three(per_head):
    return jnp.concatenate(split(per_head, 3), axis=0)


def spread(three, first, lanes, width):
    heads = three.shape[0] // 3
    return mm_tn(three, spread_map(heads, width, first, lanes))


def scan_tokens(per_head, backward):
    heads, length = per_head.shape
    source = iota((length, length), 0)
    target = iota((length, length), 1)
    keep = source >= target if backward else source <= target
    sums = mm(rows_of_three(per_head), jnp.where(keep, 1.0, 0.0).astype(BF16))
    return sums[:heads] + sums[heads : 2 * heads] + sums[2 * heads :]


def channel_row(column, heads, width, first):
    mine = head_map(heads, width, first, LANES)
    return jnp.sum(jnp.where(mine, column, 0.0), axis=0, keepdims=True)


def head_column(row, heads, width, first):
    mine = head_map(heads, width, first, LANES)
    return jnp.sum(jnp.where(mine, row, 0.0), axis=1, keepdims=True)


def gate_parts(gate, grad):
    wide = gate.astype(F32)
    sigmoid = 1.0 / (1.0 + jnp.exp(-wide))
    return wide, sigmoid, grad.astype(F32) * (wide * sigmoid)


def states_kernel(chunks, size, *refs):
    sources, outs, (steps_ref, lr_ref, sems) = refs[:8], refs[8:-3], refs[-3:]
    v_ref, gate_ref, go_ref, b_ref, c_ref = outs[:5]
    cum_ref, neg_ref, decay_ref, slope_ref, skip_ref = outs[5:10]
    mine_refs, other_refs = outs[10 : 10 + chunks], outs[10 + chunks :]
    targets = (v_ref, gate_ref, go_ref, b_ref, c_ref, steps_ref, lr_ref, skip_ref)
    copies = [
        pltpu.make_async_copy(source, target, sems.at[i])
        for i, (source, target) in enumerate(zip(sources, targets))
    ]
    for i in (6, 5, 3, 4, 0, 1, 2, 7):
        copies[i].start()
    copies[6].wait()
    copies[5].wait()
    length, channels = v_ref.shape
    heads = steps_ref.shape[0]
    width = channels // heads
    lower = lax.axis_index("seq") < size // 2 if size > 1 else True
    rates = jnp.exp(to_column(lr_ref[...]))
    cumulative = scan_tokens(-rates * steps_ref[...], False)
    total = cumulative[:, -1:]
    decay = jnp.exp(total)
    cum_ref[...] = cumulative
    neg_ref[...] = jnp.broadcast_to(-rates, (heads, length))
    growth = rows_of_three(jnp.exp(cumulative))
    fall = rows_of_three(jnp.exp(total - cumulative))
    copies[3].wait()
    copies[4].wait()
    b_t = b_ref[...].astype(F32).T.astype(BF16)
    c_t = c_ref[...].astype(F32).T.astype(BF16)
    for i in (0, 1, 2, 7):
        copies[i].wait()
    rows = b_t.shape[0] // chunks
    for first in range(0, channels, LANES):
        here = pl.ds(first, LANES)
        _, _, grad_y = gate_parts(gate_ref[:, here], go_ref[:, here])
        high, low = split(spread(growth, first, LANES, width) * grad_y, 2)
        pulled = mm(c_t, high) + mm(c_t, low)
        scaled = (spread(fall, first, LANES, width) * v_ref[:, here].astype(F32)).astype(BF16)
        local = mm(b_t, scaled)
        mine = jnp.where(lower, local, pulled)
        other = jnp.where(lower, pulled, local)
        for i in range(chunks):
            mine_refs[i][:, here] = mine[i * rows : (i + 1) * rows]
            other_refs[i][:, here] = other[i * rows : (i + 1) * rows]
        decay_ref[:, here] = channel_row(decay, heads, width, first)
        slope_ref[:, here] = channel_row(total * decay, heads, width, first)


def intra_kernel(
    v_ref, gate_ref, go_ref, b_ref, c_ref, cum_ref,
    intra_ref, inner_ref, sum_b_ref, sum_c_ref, grad_t_ref, inner_t_ref, acc_ref,
):
    length, channels = v_ref.shape
    heads = cum_ref.shape[0]
    width = channels // heads
    half = length // 2
    pair = 2 * width
    cumulative = cum_ref[...]
    columns = cumulative.T
    scores = mm_nt(c_ref[...], b_ref[...])
    causal = iota((half, half), 0) >= iota((half, half), 1)
    left = iota((1, pair), 1) < width
    acc_ref[...] = jnp.zeros_like(acc_ref)

    def blocks(x):
        return x[:half, :half], x[half:, :half], x[half:, half:]

    scores_00, scores_10, scores_11 = blocks(scores)
    for first in range(0, channels, pair):
        here = pl.ds(first, pair)
        _, _, grad_y = gate_parts(gate_ref[:, here], go_ref[:, here])
        grad_t_ref[here, :] = grad_y.T.astype(BF16)
        vals = v_ref[:, here]
        pieces = []
        for side in range(2):
            head = first // width + side
            own = left if side == 0 else jnp.logical_not(left)
            row = cumulative[head : head + 1, :]
            column = columns[:, head : head + 1]
            row_0, row_1 = row[:, :half], row[:, half:]
            column_0, column_1 = column[:half], column[half:]
            decay_00 = jnp.exp(jnp.where(causal, column_0 - row_0, -1e30))
            decay_10 = jnp.exp(column_1 - row_0)
            decay_11 = jnp.exp(jnp.where(causal, column_1 - row_1, -1e30))
            mix_00 = (scores_00 * decay_00).astype(BF16)
            mix_10 = (scores_10 * decay_10).astype(BF16)
            mix_11 = (scores_11 * decay_11).astype(BF16)
            low_rows = jnp.concatenate([mix_10, mix_11], axis=1)
            pieces.append((mm(mix_00, vals[:half]), mm(low_rows, vals)))
            head_grad = jnp.where(own, grad_y, 0.0).astype(BF16)
            mixed_0 = mm_nt(head_grad[:half], vals[:half])
            mixed_1 = mm_nt(head_grad[half:], vals)
            acc_ref[:half, :half] += mixed_0 * decay_00
            acc_ref[half:, :half] += mixed_1[:, :half] * decay_10
            acc_ref[half:, half:] += mixed_1[:, half:] * decay_11
            mine = pl.ds(first + side * width, width)
            grad_t = grad_t_ref[mine, :]
            inner_t_ref[mine, :half] = mm(grad_t[:, :half], mix_00) + mm(grad_t[:, half:], mix_10)
            inner_t_ref[mine, half:] = mm(grad_t[:, half:], mix_11)
        intra_ref[:half, here] = jnp.where(left, pieces[0][0], pieces[1][0])
        intra_ref[half:, here] = jnp.where(left, pieces[0][1], pieces[1][1])
        inner_ref[:, here] = inner_t_ref[here, :].T
    shares = acc_ref[...]
    high, low = split(shares, 2)
    sum_c_ref[...] = mm(high, b_ref[...]) + mm(low, b_ref[...])
    high, low = split(shares.T, 2)
    sum_b_ref[...] = mm(high, c_ref[...]) + mm(low, c_ref[...])


def prepare_kernel(
    v_ref, gate_ref, go_ref, b_ref, c_ref, cum_ref, skip_ref, intra_ref, in_inner_ref, after_ref,
    coef_ref, mamba_ref, inner_ref, growth_ref, fall_ref, gy_ref,
    high_ref, low_ref, scaled_ref, q_ref, r_ref, gcum_ref, parts_ref,
):
    length, channels = v_ref.shape
    heads = cum_ref.shape[0]
    width = channels // heads
    cumulative = cum_ref[...]
    total = cumulative[:, -1:]
    left_over = total - cumulative
    growth_three = rows_of_three(jnp.exp(cumulative))
    fall_three = rows_of_three(jnp.exp(left_over))
    growth_slope = rows_of_three(cumulative * jnp.exp(cumulative))
    fall_slope = rows_of_three(left_over * jnp.exp(left_over))
    b_t = b_ref[...].astype(F32).T.astype(BF16)
    c_t = c_ref[...].astype(F32).T.astype(BF16)
    skip_column = to_column(skip_ref[...])
    grad_cum = jnp.zeros((heads, length), F32)
    skip_part = jnp.zeros((heads, 1), F32)
    for first in range(0, channels, LANES):
        here = pl.ds(first, LANES)
        wide, sigmoid, grad_y = gate_parts(gate_ref[:, here], go_ref[:, here])
        vals = v_ref[:, here].astype(F32)
        skip = channel_row(skip_column, heads, width, first)
        growth = spread(growth_three, first, LANES, width)
        fall = spread(fall_three, first, LANES, width)
        growth_ref[:, here] = growth
        fall_ref[:, here] = fall
        gy_ref[:, here] = grad_y
        coef_ref[:, here] = go_ref[:, here].astype(F32) * sigmoid * (1.0 + wide * (1.0 - sigmoid))
        high, low = split(growth * grad_y, 2)
        high_ref[:, here] = high
        low_ref[:, here] = low
        scaled_ref[:, here] = (fall * vals).astype(BF16)
        intra = intra_ref[:, here]
        inner = in_inner_ref[:, here]
        mamba_ref[:, here] = intra + skip * vals
        inner_ref[:, here] = inner + skip * grad_y
        high, low = split(grad_y.astype(BF16).astype(F32) * intra - vals * inner, 2)
        head_rows = jnp.where(head_map(heads, width, first, LANES), 1.0, 0.0).astype(BF16)
        grad_cum = grad_cum + mm_nt(head_rows, high) + mm_nt(head_rows, low)
        skip_row = jnp.sum(grad_y * vals, axis=0, keepdims=True)
        skip_part = skip_part + head_column(skip_row, heads, width, first)
        high, low = split(spread(growth_slope, first, LANES, width) * grad_y, 2)
        q_ref[:, here] = mm(c_t, high) + mm(c_t, low)
        high, low = split(spread(fall_slope, first, LANES, width) * vals, 2)
        r_ref[:, here] = mm(b_t, high) + mm(b_t, low)
    gcum_ref[...] = grad_cum
    rate_part = jnp.sum(grad_cum * cumulative, axis=1, keepdims=True)
    parts_ref[...] = jnp.concatenate([to_row(rate_part), to_row(skip_part)], axis=0)


def pick(size, first, second, last):
    if size == 1:
        return jnp.zeros_like(first), jnp.zeros_like(first)
    if size % 2:
        return first, second
    index = lax.axis_index("seq")
    lower = index < size // 2
    edge = jnp.logical_or(index == 0, index == size - 1)
    first = jnp.where(edge, 0.0, first)
    second = jnp.where(edge, last, second)
    return jnp.where(lower, first, second), jnp.where(lower, second, first)


def picked(size, states, here):
    both = [pick(size, *(ref[:, here] for ref in state)) for state in states]
    return jnp.concatenate([x[0] for x in both], axis=0), jnp.concatenate([x[1] for x in both], axis=0)


def rate_kernel(size, pieces, start, heads, final, *refs):
    states, refs = [refs[3 * i : 3 * i + 3] for i in range(pieces)], refs[3 * pieces :]
    q_ref, r_ref, slope_ref, row_ref, parts_ref, out_ref = *refs[:5], refs[-1]
    rows, channels = pieces * states[0][0].shape[0], q_ref.shape[1]
    here = slice(start, start + rows)
    rate_part = jnp.zeros((heads, 1), F32)
    for begin in range(0, channels, LANES):
        lanes = pl.ds(begin, LANES)
        entering, after = picked(size, states, lanes)
        terms = entering * q_ref[here, lanes] + after * (
            r_ref[here, lanes] + slope_ref[:, lanes] * entering
        )
        row = row_ref[:, lanes] + jnp.sum(terms, axis=0, keepdims=True)
        if final:
            rate_part = rate_part + head_column(row, heads, channels // heads, begin)
        else:
            out_ref[:, lanes] = row
    if final:
        base = parts_ref[...]
        out_ref[...] = jnp.concatenate([base[:1] + to_row(rate_part), base[1:]], axis=0)


def share_kernel(size, pieces, start, *refs):
    states, refs = [refs[3 * i : 3 * i + 3] for i in range(pieces)], refs[3 * pieces :]
    high_ref, low_ref, scaled_ref, sum_b_ref, sum_c_ref = refs[:5]
    rows, channels = pieces * states[0][0].shape[0], scaled_ref.shape[1]
    here = slice(start, start + rows)
    grad_b = sum_b_ref[:, here]
    grad_c = sum_c_ref[:, here]
    for begin in range(0, channels, LANES):
        lanes = pl.ds(begin, LANES)
        entering, after = picked(size, states, lanes)
        enter_high, enter_low = split(entering, 2)
        after_high, after_low = split(after, 2)
        high, low, scaled = high_ref[:, lanes], low_ref[:, lanes], scaled_ref[:, lanes]
        grad_c = grad_c + mm_nt(high, enter_high) + (mm_nt(high, enter_low) + mm_nt(low, enter_high))
        grad_b = grad_b + mm_nt(scaled, after_high) + mm_nt(scaled, after_low)
    refs[-1][...] = jnp.concatenate([grad_b, grad_c], axis=1)


def rest_kernel(size, pieces, *refs):
    states, refs = [refs[3 * i : 3 * i + 3] for i in range(pieces)], refs[3 * pieces :]
    (
        v_ref, b_ref, c_ref, coef_ref, mamba_ref, inner_ref, growth_ref, fall_ref, gy_ref,
        gcum_ref, decay_ref, neg_ref, _, gv_ref, gg_ref, gs_ref, total_ref,
    ) = refs
    length, channels = v_ref.shape
    heads = gcum_ref.shape[0]
    width = channels // heads
    block_b, block_c = b_ref[...], c_ref[...]
    grad_cum = gcum_ref[...]
    grad_total = jnp.zeros((heads, 1), F32)
    for first in range(0, channels, LANES):
        here = pl.ds(first, LANES)
        entering, after = picked(size, states, here)
        enter_high, enter_low = split(entering, 2)
        after_high, after_low = split(after, 2)
        inter = growth_ref[:, here] * (mm(block_c, enter_high) + mm(block_c, enter_low))
        outer = fall_ref[:, here] * (mm(block_b, after_high) + mm(block_b, after_low))
        gg_ref[0, :, here] = (coef_ref[:, here] * (mamba_ref[:, here] + inter)).astype(BF16)
        gv_ref[0, :, here] = (inner_ref[:, here] + outer).astype(BF16)
        pulled = v_ref[:, here].astype(F32) * outer
        high, low = split(gy_ref[:, here] * inter - pulled, 2)
        head_rows = jnp.where(head_map(heads, width, first, LANES), 1.0, 0.0).astype(BF16)
        grad_cum = grad_cum + mm_nt(head_rows, high) + mm_nt(head_rows, low)
        total_row = jnp.sum(pulled, axis=0, keepdims=True) + decay_ref[:, here] * jnp.sum(
            after * entering, axis=0, keepdims=True
        )
        grad_total = grad_total + head_column(total_row, heads, width, first)
    gs_ref[0] = neg_ref[...] * (scan_tokens(grad_cum, True) + grad_total)
    total_ref[...] = to_row(grad_total)


def tree(values):
    while len(values) > 1:
        values = [sum(values[i + 1 : i + 2], values[i]) for i in range(0, len(values), 2)]
    return values[0]


def add_kernel(x_ref, y_ref, *refs):
    refs[-1][...] = x_ref[...] + y_ref[...]


def last_kernel(counts, *refs):
    refs, (gb_ref, gc_ref, rate_ref, skip_ref) = refs[:-4], refs[-4:]
    sums = []
    for count in counts:
        sums.append(tree([ref[...] for ref in refs[:count]]))
        refs = refs[count:]
    *shares, small = sums
    start = 0
    for both in shares:
        rows = both.shape[1] // 2
        gb_ref[0, :, start : start + rows] = both[:, :rows]
        gc_ref[0, :, start : start + rows] = both[:, rows:]
        start += rows
    rate_ref[...] = small[:1]
    skip_ref[...] = small[1:]


def call(kernel, outs, scratch=(), flops=0, space=pltpu.VMEM, after=()):
    def run(*args):
        if space == pltpu.HBM:
            args = [pltpu.with_memory_space_constraint(a, space) for a in args]
        specs = [pl.BlockSpec(memory_space=space)] * len(args)
        specs += [pl.BlockSpec(memory_space=pl.ANY)] * len(after)
        args = (*args, *after)
        size = sum(a.size * a.dtype.itemsize for a in (*args, *outs))
        return pl.pallas_call(
            kernel,
            out_shape=tuple(outs),
            in_specs=specs,
            out_specs=tuple(pl.BlockSpec(memory_space=pltpu.VMEM) for _ in outs),
            scratch_shapes=list(scratch),
            compiler_params=pltpu.CompilerParams(vmem_limit_bytes=VMEM_LIMIT),
            cost_estimate=pl.CostEstimate(flops=flops, bytes_accessed=size, transcendentals=0),
        )(*args)

    return run


def swap(x, axis, size, bit):
    return lax.ppermute(x, axis, [(i, i ^ bit) for i in range(size)])


def hop(x, sizes, step):
    size, copies = sizes["seq"], sizes["replica"]
    pairs = []
    for copy in range(copies):
        for place in range(size):
            to = (copy ^ 1 if copies % 2 == 0 else copy, place)
            for low in (step, size - 2 - step):
                if place in (low, low + 1):
                    to = (copy, 2 * low + 1 - place)
            pairs.append((copy * size + place, to[0] * size + to[1]))
    return lax.ppermute(x, ("replica", "seq"), pairs)


def pass_kernel(*refs):
    got_ref, base_ref, decay_ref = refs[:3]
    refs[-1][...] = decay_ref[...] * got_ref[...] + base_ref[...]


def pass_on(got, base, decay, after):
    return call(pass_kernel, [jax.ShapeDtypeStruct(base.shape, F32)], flops=2 * base.size, after=after)(
        got, base, decay
    )[0]


def chain(sizes, mine, other, decay, work):
    chunks = len(mine)
    size = sizes["seq"]
    if size == 1:
        for k in sorted(work):
            work[k](())
        return [(x, x, x) for x in mine]
    if size % 2:
        raise NotImplementedError
    index = lax.axis_index("seq")
    place = jnp.minimum(index, size - 1 - index)
    middle = size // 2 - 1
    got = {(0, c): hop(mine[c], sizes, 0) for c in range(chunks)}
    steps = [
        (at + c + (LAG if at > middle else 0), at, c) for at in range(1, size - 1) for c in range(chunks)
    ]
    token = ()
    for count, (_, at, c) in enumerate(sorted(steps)):
        if count in work:
            token = work[count](token)
        if at > middle and c > 1:
            token = (*token, got[at, c - 2])
        base = mine[c] if at <= middle else other[c]
        pay = pass_on(got[at - 1, c], base, decay, token)
        got[at, c] = hop(pay, sizes, at)
        token = (pay,)
    for k in sorted(work):
        if k >= len(steps):
            token = work[k](token)
    states = []
    for c in range(chunks):
        first, second, last = got[0, c], got[middle, c], got[size - 2, c]
        for at in range(1, middle):
            first = jnp.where(place == at + 1, got[at, c], first)
        for at in range(middle + 1, size - 2):
            second = jnp.where(place == size - 2 - at, got[at, c], second)
        states.append((first, second, last))
    return states


def sum_terms(x, axis, size):
    if size == 1:
        return [x]
    if size == 4:
        return [x] + [swap(x, axis, size, bit) for bit in (1, 2, 3)]
    if size & (size - 1):
        return [lax.psum(x, axis)]
    bit = 1
    while 2 * bit < size:
        x = x + swap(x, axis, size, bit)
        bit *= 2
    return [x, swap(x, axis, size, bit)]


def small_terms(x, axes, sizes, between):
    bits = [(axis, 1 << k) for axis in axes for k in range(sizes[axis].bit_length() - 1)]
    if any(sizes[axis] & (sizes[axis] - 1) for axis in axes):
        x = lax.psum(x, tuple(axes))
        between((x,))
        return [x]
    after = ()
    for count, (axis, bit) in enumerate(bits):
        theirs = swap(x, axis, sizes[axis], bit)
        if count == len(bits) - 1:
            break
        x = call(add_kernel, [jax.ShapeDtypeStruct(x.shape, F32)], after=after)(x, theirs)[0]
        after = between((x,)) if count == 0 else ()
    if len(bits) < 2:
        between((x,))
    return [x, theirs] if bits else [x]


def shards(sizes, values, gate_in, in_b, in_c, step_sizes, log_rates, skip_gain, grad_out):
    like = jax.ShapeDtypeStruct
    length, channels = values.shape[1:]
    heads = step_sizes.shape[1]
    state = in_b.shape[2]
    seq = sizes["seq"]
    rows = state // CHUNKS
    wide = like((length, channels), F32)
    wide_b = like((length, channels), BF16)
    share = like((length, state), F32)
    small = like((heads, length), F32)
    row = like((1, channels), F32)
    piece = like((rows, channels), F32)
    maps = like((length, state), BF16)

    out = call(
        functools.partial(states_kernel, CHUNKS, seq),
        [wide_b, wide_b, wide_b, maps, maps, small, small, row, row, like((1, heads), F32)]
        + [piece] * (2 * CHUNKS),
        [
            pltpu.VMEM((heads, length), F32),
            pltpu.VMEM((1, heads), F32),
            pltpu.SemaphoreType.DMA((8,)),
        ],
        flops=8 * length * channels * state,
        space=pltpu.HBM,
    )(
        values[0], gate_in[0], grad_out[0], in_b[0], in_c[0], step_sizes[0],
        log_rates.reshape(1, heads), skip_gain.reshape(1, heads),
    )
    vals, gate, grad, block_b, block_c, cumulative, negative, decay, slope, skip = out[:10]
    mine, other = out[10 : 10 + CHUNKS], out[10 + CHUNKS :]

    made = {}

    def intra(after):
        made["intra"] = call(
            intra_kernel,
            [wide, wide, share, share],
            [
                pltpu.VMEM((channels, length), BF16),
                pltpu.VMEM((channels, length), F32),
                pltpu.VMEM((length, length), F32),
            ],
            flops=16 * length * length * channels,
        )(vals, gate, grad, block_b, block_c, cumulative)
        return (made["intra"][2],)

    def prepare(after):
        made["prepare"] = call(
            prepare_kernel,
            [wide] * 6 + [wide_b] * 3 + [like((state, channels), F32)] * 2 + [small, like((2, heads), F32)],
            flops=16 * length * state * channels,
        )(
            vals, gate, grad, block_b, block_c, cumulative, skip,
            *made["intra"][:2], *(after if after else made["intra"][2:3]),
        )
        return (made["prepare"][-2],)

    states = chain(sizes, mine, other, decay, {0: intra, max(seq - 2, 0) * CHUNKS - 1: prepare})
    sum_b, sum_c = made["intra"][2:]
    (
        coef, mamba, inner, growth, fall, grad_y, high, low, scaled, q, r, grad_cum, parts,
    ) = made["prepare"]

    rate_row = jnp.zeros((1, channels), F32)
    terms, counts = [], []
    for i in range(PARTS):
        final = i == PARTS - 1
        count = CHUNKS // PARTS
        own = [x for group in states[i * count : (i + 1) * count] for x in group]
        rate_row = call(
            functools.partial(rate_kernel, seq, count, i * rows * count, heads, final),
            [like((2, heads), F32) if final else row],
        )(*own, q, r, slope, rate_row, parts)[0]
        share_of = call(
            functools.partial(share_kernel, seq, count, i * rows * count),
            [like((length, 2 * rows * count), F32)],
            flops=10 * length * channels * rows * count,
            after=(rate_row,),
        )(*own, high, low, scaled, sum_b, sum_c)[0]
        own = sum_terms(share_of, "tensor", sizes["tensor"])
        terms += own
        counts.append(len(own))

    def rest(after):
        made["rest"] = call(
            functools.partial(rest_kernel, seq, CHUNKS),
            [like((1, length, channels), BF16)] * 2
            + [like((1, heads, length), F32), like((1, heads), F32)],
            flops=10 * length * channels * state,
            after=after,
        )(
            *(x for group in states for x in group),
            vals, block_b, block_c, coef, mamba, inner, growth, fall, grad_y, grad_cum, decay, negative,
        )
        return (made["rest"][3],)

    own = small_terms(rate_row, ("replica", "seq"), sizes, rest)
    terms += own
    counts.append(len(own))
    grad_values, grad_gate, grad_steps, _ = made["rest"]
    grad_b, grad_c, rate_sum, skip_sum = call(
        functools.partial(last_kernel, tuple(counts)),
        [like((1, length, state), F32)] * 2 + [like((1, heads), F32)] * 2,
    )(*terms)
    return (
        grad_values,
        grad_gate,
        grad_b,
        grad_c,
        grad_steps,
        rate_sum.reshape(heads),
        skip_sum.reshape(heads),
    )


def solution(mesh):
    in_specs = (
        P("replica", "seq", "tensor"),
        P("replica", "seq", "tensor"),
        P("replica", "seq", None),
        P("replica", "seq", None),
        P("replica", "tensor", "seq"),
        P("tensor"),
        P("tensor"),
        P("replica", "seq", "tensor"),
    )
    out_specs = (
        P("replica", "seq", "tensor"),
        P("replica", "seq", "tensor"),
        P("replica", "seq", None),
        P("replica", "seq", None),
        P("replica", "tensor", "seq"),
        P("tensor"),
        P("tensor"),
    )
    body = functools.partial(shards, dict(mesh.shape))
    return jax.shard_map(body, mesh=mesh, in_specs=in_specs, out_specs=out_specs, check_vma=False)
```

profile of v0, /device:TPU:0, one launch (start us, length us, event | category | flops | bytes accessed | tf_op | source)
XLA Modules:
  0.0 50.1 jit_solution(17545469917033760167)
XLA Ops:
  0.6 2.8 %shard_map.135 = (bf16[256,1024]{1,0:T(8,128)(2,1)S(1)}, bf16[256,1024]{1,0:T(8,128)(2,1)S(1)}, bf16[256,1024]{1,0:T(8,128)(2,1)S(1)}, bf16[256,128]{1,0:T(8,128...) custom-call(bf16[256,1024]{1,0:T(8,128)(2,1)} %bitcast.10, ...), custom_call_target="tpu_custom_call" | custom-call | flops 268435456 | bytes 4513984 | tf_op jit(solution)/shard_map/pallas_call | solution.py:391
  3.4 3.1 %collective-permute-start = (f32[32,1024]{1,0:T(8,128)S(1)}, f32[32,1024]{1,0:T(8,128)S(1)}, u32[]{:S(2)}, u32[]{:S(2)}) collective-permute-start(f32[32,1024]{1,0:T(8,128)S(1)} %get-tuple-element.50.refs_1_), channel_id=1, source_target_pairs={{0,4},{4,0},{8,12},{12,8},{16,20},{20,16},{24,28},{28,24},{1,5},{5... | collective-permute-start | bytes 393224 | tf_op jit(solution)/shard_map/ppermute | solution.py:418
  6.5 0.1 collective-permute-start.4
  6.6 1.9 %collective-permute-start.3 = (f32[32,1024]{1,0:T(8,128)S(1)}, f32[32,1024]{1,0:T(8,128)S(1)}, u32[]{:S(2)}, u32[]{:S(2)}) collective-permute-start(f32[32,1024]{1,0:T(8,128)S(1)} %get-tuple-element.61.refs_1_), channel_id=1, source_target_pairs={{0,4},{4,0},{8,12},{12,8},{16,20},{20,16},{24,28},{28,24},{1,5},{5... | collective-permute-start | bytes 393224 | tf_op jit(solution)/shard_map/ppermute | solution.py:418
  8.5 0.1 collective-permute-start.2
  8.6 2.5 %shard_map.136 = (f32[256,1024]{1,0:T(8,128)S(1)}, f32[256,1024]{1,0:T(8,128)S(1)}, f32[256,128]{1,0:T(8,128)S(1)}, f32[256,128]{1,0:T(8,128)S(1)}) custom-call(bf16[256,1024]{1,0:T(8,128)(2,1)S(1)} %get-tuple-element.52.v_ref.refs_12_, bf16[256,1024]{1,0:T(8,128)(2,1)S(1)} %get-tuple-element.53.gate_ref, bf16[256,1024]{1,0:T(8,128)(2,1)S(1)} %get-tuple-element.54.go_ref, ...), custom_call_target="tpu_custom_call" | custom-call | flops 1073741824 | bytes 4079616 | tf_op jit(solution)/shard_map/pallas_call | solution.py:391
  11.1 0.0 collective-permute-done.refs_0_
  11.2 0.1 collective-permute-start.1
  11.3 2.4 %collective-permute-done.4.refs_0_.refs_3_ = f32[32,1024]{1,0:T(8,128)S(1)} collective-permute-done((f32[32,1024]{1,0:T(8,128)S(1)}, f32[32,1024]{1,0:T(8,128)S(1)}, u32[]{:S(2)}, u32[]{:S(2)}) %collective-permute-start.4) | collective-permute-done | bytes 131104 | tf_op jit(solution)/shard_map/ppermute | solution.py:418
  13.7 0.1 collective-permute-start.6
  13.7 2.7 %collective-permute-done.3.refs_0_.refs_6_ = f32[32,1024]{1,0:T(8,128)S(1)} collective-permute-done((f32[32,1024]{1,0:T(8,128)S(1)}, f32[32,1024]{1,0:T(8,128)S(1)}, u32[]{:S(2)}, u32[]{:S(2)}) %collective-permute-start.3) | collective-permute-done | bytes 131104 | tf_op jit(solution)/shard_map/ppermute | solution.py:418
  16.5 0.1 collective-permute-start.8
  16.5 1.9 %collective-permute-done.2.refs_0_.refs_3_.refs_9_ = f32[32,1024]{1,0:T(8,128)S(1)} collective-permute-done((f32[32,1024]{1,0:T(8,128)S(1)}, f32[32,1024]{1,0:T(8,128)S(1)}, u32[]{:S(2)}, u32[]{:S(2)}) %collective-permute-start.2) | collective-permute-done | bytes 131104 | tf_op jit(solution)/shard_map/ppermute | solution.py:418
  18.4 0.0 collective-permute-done.1.refs_0_.refs_1_
  18.5 1.8 %collective-permute-start.5 = (f32[32,1024]{1,0:T(8,128)S(1)}, f32[32,1024]{1,0:T(8,128)S(1)}, u32[]{:S(2)}, u32[]{:S(2)}) collective-permute-start(f32[32,1024]{1,0:T(8,128)S(1)} %shard_map.141.refs_3_), channel_id=1, source_target_pairs={{0,4},{4,0},{8,12},{12,8},{16,20},{20,16},{24,28},{28,24},{1,5},{5... | collective-permute-start | bytes 393224 | tf_op jit(solution)/shard_map/ppermute | solution.py:418
  20.3 0.0 collective-permute-start.10
  20.3 0.0 collective-permute-done.6.refs_0_.refs_4_
  20.3 3.2 %collective-permute-start.7 = (f32[32,1024]{1,0:T(8,128)S(1)}, f32[32,1024]{1,0:T(8,128)S(1)}, u32[]{:S(2)}, u32[]{:S(2)}) collective-permute-start(f32[32,1024]{1,0:T(8,128)S(1)} %shard_map.142.refs_3_), channel_id=1, source_target_pairs={{0,4},{4,0},{8,12},{12,8},{16,20},{20,16},{24,28},{28,24},{1,5},{5... | collective-permute-start | bytes 393224 | tf_op jit(solution)/shard_map/ppermute | solution.py:418
  23.5 0.0 collective-permute-done.8.refs_0_.refs_1_.refs_7_
  23.5 0.0 collective-permute-done.5.refs_4_.refs_2_
  23.6 2.5 %collective-permute-start.9 = (f32[32,1024]{1,0:T(8,128)S(1)}, f32[32,1024]{1,0:T(8,128)S(1)}, u32[]{:S(2)}, u32[]{:S(2)}) collective-permute-start(f32[32,1024]{1,0:T(8,128)S(1)} %shard_map.143.after_ref), channel_id=1, source_target_pairs={{0,4},{4,0},{8,12},{12,8},{16,20},{20,16},{24,28},{28,24},{1,5},{5... | collective-permute-start | bytes 393224 | tf_op jit(solution)/shard_map/ppermute | solution.py:418
  26.1 2.5 %shard_map.144 = (f32[256,1024]{1,0:T(8,128)S(1)}, f32[256,1024]{1,0:T(8,128)S(1)}, f32[256,1024]{1,0:T(8,128)S(1)}, f32[256,1024]{1,0:T(8,128)S(1)}, f32[256,10...) custom-call(bf16[256,1024]{1,0:T(8,128)(2,1)S(1)} %get-tuple-element, ...), custom_call_target="tpu_custom_call" | custom-call | flops 536870912 | bytes 12878016 | tf_op jit(solution)/shard_map/pallas_call | solution.py:391
  28.7 0.0 collective-permute-done.10.refs_0_.refs_4_.refs_10_
  28.7 0.0 collective-permute-done.7.refs_4_.refs_5_
  28.7 1.1 %collective-permute-start.11 = (f32[32,1024]{1,0:T(8,128)S(1)}, f32[32,1024]{1,0:T(8,128)S(1)}, u32[]{:S(2)}, u32[]{:S(2)}) collective-permute-start(f32[32,1024]{1,0:T(8,128)S(1)} %shard_map.145), channel_id=1, source_target_pairs={{0,4},{4,0},{8,12},{12,8},{16,20},{20,16},{24,28},{28,24},{1,5},{5... | collective-permute-start | bytes 393224 | tf_op jit(solution)/shard_map/ppermute | solution.py:418
  29.8 0.1 shard_map.146.refs_9_.refs_11_
  29.9 0.9 %shard_map.150.refs_0_ = f32[256,128]{1,0:T(8,128)S(1)} custom-call(f32[32,1024]{1,0:T(8,128)S(1)} %collective-permute-done.refs_0_, f32[32,1024]{1,0:T(8,128)S(1)} %collective-permute-done.1.refs_0_.refs_1_, f32[32,1024]{1,0:T(8,128)S(1)} %collective-permute-done.5.refs_4_.refs_2_, f32[32,1024]{1,0:T(8,128)S(1)} %collective-permute-done.4.refs_0_.refs_3_, ...), custom_call_target="tpu_custom_call" | custom-call | flops 167772160 | bytes 2756608 | tf_op jit(solution)/shard_map/pallas_call | solution.py:391
  30.8 1.5 %collective-permute-start.13 = (f32[256,128]{1,0:T(8,128)S(1)}, f32[256,128]{1,0:T(8,128)S(1)}, u32[]{:S(2)}, u32[]{:S(2)}) collective-permute-start(f32[256,128]{1,0:T(8,128)S(1)} %shard_map.150.refs_0_), channel_id=1, source_target_pairs={{0,1},{1,0},{2,3},{3,2},{4,5},{5,4},{6,7},{7,6},{8,9},{9,8},{10,11... | collective-permute-start | bytes 393224 | tf_op jit(solution)/shard_map/ppermute | solution.py:405
  32.4 1.5 %collective-permute-start.14 = (f32[256,128]{1,0:T(8,128)S(1)}, f32[256,128]{1,0:T(8,128)S(1)}, u32[]{:S(2)}, u32[]{:S(2)}) collective-permute-start(f32[256,128]{1,0:T(8,128)S(1)} %shard_map.150.refs_0_), channel_id=1, source_target_pairs={{0,2},{1,3},{2,0},{3,1},{4,6},{5,7},{6,4},{7,5},{8,10},{9,11},{10,... | collective-permute-start | bytes 393224 | tf_op jit(solution)/shard_map/ppermute | solution.py:405
  33.9 0.5 collective-permute-start.15
  34.4 0.0 collective-permute-done.11.refs_5_.refs_11_
  34.4 0.0 collective-permute-done.9.refs_2_.refs_8_
  34.4 0.2 shard_map.147.x_ref.refs_11_
  34.6 0.0 collective-permute-start.12
  34.7 1.0 %shard_map.151.refs_4_ = f32[256,128]{1,0:T(8,128)S(1)} custom-call(f32[32,1024]{1,0:T(8,128)S(1)} %collective-permute-done.3.refs_0_.refs_6_, f32[32,1024]{1,0:T(8,128)S(1)} %collective-permute-done.8.refs_0_.refs_1_.refs_7_, f32[32,1024]{1,0:T(8,128)S(1)} %collective-permute-done.9.refs_2_.refs_8_, ...), custom_call_target="tpu_custom_call" | custom-call | flops 167772160 | bytes 2752640 | tf_op jit(solution)/shard_map/pallas_call | solution.py:391
  35.7 1.6 %collective-permute-start.16 = (f32[256,128]{1,0:T(8,128)S(1)}, f32[256,128]{1,0:T(8,128)S(1)}, u32[]{:S(2)}, u32[]{:S(2)}) collective-permute-start(f32[256,128]{1,0:T(8,128)S(1)} %shard_map.151.refs_4_), channel_id=1, source_target_pairs={{0,1},{1,0},{2,3},{3,2},{4,5},{5,4},{6,7},{7,6},{8,9},{9,8},{10,11... | collective-permute-start | bytes 393224 | tf_op jit(solution)/shard_map/ppermute | solution.py:405
  37.2 0.0 collective-permute-done.12.y_ref
  37.3 1.0 %collective-permute-start.19 = (f32[2,16]{1,0:T(2,128)S(1)}, f32[2,16]{1,0:T(2,128)S(1)}, u32[]{:S(2)}, u32[]{:S(2)}) collective-permute-start(f32[2,16]{1,0:T(2,128)S(1)} %shard_map.148.refs_24_.x_ref), channel_id=1, source_target_pairs={{0,4},{4,0},{8,12},{12,8},{1,5},{5,1},{9,13},{13,9},{2,6},{6,2},{1... | collective-permute-start | bytes 392 | tf_op jit(solution)/shard_map/ppermute | solution.py:405
  38.3 0.0 collective-permute-done.13.refs_1_
  38.3 1.5 %collective-permute-start.17 = (f32[256,128]{1,0:T(8,128)S(1)}, f32[256,128]{1,0:T(8,128)S(1)}, u32[]{:S(2)}, u32[]{:S(2)}) collective-permute-start(f32[256,128]{1,0:T(8,128)S(1)} %shard_map.151.refs_4_), channel_id=1, source_target_pairs={{0,2},{1,3},{2,0},{3,1},{4,6},{5,7},{6,4},{7,5},{8,10},{9,11},{10,... | collective-permute-start | bytes 393224 | tf_op jit(solution)/shard_map/ppermute | solution.py:405
  39.8 1.0 %collective-permute-done.19.y_ref = f32[2,16]{1,0:T(2,128)S(1)} collective-permute-done((f32[2,16]{1,0:T(2,128)S(1)}, f32[2,16]{1,0:T(2,128)S(1)}, u32[]{:S(2)}, u32[]{:S(2)}) %collective-permute-start.19) | collective-permute-done | bytes 160 | tf_op jit(solution)/shard_map/ppermute | solution.py:405
  40.8 1.5 %collective-permute-start.18 = (f32[256,128]{1,0:T(8,128)S(1)}, f32[256,128]{1,0:T(8,128)S(1)}, u32[]{:S(2)}, u32[]{:S(2)}) collective-permute-start(f32[256,128]{1,0:T(8,128)S(1)} %shard_map.151.refs_4_), channel_id=1, source_target_pairs={{0,3},{1,2},{2,1},{3,0},{4,7},{5,6},{6,5},{7,4},{8,11},{9,10},{10,... | collective-permute-start | bytes 393224 | tf_op jit(solution)/shard_map/ppermute | solution.py:405
  42.3 2.5 %shard_map.149 = (bf16[1,256,1024]{2,1,0:T(8,128)(2,1)}, bf16[1,256,1024]{2,1,0:T(8,128)(2,1)}, f32[1,16,256]{2,1,0:T(8,128)}, f32[1,16]{1,0:T(1,128)S(1)}) custom-call(f32[32,1024]{1,0:T(8,128)S(1)} %collective-permute-done.refs_0_, f32[32,1024]{1,0:T(8,128)S(1)} %collective-permute-done.1.refs_0_.refs_1_, ...), custom_call_target="tpu_custom_call" | custom-call | flops 335544320 | bytes 9621696 | tf_op jit(solution)/shard_map/pallas_call | solution.py:391
  44.8 0.0 collective-permute-done.14.refs_2_
  44.8 2.7 %collective-permute-start.20 = (f32[2,16]{1,0:T(2,128)S(1)}, f32[2,16]{1,0:T(2,128)S(1)}, u32[]{:S(2)}, u32[]{:S(2)}) collective-permute-start(f32[2,16]{1,0:T(2,128)S(1)} %shard_map.152.refs_8_), channel_id=1, source_target_pairs={{0,8},{4,12},{8,0},{12,4},{1,9},{5,13},{9,1},{13,5},{2,10},{6,14},... | collective-permute-start | bytes 392 | tf_op jit(solution)/shard_map/ppermute | solution.py:405
  47.5 0.0 collective-permute-done.15.refs_3_
  47.5 1.8 %collective-permute-done.20.refs_9_ = f32[2,16]{1,0:T(2,128)S(1)} collective-permute-done((f32[2,16]{1,0:T(2,128)S(1)}, f32[2,16]{1,0:T(2,128)S(1)}, u32[]{:S(2)}, u32[]{:S(2)}) %collective-permute-start.20) | collective-permute-done | bytes 160 | tf_op jit(solution)/shard_map/ppermute | solution.py:405
  49.3 0.0 collective-permute-done.16.refs_5_
  49.3 0.0 collective-permute-done.17.refs_6_
  49.3 0.0 collective-permute-done.18.refs_7_
  49.3 0.8 %shard_map.153 = (f32[1,256,128]{2,1,0:T(8,128)}, f32[1,256,128]{2,1,0:T(8,128)}, f32[1,16]{1,0:T(1,128)}, f32[1,16]{1,0:T(1,128)}) custom-call(f32[256,128]{1,0:T(8,128)S(1)} %shard_map.150.refs_0_, f32[256,128]{1,0:T(8,128)S(1)} %collective-permute-done.13.refs_1_, f32[256,128]{1,0:T(8,128)S(1)} %collective-permute-done.14.refs_2_, ...), custom_call_target="tpu_custom_call" | custom-call | bytes 1311104 | tf_op jit(solution)/shard_map/pallas_call | solution.py:391
  (11 shorter events, 0.2 us)
Async XLA Ops:
  3.4 7.7 %collective-permute-start = (f32[32,1024]{1,0:T(8,128)S(1)}, f32[32,1024]{1,0:T(8,128)S(1)}, u32[]{:S(2)}, u32[]{:S(2)}) collective-permute-start(f32[32,1024]{1,0:T(8,128)S(1)} %get-tuple-element.50.refs_1_), channel_id=1, source_target_pairs={{0,4},{4,0},{8,12},{12,8},{16,20},{20,16},{24,28},{28,24},{1,5},{5... | collective-permute-start | bytes 393224 | tf_op jit(solution)/shard_map/ppermute | solution.py:418
  6.5 7.1 %collective-permute-start.4 = (f32[32,1024]{1,0:T(8,128)S(1)}, f32[32,1024]{1,0:T(8,128)S(1)}, u32[]{:S(2)}, u32[]{:S(2)}) collective-permute-start(f32[32,1024]{1,0:T(8,128)S(1)} %get-tuple-element.62.refs_1_), channel_id=1, source_target_pairs={{0,4},{4,0},{8,12},{12,8},{16,20},{20,16},{24,28},{28,24},{1,5},{5... | collective-permute-start | bytes 393224 | tf_op jit(solution)/shard_map/ppermute | solution.py:418
  6.6 9.9 %collective-permute-start.3 = (f32[32,1024]{1,0:T(8,128)S(1)}, f32[32,1024]{1,0:T(8,128)S(1)}, u32[]{:S(2)}, u32[]{:S(2)}) collective-permute-start(f32[32,1024]{1,0:T(8,128)S(1)} %get-tuple-element.61.refs_1_), channel_id=1, source_target_pairs={{0,4},{4,0},{8,12},{12,8},{16,20},{20,16},{24,28},{28,24},{1,5},{5... | collective-permute-start | bytes 393224 | tf_op jit(solution)/shard_map/ppermute | solution.py:418
  8.5 9.9 %collective-permute-start.2 = (f32[32,1024]{1,0:T(8,128)S(1)}, f32[32,1024]{1,0:T(8,128)S(1)}, u32[]{:S(2)}, u32[]{:S(2)}) collective-permute-start(f32[32,1024]{1,0:T(8,128)S(1)} %get-tuple-element.60.refs_1_), channel_id=1, source_target_pairs={{0,4},{4,0},{8,12},{12,8},{16,20},{20,16},{24,28},{28,24},{1,5},{5... | collective-permute-start | bytes 393224 | tf_op jit(solution)/shard_map/ppermute | solution.py:418
  11.2 7.3 %collective-permute-start.1 = (f32[32,1024]{1,0:T(8,128)S(1)}, f32[32,1024]{1,0:T(8,128)S(1)}, u32[]{:S(2)}, u32[]{:S(2)}) collective-permute-start(f32[32,1024]{1,0:T(8,128)S(1)} %shard_map.137.refs_3_), channel_id=1, source_target_pairs={{0,16},{4,8},{8,4},{12,28},{16,0},{20,24},{24,20},{28,12},{1,17},{... | collective-permute-start | bytes 393224 | tf_op jit(solution)/shard_map/ppermute | solution.py:418
  13.7 6.6 %collective-permute-start.6 = (f32[32,1024]{1,0:T(8,128)S(1)}, f32[32,1024]{1,0:T(8,128)S(1)}, u32[]{:S(2)}, u32[]{:S(2)}) collective-permute-start(f32[32,1024]{1,0:T(8,128)S(1)} %shard_map.138.refs_3_), channel_id=1, source_target_pairs={{0,16},{4,8},{8,4},{12,28},{16,0},{20,24},{24,20},{28,12},{1,17},{... | collective-permute-start | bytes 393224 | tf_op jit(solution)/shard_map/ppermute | solution.py:418
  16.5 7.1 %collective-permute-start.8 = (f32[32,1024]{1,0:T(8,128)S(1)}, f32[32,1024]{1,0:T(8,128)S(1)}, u32[]{:S(2)}, u32[]{:S(2)}) collective-permute-start(f32[32,1024]{1,0:T(8,128)S(1)} %shard_map.139.refs_3_), channel_id=1, source_target_pairs={{0,16},{4,8},{8,4},{12,28},{16,0},{20,24},{24,20},{28,12},{1,17},{... | collective-permute-start | bytes 393224 | tf_op jit(solution)/shard_map/ppermute | solution.py:418
  18.5 5.1 %collective-permute-start.5 = (f32[32,1024]{1,0:T(8,128)S(1)}, f32[32,1024]{1,0:T(8,128)S(1)}, u32[]{:S(2)}, u32[]{:S(2)}) collective-permute-start(f32[32,1024]{1,0:T(8,128)S(1)} %shard_map.141.refs_3_), channel_id=1, source_target_pairs={{0,4},{4,0},{8,12},{12,8},{16,20},{20,16},{24,28},{28,24},{1,5},{5... | collective-permute-start | bytes 393224 | tf_op jit(solution)/shard_map/ppermute | solution.py:418
  20.3 8.4 %collective-permute-start.10 = (f32[32,1024]{1,0:T(8,128)S(1)}, f32[32,1024]{1,0:T(8,128)S(1)}, u32[]{:S(2)}, u32[]{:S(2)}) collective-permute-start(f32[32,1024]{1,0:T(8,128)S(1)} %shard_map.140.refs_3_), channel_id=1, source_target_pairs={{0,16},{4,8},{8,4},{12,28},{16,0},{20,24},{24,20},{28,12},{1,17},{... | collective-permute-start | bytes 393224 | tf_op jit(solution)/shard_map/ppermute | solution.py:418
  20.3 8.4 %collective-permute-start.7 = (f32[32,1024]{1,0:T(8,128)S(1)}, f32[32,1024]{1,0:T(8,128)S(1)}, u32[]{:S(2)}, u32[]{:S(2)}) collective-permute-start(f32[32,1024]{1,0:T(8,128)S(1)} %shard_map.142.refs_3_), channel_id=1, source_target_pairs={{0,4},{4,0},{8,12},{12,8},{16,20},{20,16},{24,28},{28,24},{1,5},{5... | collective-permute-start | bytes 393224 | tf_op jit(solution)/shard_map/ppermute | solution.py:418
  23.6 10.8 %collective-permute-start.9 = (f32[32,1024]{1,0:T(8,128)S(1)}, f32[32,1024]{1,0:T(8,128)S(1)}, u32[]{:S(2)}, u32[]{:S(2)}) collective-permute-start(f32[32,1024]{1,0:T(8,128)S(1)} %shard_map.143.after_ref), channel_id=1, source_target_pairs={{0,4},{4,0},{8,12},{12,8},{16,20},{20,16},{24,28},{28,24},{1,5},{5... | collective-permute-start | bytes 393224 | tf_op jit(solution)/shard_map/ppermute | solution.py:418
  28.7 5.7 %collective-permute-start.11 = (f32[32,1024]{1,0:T(8,128)S(1)}, f32[32,1024]{1,0:T(8,128)S(1)}, u32[]{:S(2)}, u32[]{:S(2)}) collective-permute-start(f32[32,1024]{1,0:T(8,128)S(1)} %shard_map.145), channel_id=1, source_target_pairs={{0,4},{4,0},{8,12},{12,8},{16,20},{20,16},{24,28},{28,24},{1,5},{5... | collective-permute-start | bytes 393224 | tf_op jit(solution)/shard_map/ppermute | solution.py:418
  30.8 7.4 %collective-permute-start.13 = (f32[256,128]{1,0:T(8,128)S(1)}, f32[256,128]{1,0:T(8,128)S(1)}, u32[]{:S(2)}, u32[]{:S(2)}) collective-permute-start(f32[256,128]{1,0:T(8,128)S(1)} %shard_map.150.refs_0_), channel_id=1, source_target_pairs={{0,1},{1,0},{2,3},{3,2},{4,5},{5,4},{6,7},{7,6},{8,9},{9,8},{10,11... | collective-permute-start | bytes 393224 | tf_op jit(solution)/shard_map/ppermute | solution.py:405
  32.4 12.4 %collective-permute-start.14 = (f32[256,128]{1,0:T(8,128)S(1)}, f32[256,128]{1,0:T(8,128)S(1)}, u32[]{:S(2)}, u32[]{:S(2)}) collective-permute-start(f32[256,128]{1,0:T(8,128)S(1)} %shard_map.150.refs_0_), channel_id=1, source_target_pairs={{0,2},{1,3},{2,0},{3,1},{4,6},{5,7},{6,4},{7,5},{8,10},{9,11},{10,... | collective-permute-start | bytes 393224 | tf_op jit(solution)/shard_map/ppermute | solution.py:405
  33.9 13.6 %collective-permute-start.15 = (f32[256,128]{1,0:T(8,128)S(1)}, f32[256,128]{1,0:T(8,128)S(1)}, u32[]{:S(2)}, u32[]{:S(2)}) collective-permute-start(f32[256,128]{1,0:T(8,128)S(1)} %shard_map.150.refs_0_), channel_id=1, source_target_pairs={{0,3},{1,2},{2,1},{3,0},{4,7},{5,6},{6,5},{7,4},{8,11},{9,10},{10,... | collective-permute-start | bytes 393224 | tf_op jit(solution)/shard_map/ppermute | solution.py:405
  34.6 2.6 %collective-permute-start.12 = (f32[2,16]{1,0:T(2,128)S(1)}, f32[2,16]{1,0:T(2,128)S(1)}, u32[]{:S(2)}, u32[]{:S(2)}) collective-permute-start(f32[2,16]{1,0:T(2,128)S(1)} %shard_map.147.x_ref.refs_11_), channel_id=1, source_target_pairs={{0,16},{16,0},{1,17},{17,1},{2,18},{18,2},{3,19},{19,3},{4,20},{20... | collective-permute-start | bytes 392 | tf_op jit(solution)/shard_map/ppermute | solution.py:405
  35.7 13.6 %collective-permute-start.16 = (f32[256,128]{1,0:T(8,128)S(1)}, f32[256,128]{1,0:T(8,128)S(1)}, u32[]{:S(2)}, u32[]{:S(2)}) collective-permute-start(f32[256,128]{1,0:T(8,128)S(1)} %shard_map.151.refs_4_), channel_id=1, source_target_pairs={{0,1},{1,0},{2,3},{3,2},{4,5},{5,4},{6,7},{7,6},{8,9},{9,8},{10,11... | collective-permute-start | bytes 393224 | tf_op jit(solution)/shard_map/ppermute | solution.py:405
  37.3 3.6 %collective-permute-start.19 = (f32[2,16]{1,0:T(2,128)S(1)}, f32[2,16]{1,0:T(2,128)S(1)}, u32[]{:S(2)}, u32[]{:S(2)}) collective-permute-start(f32[2,16]{1,0:T(2,128)S(1)} %shard_map.148.refs_24_.x_ref), channel_id=1, source_target_pairs={{0,4},{4,0},{8,12},{12,8},{1,5},{5,1},{9,13},{13,9},{2,6},{6,2},{1... | collective-permute-start | bytes 392 | tf_op jit(solution)/shard_map/ppermute | solution.py:405
  38.3 11.0 %collective-permute-start.17 = (f32[256,128]{1,0:T(8,128)S(1)}, f32[256,128]{1,0:T(8,128)S(1)}, u32[]{:S(2)}, u32[]{:S(2)}) collective-permute-start(f32[256,128]{1,0:T(8,128)S(1)} %shard_map.151.refs_4_), channel_id=1, source_target_pairs={{0,2},{1,3},{2,0},{3,1},{4,6},{5,7},{6,4},{7,5},{8,10},{9,11},{10,... | collective-permute-start | bytes 393224 | tf_op jit(solution)/shard_map/ppermute | solution.py:405
  40.8 8.5 %collective-permute-start.18 = (f32[256,128]{1,0:T(8,128)S(1)}, f32[256,128]{1,0:T(8,128)S(1)}, u32[]{:S(2)}, u32[]{:S(2)}) collective-permute-start(f32[256,128]{1,0:T(8,128)S(1)} %shard_map.151.refs_4_), channel_id=1, source_target_pairs={{0,3},{1,2},{2,1},{3,0},{4,7},{5,6},{6,5},{7,4},{8,11},{9,10},{10,... | collective-permute-start | bytes 393224 | tf_op jit(solution)/shard_map/ppermute | solution.py:405
  44.8 4.5 %collective-permute-start.20 = (f32[2,16]{1,0:T(2,128)S(1)}, f32[2,16]{1,0:T(2,128)S(1)}, u32[]{:S(2)}, u32[]{:S(2)}) collective-permute-start(f32[2,16]{1,0:T(2,128)S(1)} %shard_map.152.refs_8_), channel_id=1, source_target_pairs={{0,8},{4,12},{8,0},{12,4},{1,9},{5,13},{9,1},{13,5},{2,10},{6,14},... | collective-permute-start | bytes 392 | tf_op jit(solution)/shard_map/ppermute | solution.py:405
where the time goes:
time: 50.3 us; the launch traced here: 50.1 us
  starting transfers between devices  26 us (52%)
  Pallas kernels  13.6 us (27%)
  waiting for transfers between devices  9.82 us (20%)
  between operations  0.79 us (2%)
    ppermute x12, starting transfers between devices, hop(): return lax.ppermute(x, ('replica', 'seq'), pairs)  14 us
    pallas_call x19, Pallas kernels, run(): pl.pallas_call(kernel, out_shape=tuple(outs), in_specs=specs, out_specs=t...  13.6 us
    ppermute x9, starting transfers between devices, swap(): return lax.ppermute(x, axis, [(i, i ^ bit) for i in range(size)])  11.9 us
    ppermute x12, waiting for transfers between devices, hop(): return lax.ppermute(x, ('replica', 'seq'), pairs)  7.03 us
    ppermute x9, waiting for transfers between devices, swap(): return lax.ppermute(x, axis, [(i, i ^ bit) for i in range(size)])  2.79 us
  transfers between devices with their start and end apart: 21, of which 5 were waited for; matrix products, arithmetic and copies ran while one was open for 0% of the time, Pallas kernels for 20%

commit v1 on v0

--- a/solution.py
+++ b/solution.py
@@ -13,7 +13,7 @@
 LANES = 256
 CHUNKS = 4
 PARTS = 2
-LAG = 2
+LAG = 1
 
 
 def split(x, parts):
@@ -209,23 +209,45 @@
     sum_b_ref[...] = mm(high, c_ref[...]) + mm(low, c_ref[...])
 
 
-def prepare_kernel(
-    v_ref, gate_ref, go_ref, b_ref, c_ref, cum_ref, skip_ref, intra_ref, in_inner_ref, after_ref,
-    coef_ref, mamba_ref, inner_ref, growth_ref, fall_ref, gy_ref,
-    high_ref, low_ref, scaled_ref, q_ref, r_ref, gcum_ref, parts_ref,
+def factors_kernel(
+    v_ref, gate_ref, go_ref, b_ref, c_ref, cum_ref, after_ref,
+    high_ref, low_ref, scaled_ref, q_ref, r_ref,
 ):
     length, channels = v_ref.shape
     heads = cum_ref.shape[0]
     width = channels // heads
     cumulative = cum_ref[...]
-    total = cumulative[:, -1:]
-    left_over = total - cumulative
-    growth_three = rows_of_three(jnp.exp(cumulative))
-    fall_three = rows_of_three(jnp.exp(left_over))
+    left_over = cumulative[:, -1:] - cumulative
+    growth = rows_of_three(jnp.exp(cumulative))
+    fall = rows_of_three(jnp.exp(left_over))
     growth_slope = rows_of_three(cumulative * jnp.exp(cumulative))
     fall_slope = rows_of_three(left_over * jnp.exp(left_over))
     b_t = b_ref[...].astype(F32).T.astype(BF16)
     c_t = c_ref[...].astype(F32).T.astype(BF16)
+    for first in range(0, channels, LANES):
+        here = pl.ds(first, LANES)
+        _, _, grad_y = gate_parts(gate_ref[:, here], go_ref[:, here])
+        vals = v_ref[:, here].astype(F32)
+        high, low = split(spread(growth, first, LANES, width) * grad_y, 2)
+        high_ref[:, here] = high
+        low_ref[:, here] = low
+        scaled_ref[:, here] = (spread(fall, first, LANES, width) * vals).astype(BF16)
+        high, low = split(spread(growth_slope, first, LANES, width) * grad_y, 2)
+        q_ref[:, here] = mm(c_t, high) + mm(c_t, low)
+        high, low = split(spread(fall_slope, first, LANES, width) * vals, 2)
+        r_ref[:, here] = mm(b_t, high) + mm(b_t, low)
+
+
+def prepare_kernel(
+    v_ref, gate_ref, go_ref, cum_ref, skip_ref, intra_ref, in_inner_ref, after_ref,
+    coef_ref, mamba_ref, inner_ref, growth_ref, fall_ref, gy_ref, gcum_ref, parts_ref,
+):
+    length, channels = v_ref.shape
+    heads = cum_ref.shape[0]
+    width = channels // heads
+    cumulative = cum_ref[...]
+    growth_three = rows_of_three(jnp.exp(cumulative))
+    fall_three = rows_of_three(jnp.exp(cumulative[:, -1:] - cumulative))
     skip_column = to_column(skip_ref[...])
     grad_cum = jnp.zeros((heads, length), F32)
     skip_part = jnp.zeros((heads, 1), F32)
@@ -234,16 +256,10 @@
         wide, sigmoid, grad_y = gate_parts(gate_ref[:, here], go_ref[:, here])
         vals = v_ref[:, here].astype(F32)
         skip = channel_row(skip_column, heads, width, first)
-        growth = spread(growth_three, first, LANES, width)
-        fall = spread(fall_three, first, LANES, width)
-        growth_ref[:, here] = growth
-        fall_ref[:, here] = fall
+        growth_ref[:, here] = spread(growth_three, first, LANES, width)
+        fall_ref[:, here] = spread(fall_three, first, LANES, width)
         gy_ref[:, here] = grad_y
         coef_ref[:, here] = go_ref[:, here].astype(F32) * sigmoid * (1.0 + wide * (1.0 - sigmoid))
-        high, low = split(growth * grad_y, 2)
-        high_ref[:, here] = high
-        low_ref[:, here] = low
-        scaled_ref[:, here] = (fall * vals).astype(BF16)
         intra = intra_ref[:, here]
         inner = in_inner_ref[:, here]
         mamba_ref[:, here] = intra + skip * vals
@@ -253,10 +269,6 @@
         grad_cum = grad_cum + mm_nt(head_rows, high) + mm_nt(head_rows, low)
         skip_row = jnp.sum(grad_y * vals, axis=0, keepdims=True)
         skip_part = skip_part + head_column(skip_row, heads, width, first)
-        high, low = split(spread(growth_slope, first, LANES, width) * grad_y, 2)
-        q_ref[:, here] = mm(c_t, high) + mm(c_t, low)
-        high, low = split(spread(fall_slope, first, LANES, width) * vals, 2)
-        r_ref[:, here] = mm(b_t, high) + mm(b_t, low)
     gcum_ref[...] = grad_cum
     rate_part = jnp.sum(grad_cum * cumulative, axis=1, keepdims=True)
     parts_ref[...] = jnp.concatenate([to_row(rate_part), to_row(skip_part)], axis=0)
@@ -449,8 +461,8 @@
     for count, (_, at, c) in enumerate(sorted(steps)):
         if count in work:
             token = work[count](token)
-        if at > middle and c > 1:
-            token = (*token, got[at, c - 2])
+        if at > middle and c > 2:
+            token = (*token, got[at, c - 3])
         base = mine[c] if at <= middle else other[c]
         pay = pass_on(got[at - 1, c], base, decay, token)
         got[at, c] = hop(pay, sizes, at)
@@ -549,22 +561,30 @@
         )(vals, gate, grad, block_b, block_c, cumulative)
         return (made["intra"][2],)
 
+    def factors(after):
+        made["factors"] = call(
+            factors_kernel,
+            [wide_b] * 3 + [like((state, channels), F32)] * 2,
+            flops=8 * length * state * channels,
+        )(vals, gate, grad, block_b, block_c, cumulative, *(after if after else made["intra"][2:3]))
+        return (made["factors"][-1],)
+
     def prepare(after):
         made["prepare"] = call(
             prepare_kernel,
-            [wide] * 6 + [wide_b] * 3 + [like((state, channels), F32)] * 2 + [small, like((2, heads), F32)],
-            flops=16 * length * state * channels,
+            [wide] * 6 + [small, like((2, heads), F32)],
+            flops=8 * length * state * channels,
         )(
-            vals, gate, grad, block_b, block_c, cumulative, skip,
+            vals, gate, grad, cumulative, skip,
             *made["intra"][:2], *(after if after else made["intra"][2:3]),
         )
-        return (made["prepare"][-2],)
-
-    states = chain(sizes, mine, other, decay, {0: intra, max(seq - 2, 0) * CHUNKS - 1: prepare})
+        return (made["prepare"][-1],)
+
+    last_middle = (max(seq // 2 - 1, 1) - 1) * CHUNKS + CHUNKS
+    states = chain(sizes, mine, other, decay, {0: intra, 1: factors, last_middle + LAG: prepare})
     sum_b, sum_c = made["intra"][2:]
-    (
-        coef, mamba, inner, growth, fall, grad_y, high, low, scaled, q, r, grad_cum, parts,
-    ) = made["prepare"]
+    high, low, scaled, q, r = made["factors"]
+    coef, mamba, inner, growth, fall, grad_y, grad_cum, parts = made["prepare"]
 
     rate_row = jnp.zeros((1, channels), F32)
     terms, counts = [], []

time: 50.3 us -> 49.3 us (0.980)
  waiting for transfers between devices: 9.82 us -> 6.73 us
  starting transfers between devices: 26 us -> 27.8 us
    ppermute x12, waiting for transfers between devices: 7.03 us -> 2.17 us  [hop(): return lax.ppermute(x, ('replica', 'seq'), pairs)]
    ppermute x12, starting transfers between devices: 14 us -> 17.7 us  [hop(): return lax.ppermute(x, ('replica', 'seq'), pairs)]
    ppermute x9, waiting for transfers between devices: 2.79 us -> 4.57 us  [swap(): return lax.ppermute(x, axis, [(i, i ^ bit) for i in range(size)])]
    ppermute x9, starting transfers between devices: 11.9 us -> 10.2 us  [swap(): return lax.ppermute(x, axis, [(i, i ^ bit) for i in range(size)])]
    pallas_call x19 -> x20, Pallas kernels: 13.6 us -> 13.8 us  [run(): pl.pallas_call(kernel, out_shape=tuple(outs), in_specs=specs, out_specs=t...]
  transfers between devices with their start and end apart: 21 -> 21, of which waited for: 5 -> 5; matrix products, arithmetic and copies ran while one was open for 0% -> 0% of each run, Pallas kernels for 20% -> 21%
where the time goes in v1:
time: 49.3 us; the launch traced here: 49.2 us
  starting transfers between devices  27.8 us (56%)
  Pallas kernels  13.8 us (28%)
  waiting for transfers between devices  6.73 us (14%)
  between operations  0.79 us (2%)
    ppermute x12, starting transfers between devices, hop(): return lax.ppermute(x, ('replica', 'seq'), pairs)  17.7 us
    pallas_call x20, Pallas kernels, run(): pl.pallas_call(kernel, out_shape=tuple(outs), in_specs=specs, out_specs=t...  13.8 us
    ppermute x9, starting transfers between devices, swap(): return lax.ppermute(x, axis, [(i, i ^ bit) for i in range(size)])  10.2 us
    ppermute x9, waiting for transfers between devices, swap(): return lax.ppermute(x, axis, [(i, i ^ bit) for i in range(size)])  4.57 us
    ppermute x12, waiting for transfers between devices, hop(): return lax.ppermute(x, ('replica', 'seq'), pairs)  2.17 us
  transfers between devices with their start and end apart: 21, of which 5 were waited for; matrix products, arithmetic and copies ran while one was open for 0% of the time, Pallas kernels for 21%

profile of v1, /device:TPU:0, one launch (start us, length us, event | category | flops | bytes accessed | tf_op | source)
XLA Modules:
  0.0 49.2 jit_solution(18242667647595535014)
XLA Ops:
  0.6 2.8 %shard_map.135 = (bf16[256,1024]{1,0:T(8,128)(2,1)S(1)}, bf16[256,1024]{1,0:T(8,128)(2,1)S(1)}, bf16[256,1024]{1,0:T(8,128)(2,1)S(1)}, bf16[256,128]{1,0:T(8,128...) custom-call(bf16[256,1024]{1,0:T(8,128)(2,1)} %bitcast.10, ...), custom_call_target="tpu_custom_call" | custom-call | flops 268435456 | bytes 4513984 | tf_op jit(solution)/shard_map/pallas_call | solution.py:403
  3.4 3.1 %collective-permute-start = (f32[32,1024]{1,0:T(8,128)S(1)}, f32[32,1024]{1,0:T(8,128)S(1)}, u32[]{:S(2)}, u32[]{:S(2)}) collective-permute-start(f32[32,1024]{1,0:T(8,128)S(1)} %get-tuple-element.50.refs_1_), channel_id=1, source_target_pairs={{0,4},{4,0},{8,12},{12,8},{16,20},{20,16},{24,28},{28,24},{1,5},{5... | collective-permute-start | bytes 393224 | tf_op jit(solution)/shard_map/ppermute | solution.py:430
  6.5 0.1 collective-permute-start.3
  6.6 1.9 %collective-permute-start.2 = (f32[32,1024]{1,0:T(8,128)S(1)}, f32[32,1024]{1,0:T(8,128)S(1)}, u32[]{:S(2)}, u32[]{:S(2)}) collective-permute-start(f32[32,1024]{1,0:T(8,128)S(1)} %get-tuple-element.60.refs_1_), channel_id=1, source_target_pairs={{0,4},{4,0},{8,12},{12,8},{16,20},{20,16},{24,28},{28,24},{1,5},{5... | collective-permute-start | bytes 393224 | tf_op jit(solution)/shard_map/ppermute | solution.py:430
  8.5 2.5 %shard_map.136 = (f32[256,1024]{1,0:T(8,128)S(1)}, f32[256,1024]{1,0:T(8,128)S(1)}, f32[256,128]{1,0:T(8,128)S(1)}, f32[256,128]{1,0:T(8,128)S(1)}) custom-call(bf16[256,1024]{1,0:T(8,128)(2,1)S(1)} %get-tuple-element.52.v_ref.refs_12_, bf16[256,1024]{1,0:T(8,128)(2,1)S(1)} %get-tuple-element.53.gate_ref, bf16[256,1024]{1,0:T(8,128)(2,1)S(1)} %get-tuple-element.54.go_ref, ...), custom_call_target="tpu_custom_call" | custom-call | flops 1073741824 | bytes 4079616 | tf_op jit(solution)/shard_map/pallas_call | solution.py:403
  11.1 0.0 collective-permute-done.refs_0_
  11.1 0.1 collective-permute-start.1
  11.2 3.4 %collective-permute-start.6 = (f32[32,1024]{1,0:T(8,128)S(1)}, f32[32,1024]{1,0:T(8,128)S(1)}, u32[]{:S(2)}, u32[]{:S(2)}) collective-permute-start(f32[32,1024]{1,0:T(8,128)S(1)} %get-tuple-element.67.refs_1_), channel_id=1, source_target_pairs={{0,4},{4,0},{8,12},{12,8},{16,20},{20,16},{24,28},{28,24},{1,5},{5... | collective-permute-start | bytes 393224 | tf_op jit(solution)/shard_map/ppermute | solution.py:430
  14.6 1.3 %shard_map.138 = (bf16[256,1024]{1,0:T(8,128)(2,1)S(1)}, bf16[256,1024]{1,0:T(8,128)(2,1)S(1)}, bf16[256,1024]{1,0:T(8,128)(2,1)S(1)}, f32[128,1024]{1,0:T(8,128)S(1)}, f32[128,1024]{1,0:T(8,128)S(1)}) custom-call(bf16[256,1024]{1,0:T(8,128)(2,1)S(1)} %get-tuple-element.52.v_ref.refs_12_, bf16[256,1024]{1,0:T(8,128)(2,1)S(1)} %get-tuple-element.53.gate_ref, ...), custom_call_target="tpu_custom_call" | custom-call | flops 268435456 | bytes 4472832 | tf_op jit(solution)/shard_map/pallas_call | solution.py:403
  15.8 0.0 collective-permute-done.3.refs_0_.refs_3_
  15.9 0.1 collective-permute-start.5
  16.0 0.5 collective-permute-done.2.refs_0_.refs_6_
  16.5 0.1 collective-permute-start.8
  16.6 0.0 collective-permute-done.1.refs_0_.refs_1_
  16.6 3.7 %collective-permute-start.4 = (f32[32,1024]{1,0:T(8,128)S(1)}, f32[32,1024]{1,0:T(8,128)S(1)}, u32[]{:S(2)}, u32[]{:S(2)}) collective-permute-start(f32[32,1024]{1,0:T(8,128)S(1)} %shard_map.141.refs_3_), channel_id=1, source_target_pairs={{0,4},{4,0},{8,12},{12,8},{16,20},{20,16},{24,28},{28,24},{1,5},{5... | collective-permute-start | bytes 393224 | tf_op jit(solution)/shard_map/ppermute | solution.py:430
  20.3 0.0 collective-permute-done.6.refs_0_.refs_3_.refs_9_
  20.3 0.1 collective-permute-start.10
  20.4 1.4 %shard_map.143 = (f32[256,1024]{1,0:T(8,128)S(1)}, f32[256,1024]{1,0:T(8,128)S(1)}, f32[256,1024]{1,0:T(8,128)S(1)}, f32[256,1024]{1,0:T(8,128)S(1)}, f32[256,10...) custom-call(bf16[256,1024]{1,0:T(8,128)(2,1)S(1)} %get-tuple-element.52.v_ref.refs_12_, ...), custom_call_target="tpu_custom_call" | custom-call | flops 268435456 | bytes 10125504 | tf_op jit(solution)/shard_map/pallas_call | solution.py:403
  21.8 0.0 collective-permute-done.5.refs_0_.refs_4_
  21.8 1.6 %collective-permute-start.7 = (f32[32,1024]{1,0:T(8,128)S(1)}, f32[32,1024]{1,0:T(8,128)S(1)}, u32[]{:S(2)}, u32[]{:S(2)}) collective-permute-start(f32[32,1024]{1,0:T(8,128)S(1)} %shard_map.144.refs_3_), channel_id=1, source_target_pairs={{0,4},{4,0},{8,12},{12,8},{16,20},{20,16},{24,28},{28,24},{1,5},{5... | collective-permute-start | bytes 393224 | tf_op jit(solution)/shard_map/ppermute | solution.py:430
  23.5 0.0 collective-permute-done.8.refs_0_.refs_1_.refs_7_
  23.5 1.7 %collective-permute-start.9 = (f32[32,1024]{1,0:T(8,128)S(1)}, f32[32,1024]{1,0:T(8,128)S(1)}, u32[]{:S(2)}, u32[]{:S(2)}) collective-permute-start(f32[32,1024]{1,0:T(8,128)S(1)} %shard_map.145.refs_3_), channel_id=1, source_target_pairs={{0,4},{4,0},{8,12},{12,8},{16,20},{20,16},{24,28},{28,24},{1,5},{5... | collective-permute-start | bytes 393224 | tf_op jit(solution)/shard_map/ppermute | solution.py:430
  25.2 0.0 collective-permute-done.4.refs_4_.refs_2_
  25.2 0.0 collective-permute-done.10.refs_0_.refs_4_.refs_10_
  25.2 1.9 %collective-permute-start.11 = (f32[32,1024]{1,0:T(8,128)S(1)}, f32[32,1024]{1,0:T(8,128)S(1)}, u32[]{:S(2)}, u32[]{:S(2)}) collective-permute-start(f32[32,1024]{1,0:T(8,128)S(1)} %shard_map.146), channel_id=1, source_target_pairs={{0,4},{4,0},{8,12},{12,8},{16,20},{20,16},{24,28},{28,24},{1,5},{5... | collective-permute-start | bytes 393224 | tf_op jit(solution)/shard_map/ppermute | solution.py:430
  27.1 1.1 %collective-permute-done.7.refs_5_ = f32[32,1024]{1,0:T(8,128)S(1)} collective-permute-done((f32[32,1024]{1,0:T(8,128)S(1)}, f32[32,1024]{1,0:T(8,128)S(1)}, u32[]{:S(2)}, u32[]{:S(2)}) %collective-permute-start.7) | collective-permute-done | bytes 131104 | tf_op jit(solution)/shard_map/ppermute | solution.py:430
  28.2 0.1 shard_map.147.refs_9_.refs_11_
  28.3 0.9 %shard_map.151.refs_0_ = f32[256,128]{1,0:T(8,128)S(1)} custom-call(f32[32,1024]{1,0:T(8,128)S(1)} %collective-permute-done.refs_0_, f32[32,1024]{1,0:T(8,128)S(1)} %collective-permute-done.1.refs_0_.refs_1_, f32[32,1024]{1,0:T(8,128)S(1)} %collective-permute-done.4.refs_4_.refs_2_, f32[32,1024]{1,0:T(8,128)S(1)} %collective-permute-done.3.refs_0_.refs_3_, ...), custom_call_target="tpu_custom_call" | custom-call | flops 167772160 | bytes 2756608 | tf_op jit(solution)/shard_map/pallas_call | solution.py:403
  29.2 1.6 %collective-permute-start.13 = (f32[256,128]{1,0:T(8,128)S(1)}, f32[256,128]{1,0:T(8,128)S(1)}, u32[]{:S(2)}, u32[]{:S(2)}) collective-permute-start(f32[256,128]{1,0:T(8,128)S(1)} %shard_map.151.refs_0_), channel_id=1, source_target_pairs={{0,1},{1,0},{2,3},{3,2},{4,5},{5,4},{6,7},{7,6},{8,9},{9,8},{10,11... | collective-permute-start | bytes 393224 | tf_op jit(solution)/shard_map/ppermute | solution.py:417
  30.8 1.5 %collective-permute-start.14 = (f32[256,128]{1,0:T(8,128)S(1)}, f32[256,128]{1,0:T(8,128)S(1)}, u32[]{:S(2)}, u32[]{:S(2)}) collective-permute-start(f32[256,128]{1,0:T(8,128)S(1)} %shard_map.151.refs_0_), channel_id=1, source_target_pairs={{0,2},{1,3},{2,0},{3,1},{4,6},{5,7},{6,4},{7,5},{8,10},{9,11},{10,... | collective-permute-start | bytes 393224 | tf_op jit(solution)/shard_map/ppermute | solution.py:417
  32.3 0.5 collective-permute-start.15
  32.8 0.0 collective-permute-done.9.refs_2_.refs_8_
  32.8 0.6 %collective-permute-done.11.refs_5_.refs_11_ = f32[32,1024]{1,0:T(8,128)S(1)} collective-permute-done((f32[32,1024]{1,0:T(8,128)S(1)}, f32[32,1024]{1,0:T(8,128)S(1)}, u32[]{:S(2)}, u32[]{:S(2)}) %collective-permute-start.11) | collective-permute-done | bytes 131104 | tf_op jit(solution)/shard_map/ppermute | solution.py:430
  33.4 0.2 shard_map.148.x_ref.refs_11_
  33.6 0.0 collective-permute-start.12
  33.7 1.0 %shard_map.152.refs_4_ = f32[256,128]{1,0:T(8,128)S(1)} custom-call(f32[32,1024]{1,0:T(8,128)S(1)} %collective-permute-done.2.refs_0_.refs_6_, f32[32,1024]{1,0:T(8,128)S(1)} %collective-permute-done.8.refs_0_.refs_1_.refs_7_, f32[32,1024]{1,0:T(8,128)S(1)} %collective-permute-done.9.refs_2_.refs_8_, ...), custom_call_target="tpu_custom_call" | custom-call | flops 167772160 | bytes 2752640 | tf_op jit(solution)/shard_map/pallas_call | solution.py:403
  34.7 1.6 %collective-permute-start.16 = (f32[256,128]{1,0:T(8,128)S(1)}, f32[256,128]{1,0:T(8,128)S(1)}, u32[]{:S(2)}, u32[]{:S(2)}) collective-permute-start(f32[256,128]{1,0:T(8,128)S(1)} %shard_map.152.refs_4_), channel_id=1, source_target_pairs={{0,1},{1,0},{2,3},{3,2},{4,5},{5,4},{6,7},{7,6},{8,9},{9,8},{10,11... | collective-permute-start | bytes 393224 | tf_op jit(solution)/shard_map/ppermute | solution.py:417
  36.2 0.0 collective-permute-done.12.y_ref
  36.3 1.1 %collective-permute-start.19 = (f32[2,16]{1,0:T(2,128)S(1)}, f32[2,16]{1,0:T(2,128)S(1)}, u32[]{:S(2)}, u32[]{:S(2)}) collective-permute-start(f32[2,16]{1,0:T(2,128)S(1)} %shard_map.149.refs_24_.x_ref), channel_id=1, source_target_pairs={{0,4},{4,0},{8,12},{12,8},{1,5},{5,1},{9,13},{13,9},{2,6},{6,2},{1... | collective-permute-start | bytes 392 | tf_op jit(solution)/shard_map/ppermute | solution.py:417
  37.3 0.0 collective-permute-done.13.refs_1_
  37.3 1.5 %collective-permute-start.17 = (f32[256,128]{1,0:T(8,128)S(1)}, f32[256,128]{1,0:T(8,128)S(1)}, u32[]{:S(2)}, u32[]{:S(2)}) collective-permute-start(f32[256,128]{1,0:T(8,128)S(1)} %shard_map.152.refs_4_), channel_id=1, source_target_pairs={{0,2},{1,3},{2,0},{3,1},{4,6},{5,7},{6,4},{7,5},{8,10},{9,11},{10,... | collective-permute-start | bytes 393224 | tf_op jit(solution)/shard_map/ppermute | solution.py:417
  38.9 1.0 %collective-permute-done.19.y_ref = f32[2,16]{1,0:T(2,128)S(1)} collective-permute-done((f32[2,16]{1,0:T(2,128)S(1)}, f32[2,16]{1,0:T(2,128)S(1)}, u32[]{:S(2)}, u32[]{:S(2)}) %collective-permute-start.19) | collective-permute-done | bytes 160 | tf_op jit(solution)/shard_map/ppermute | solution.py:417
  39.8 1.5 %collective-permute-start.18 = (f32[256,128]{1,0:T(8,128)S(1)}, f32[256,128]{1,0:T(8,128)S(1)}, u32[]{:S(2)}, u32[]{:S(2)}) collective-permute-start(f32[256,128]{1,0:T(8,128)S(1)} %shard_map.152.refs_4_), channel_id=1, source_target_pairs={{0,3},{1,2},{2,1},{3,0},{4,7},{5,6},{6,5},{7,4},{8,11},{9,10},{10,... | collective-permute-start | bytes 393224 | tf_op jit(solution)/shard_map/ppermute | solution.py:417
  41.3 2.5 %shard_map.150 = (bf16[1,256,1024]{2,1,0:T(8,128)(2,1)}, bf16[1,256,1024]{2,1,0:T(8,128)(2,1)}, f32[1,16,256]{2,1,0:T(8,128)}, f32[1,16]{1,0:T(1,128)S(1)}) custom-call(f32[32,1024]{1,0:T(8,128)S(1)} %collective-permute-done.refs_0_, f32[32,1024]{1,0:T(8,128)S(1)} %collective-permute-done.1.refs_0_.refs_1_, ...), custom_call_target="tpu_custom_call" | custom-call | flops 335544320 | bytes 9621696 | tf_op jit(solution)/shard_map/pallas_call | solution.py:403
  43.8 0.0 collective-permute-done.14.refs_2_
  43.8 0.9 %collective-permute-start.20 = (f32[2,16]{1,0:T(2,128)S(1)}, f32[2,16]{1,0:T(2,128)S(1)}, u32[]{:S(2)}, u32[]{:S(2)}) collective-permute-start(f32[2,16]{1,0:T(2,128)S(1)} %shard_map.153.refs_8_), channel_id=1, source_target_pairs={{0,8},{4,12},{8,0},{12,4},{1,9},{5,13},{9,1},{13,5},{2,10},{6,14},... | collective-permute-start | bytes 392 | tf_op jit(solution)/shard_map/ppermute | solution.py:417
  44.7 0.0 collective-permute-done.15.refs_3_
  44.7 3.6 %collective-permute-done.20.refs_9_ = f32[2,16]{1,0:T(2,128)S(1)} collective-permute-done((f32[2,16]{1,0:T(2,128)S(1)}, f32[2,16]{1,0:T(2,128)S(1)}, u32[]{:S(2)}, u32[]{:S(2)}) %collective-permute-start.20) | collective-permute-done | bytes 160 | tf_op jit(solution)/shard_map/ppermute | solution.py:417
  48.3 0.0 collective-permute-done.16.refs_5_
  48.3 0.0 collective-permute-done.17.refs_6_
  48.3 0.0 collective-permute-done.18.refs_7_
  48.3 0.8 %shard_map.154 = (f32[1,256,128]{2,1,0:T(8,128)}, f32[1,256,128]{2,1,0:T(8,128)}, f32[1,16]{1,0:T(1,128)}, f32[1,16]{1,0:T(1,128)}) custom-call(f32[256,128]{1,0:T(8,128)S(1)} %shard_map.151.refs_0_, f32[256,128]{1,0:T(8,128)S(1)} %collective-permute-done.13.refs_1_, f32[256,128]{1,0:T(8,128)S(1)} %collective-permute-done.14.refs_2_, ...), custom_call_target="tpu_custom_call" | custom-call | bytes 1311104 | tf_op jit(solution)/shard_map/pallas_call | solution.py:403
  (11 shorter events, 0.2 us)
Async XLA Ops:
  3.4 7.7 %collective-permute-start = (f32[32,1024]{1,0:T(8,128)S(1)}, f32[32,1024]{1,0:T(8,128)S(1)}, u32[]{:S(2)}, u32[]{:S(2)}) collective-permute-start(f32[32,1024]{1,0:T(8,128)S(1)} %get-tuple-element.50.refs_1_), channel_id=1, source_target_pairs={{0,4},{4,0},{8,12},{12,8},{16,20},{20,16},{24,28},{28,24},{1,5},{5... | collective-permute-start | bytes 393224 | tf_op jit(solution)/shard_map/ppermute | solution.py:430
  6.5 9.3 %collective-permute-start.3 = (f32[32,1024]{1,0:T(8,128)S(1)}, f32[32,1024]{1,0:T(8,128)S(1)}, u32[]{:S(2)}, u32[]{:S(2)}) collective-permute-start(f32[32,1024]{1,0:T(8,128)S(1)} %get-tuple-element.61.refs_1_), channel_id=1, source_target_pairs={{0,4},{4,0},{8,12},{12,8},{16,20},{20,16},{24,28},{28,24},{1,5},{5... | collective-permute-start | bytes 393224 | tf_op jit(solution)/shard_map/ppermute | solution.py:430
  6.6 9.9 %collective-permute-start.2 = (f32[32,1024]{1,0:T(8,128)S(1)}, f32[32,1024]{1,0:T(8,128)S(1)}, u32[]{:S(2)}, u32[]{:S(2)}) collective-permute-start(f32[32,1024]{1,0:T(8,128)S(1)} %get-tuple-element.60.refs_1_), channel_id=1, source_target_pairs={{0,4},{4,0},{8,12},{12,8},{16,20},{20,16},{24,28},{28,24},{1,5},{5... | collective-permute-start | bytes 393224 | tf_op jit(solution)/shard_map/ppermute | solution.py:430
  11.1 5.4 %collective-permute-start.1 = (f32[32,1024]{1,0:T(8,128)S(1)}, f32[32,1024]{1,0:T(8,128)S(1)}, u32[]{:S(2)}, u32[]{:S(2)}) collective-permute-start(f32[32,1024]{1,0:T(8,128)S(1)} %shard_map.137.after_ref), channel_id=1, source_target_pairs={{0,16},{4,8},{8,4},{12,28},{16,0},{20,24},{24,20},{28,12},{1,17},{... | collective-permute-start | bytes 393224 | tf_op jit(solution)/shard_map/ppermute | solution.py:430
  11.2 9.1 %collective-permute-start.6 = (f32[32,1024]{1,0:T(8,128)S(1)}, f32[32,1024]{1,0:T(8,128)S(1)}, u32[]{:S(2)}, u32[]{:S(2)}) collective-permute-start(f32[32,1024]{1,0:T(8,128)S(1)} %get-tuple-element.67.refs_1_), channel_id=1, source_target_pairs={{0,4},{4,0},{8,12},{12,8},{16,20},{20,16},{24,28},{28,24},{1,5},{5... | collective-permute-start | bytes 393224 | tf_op jit(solution)/shard_map/ppermute | solution.py:430
  15.9 5.9 %collective-permute-start.5 = (f32[32,1024]{1,0:T(8,128)S(1)}, f32[32,1024]{1,0:T(8,128)S(1)}, u32[]{:S(2)}, u32[]{:S(2)}) collective-permute-start(f32[32,1024]{1,0:T(8,128)S(1)} %shard_map.139.refs_3_), channel_id=1, source_target_pairs={{0,16},{4,8},{8,4},{12,28},{16,0},{20,24},{24,20},{28,12},{1,17},{... | collective-permute-start | bytes 393224 | tf_op jit(solution)/shard_map/ppermute | solution.py:430
  16.5 7.0 %collective-permute-start.8 = (f32[32,1024]{1,0:T(8,128)S(1)}, f32[32,1024]{1,0:T(8,128)S(1)}, u32[]{:S(2)}, u32[]{:S(2)}) collective-permute-start(f32[32,1024]{1,0:T(8,128)S(1)} %shard_map.140.refs_3_), channel_id=1, source_target_pairs={{0,16},{4,8},{8,4},{12,28},{16,0},{20,24},{24,20},{28,12},{1,17},{... | collective-permute-start | bytes 393224 | tf_op jit(solution)/shard_map/ppermute | solution.py:430
  16.6 8.6 %collective-permute-start.4 = (f32[32,1024]{1,0:T(8,128)S(1)}, f32[32,1024]{1,0:T(8,128)S(1)}, u32[]{:S(2)}, u32[]{:S(2)}) collective-permute-start(f32[32,1024]{1,0:T(8,128)S(1)} %shard_map.141.refs_3_), channel_id=1, source_target_pairs={{0,4},{4,0},{8,12},{12,8},{16,20},{20,16},{24,28},{28,24},{1,5},{5... | collective-permute-start | bytes 393224 | tf_op jit(solution)/shard_map/ppermute | solution.py:430
  20.3 4.9 %collective-permute-start.10 = (f32[32,1024]{1,0:T(8,128)S(1)}, f32[32,1024]{1,0:T(8,128)S(1)}, u32[]{:S(2)}, u32[]{:S(2)}) collective-permute-start(f32[32,1024]{1,0:T(8,128)S(1)} %shard_map.142.after_ref), channel_id=1, source_target_pairs={{0,16},{4,8},{8,4},{12,28},{16,0},{20,24},{24,20},{28,12},{1,17},{... | collective-permute-start | bytes 393224 | tf_op jit(solution)/shard_map/ppermute | solution.py:430
  21.8 6.4 %collective-permute-start.7 = (f32[32,1024]{1,0:T(8,128)S(1)}, f32[32,1024]{1,0:T(8,128)S(1)}, u32[]{:S(2)}, u32[]{:S(2)}) collective-permute-start(f32[32,1024]{1,0:T(8,128)S(1)} %shard_map.144.refs_3_), channel_id=1, source_target_pairs={{0,4},{4,0},{8,12},{12,8},{16,20},{20,16},{24,28},{28,24},{1,5},{5... | collective-permute-start | bytes 393224 | tf_op jit(solution)/shard_map/ppermute | solution.py:430
  23.5 9.3 %collective-permute-start.9 = (f32[32,1024]{1,0:T(8,128)S(1)}, f32[32,1024]{1,0:T(8,128)S(1)}, u32[]{:S(2)}, u32[]{:S(2)}) collective-permute-start(f32[32,1024]{1,0:T(8,128)S(1)} %shard_map.145.refs_3_), channel_id=1, source_target_pairs={{0,4},{4,0},{8,12},{12,8},{16,20},{20,16},{24,28},{28,24},{1,5},{5... | collective-permute-start | bytes 393224 | tf_op jit(solution)/shard_map/ppermute | solution.py:430
  25.2 8.2 %collective-permute-start.11 = (f32[32,1024]{1,0:T(8,128)S(1)}, f32[32,1024]{1,0:T(8,128)S(1)}, u32[]{:S(2)}, u32[]{:S(2)}) collective-permute-start(f32[32,1024]{1,0:T(8,128)S(1)} %shard_map.146), channel_id=1, source_target_pairs={{0,4},{4,0},{8,12},{12,8},{16,20},{20,16},{24,28},{28,24},{1,5},{5... | collective-permute-start | bytes 393224 | tf_op jit(solution)/shard_map/ppermute | solution.py:430
  29.2 8.1 %collective-permute-start.13 = (f32[256,128]{1,0:T(8,128)S(1)}, f32[256,128]{1,0:T(8,128)S(1)}, u32[]{:S(2)}, u32[]{:S(2)}) collective-permute-start(f32[256,128]{1,0:T(8,128)S(1)} %shard_map.151.refs_0_), channel_id=1, source_target_pairs={{0,1},{1,0},{2,3},{3,2},{4,5},{5,4},{6,7},{7,6},{8,9},{9,8},{10,11... | collective-permute-start | bytes 393224 | tf_op jit(solution)/shard_map/ppermute | solution.py:417
  30.8 13.0 %collective-permute-start.14 = (f32[256,128]{1,0:T(8,128)S(1)}, f32[256,128]{1,0:T(8,128)S(1)}, u32[]{:S(2)}, u32[]{:S(2)}) collective-permute-start(f32[256,128]{1,0:T(8,128)S(1)} %shard_map.151.refs_0_), channel_id=1, source_target_pairs={{0,2},{1,3},{2,0},{3,1},{4,6},{5,7},{6,4},{7,5},{8,10},{9,11},{10,... | collective-permute-start | bytes 393224 | tf_op jit(solution)/shard_map/ppermute | solution.py:417
  32.3 12.4 %collective-permute-start.15 = (f32[256,128]{1,0:T(8,128)S(1)}, f32[256,128]{1,0:T(8,128)S(1)}, u32[]{:S(2)}, u32[]{:S(2)}) collective-permute-start(f32[256,128]{1,0:T(8,128)S(1)} %shard_map.151.refs_0_), channel_id=1, source_target_pairs={{0,3},{1,2},{2,1},{3,0},{4,7},{5,6},{6,5},{7,4},{8,11},{9,10},{10,... | collective-permute-start | bytes 393224 | tf_op jit(solution)/shard_map/ppermute | solution.py:417
  33.6 2.6 %collective-permute-start.12 = (f32[2,16]{1,0:T(2,128)S(1)}, f32[2,16]{1,0:T(2,128)S(1)}, u32[]{:S(2)}, u32[]{:S(2)}) collective-permute-start(f32[2,16]{1,0:T(2,128)S(1)} %shard_map.148.x_ref.refs_11_), channel_id=1, source_target_pairs={{0,16},{16,0},{1,17},{17,1},{2,18},{18,2},{3,19},{19,3},{4,20},{20... | collective-permute-start | bytes 392 | tf_op jit(solution)/shard_map/ppermute | solution.py:417
  34.7 13.6 %collective-permute-start.16 = (f32[256,128]{1,0:T(8,128)S(1)}, f32[256,128]{1,0:T(8,128)S(1)}, u32[]{:S(2)}, u32[]{:S(2)}) collective-permute-start(f32[256,128]{1,0:T(8,128)S(1)} %shard_map.152.refs_4_), channel_id=1, source_target_pairs={{0,1},{1,0},{2,3},{3,2},{4,5},{5,4},{6,7},{7,6},{8,9},{9,8},{10,11... | collective-permute-start | bytes 393224 | tf_op jit(solution)/shard_map/ppermute | solution.py:417
  36.3 3.6 %collective-permute-start.19 = (f32[2,16]{1,0:T(2,128)S(1)}, f32[2,16]{1,0:T(2,128)S(1)}, u32[]{:S(2)}, u32[]{:S(2)}) collective-permute-start(f32[2,16]{1,0:T(2,128)S(1)} %shard_map.149.refs_24_.x_ref), channel_id=1, source_target_pairs={{0,4},{4,0},{8,12},{12,8},{1,5},{5,1},{9,13},{13,9},{2,6},{6,2},{1... | collective-permute-start | bytes 392 | tf_op jit(solution)/shard_map/ppermute | solution.py:417
  37.3 11.0 %collective-permute-start.17 = (f32[256,128]{1,0:T(8,128)S(1)}, f32[256,128]{1,0:T(8,128)S(1)}, u32[]{:S(2)}, u32[]{:S(2)}) collective-permute-start(f32[256,128]{1,0:T(8,128)S(1)} %shard_map.152.refs_4_), channel_id=1, source_target_pairs={{0,2},{1,3},{2,0},{3,1},{4,6},{5,7},{6,4},{7,5},{8,10},{9,11},{10,... | collective-permute-start | bytes 393224 | tf_op jit(solution)/shard_map/ppermute | solution.py:417
  39.8 8.5 %collective-permute-start.18 = (f32[256,128]{1,0:T(8,128)S(1)}, f32[256,128]{1,0:T(8,128)S(1)}, u32[]{:S(2)}, u32[]{:S(2)}) collective-permute-start(f32[256,128]{1,0:T(8,128)S(1)} %shard_map.152.refs_4_), channel_id=1, source_target_pairs={{0,3},{1,2},{2,1},{3,0},{4,7},{5,6},{6,5},{7,4},{8,11},{9,10},{10,... | collective-permute-start | bytes 393224 | tf_op jit(solution)/shard_map/ppermute | solution.py:417
  43.8 4.5 %collective-permute-start.20 = (f32[2,16]{1,0:T(2,128)S(1)}, f32[2,16]{1,0:T(2,128)S(1)}, u32[]{:S(2)}, u32[]{:S(2)}) collective-permute-start(f32[2,16]{1,0:T(2,128)S(1)} %shard_map.153.refs_8_), channel_id=1, source_target_pairs={{0,8},{4,12},{8,0},{12,4},{1,9},{5,13},{9,1},{13,5},{2,10},{6,14},... | collective-permute-start | bytes 392 | tf_op jit(solution)/shard_map/ppermute | solution.py:417

commit v2 on v1

--- a/solution.py
+++ b/solution.py
@@ -336,7 +336,7 @@
     states, refs = [refs[3 * i : 3 * i + 3] for i in range(pieces)], refs[3 * pieces :]
     (
         v_ref, b_ref, c_ref, coef_ref, mamba_ref, inner_ref, growth_ref, fall_ref, gy_ref,
-        gcum_ref, decay_ref, neg_ref, _, gv_ref, gg_ref, gs_ref, total_ref,
+        gcum_ref, decay_ref, neg_ref, *_, gv_ref, gg_ref, gs_ref,
     ) = refs
     length, channels = v_ref.shape
     heads = gcum_ref.shape[0]
@@ -362,7 +362,6 @@
         )
         grad_total = grad_total + head_column(total_row, heads, width, first)
     gs_ref[0] = neg_ref[...] * (scan_tokens(grad_cum, True) + grad_total)
-    total_ref[...] = to_row(grad_total)
 
 
 def tree(values):
@@ -373,6 +372,10 @@
 
 def add_kernel(x_ref, y_ref, *refs):
     refs[-1][...] = x_ref[...] + y_ref[...]
+
+
+def sum_kernel(*refs):
+    refs[-1][...] = tree([ref[...] for ref in refs[:-1]])
 
 
 def last_kernel(counts, *refs):
@@ -501,15 +504,12 @@
         x = lax.psum(x, tuple(axes))
         between((x,))
         return [x]
-    after = ()
     for count, (axis, bit) in enumerate(bits):
         theirs = swap(x, axis, sizes[axis], bit)
         if count == len(bits) - 1:
             break
-        x = call(add_kernel, [jax.ShapeDtypeStruct(x.shape, F32)], after=after)(x, theirs)[0]
-        after = between((x,)) if count == 0 else ()
-    if len(bits) < 2:
-        between((x,))
+        x = call(add_kernel, [jax.ShapeDtypeStruct(x.shape, F32)])(x, theirs)[0]
+    between((x,))
     return [x, theirs] if bits else [x]
 
 
@@ -587,7 +587,7 @@
     coef, mamba, inner, growth, fall, grad_y, grad_cum, parts = made["prepare"]
 
     rate_row = jnp.zeros((1, channels), F32)
-    terms, counts = [], []
+    terms, counts, done = [], [], []
     for i in range(PARTS):
         final = i == PARTS - 1
         count = CHUNKS // PARTS
@@ -603,26 +603,27 @@
             after=(rate_row,),
         )(*own, high, low, scaled, sum_b, sum_c)[0]
         own = sum_terms(share_of, "tensor", sizes["tensor"])
+        if not final:
+            own = [call(sum_kernel, [like(share_of.shape, F32)])(*own)[0]]
+            done += own
         terms += own
         counts.append(len(own))
 
     def rest(after):
         made["rest"] = call(
             functools.partial(rest_kernel, seq, CHUNKS),
-            [like((1, length, channels), BF16)] * 2
-            + [like((1, heads, length), F32), like((1, heads), F32)],
+            [like((1, length, channels), BF16)] * 2 + [like((1, heads, length), F32)],
             flops=10 * length * channels * state,
-            after=after,
+            after=(*after, *done),
         )(
             *(x for group in states for x in group),
             vals, block_b, block_c, coef, mamba, inner, growth, fall, grad_y, grad_cum, decay, negative,
         )
-        return (made["rest"][3],)
 
     own = small_terms(rate_row, ("replica", "seq"), sizes, rest)
     terms += own
     counts.append(len(own))
-    grad_values, grad_gate, grad_steps, _ = made["rest"]
+    grad_values, grad_gate, grad_steps = made["rest"]
     grad_b, grad_c, rate_sum, skip_sum = call(
         functools.partial(last_kernel, tuple(counts)),
         [like((1, length, state), F32)] * 2 + [like((1, heads), F32)] * 2,

time: 49.3 us -> 47.6 us (0.966)
  starting transfers between devices: 27.8 us -> 26.3 us
    ppermute x9, starting transfers between devices: 10.2 us -> 8.63 us  [swap(): return lax.ppermute(x, axis, [(i, i ^ bit) for i in range(size)])]
    pallas_call x20 -> x21, Pallas kernels: 13.8 us -> 13.7 us  [run(): pl.pallas_call(kernel, out_shape=tuple(outs), in_specs=specs, out_specs=t...]
  transfers between devices with their start and end apart: 21 -> 21, of which waited for: 5 -> 6; matrix products, arithmetic and copies ran while one was open for 0% -> 0% of each run, Pallas kernels for 21% -> 21%
where the time goes in v2:
time: 47.6 us; the launch traced here: 47.4 us
  starting transfers between devices  26.3 us (55%)
  Pallas kernels  13.7 us (29%)
  waiting for transfers between devices  6.55 us (14%)
  between operations  0.8 us (2%)
    ppermute x12, starting transfers between devices, hop(): return lax.ppermute(x, ('replica', 'seq'), pairs)  17.7 us
    pallas_call x21, Pallas kernels, run(): pl.pallas_call(kernel, out_shape=tuple(outs), in_specs=specs, out_specs=t...  13.7 us
    ppermute x9, starting transfers between devices, swap(): return lax.ppermute(x, axis, [(i, i ^ bit) for i in range(size)])  8.63 us
    ppermute x9, waiting for transfers between devices, swap(): return lax.ppermute(x, axis, [(i, i ^ bit) for i in range(size)])  4.39 us
    ppermute x12, waiting for transfers between devices, hop(): return lax.ppermute(x, ('replica', 'seq'), pairs)  2.16 us
  transfers between devices with their start and end apart: 21, of which 6 were waited for; matrix products, arithmetic and copies ran while one was open for 0% of the time, Pallas kernels for 21%

profile of v2, /device:TPU:0, one launch (start us, length us, event | category | flops | bytes accessed | tf_op | source)
XLA Modules:
  0.0 47.4 jit_solution(6430412623332508852)
XLA Ops:
  0.6 2.8 %shard_map.135 = (bf16[256,1024]{1,0:T(8,128)(2,1)S(1)}, bf16[256,1024]{1,0:T(8,128)(2,1)S(1)}, bf16[256,1024]{1,0:T(8,128)(2,1)S(1)}, bf16[256,128]{1,0:T(8,128...) custom-call(bf16[256,1024]{1,0:T(8,128)(2,1)} %bitcast.10, ...), custom_call_target="tpu_custom_call" | custom-call | flops 268435456 | bytes 4513984 | tf_op jit(solution)/shard_map/pallas_call | solution.py:406
  3.4 3.1 %collective-permute-start = (f32[32,1024]{1,0:T(8,128)S(1)}, f32[32,1024]{1,0:T(8,128)S(1)}, u32[]{:S(2)}, u32[]{:S(2)}) collective-permute-start(f32[32,1024]{1,0:T(8,128)S(1)} %get-tuple-element.49.refs_1_), channel_id=1, source_target_pairs={{0,4},{4,0},{8,12},{12,8},{16,20},{20,16},{24,28},{28,24},{1,5},{5... | collective-permute-start | bytes 393224 | tf_op jit(solution)/shard_map/ppermute | solution.py:433
  6.5 0.1 collective-permute-start.3
  6.6 1.9 %collective-permute-start.2 = (f32[32,1024]{1,0:T(8,128)S(1)}, f32[32,1024]{1,0:T(8,128)S(1)}, u32[]{:S(2)}, u32[]{:S(2)}) collective-permute-start(f32[32,1024]{1,0:T(8,128)S(1)} %get-tuple-element.59.refs_1_), channel_id=1, source_target_pairs={{0,4},{4,0},{8,12},{12,8},{16,20},{20,16},{24,28},{28,24},{1,5},{5... | collective-permute-start | bytes 393224 | tf_op jit(solution)/shard_map/ppermute | solution.py:433
  8.5 2.5 %shard_map.136 = (f32[256,1024]{1,0:T(8,128)S(1)}, f32[256,1024]{1,0:T(8,128)S(1)}, f32[256,128]{1,0:T(8,128)S(1)}, f32[256,128]{1,0:T(8,128)S(1)}) custom-call(bf16[256,1024]{1,0:T(8,128)(2,1)S(1)} %get-tuple-element.51.v_ref.refs_12_, bf16[256,1024]{1,0:T(8,128)(2,1)S(1)} %get-tuple-element.52.gate_ref, bf16[256,1024]{1,0:T(8,128)(2,1)S(1)} %get-tuple-element.53.go_ref, ...), custom_call_target="tpu_custom_call" | custom-call | flops 1073741824 | bytes 4079616 | tf_op jit(solution)/shard_map/pallas_call | solution.py:406
  11.1 0.0 collective-permute-done.refs_0_
  11.1 0.1 collective-permute-start.1
  11.2 3.4 %collective-permute-start.6 = (f32[32,1024]{1,0:T(8,128)S(1)}, f32[32,1024]{1,0:T(8,128)S(1)}, u32[]{:S(2)}, u32[]{:S(2)}) collective-permute-start(f32[32,1024]{1,0:T(8,128)S(1)} %get-tuple-element.66.refs_1_), channel_id=1, source_target_pairs={{0,4},{4,0},{8,12},{12,8},{16,20},{20,16},{24,28},{28,24},{1,5},{5... | collective-permute-start | bytes 393224 | tf_op jit(solution)/shard_map/ppermute | solution.py:433
  14.6 1.3 %shard_map.138 = (bf16[256,1024]{1,0:T(8,128)(2,1)S(1)}, bf16[256,1024]{1,0:T(8,128)(2,1)S(1)}, bf16[256,1024]{1,0:T(8,128)(2,1)S(1)}, f32[128,1024]{1,0:T(8,128)S(1)}, f32[128,1024]{1,0:T(8,128)S(1)}) custom-call(bf16[256,1024]{1,0:T(8,128)(2,1)S(1)} %get-tuple-element.51.v_ref.refs_12_, bf16[256,1024]{1,0:T(8,128)(2,1)S(1)} %get-tuple-element.52.gate_ref, ...), custom_call_target="tpu_custom_call" | custom-call | flops 268435456 | bytes 4472832 | tf_op jit(solution)/shard_map/pallas_call | solution.py:406
  15.8 0.0 collective-permute-done.3.refs_0_.refs_3_
  15.9 0.1 collective-permute-start.5
  16.0 0.5 %collective-permute-done.2.refs_0_.refs_6_ = f32[32,1024]{1,0:T(8,128)S(1)} collective-permute-done((f32[32,1024]{1,0:T(8,128)S(1)}, f32[32,1024]{1,0:T(8,128)S(1)}, u32[]{:S(2)}, u32[]{:S(2)}) %collective-permute-start.2) | collective-permute-done | bytes 131104 | tf_op jit(solution)/shard_map/ppermute | solution.py:433
  16.5 0.1 collective-permute-start.8
  16.6 0.0 collective-permute-done.1.refs_0_.refs_1_
  16.6 3.7 %collective-permute-start.4 = (f32[32,1024]{1,0:T(8,128)S(1)}, f32[32,1024]{1,0:T(8,128)S(1)}, u32[]{:S(2)}, u32[]{:S(2)}) collective-permute-start(f32[32,1024]{1,0:T(8,128)S(1)} %shard_map.141.refs_3_), channel_id=1, source_target_pairs={{0,4},{4,0},{8,12},{12,8},{16,20},{20,16},{24,28},{28,24},{1,5},{5... | collective-permute-start | bytes 393224 | tf_op jit(solution)/shard_map/ppermute | solution.py:433
  20.3 0.0 collective-permute-done.6.refs_0_.refs_3_.refs_9_
  20.3 0.1 collective-permute-start.10
  20.4 1.4 %shard_map.143 = (f32[256,1024]{1,0:T(8,128)S(1)}, f32[256,1024]{1,0:T(8,128)S(1)}, f32[256,1024]{1,0:T(8,128)S(1)}, f32[256,1024]{1,0:T(8,128)S(1)}, f32[256,10...) custom-call(bf16[256,1024]{1,0:T(8,128)(2,1)S(1)} %get-tuple-element.51.v_ref.refs_12_, ...), custom_call_target="tpu_custom_call" | custom-call | flops 268435456 | bytes 10125504 | tf_op jit(solution)/shard_map/pallas_call | solution.py:406
  21.8 0.0 collective-permute-done.5.refs_0_.refs_4_
  21.8 1.6 %collective-permute-start.7 = (f32[32,1024]{1,0:T(8,128)S(1)}, f32[32,1024]{1,0:T(8,128)S(1)}, u32[]{:S(2)}, u32[]{:S(2)}) collective-permute-start(f32[32,1024]{1,0:T(8,128)S(1)} %shard_map.144.refs_3_), channel_id=1, source_target_pairs={{0,4},{4,0},{8,12},{12,8},{16,20},{20,16},{24,28},{28,24},{1,5},{5... | collective-permute-start | bytes 393224 | tf_op jit(solution)/shard_map/ppermute | solution.py:433
  23.5 0.0 collective-permute-done.8.refs_0_.refs_1_.refs_7_
  23.5 1.7 %collective-permute-start.9 = (f32[32,1024]{1,0:T(8,128)S(1)}, f32[32,1024]{1,0:T(8,128)S(1)}, u32[]{:S(2)}, u32[]{:S(2)}) collective-permute-start(f32[32,1024]{1,0:T(8,128)S(1)} %shard_map.145.refs_3_), channel_id=1, source_target_pairs={{0,4},{4,0},{8,12},{12,8},{16,20},{20,16},{24,28},{28,24},{1,5},{5... | collective-permute-start | bytes 393224 | tf_op jit(solution)/shard_map/ppermute | solution.py:433
  25.2 0.0 collective-permute-done.4.refs_4_.refs_2_
  25.2 0.0 collective-permute-done.10.refs_0_.refs_4_.refs_10_
  25.2 1.9 %collective-permute-start.11 = (f32[32,1024]{1,0:T(8,128)S(1)}, f32[32,1024]{1,0:T(8,128)S(1)}, u32[]{:S(2)}, u32[]{:S(2)}) collective-permute-start(f32[32,1024]{1,0:T(8,128)S(1)} %shard_map.146), channel_id=1, source_target_pairs={{0,4},{4,0},{8,12},{12,8},{16,20},{20,16},{24,28},{28,24},{1,5},{5... | collective-permute-start | bytes 393224 | tf_op jit(solution)/shard_map/ppermute | solution.py:433
  27.1 1.1 %collective-permute-done.7.refs_5_ = f32[32,1024]{1,0:T(8,128)S(1)} collective-permute-done((f32[32,1024]{1,0:T(8,128)S(1)}, f32[32,1024]{1,0:T(8,128)S(1)}, u32[]{:S(2)}, u32[]{:S(2)}) %collective-permute-start.7) | collective-permute-done | bytes 131104 | tf_op jit(solution)/shard_map/ppermute | solution.py:433
  28.2 0.1 shard_map.147.refs_9_.refs_11_
  28.3 0.9 %shard_map.151.refs_0_ = f32[256,128]{1,0:T(8,128)S(1)} custom-call(f32[32,1024]{1,0:T(8,128)S(1)} %collective-permute-done.refs_0_, f32[32,1024]{1,0:T(8,128)S(1)} %collective-permute-done.1.refs_0_.refs_1_, f32[32,1024]{1,0:T(8,128)S(1)} %collective-permute-done.4.refs_4_.refs_2_, f32[32,1024]{1,0:T(8,128)S(1)} %collective-permute-done.3.refs_0_.refs_3_, ...), custom_call_target="tpu_custom_call" | custom-call | flops 167772160 | bytes 2756608 | tf_op jit(solution)/shard_map/pallas_call | solution.py:406
  29.2 1.6 %collective-permute-start.14 = (f32[256,128]{1,0:T(8,128)S(1)}, f32[256,128]{1,0:T(8,128)S(1)}, u32[]{:S(2)}, u32[]{:S(2)}) collective-permute-start(f32[256,128]{1,0:T(8,128)S(1)} %shard_map.151.refs_0_), channel_id=1, source_target_pairs={{0,1},{1,0},{2,3},{3,2},{4,5},{5,4},{6,7},{7,6},{8,9},{9,8},{10,11... | collective-permute-start | bytes 393224 | tf_op jit(solution)/shard_map/ppermute | solution.py:420
  30.8 1.5 %collective-permute-start.15 = (f32[256,128]{1,0:T(8,128)S(1)}, f32[256,128]{1,0:T(8,128)S(1)}, u32[]{:S(2)}, u32[]{:S(2)}) collective-permute-start(f32[256,128]{1,0:T(8,128)S(1)} %shard_map.151.refs_0_), channel_id=1, source_target_pairs={{0,2},{1,3},{2,0},{3,1},{4,6},{5,7},{6,4},{7,5},{8,10},{9,11},{10,... | collective-permute-start | bytes 393224 | tf_op jit(solution)/shard_map/ppermute | solution.py:420
  32.3 0.5 %collective-permute-start.16 = (f32[256,128]{1,0:T(8,128)S(1)}, f32[256,128]{1,0:T(8,128)S(1)}, u32[]{:S(2)}, u32[]{:S(2)}) collective-permute-start(f32[256,128]{1,0:T(8,128)S(1)} %shard_map.151.refs_0_), channel_id=1, source_target_pairs={{0,3},{1,2},{2,1},{3,0},{4,7},{5,6},{6,5},{7,4},{8,11},{9,10},{10,... | collective-permute-start | bytes 393224 | tf_op jit(solution)/shard_map/ppermute | solution.py:420
  32.8 0.0 collective-permute-done.9.refs_2_.refs_8_
  32.8 0.6 %collective-permute-done.11.refs_5_.refs_11_ = f32[32,1024]{1,0:T(8,128)S(1)} collective-permute-done((f32[32,1024]{1,0:T(8,128)S(1)}, f32[32,1024]{1,0:T(8,128)S(1)}, u32[]{:S(2)}, u32[]{:S(2)}) %collective-permute-start.11) | collective-permute-done | bytes 131104 | tf_op jit(solution)/shard_map/ppermute | solution.py:433
  33.4 0.2 shard_map.148.x_ref.refs_11_
  33.6 0.0 collective-permute-start.12
  33.7 1.0 %shard_map.154.refs_1_ = f32[256,128]{1,0:T(8,128)S(1)} custom-call(f32[32,1024]{1,0:T(8,128)S(1)} %collective-permute-done.2.refs_0_.refs_6_, f32[32,1024]{1,0:T(8,128)S(1)} %collective-permute-done.8.refs_0_.refs_1_.refs_7_, f32[32,1024]{1,0:T(8,128)S(1)} %collective-permute-done.9.refs_2_.refs_8_, ...), custom_call_target="tpu_custom_call" | custom-call | flops 167772160 | bytes 2752640 | tf_op jit(solution)/shard_map/pallas_call | solution.py:406
  34.7 1.6 %collective-permute-start.17 = (f32[256,128]{1,0:T(8,128)S(1)}, f32[256,128]{1,0:T(8,128)S(1)}, u32[]{:S(2)}, u32[]{:S(2)}) collective-permute-start(f32[256,128]{1,0:T(8,128)S(1)} %shard_map.154.refs_1_), channel_id=1, source_target_pairs={{0,1},{1,0},{2,3},{3,2},{4,5},{5,4},{6,7},{7,6},{8,9},{9,8},{10,11... | collective-permute-start | bytes 393224 | tf_op jit(solution)/shard_map/ppermute | solution.py:420
  36.2 0.0 collective-permute-done.14.refs_1_
  36.2 1.5 %collective-permute-start.18 = (f32[256,128]{1,0:T(8,128)S(1)}, f32[256,128]{1,0:T(8,128)S(1)}, u32[]{:S(2)}, u32[]{:S(2)}) collective-permute-start(f32[256,128]{1,0:T(8,128)S(1)} %shard_map.154.refs_1_), channel_id=1, source_target_pairs={{0,2},{1,3},{2,0},{3,1},{4,6},{5,7},{6,4},{7,5},{8,10},{9,11},{10,... | collective-permute-start | bytes 393224 | tf_op jit(solution)/shard_map/ppermute | solution.py:420
  37.8 0.0 collective-permute-done.12.y_ref
  37.8 0.6 %collective-permute-start.19 = (f32[256,128]{1,0:T(8,128)S(1)}, f32[256,128]{1,0:T(8,128)S(1)}, u32[]{:S(2)}, u32[]{:S(2)}) collective-permute-start(f32[256,128]{1,0:T(8,128)S(1)} %shard_map.154.refs_1_), channel_id=1, source_target_pairs={{0,3},{1,2},{2,1},{3,0},{4,7},{5,6},{6,5},{7,4},{8,11},{9,10},{10,... | collective-permute-start | bytes 393224 | tf_op jit(solution)/shard_map/ppermute | solution.py:420
  38.4 0.1 collective-permute-done.15.refs_2_
  38.6 0.8 %collective-permute-start.13 = (f32[2,16]{1,0:T(2,128)S(1)}, f32[2,16]{1,0:T(2,128)S(1)}, u32[]{:S(2)}, u32[]{:S(2)}) collective-permute-start(f32[2,16]{1,0:T(2,128)S(1)} %shard_map.149.x_ref), channel_id=1, source_target_pairs={{0,4},{4,0},{8,12},{12,8},{1,5},{5,1},{9,13},{13,9},{2,6},{6,2},{1... | collective-permute-start | bytes 392 | tf_op jit(solution)/shard_map/ppermute | solution.py:420
  39.3 0.0 collective-permute-done.16.refs_3_
  39.4 2.8 %collective-permute-done.13.y_ref = f32[2,16]{1,0:T(2,128)S(1)} collective-permute-done((f32[2,16]{1,0:T(2,128)S(1)}, f32[2,16]{1,0:T(2,128)S(1)}, u32[]{:S(2)}, u32[]{:S(2)}) %collective-permute-start.13) | collective-permute-done | bytes 160 | tf_op jit(solution)/shard_map/ppermute | solution.py:420
  42.1 0.6 %collective-permute-start.20 = (f32[2,16]{1,0:T(2,128)S(1)}, f32[2,16]{1,0:T(2,128)S(1)}, u32[]{:S(2)}, u32[]{:S(2)}) collective-permute-start(f32[2,16]{1,0:T(2,128)S(1)} %shard_map.150.refs_24_.refs_5_), channel_id=1, source_target_pairs={{0,8},{4,12},{8,0},{12,4},{1,9},{5,13},{9,1},{13,5},{2,10},{6,14},... | collective-permute-start | bytes 392 | tf_op jit(solution)/shard_map/ppermute | solution.py:420
  42.7 2.4 %shard_map.153 = (bf16[1,256,1024]{2,1,0:T(8,128)(2,1)}, bf16[1,256,1024]{2,1,0:T(8,128)(2,1)}, f32[1,16,256]{2,1,0:T(8,128)}) custom-call(f32[32,1024]{1,0:T(8,128)S(1)} %collective-permute-done.refs_0_, f32[32,1024]{1,0:T(8,128)S(1)} %collective-permute-done.1.refs_0_.refs_1_, f32[32,1024]{1,0:T(8,128)S(1)} %collective-permute-done.4.refs_4_.refs_2_, ...), custom_call_target="tpu_custom_call" | custom-call | flops 335544320 | bytes 9752704 | tf_op jit(solution)/shard_map/pallas_call | solution.py:406
  45.2 1.4 %collective-permute-done.20.refs_6_ = f32[2,16]{1,0:T(2,128)S(1)} collective-permute-done((f32[2,16]{1,0:T(2,128)S(1)}, f32[2,16]{1,0:T(2,128)S(1)}, u32[]{:S(2)}, u32[]{:S(2)}) %collective-permute-start.20) | collective-permute-done | bytes 160 | tf_op jit(solution)/shard_map/ppermute | solution.py:420
  46.6 0.0 collective-permute-done.17.refs_2_
  46.6 0.0 collective-permute-done.18.refs_3_
  46.6 0.0 collective-permute-done.19.refs_4_
  46.6 0.8 %shard_map.155 = (f32[1,256,128]{2,1,0:T(8,128)}, f32[1,256,128]{2,1,0:T(8,128)}, f32[1,16]{1,0:T(1,128)}, f32[1,16]{1,0:T(1,128)}) custom-call(f32[256,128]{1,0:T(8,128)S(1)} %shard_map.152.refs_25_.refs_0_, f32[256,128]{1,0:T(8,128)S(1)} %shard_map.154.refs_1_, f32[256,128]{1,0:T(8,128)S(1)} %collective-permute-done.17.refs_2_, ...), custom_call_target="tpu_custom_call" | custom-call | bytes 917888 | tf_op jit(solution)/shard_map/pallas_call | solution.py:406
  (12 shorter events, 0.2 us)
Async XLA Ops:
  3.4 7.7 %collective-permute-start = (f32[32,1024]{1,0:T(8,128)S(1)}, f32[32,1024]{1,0:T(8,128)S(1)}, u32[]{:S(2)}, u32[]{:S(2)}) collective-permute-start(f32[32,1024]{1,0:T(8,128)S(1)} %get-tuple-element.49.refs_1_), channel_id=1, source_target_pairs={{0,4},{4,0},{8,12},{12,8},{16,20},{20,16},{24,28},{28,24},{1,5},{5... | collective-permute-start | bytes 393224 | tf_op jit(solution)/shard_map/ppermute | solution.py:433
  6.5 9.3 %collective-permute-start.3 = (f32[32,1024]{1,0:T(8,128)S(1)}, f32[32,1024]{1,0:T(8,128)S(1)}, u32[]{:S(2)}, u32[]{:S(2)}) collective-permute-start(f32[32,1024]{1,0:T(8,128)S(1)} %get-tuple-element.60.refs_1_), channel_id=1, source_target_pairs={{0,4},{4,0},{8,12},{12,8},{16,20},{20,16},{24,28},{28,24},{1,5},{5... | collective-permute-start | bytes 393224 | tf_op jit(solution)/shard_map/ppermute | solution.py:433
  6.6 9.9 %collective-permute-start.2 = (f32[32,1024]{1,0:T(8,128)S(1)}, f32[32,1024]{1,0:T(8,128)S(1)}, u32[]{:S(2)}, u32[]{:S(2)}) collective-permute-start(f32[32,1024]{1,0:T(8,128)S(1)} %get-tuple-element.59.refs_1_), channel_id=1, source_target_pairs={{0,4},{4,0},{8,12},{12,8},{16,20},{20,16},{24,28},{28,24},{1,5},{5... | collective-permute-start | bytes 393224 | tf_op jit(solution)/shard_map/ppermute | solution.py:433
  11.1 5.4 %collective-permute-start.1 = (f32[32,1024]{1,0:T(8,128)S(1)}, f32[32,1024]{1,0:T(8,128)S(1)}, u32[]{:S(2)}, u32[]{:S(2)}) collective-permute-start(f32[32,1024]{1,0:T(8,128)S(1)} %shard_map.137.after_ref), channel_id=1, source_target_pairs={{0,16},{4,8},{8,4},{12,28},{16,0},{20,24},{24,20},{28,12},{1,17},{... | collective-permute-start | bytes 393224 | tf_op jit(solution)/shard_map/ppermute | solution.py:433
  11.2 9.1 %collective-permute-start.6 = (f32[32,1024]{1,0:T(8,128)S(1)}, f32[32,1024]{1,0:T(8,128)S(1)}, u32[]{:S(2)}, u32[]{:S(2)}) collective-permute-start(f32[32,1024]{1,0:T(8,128)S(1)} %get-tuple-element.66.refs_1_), channel_id=1, source_target_pairs={{0,4},{4,0},{8,12},{12,8},{16,20},{20,16},{24,28},{28,24},{1,5},{5... | collective-permute-start | bytes 393224 | tf_op jit(solution)/shard_map/ppermute | solution.py:433
  15.9 5.9 %collective-permute-start.5 = (f32[32,1024]{1,0:T(8,128)S(1)}, f32[32,1024]{1,0:T(8,128)S(1)}, u32[]{:S(2)}, u32[]{:S(2)}) collective-permute-start(f32[32,1024]{1,0:T(8,128)S(1)} %shard_map.139.refs_3_), channel_id=1, source_target_pairs={{0,16},{4,8},{8,4},{12,28},{16,0},{20,24},{24,20},{28,12},{1,17},{... | collective-permute-start | bytes 393224 | tf_op jit(solution)/shard_map/ppermute | solution.py:433
  16.5 7.0 %collective-permute-start.8 = (f32[32,1024]{1,0:T(8,128)S(1)}, f32[32,1024]{1,0:T(8,128)S(1)}, u32[]{:S(2)}, u32[]{:S(2)}) collective-permute-start(f32[32,1024]{1,0:T(8,128)S(1)} %shard_map.140.refs_3_), channel_id=1, source_target_pairs={{0,16},{4,8},{8,4},{12,28},{16,0},{20,24},{24,20},{28,12},{1,17},{... | collective-permute-start | bytes 393224 | tf_op jit(solution)/shard_map/ppermute | solution.py:433
  16.6 8.6 %collective-permute-start.4 = (f32[32,1024]{1,0:T(8,128)S(1)}, f32[32,1024]{1,0:T(8,128)S(1)}, u32[]{:S(2)}, u32[]{:S(2)}) collective-permute-start(f32[32,1024]{1,0:T(8,128)S(1)} %shard_map.141.refs_3_), channel_id=1, source_target_pairs={{0,4},{4,0},{8,12},{12,8},{16,20},{20,16},{24,28},{28,24},{1,5},{5... | collective-permute-start | bytes 393224 | tf_op jit(solution)/shard_map/ppermute | solution.py:433
  20.3 4.9 %collective-permute-start.10 = (f32[32,1024]{1,0:T(8,128)S(1)}, f32[32,1024]{1,0:T(8,128)S(1)}, u32[]{:S(2)}, u32[]{:S(2)}) collective-permute-start(f32[32,1024]{1,0:T(8,128)S(1)} %shard_map.142.after_ref), channel_id=1, source_target_pairs={{0,16},{4,8},{8,4},{12,28},{16,0},{20,24},{24,20},{28,12},{1,17},{... | collective-permute-start | bytes 393224 | tf_op jit(solution)/shard_map/ppermute | solution.py:433
  21.8 6.4 %collective-permute-start.7 = (f32[32,1024]{1,0:T(8,128)S(1)}, f32[32,1024]{1,0:T(8,128)S(1)}, u32[]{:S(2)}, u32[]{:S(2)}) collective-permute-start(f32[32,1024]{1,0:T(8,128)S(1)} %shard_map.144.refs_3_), channel_id=1, source_target_pairs={{0,4},{4,0},{8,12},{12,8},{16,20},{20,16},{24,28},{28,24},{1,5},{5... | collective-permute-start | bytes 393224 | tf_op jit(solution)/shard_map/ppermute | solution.py:433
  23.5 9.3 %collective-permute-start.9 = (f32[32,1024]{1,0:T(8,128)S(1)}, f32[32,1024]{1,0:T(8,128)S(1)}, u32[]{:S(2)}, u32[]{:S(2)}) collective-permute-start(f32[32,1024]{1,0:T(8,128)S(1)} %shard_map.145.refs_3_), channel_id=1, source_target_pairs={{0,4},{4,0},{8,12},{12,8},{16,20},{20,16},{24,28},{28,24},{1,5},{5... | collective-permute-start | bytes 393224 | tf_op jit(solution)/shard_map/ppermute | solution.py:433
  25.2 8.2 %collective-permute-start.11 = (f32[32,1024]{1,0:T(8,128)S(1)}, f32[32,1024]{1,0:T(8,128)S(1)}, u32[]{:S(2)}, u32[]{:S(2)}) collective-permute-start(f32[32,1024]{1,0:T(8,128)S(1)} %shard_map.146), channel_id=1, source_target_pairs={{0,4},{4,0},{8,12},{12,8},{16,20},{20,16},{24,28},{28,24},{1,5},{5... | collective-permute-start | bytes 393224 | tf_op jit(solution)/shard_map/ppermute | solution.py:433
  29.2 7.0 %collective-permute-start.14 = (f32[256,128]{1,0:T(8,128)S(1)}, f32[256,128]{1,0:T(8,128)S(1)}, u32[]{:S(2)}, u32[]{:S(2)}) collective-permute-start(f32[256,128]{1,0:T(8,128)S(1)} %shard_map.151.refs_0_), channel_id=1, source_target_pairs={{0,1},{1,0},{2,3},{3,2},{4,5},{5,4},{6,7},{7,6},{8,9},{9,8},{10,11... | collective-permute-start | bytes 393224 | tf_op jit(solution)/shard_map/ppermute | solution.py:420
  30.8 7.8 %collective-permute-start.15 = (f32[256,128]{1,0:T(8,128)S(1)}, f32[256,128]{1,0:T(8,128)S(1)}, u32[]{:S(2)}, u32[]{:S(2)}) collective-permute-start(f32[256,128]{1,0:T(8,128)S(1)} %shard_map.151.refs_0_), channel_id=1, source_target_pairs={{0,2},{1,3},{2,0},{3,1},{4,6},{5,7},{6,4},{7,5},{8,10},{9,11},{10,... | collective-permute-start | bytes 393224 | tf_op jit(solution)/shard_map/ppermute | solution.py:420
  32.3 7.0 %collective-permute-start.16 = (f32[256,128]{1,0:T(8,128)S(1)}, f32[256,128]{1,0:T(8,128)S(1)}, u32[]{:S(2)}, u32[]{:S(2)}) collective-permute-start(f32[256,128]{1,0:T(8,128)S(1)} %shard_map.151.refs_0_), channel_id=1, source_target_pairs={{0,3},{1,2},{2,1},{3,0},{4,7},{5,6},{6,5},{7,4},{8,11},{9,10},{10,... | collective-permute-start | bytes 393224 | tf_op jit(solution)/shard_map/ppermute | solution.py:420
  33.6 4.1 %collective-permute-start.12 = (f32[2,16]{1,0:T(2,128)S(1)}, f32[2,16]{1,0:T(2,128)S(1)}, u32[]{:S(2)}, u32[]{:S(2)}) collective-permute-start(f32[2,16]{1,0:T(2,128)S(1)} %shard_map.148.x_ref.refs_11_), channel_id=1, source_target_pairs={{0,16},{16,0},{1,17},{17,1},{2,18},{18,2},{3,19},{19,3},{4,20},{20... | collective-permute-start | bytes 392 | tf_op jit(solution)/shard_map/ppermute | solution.py:420
  34.7 11.9 %collective-permute-start.17 = (f32[256,128]{1,0:T(8,128)S(1)}, f32[256,128]{1,0:T(8,128)S(1)}, u32[]{:S(2)}, u32[]{:S(2)}) collective-permute-start(f32[256,128]{1,0:T(8,128)S(1)} %shard_map.154.refs_1_), channel_id=1, source_target_pairs={{0,1},{1,0},{2,3},{3,2},{4,5},{5,4},{6,7},{7,6},{8,9},{9,8},{10,11... | collective-permute-start | bytes 393224 | tf_op jit(solution)/shard_map/ppermute | solution.py:420
  36.2 10.4 %collective-permute-start.18 = (f32[256,128]{1,0:T(8,128)S(1)}, f32[256,128]{1,0:T(8,128)S(1)}, u32[]{:S(2)}, u32[]{:S(2)}) collective-permute-start(f32[256,128]{1,0:T(8,128)S(1)} %shard_map.154.refs_1_), channel_id=1, source_target_pairs={{0,2},{1,3},{2,0},{3,1},{4,6},{5,7},{6,4},{7,5},{8,10},{9,11},{10,... | collective-permute-start | bytes 393224 | tf_op jit(solution)/shard_map/ppermute | solution.py:420
  37.8 8.9 %collective-permute-start.19 = (f32[256,128]{1,0:T(8,128)S(1)}, f32[256,128]{1,0:T(8,128)S(1)}, u32[]{:S(2)}, u32[]{:S(2)}) collective-permute-start(f32[256,128]{1,0:T(8,128)S(1)} %shard_map.154.refs_1_), channel_id=1, source_target_pairs={{0,3},{1,2},{2,1},{3,0},{4,7},{5,6},{6,5},{7,4},{8,11},{9,10},{10,... | collective-permute-start | bytes 393224 | tf_op jit(solution)/shard_map/ppermute | solution.py:420
  38.6 3.6 %collective-permute-start.13 = (f32[2,16]{1,0:T(2,128)S(1)}, f32[2,16]{1,0:T(2,128)S(1)}, u32[]{:S(2)}, u32[]{:S(2)}) collective-permute-start(f32[2,16]{1,0:T(2,128)S(1)} %shard_map.149.x_ref), channel_id=1, source_target_pairs={{0,4},{4,0},{8,12},{12,8},{1,5},{5,1},{9,13},{13,9},{2,6},{6,2},{1... | collective-permute-start | bytes 392 | tf_op jit(solution)/shard_map/ppermute | solution.py:420
  42.1 4.5 %collective-permute-start.20 = (f32[2,16]{1,0:T(2,128)S(1)}, f32[2,16]{1,0:T(2,128)S(1)}, u32[]{:S(2)}, u32[]{:S(2)}) collective-permute-start(f32[2,16]{1,0:T(2,128)S(1)} %shard_map.150.refs_24_.refs_5_), channel_id=1, source_target_pairs={{0,8},{4,12},{8,0},{12,4},{1,9},{5,13},{9,1},{13,5},{2,10},{6,14},... | collective-permute-start | bytes 392 | tf_op jit(solution)/shard_map/ppermute | solution.py:420

commit v3 on v1

--- a/solution.py
+++ b/solution.py
@@ -336,7 +336,7 @@
     states, refs = [refs[3 * i : 3 * i + 3] for i in range(pieces)], refs[3 * pieces :]
     (
         v_ref, b_ref, c_ref, coef_ref, mamba_ref, inner_ref, growth_ref, fall_ref, gy_ref,
-        gcum_ref, decay_ref, neg_ref, _, gv_ref, gg_ref, gs_ref, total_ref,
+        gcum_ref, decay_ref, neg_ref, *_, gv_ref, gg_ref, gs_ref, total_ref,
     ) = refs
     length, channels = v_ref.shape
     heads = gcum_ref.shape[0]
@@ -373,6 +373,10 @@
 
 def add_kernel(x_ref, y_ref, *refs):
     refs[-1][...] = x_ref[...] + y_ref[...]
+
+
+def sum_kernel(*refs):
+    refs[-1][...] = tree([ref[...] for ref in refs[:-1]])
 
 
 def last_kernel(counts, *refs):
@@ -587,7 +591,7 @@
     coef, mamba, inner, growth, fall, grad_y, grad_cum, parts = made["prepare"]
 
     rate_row = jnp.zeros((1, channels), F32)
-    terms, counts = [], []
+    terms, counts, done = [], [], []
     for i in range(PARTS):
         final = i == PARTS - 1
         count = CHUNKS // PARTS
@@ -603,6 +607,9 @@
             after=(rate_row,),
         )(*own, high, low, scaled, sum_b, sum_c)[0]
         own = sum_terms(share_of, "tensor", sizes["tensor"])
+        if not final:
+            own = [call(sum_kernel, [like(share_of.shape, F32)])(*own)[0]]
+            done += own
         terms += own
         counts.append(len(own))
 
@@ -612,14 +619,14 @@
             [like((1, length, channels), BF16)] * 2
             + [like((1, heads, length), F32), like((1, heads), F32)],
             flops=10 * length * channels * state,
-            after=after,
+            after=(*after, *done),
         )(
             *(x for group in states for x in group),
             vals, block_b, block_c, coef, mamba, inner, growth, fall, grad_y, grad_cum, decay, negative,
         )
         return (made["rest"][3],)
 
-    own = small_terms(rate_row, ("replica", "seq"), sizes, rest)
+    own = small_terms(rate_row, ("seq", "replica"), sizes, rest)
     terms += own
     counts.append(len(own))
     grad_values, grad_gate, grad_steps, _ = made["rest"]

time: 49.3 us -> 48.9 us (level)
  starting transfers between devices: 27.8 us -> 25.8 us
  waiting for transfers between devices: 6.73 us -> 8.44 us
    ppermute x9, starting transfers between devices: 10.2 us -> 8.08 us  [swap(): return lax.ppermute(x, axis, [(i, i ^ bit) for i in range(size)])]
    ppermute x9, waiting for transfers between devices: 4.57 us -> 6.28 us  [swap(): return lax.ppermute(x, axis, [(i, i ^ bit) for i in range(size)])]
    pallas_call x20 -> x21, Pallas kernels: 13.8 us -> 13.8 us  [run(): pl.pallas_call(kernel, out_shape=tuple(outs), in_specs=specs, out_specs=t...]
  transfers between devices with their start and end apart: 21 -> 21, of which waited for: 5 -> 7; matrix products, arithmetic and copies ran while one was open for 0% -> 0% of each run, Pallas kernels for 21% -> 21%
where the time goes in v3:
time: 48.9 us; the launch traced here: 48.8 us
  starting transfers between devices  25.8 us (53%)
  Pallas kernels  13.8 us (28%)
  waiting for transfers between devices  8.44 us (17%)
  between operations  0.79 us (2%)
    ppermute x12, starting transfers between devices, hop(): return lax.ppermute(x, ('replica', 'seq'), pairs)  17.7 us
    pallas_call x21, Pallas kernels, run(): pl.pallas_call(kernel, out_shape=tuple(outs), in_specs=specs, out_specs=t...  13.8 us
    ppermute x9, starting transfers between devices, swap(): return lax.ppermute(x, axis, [(i, i ^ bit) for i in range(size)])  8.08 us
    ppermute x9, waiting for transfers between devices, swap(): return lax.ppermute(x, axis, [(i, i ^ bit) for i in range(size)])  6.28 us
    ppermute x12, waiting for transfers between devices, hop(): return lax.ppermute(x, ('replica', 'seq'), pairs)  2.16 us
  transfers between devices with their start and end apart: 21, of which 7 were waited for; matrix products, arithmetic and copies ran while one was open for 0% of the time, Pallas kernels for 21%

profile of v3, /device:TPU:0, one launch (start us, length us, event | category | flops | bytes accessed | tf_op | source)
XLA Modules:
  0.0 48.8 jit_solution(3692305567433868111)
XLA Ops:
  0.6 2.8 %shard_map.135 = (bf16[256,1024]{1,0:T(8,128)(2,1)S(1)}, bf16[256,1024]{1,0:T(8,128)(2,1)S(1)}, bf16[256,1024]{1,0:T(8,128)(2,1)S(1)}, bf16[256,128]{1,0:T(8,128...) custom-call(bf16[256,1024]{1,0:T(8,128)(2,1)} %bitcast.10, ...), custom_call_target="tpu_custom_call" | custom-call | flops 268435456 | bytes 4513984 | tf_op jit(solution)/shard_map/pallas_call | solution.py:407
  3.4 3.1 %collective-permute-start = (f32[32,1024]{1,0:T(8,128)S(1)}, f32[32,1024]{1,0:T(8,128)S(1)}, u32[]{:S(2)}, u32[]{:S(2)}) collective-permute-start(f32[32,1024]{1,0:T(8,128)S(1)} %get-tuple-element.50.refs_1_), channel_id=1, source_target_pairs={{0,4},{4,0},{8,12},{12,8},{16,20},{20,16},{24,28},{28,24},{1,5},{5... | collective-permute-start | bytes 393224 | tf_op jit(solution)/shard_map/ppermute | solution.py:434
  6.5 0.1 collective-permute-start.3
  6.6 1.9 %collective-permute-start.2 = (f32[32,1024]{1,0:T(8,128)S(1)}, f32[32,1024]{1,0:T(8,128)S(1)}, u32[]{:S(2)}, u32[]{:S(2)}) collective-permute-start(f32[32,1024]{1,0:T(8,128)S(1)} %get-tuple-element.60.refs_1_), channel_id=1, source_target_pairs={{0,4},{4,0},{8,12},{12,8},{16,20},{20,16},{24,28},{28,24},{1,5},{5... | collective-permute-start | bytes 393224 | tf_op jit(solution)/shard_map/ppermute | solution.py:434
  8.5 2.5 %shard_map.136 = (f32[256,1024]{1,0:T(8,128)S(1)}, f32[256,1024]{1,0:T(8,128)S(1)}, f32[256,128]{1,0:T(8,128)S(1)}, f32[256,128]{1,0:T(8,128)S(1)}) custom-call(bf16[256,1024]{1,0:T(8,128)(2,1)S(1)} %get-tuple-element.52.v_ref.refs_12_, bf16[256,1024]{1,0:T(8,128)(2,1)S(1)} %get-tuple-element.53.gate_ref, bf16[256,1024]{1,0:T(8,128)(2,1)S(1)} %get-tuple-element.54.go_ref, ...), custom_call_target="tpu_custom_call" | custom-call | flops 1073741824 | bytes 4079616 | tf_op jit(solution)/shard_map/pallas_call | solution.py:407
  11.1 0.0 collective-permute-done.refs_0_
  11.1 0.1 collective-permute-start.1
  11.2 3.4 %collective-permute-start.6 = (f32[32,1024]{1,0:T(8,128)S(1)}, f32[32,1024]{1,0:T(8,128)S(1)}, u32[]{:S(2)}, u32[]{:S(2)}) collective-permute-start(f32[32,1024]{1,0:T(8,128)S(1)} %get-tuple-element.67.refs_1_), channel_id=1, source_target_pairs={{0,4},{4,0},{8,12},{12,8},{16,20},{20,16},{24,28},{28,24},{1,5},{5... | collective-permute-start | bytes 393224 | tf_op jit(solution)/shard_map/ppermute | solution.py:434
  14.6 1.3 %shard_map.138 = (bf16[256,1024]{1,0:T(8,128)(2,1)S(1)}, bf16[256,1024]{1,0:T(8,128)(2,1)S(1)}, bf16[256,1024]{1,0:T(8,128)(2,1)S(1)}, f32[128,1024]{1,0:T(8,128)S(1)}, f32[128,1024]{1,0:T(8,128)S(1)}) custom-call(bf16[256,1024]{1,0:T(8,128)(2,1)S(1)} %get-tuple-element.52.v_ref.refs_12_, bf16[256,1024]{1,0:T(8,128)(2,1)S(1)} %get-tuple-element.53.gate_ref, ...), custom_call_target="tpu_custom_call" | custom-call | flops 268435456 | bytes 4472832 | tf_op jit(solution)/shard_map/pallas_call | solution.py:407
  15.8 0.0 collective-permute-done.3.refs_0_.refs_3_
  15.9 0.1 collective-permute-start.5
  16.0 0.5 collective-permute-done.2.refs_0_.refs_6_
  16.5 0.1 collective-permute-start.8
  16.6 0.0 collective-permute-done.1.refs_0_.refs_1_
  16.6 3.7 %collective-permute-start.4 = (f32[32,1024]{1,0:T(8,128)S(1)}, f32[32,1024]{1,0:T(8,128)S(1)}, u32[]{:S(2)}, u32[]{:S(2)}) collective-permute-start(f32[32,1024]{1,0:T(8,128)S(1)} %shard_map.141.refs_3_), channel_id=1, source_target_pairs={{0,4},{4,0},{8,12},{12,8},{16,20},{20,16},{24,28},{28,24},{1,5},{5... | collective-permute-start | bytes 393224 | tf_op jit(solution)/shard_map/ppermute | solution.py:434
  20.3 0.0 collective-permute-done.6.refs_0_.refs_3_.refs_9_
  20.3 0.1 collective-permute-start.10
  20.4 1.4 %shard_map.143 = (f32[256,1024]{1,0:T(8,128)S(1)}, f32[256,1024]{1,0:T(8,128)S(1)}, f32[256,1024]{1,0:T(8,128)S(1)}, f32[256,1024]{1,0:T(8,128)S(1)}, f32[256,10...) custom-call(bf16[256,1024]{1,0:T(8,128)(2,1)S(1)} %get-tuple-element.52.v_ref.refs_12_, ...), custom_call_target="tpu_custom_call" | custom-call | flops 268435456 | bytes 10125504 | tf_op jit(solution)/shard_map/pallas_call | solution.py:407
  21.8 0.0 collective-permute-done.5.refs_0_.refs_4_
  21.8 1.6 %collective-permute-start.7 = (f32[32,1024]{1,0:T(8,128)S(1)}, f32[32,1024]{1,0:T(8,128)S(1)}, u32[]{:S(2)}, u32[]{:S(2)}) collective-permute-start(f32[32,1024]{1,0:T(8,128)S(1)} %shard_map.144.refs_3_), channel_id=1, source_target_pairs={{0,4},{4,0},{8,12},{12,8},{16,20},{20,16},{24,28},{28,24},{1,5},{5... | collective-permute-start | bytes 393224 | tf_op jit(solution)/shard_map/ppermute | solution.py:434
  23.5 0.0 collective-permute-done.8.refs_0_.refs_1_.refs_7_
  23.5 1.7 %collective-permute-start.9 = (f32[32,1024]{1,0:T(8,128)S(1)}, f32[32,1024]{1,0:T(8,128)S(1)}, u32[]{:S(2)}, u32[]{:S(2)}) collective-permute-start(f32[32,1024]{1,0:T(8,128)S(1)} %shard_map.145.refs_3_), channel_id=1, source_target_pairs={{0,4},{4,0},{8,12},{12,8},{16,20},{20,16},{24,28},{28,24},{1,5},{5... | collective-permute-start | bytes 393224 | tf_op jit(solution)/shard_map/ppermute | solution.py:434
  25.2 0.0 collective-permute-done.4.refs_4_.refs_2_
  25.2 0.0 collective-permute-done.10.refs_0_.refs_4_.refs_10_
  25.2 1.9 %collective-permute-start.11 = (f32[32,1024]{1,0:T(8,128)S(1)}, f32[32,1024]{1,0:T(8,128)S(1)}, u32[]{:S(2)}, u32[]{:S(2)}) collective-permute-start(f32[32,1024]{1,0:T(8,128)S(1)} %shard_map.146), channel_id=1, source_target_pairs={{0,4},{4,0},{8,12},{12,8},{16,20},{20,16},{24,28},{28,24},{1,5},{5... | collective-permute-start | bytes 393224 | tf_op jit(solution)/shard_map/ppermute | solution.py:434
  27.1 1.0 %collective-permute-done.7.refs_5_ = f32[32,1024]{1,0:T(8,128)S(1)} collective-permute-done((f32[32,1024]{1,0:T(8,128)S(1)}, f32[32,1024]{1,0:T(8,128)S(1)}, u32[]{:S(2)}, u32[]{:S(2)}) %collective-permute-start.7) | collective-permute-done | bytes 131104 | tf_op jit(solution)/shard_map/ppermute | solution.py:434
  28.2 0.1 shard_map.147.refs_9_.refs_11_
  28.3 0.9 %shard_map.150.refs_0_ = f32[256,128]{1,0:T(8,128)S(1)} custom-call(f32[32,1024]{1,0:T(8,128)S(1)} %collective-permute-done.refs_0_, f32[32,1024]{1,0:T(8,128)S(1)} %collective-permute-done.1.refs_0_.refs_1_, f32[32,1024]{1,0:T(8,128)S(1)} %collective-permute-done.4.refs_4_.refs_2_, f32[32,1024]{1,0:T(8,128)S(1)} %collective-permute-done.3.refs_0_.refs_3_, ...), custom_call_target="tpu_custom_call" | custom-call | flops 167772160 | bytes 2756608 | tf_op jit(solution)/shard_map/pallas_call | solution.py:407
  29.2 1.5 %collective-permute-start.13 = (f32[256,128]{1,0:T(8,128)S(1)}, f32[256,128]{1,0:T(8,128)S(1)}, u32[]{:S(2)}, u32[]{:S(2)}) collective-permute-start(f32[256,128]{1,0:T(8,128)S(1)} %shard_map.150.refs_0_), channel_id=1, source_target_pairs={{0,1},{1,0},{2,3},{3,2},{4,5},{5,4},{6,7},{7,6},{8,9},{9,8},{10,11... | collective-permute-start | bytes 393224 | tf_op jit(solution)/shard_map/ppermute | solution.py:421
  30.8 1.5 %collective-permute-start.14 = (f32[256,128]{1,0:T(8,128)S(1)}, f32[256,128]{1,0:T(8,128)S(1)}, u32[]{:S(2)}, u32[]{:S(2)}) collective-permute-start(f32[256,128]{1,0:T(8,128)S(1)} %shard_map.150.refs_0_), channel_id=1, source_target_pairs={{0,2},{1,3},{2,0},{3,1},{4,6},{5,7},{6,4},{7,5},{8,10},{9,11},{10,... | collective-permute-start | bytes 393224 | tf_op jit(solution)/shard_map/ppermute | solution.py:421
  32.3 0.5 %collective-permute-start.15 = (f32[256,128]{1,0:T(8,128)S(1)}, f32[256,128]{1,0:T(8,128)S(1)}, u32[]{:S(2)}, u32[]{:S(2)}) collective-permute-start(f32[256,128]{1,0:T(8,128)S(1)} %shard_map.150.refs_0_), channel_id=1, source_target_pairs={{0,3},{1,2},{2,1},{3,0},{4,7},{5,6},{6,5},{7,4},{8,11},{9,10},{10,... | collective-permute-start | bytes 393224 | tf_op jit(solution)/shard_map/ppermute | solution.py:421
  32.8 0.0 collective-permute-done.9.refs_2_.refs_8_
  32.8 0.6 %collective-permute-done.11.refs_5_.refs_11_ = f32[32,1024]{1,0:T(8,128)S(1)} collective-permute-done((f32[32,1024]{1,0:T(8,128)S(1)}, f32[32,1024]{1,0:T(8,128)S(1)}, u32[]{:S(2)}, u32[]{:S(2)}) %collective-permute-start.11) | collective-permute-done | bytes 131104 | tf_op jit(solution)/shard_map/ppermute | solution.py:434
  33.4 0.2 shard_map.148.x_ref.refs_11_
  33.6 1.0 %shard_map.153.refs_1_ = f32[256,128]{1,0:T(8,128)S(1)} custom-call(f32[32,1024]{1,0:T(8,128)S(1)} %collective-permute-done.2.refs_0_.refs_6_, f32[32,1024]{1,0:T(8,128)S(1)} %collective-permute-done.8.refs_0_.refs_1_.refs_7_, f32[32,1024]{1,0:T(8,128)S(1)} %collective-permute-done.9.refs_2_.refs_8_, ...), custom_call_target="tpu_custom_call" | custom-call | flops 167772160 | bytes 2752640 | tf_op jit(solution)/shard_map/pallas_call | solution.py:407
  34.6 1.6 %collective-permute-start.16 = (f32[256,128]{1,0:T(8,128)S(1)}, f32[256,128]{1,0:T(8,128)S(1)}, u32[]{:S(2)}, u32[]{:S(2)}) collective-permute-start(f32[256,128]{1,0:T(8,128)S(1)} %shard_map.153.refs_1_), channel_id=1, source_target_pairs={{0,1},{1,0},{2,3},{3,2},{4,5},{5,4},{6,7},{7,6},{8,9},{9,8},{10,11... | collective-permute-start | bytes 393224 | tf_op jit(solution)/shard_map/ppermute | solution.py:421
  36.2 1.5 %collective-permute-start.17 = (f32[256,128]{1,0:T(8,128)S(1)}, f32[256,128]{1,0:T(8,128)S(1)}, u32[]{:S(2)}, u32[]{:S(2)}) collective-permute-start(f32[256,128]{1,0:T(8,128)S(1)} %shard_map.153.refs_1_), channel_id=1, source_target_pairs={{0,2},{1,3},{2,0},{3,1},{4,6},{5,7},{6,4},{7,5},{8,10},{9,11},{10,... | collective-permute-start | bytes 393224 | tf_op jit(solution)/shard_map/ppermute | solution.py:421
  37.7 0.0 collective-permute-done.13.refs_1_
  37.7 0.5 collective-permute-start.18
  38.2 0.6 %collective-permute-done.14.refs_2_ = f32[256,128]{1,0:T(8,128)S(1)} collective-permute-done((f32[256,128]{1,0:T(8,128)S(1)}, f32[256,128]{1,0:T(8,128)S(1)}, u32[]{:S(2)}, u32[]{:S(2)}) %collective-permute-start.14) | collective-permute-done | bytes 131104 | tf_op jit(solution)/shard_map/ppermute | solution.py:421
  38.8 0.5 %collective-permute-start.12 = (f32[2,16]{1,0:T(2,128)S(1)}, f32[2,16]{1,0:T(2,128)S(1)}, u32[]{:S(2)}, u32[]{:S(2)}) collective-permute-start(f32[2,16]{1,0:T(2,128)S(1)} %shard_map.148.x_ref.refs_11_), channel_id=1, source_target_pairs={{0,4},{4,0},{8,12},{12,8},{1,5},{5,1},{9,13},{13,9},{2,6},{6,2},{1... | collective-permute-start | bytes 392 | tf_op jit(solution)/shard_map/ppermute | solution.py:421
  39.3 0.0 collective-permute-done.15.refs_3_
  39.3 3.0 %collective-permute-done.12.y_ref = f32[2,16]{1,0:T(2,128)S(1)} collective-permute-done((f32[2,16]{1,0:T(2,128)S(1)}, f32[2,16]{1,0:T(2,128)S(1)}, u32[]{:S(2)}, u32[]{:S(2)}) %collective-permute-start.12) | collective-permute-done | bytes 160 | tf_op jit(solution)/shard_map/ppermute | solution.py:421
  42.3 0.5 collective-permute-start.19
  42.8 2.5 %shard_map.152 = (bf16[1,256,1024]{2,1,0:T(8,128)(2,1)}, bf16[1,256,1024]{2,1,0:T(8,128)(2,1)}, f32[1,16,256]{2,1,0:T(8,128)}, f32[1,16]{1,0:T(1,128)S(1)}) custom-call(f32[32,1024]{1,0:T(8,128)S(1)} %collective-permute-done.refs_0_, f32[32,1024]{1,0:T(8,128)S(1)} %collective-permute-done.1.refs_0_.refs_1_, ...), custom_call_target="tpu_custom_call" | custom-call | flops 335544320 | bytes 9752768 | tf_op jit(solution)/shard_map/pallas_call | solution.py:407
  45.3 1.5 %collective-permute-done.19.y_ref = f32[2,16]{1,0:T(2,128)S(1)} collective-permute-done((f32[2,16]{1,0:T(2,128)S(1)}, f32[2,16]{1,0:T(2,128)S(1)}, u32[]{:S(2)}, u32[]{:S(2)}) %collective-permute-start.19) | collective-permute-done | bytes 160 | tf_op jit(solution)/shard_map/ppermute | solution.py:421
  46.8 0.0 collective-permute-start.20
  46.8 1.1 %collective-permute-done.20.refs_6_ = f32[2,16]{1,0:T(2,128)S(1)} collective-permute-done((f32[2,16]{1,0:T(2,128)S(1)}, f32[2,16]{1,0:T(2,128)S(1)}, u32[]{:S(2)}, u32[]{:S(2)}) %collective-permute-start.20) | collective-permute-done | bytes 160 | tf_op jit(solution)/shard_map/ppermute | solution.py:421
  48.0 0.0 collective-permute-done.16.refs_2_
  48.0 0.0 collective-permute-done.17.refs_3_
  48.0 0.0 collective-permute-done.18.refs_4_
  48.0 0.8 %shard_map.155 = (f32[1,256,128]{2,1,0:T(8,128)}, f32[1,256,128]{2,1,0:T(8,128)}, f32[1,16]{1,0:T(1,128)}, f32[1,16]{1,0:T(1,128)}) custom-call(f32[256,128]{1,0:T(8,128)S(1)} %shard_map.151.refs_25_.refs_0_, f32[256,128]{1,0:T(8,128)S(1)} %shard_map.153.refs_1_, f32[256,128]{1,0:T(8,128)S(1)} %collective-permute-done.16.refs_2_, ...), custom_call_target="tpu_custom_call" | custom-call | bytes 917888 | tf_op jit(solution)/shard_map/pallas_call | solution.py:407
  (12 shorter events, 0.2 us)
Async XLA Ops:
  3.4 7.7 %collective-permute-start = (f32[32,1024]{1,0:T(8,128)S(1)}, f32[32,1024]{1,0:T(8,128)S(1)}, u32[]{:S(2)}, u32[]{:S(2)}) collective-permute-start(f32[32,1024]{1,0:T(8,128)S(1)} %get-tuple-element.50.refs_1_), channel_id=1, source_target_pairs={{0,4},{4,0},{8,12},{12,8},{16,20},{20,16},{24,28},{28,24},{1,5},{5... | collective-permute-start | bytes 393224 | tf_op jit(solution)/shard_map/ppermute | solution.py:434
  6.5 9.3 %collective-permute-start.3 = (f32[32,1024]{1,0:T(8,128)S(1)}, f32[32,1024]{1,0:T(8,128)S(1)}, u32[]{:S(2)}, u32[]{:S(2)}) collective-permute-start(f32[32,1024]{1,0:T(8,128)S(1)} %get-tuple-element.61.refs_1_), channel_id=1, source_target_pairs={{0,4},{4,0},{8,12},{12,8},{16,20},{20,16},{24,28},{28,24},{1,5},{5... | collective-permute-start | bytes 393224 | tf_op jit(solution)/shard_map/ppermute | solution.py:434
  6.6 9.9 %collective-permute-start.2 = (f32[32,1024]{1,0:T(8,128)S(1)}, f32[32,1024]{1,0:T(8,128)S(1)}, u32[]{:S(2)}, u32[]{:S(2)}) collective-permute-start(f32[32,1024]{1,0:T(8,128)S(1)} %get-tuple-element.60.refs_1_), channel_id=1, source_target_pairs={{0,4},{4,0},{8,12},{12,8},{16,20},{20,16},{24,28},{28,24},{1,5},{5... | collective-permute-start | bytes 393224 | tf_op jit(solution)/shard_map/ppermute | solution.py:434
  11.1 5.4 %collective-permute-start.1 = (f32[32,1024]{1,0:T(8,128)S(1)}, f32[32,1024]{1,0:T(8,128)S(1)}, u32[]{:S(2)}, u32[]{:S(2)}) collective-permute-start(f32[32,1024]{1,0:T(8,128)S(1)} %shard_map.137.after_ref), channel_id=1, source_target_pairs={{0,16},{4,8},{8,4},{12,28},{16,0},{20,24},{24,20},{28,12},{1,17},{... | collective-permute-start | bytes 393224 | tf_op jit(solution)/shard_map/ppermute | solution.py:434
  11.2 9.1 %collective-permute-start.6 = (f32[32,1024]{1,0:T(8,128)S(1)}, f32[32,1024]{1,0:T(8,128)S(1)}, u32[]{:S(2)}, u32[]{:S(2)}) collective-permute-start(f32[32,1024]{1,0:T(8,128)S(1)} %get-tuple-element.67.refs_1_), channel_id=1, source_target_pairs={{0,4},{4,0},{8,12},{12,8},{16,20},{20,16},{24,28},{28,24},{1,5},{5... | collective-permute-start | bytes 393224 | tf_op jit(solution)/shard_map/ppermute | solution.py:434
  15.9 5.9 %collective-permute-start.5 = (f32[32,1024]{1,0:T(8,128)S(1)}, f32[32,1024]{1,0:T(8,128)S(1)}, u32[]{:S(2)}, u32[]{:S(2)}) collective-permute-start(f32[32,1024]{1,0:T(8,128)S(1)} %shard_map.139.refs_3_), channel_id=1, source_target_pairs={{0,16},{4,8},{8,4},{12,28},{16,0},{20,24},{24,20},{28,12},{1,17},{... | collective-permute-start | bytes 393224 | tf_op jit(solution)/shard_map/ppermute | solution.py:434
  16.5 7.0 %collective-permute-start.8 = (f32[32,1024]{1,0:T(8,128)S(1)}, f32[32,1024]{1,0:T(8,128)S(1)}, u32[]{:S(2)}, u32[]{:S(2)}) collective-permute-start(f32[32,1024]{1,0:T(8,128)S(1)} %shard_map.140.refs_3_), channel_id=1, source_target_pairs={{0,16},{4,8},{8,4},{12,28},{16,0},{20,24},{24,20},{28,12},{1,17},{... | collective-permute-start | bytes 393224 | tf_op jit(solution)/shard_map/ppermute | solution.py:434
  16.6 8.6 %collective-permute-start.4 = (f32[32,1024]{1,0:T(8,128)S(1)}, f32[32,1024]{1,0:T(8,128)S(1)}, u32[]{:S(2)}, u32[]{:S(2)}) collective-permute-start(f32[32,1024]{1,0:T(8,128)S(1)} %shard_map.141.refs_3_), channel_id=1, source_target_pairs={{0,4},{4,0},{8,12},{12,8},{16,20},{20,16},{24,28},{28,24},{1,5},{5... | collective-permute-start | bytes 393224 | tf_op jit(solution)/shard_map/ppermute | solution.py:434
  20.3 4.9 %collective-permute-start.10 = (f32[32,1024]{1,0:T(8,128)S(1)}, f32[32,1024]{1,0:T(8,128)S(1)}, u32[]{:S(2)}, u32[]{:S(2)}) collective-permute-start(f32[32,1024]{1,0:T(8,128)S(1)} %shard_map.142.after_ref), channel_id=1, source_target_pairs={{0,16},{4,8},{8,4},{12,28},{16,0},{20,24},{24,20},{28,12},{1,17},{... | collective-permute-start | bytes 393224 | tf_op jit(solution)/shard_map/ppermute | solution.py:434
  21.8 6.4 %collective-permute-start.7 = (f32[32,1024]{1,0:T(8,128)S(1)}, f32[32,1024]{1,0:T(8,128)S(1)}, u32[]{:S(2)}, u32[]{:S(2)}) collective-permute-start(f32[32,1024]{1,0:T(8,128)S(1)} %shard_map.144.refs_3_), channel_id=1, source_target_pairs={{0,4},{4,0},{8,12},{12,8},{16,20},{20,16},{24,28},{28,24},{1,5},{5... | collective-permute-start | bytes 393224 | tf_op jit(solution)/shard_map/ppermute | solution.py:434
  23.5 9.3 %collective-permute-start.9 = (f32[32,1024]{1,0:T(8,128)S(1)}, f32[32,1024]{1,0:T(8,128)S(1)}, u32[]{:S(2)}, u32[]{:S(2)}) collective-permute-start(f32[32,1024]{1,0:T(8,128)S(1)} %shard_map.145.refs_3_), channel_id=1, source_target_pairs={{0,4},{4,0},{8,12},{12,8},{16,20},{20,16},{24,28},{28,24},{1,5},{5... | collective-permute-start | bytes 393224 | tf_op jit(solution)/shard_map/ppermute | solution.py:434
  25.2 8.2 %collective-permute-start.11 = (f32[32,1024]{1,0:T(8,128)S(1)}, f32[32,1024]{1,0:T(8,128)S(1)}, u32[]{:S(2)}, u32[]{:S(2)}) collective-permute-start(f32[32,1024]{1,0:T(8,128)S(1)} %shard_map.146), channel_id=1, source_target_pairs={{0,4},{4,0},{8,12},{12,8},{16,20},{20,16},{24,28},{28,24},{1,5},{5... | collective-permute-start | bytes 393224 | tf_op jit(solution)/shard_map/ppermute | solution.py:434
  29.2 8.5 %collective-permute-start.13 = (f32[256,128]{1,0:T(8,128)S(1)}, f32[256,128]{1,0:T(8,128)S(1)}, u32[]{:S(2)}, u32[]{:S(2)}) collective-permute-start(f32[256,128]{1,0:T(8,128)S(1)} %shard_map.150.refs_0_), channel_id=1, source_target_pairs={{0,1},{1,0},{2,3},{3,2},{4,5},{5,4},{6,7},{7,6},{8,9},{9,8},{10,11... | collective-permute-start | bytes 393224 | tf_op jit(solution)/shard_map/ppermute | solution.py:421
  30.8 8.0 %collective-permute-start.14 = (f32[256,128]{1,0:T(8,128)S(1)}, f32[256,128]{1,0:T(8,128)S(1)}, u32[]{:S(2)}, u32[]{:S(2)}) collective-permute-start(f32[256,128]{1,0:T(8,128)S(1)} %shard_map.150.refs_0_), channel_id=1, source_target_pairs={{0,2},{1,3},{2,0},{3,1},{4,6},{5,7},{6,4},{7,5},{8,10},{9,11},{10,... | collective-permute-start | bytes 393224 | tf_op jit(solution)/shard_map/ppermute | solution.py:421
  32.3 7.0 %collective-permute-start.15 = (f32[256,128]{1,0:T(8,128)S(1)}, f32[256,128]{1,0:T(8,128)S(1)}, u32[]{:S(2)}, u32[]{:S(2)}) collective-permute-start(f32[256,128]{1,0:T(8,128)S(1)} %shard_map.150.refs_0_), channel_id=1, source_target_pairs={{0,3},{1,2},{2,1},{3,0},{4,7},{5,6},{6,5},{7,4},{8,11},{9,10},{10,... | collective-permute-start | bytes 393224 | tf_op jit(solution)/shard_map/ppermute | solution.py:421
  34.6 13.3 %collective-permute-start.16 = (f32[256,128]{1,0:T(8,128)S(1)}, f32[256,128]{1,0:T(8,128)S(1)}, u32[]{:S(2)}, u32[]{:S(2)}) collective-permute-start(f32[256,128]{1,0:T(8,128)S(1)} %shard_map.153.refs_1_), channel_id=1, source_target_pairs={{0,1},{1,0},{2,3},{3,2},{4,5},{5,4},{6,7},{7,6},{8,9},{9,8},{10,11... | collective-permute-start | bytes 393224 | tf_op jit(solution)/shard_map/ppermute | solution.py:421
  36.2 11.8 %collective-permute-start.17 = (f32[256,128]{1,0:T(8,128)S(1)}, f32[256,128]{1,0:T(8,128)S(1)}, u32[]{:S(2)}, u32[]{:S(2)}) collective-permute-start(f32[256,128]{1,0:T(8,128)S(1)} %shard_map.153.refs_1_), channel_id=1, source_target_pairs={{0,2},{1,3},{2,0},{3,1},{4,6},{5,7},{6,4},{7,5},{8,10},{9,11},{10,... | collective-permute-start | bytes 393224 | tf_op jit(solution)/shard_map/ppermute | solution.py:421
  37.7 10.2 %collective-permute-start.18 = (f32[256,128]{1,0:T(8,128)S(1)}, f32[256,128]{1,0:T(8,128)S(1)}, u32[]{:S(2)}, u32[]{:S(2)}) collective-permute-start(f32[256,128]{1,0:T(8,128)S(1)} %shard_map.153.refs_1_), channel_id=1, source_target_pairs={{0,3},{1,2},{2,1},{3,0},{4,7},{5,6},{6,5},{7,4},{8,11},{9,10},{10,... | collective-permute-start | bytes 393224 | tf_op jit(solution)/shard_map/ppermute | solution.py:421
  38.8 3.6 %collective-permute-start.12 = (f32[2,16]{1,0:T(2,128)S(1)}, f32[2,16]{1,0:T(2,128)S(1)}, u32[]{:S(2)}, u32[]{:S(2)}) collective-permute-start(f32[2,16]{1,0:T(2,128)S(1)} %shard_map.148.x_ref.refs_11_), channel_id=1, source_target_pairs={{0,4},{4,0},{8,12},{12,8},{1,5},{5,1},{9,13},{13,9},{2,6},{6,2},{1... | collective-permute-start | bytes 392 | tf_op jit(solution)/shard_map/ppermute | solution.py:421
  42.3 4.5 %collective-permute-start.19 = (f32[2,16]{1,0:T(2,128)S(1)}, f32[2,16]{1,0:T(2,128)S(1)}, u32[]{:S(2)}, u32[]{:S(2)}) collective-permute-start(f32[2,16]{1,0:T(2,128)S(1)} %shard_map.149.refs_24_.x_ref), channel_id=1, source_target_pairs={{0,8},{4,12},{8,0},{12,4},{1,9},{5,13},{9,1},{13,5},{2,10},{6,14},... | collective-permute-start | bytes 392 | tf_op jit(solution)/shard_map/ppermute | solution.py:421
  46.8 1.1 %collective-permute-start.20 = (f32[2,16]{1,0:T(2,128)S(1)}, f32[2,16]{1,0:T(2,128)S(1)}, u32[]{:S(2)}, u32[]{:S(2)}) collective-permute-start(f32[2,16]{1,0:T(2,128)S(1)} %shard_map.154.refs_5_), channel_id=1, source_target_pairs={{0,16},{16,0},{1,17},{17,1},{2,18},{18,2},{3,19},{19,3},{4,20},{20... | collective-permute-start | bytes 392 | tf_op jit(solution)/shard_map/ppermute | solution.py:421

commit v4 on v2

--- a/solution.py
+++ b/solution.py
@@ -1,4 +1,5 @@
 import functools
+import math
 
 import jax
 import jax.numpy as jnp
@@ -374,17 +375,9 @@
     refs[-1][...] = x_ref[...] + y_ref[...]
 
 
-def sum_kernel(*refs):
-    refs[-1][...] = tree([ref[...] for ref in refs[:-1]])
-
-
-def last_kernel(counts, *refs):
+def last_kernel(*refs):
     refs, (gb_ref, gc_ref, rate_ref, skip_ref) = refs[:-4], refs[-4:]
-    sums = []
-    for count in counts:
-        sums.append(tree([ref[...] for ref in refs[:count]]))
-        refs = refs[count:]
-    *shares, small = sums
+    *shares, small = [tree([ref[i] for i in range(ref.shape[0])]) for ref in refs]
     start = 0
     for both in shares:
         rows = both.shape[1] // 2
@@ -484,33 +477,11 @@
     return states
 
 
-def sum_terms(x, axis, size):
-    if size == 1:
-        return [x]
-    if size == 4:
-        return [x] + [swap(x, axis, size, bit) for bit in (1, 2, 3)]
-    if size & (size - 1):
-        return [lax.psum(x, axis)]
-    bit = 1
-    while 2 * bit < size:
-        x = x + swap(x, axis, size, bit)
-        bit *= 2
-    return [x, swap(x, axis, size, bit)]
-
-
-def small_terms(x, axes, sizes, between):
-    bits = [(axis, 1 << k) for axis in axes for k in range(sizes[axis].bit_length() - 1)]
-    if any(sizes[axis] & (sizes[axis] - 1) for axis in axes):
-        x = lax.psum(x, tuple(axes))
-        between((x,))
-        return [x]
-    for count, (axis, bit) in enumerate(bits):
-        theirs = swap(x, axis, sizes[axis], bit)
-        if count == len(bits) - 1:
-            break
-        x = call(add_kernel, [jax.ShapeDtypeStruct(x.shape, F32)])(x, theirs)[0]
-    between((x,))
-    return [x, theirs] if bits else [x]
+def sum_terms(x, axes, sizes):
+    count = math.prod(sizes[axis] for axis in axes)
+    if count == 1:
+        return x[None]
+    return lax.all_to_all(jnp.broadcast_to(x, (count, *x.shape)), axes, 0, 0)
 
 
 def shards(sizes, values, gate_in, in_b, in_c, step_sizes, log_rates, skip_gain, grad_out):
@@ -587,7 +558,7 @@
     coef, mamba, inner, growth, fall, grad_y, grad_cum, parts = made["prepare"]
 
     rate_row = jnp.zeros((1, channels), F32)
-    terms, counts, done = [], [], []
+    terms = []
     for i in range(PARTS):
         final = i == PARTS - 1
         count = CHUNKS // PARTS
@@ -602,30 +573,24 @@
             flops=10 * length * channels * rows * count,
             after=(rate_row,),
         )(*own, high, low, scaled, sum_b, sum_c)[0]
-        own = sum_terms(share_of, "tensor", sizes["tensor"])
-        if not final:
-            own = [call(sum_kernel, [like(share_of.shape, F32)])(*own)[0]]
-            done += own
-        terms += own
-        counts.append(len(own))
+        terms.append(sum_terms(share_of, ("tensor",), sizes))
 
     def rest(after):
         made["rest"] = call(
             functools.partial(rest_kernel, seq, CHUNKS),
             [like((1, length, channels), BF16)] * 2 + [like((1, heads, length), F32)],
             flops=10 * length * channels * state,
-            after=(*after, *done),
+            after=after,
         )(
             *(x for group in states for x in group),
             vals, block_b, block_c, coef, mamba, inner, growth, fall, grad_y, grad_cum, decay, negative,
         )
 
-    own = small_terms(rate_row, ("replica", "seq"), sizes, rest)
-    terms += own
-    counts.append(len(own))
+    terms.append(sum_terms(rate_row, ("replica", "seq"), sizes))
+    rest(())
     grad_values, grad_gate, grad_steps = made["rest"]
     grad_b, grad_c, rate_sum, skip_sum = call(
-        functools.partial(last_kernel, tuple(counts)),
+        last_kernel,
         [like((1, length, state), F32)] * 2 + [like((1, heads), F32)] * 2,
     )(*terms)
     return (

time: 47.6 us -> 79.7 us (1.67)
  local copies, waits for them, and re-layouts: 0.01 us -> 23.2 us
  waiting for transfers between devices: 6.55 us -> 13.5 us
  Pallas kernels: 13.7 us -> 14.5 us
    unnamed x0 -> x66, local copies, waits for them, and re-layouts: none -> 19.1 us
    all_to_all x0 -> x3, starting transfers between devices: none -> 11.2 us  [sum_terms(): return lax.all_to_all(jnp.broadcast_to(x, (count, *x.shape)), axes, 0, 0)]
    ppermute x9 -> x0, starting transfers between devices: 8.63 us -> none  [swap(): return lax.ppermute(x, axis, [(i, i ^ bit) for i in range(size)])]
    all_to_all x0 -> x3, waiting for transfers between devices: none -> 6.41 us  [sum_terms(): return lax.all_to_all(jnp.broadcast_to(x, (count, *x.shape)), axes, 0, 0)]
    ppermute x12, waiting for transfers between devices: 2.16 us -> 7.09 us  [hop(): return lax.ppermute(x, ('replica', 'seq'), pairs)]
    ppermute x9 -> x0, waiting for transfers between devices: 4.39 us -> none  [swap(): return lax.ppermute(x, axis, [(i, i ^ bit) for i in range(size)])]
    broadcast_in_dim x0 -> x3, local copies, waits for them, and re-layouts: none -> 4.07 us  [sum_terms(): return lax.all_to_all(jnp.broadcast_to(x, (count, *x.shape)), axes, 0, 0)]
    ppermute x12, starting transfers between devices: 17.7 us -> 15.6 us  [hop(): return lax.ppermute(x, ('replica', 'seq'), pairs)]
  transfers between devices with their start and end apart: 21 -> 15, of which waited for: 6 -> 5; matrix products, arithmetic and copies ran while one was open for 0% -> 0% of each run, Pallas kernels for 21% -> 12%
where the time goes in v4:
time: 79.7 us; the launch traced here: 78.9 us
  starting transfers between devices  26.8 us (34%)
  local copies, waits for them, and re-layouts  23.2 us (29%)
  Pallas kernels  14.5 us (18%)
  waiting for transfers between devices  13.5 us (17%)
  between operations  0.97 us (1%)
    unnamed x66, local copies, waits for them, and re-layouts  19.1 us
    ppermute x12, starting transfers between devices, hop(): return lax.ppermute(x, ('replica', 'seq'), pairs)  15.6 us
    pallas_call x18, Pallas kernels, run(): pl.pallas_call(kernel, out_shape=tuple(outs), in_specs=specs, out_specs=t...  14.5 us
    all_to_all x3, starting transfers between devices, sum_terms(): return lax.all_to_all(jnp.broadcast_to(x, (count, *x.shape)), axes, 0, 0)  11.2 us
    ppermute x12, waiting for transfers between devices, hop(): return lax.ppermute(x, ('replica', 'seq'), pairs)  7.09 us
    all_to_all x3, waiting for transfers between devices, sum_terms(): return lax.all_to_all(jnp.broadcast_to(x, (count, *x.shape)), axes, 0, 0)  6.41 us
    broadcast_in_dim x3, local copies, waits for them, and re-layouts, sum_terms(): return lax.all_to_all(jnp.broadcast_to(x, (count, *x.shape)), axes, 0, 0)  4.07 us
  transfers between devices with their start and end apart: 15, of which 5 were waited for; matrix products, arithmetic and copies ran while one was open for 0% of the time, Pallas kernels for 12%

profile of v4, /device:TPU:0, one launch (start us, length us, event | category | flops | bytes accessed | tf_op | source)
XLA Modules:
  0.0 78.9 jit_solution(12667598920309288748)
XLA Ops:
  0.6 2.8 %shard_map.135 = (bf16[256,1024]{1,0:T(8,128)(2,1)S(1)}, bf16[256,1024]{1,0:T(8,128)(2,1)S(1)}, bf16[256,1024]{1,0:T(8,128)(2,1)S(1)}, bf16[256,128]{1,0:T(8,128...) custom-call(bf16[256,1024]{1,0:T(8,128)(2,1)} %bitcast.10, ...), custom_call_target="tpu_custom_call" | custom-call | flops 268435456 | bytes 4513984 | tf_op jit(solution)/shard_map/pallas_call | solution.py:399
  3.4 3.1 %collective-permute-start = (f32[32,1024]{1,0:T(8,128)S(1)}, f32[32,1024]{1,0:T(8,128)S(1)}, u32[]{:S(2)}, u32[]{:S(2)}) collective-permute-start(f32[32,1024]{1,0:T(8,128)S(1)} %get-tuple-element.49.refs_1_), channel_id=1, source_target_pairs={{0,4},{4,0},{8,12},{12,8},{16,20},{20,16},{24,28},{28,24},{1,5},{5... | collective-permute-start | bytes 393224 | tf_op jit(solution)/shard_map/ppermute | solution.py:426
  6.5 0.1 collective-permute-start.3
  6.6 1.9 %collective-permute-start.2 = (f32[32,1024]{1,0:T(8,128)S(1)}, f32[32,1024]{1,0:T(8,128)S(1)}, u32[]{:S(2)}, u32[]{:S(2)}) collective-permute-start(f32[32,1024]{1,0:T(8,128)S(1)} %get-tuple-element.59.refs_1_), channel_id=1, source_target_pairs={{0,4},{4,0},{8,12},{12,8},{16,20},{20,16},{24,28},{28,24},{1,5},{5... | collective-permute-start | bytes 393224 | tf_op jit(solution)/shard_map/ppermute | solution.py:426
  8.5 2.4 %shard_map.136 = (f32[256,1024]{1,0:T(8,128)S(1)}, f32[256,1024]{1,0:T(8,128)S(1)}, f32[256,128]{1,0:T(8,128)S(1)}, f32[256,128]{1,0:T(8,128)S(1)}) custom-call(bf16[256,1024]{1,0:T(8,128)(2,1)S(1)} %get-tuple-element.51.v_ref.refs_12_, bf16[256,1024]{1,0:T(8,128)(2,1)S(1)} %get-tuple-element.52.gate_ref, bf16[256,1024]{1,0:T(8,128)(2,1)S(1)} %get-tuple-element.53.go_ref, ...), custom_call_target="tpu_custom_call" | custom-call | flops 1073741824 | bytes 4079616 | tf_op jit(solution)/shard_map/pallas_call | solution.py:399
  11.0 0.0 copy-start.19
  11.0 0.6 copy-done.19
  11.7 0.0 collective-permute-done.refs_0_
  11.7 0.6 copy-done.3
  12.3 0.0 collective-permute-start.1
  12.3 3.1 %collective-permute-start.6 = (f32[32,1024]{1,0:T(8,128)S(1)}, f32[32,1024]{1,0:T(8,128)S(1)}, u32[]{:S(2)}, u32[]{:S(2)}) collective-permute-start(f32[32,1024]{1,0:T(8,128)S(1)} %get-tuple-element.66.refs_1_), channel_id=1, source_target_pairs={{0,4},{4,0},{8,12},{12,8},{16,20},{20,16},{24,28},{28,24},{1,5},{5... | collective-permute-start | bytes 393224 | tf_op jit(solution)/shard_map/ppermute | solution.py:426
  15.5 1.3 %shard_map.138 = (bf16[256,1024]{1,0:T(8,128)(2,1)S(1)}, bf16[256,1024]{1,0:T(8,128)(2,1)S(1)}, bf16[256,1024]{1,0:T(8,128)(2,1)S(1)}, f32[128,1024]{1,0:T(8,128)S(1)}, f32[128,1024]{1,0:T(8,128)S(1)}) custom-call(bf16[256,1024]{1,0:T(8,128)(2,1)S(1)} %get-tuple-element.51.v_ref.refs_12_, bf16[256,1024]{1,0:T(8,128)(2,1)S(1)} %get-tuple-element.52.gate_ref, ...), custom_call_target="tpu_custom_call" | custom-call | flops 268435456 | bytes 4472832 | tf_op jit(solution)/shard_map/pallas_call | solution.py:399
  16.7 0.0 collective-permute-done.3.refs_0_.refs_3_
  16.8 0.1 collective-permute-start.5
  16.9 0.0 collective-permute-done.2.refs_0_.refs_6_
  16.9 0.5 collective-permute-start.8
  17.5 2.8 %collective-permute-start.4 = (f32[32,1024]{1,0:T(8,128)S(1)}, f32[32,1024]{1,0:T(8,128)S(1)}, u32[]{:S(2)}, u32[]{:S(2)}) collective-permute-start(f32[32,1024]{1,0:T(8,128)S(1)} %shard_map.141.refs_3_), channel_id=1, source_target_pairs={{0,4},{4,0},{8,12},{12,8},{16,20},{20,16},{24,28},{28,24},{1,5},{5... | collective-permute-start | bytes 393224 | tf_op jit(solution)/shard_map/ppermute | solution.py:426
  20.3 0.1 collective-permute-start.10
  20.4 1.4 %shard_map.143 = (f32[256,1024]{1,0:T(8,128)S(1)}, f32[256,1024]{1,0:T(8,128)S(1)}, f32[256,1024]{1,0:T(8,128)S(1)}, f32[256,1024]{1,0:T(8,128)S(1)}, f32[256,10...) custom-call(bf16[256,1024]{1,0:T(8,128)(2,1)S(1)} %get-tuple-element.51.v_ref.refs_12_, ...), custom_call_target="tpu_custom_call" | custom-call | flops 268435456 | bytes 10125504 | tf_op jit(solution)/shard_map/pallas_call | solution.py:399
  21.8 1.0 %copy-done.12 = f32[256,1024]{1,0:T(8,128)} copy-done((f32[256,1024]{1,0:T(8,128)}, f32[256,1024]{1,0:T(8,128)S(1)}, u32[]{:S(2)}) %copy-start.12) | copy-done | bytes 1048600
  22.8 1.0 %copy-done.14 = f32[256,1024]{1,0:T(8,128)} copy-done((f32[256,1024]{1,0:T(8,128)}, f32[256,1024]{1,0:T(8,128)S(1)}, u32[]{:S(2)}) %copy-start.14) | copy-done | bytes 1048600
  23.8 1.0 %copy-done.16 = f32[256,1024]{1,0:T(8,128)} copy-done((f32[256,1024]{1,0:T(8,128)}, f32[256,1024]{1,0:T(8,128)S(1)}, u32[]{:S(2)}) %copy-start.16) | copy-done | bytes 1048600
  24.8 0.6 copy-done.29
  25.4 1.6 %collective-permute-start.7 = (f32[32,1024]{1,0:T(8,128)S(1)}, f32[32,1024]{1,0:T(8,128)S(1)}, u32[]{:S(2)}, u32[]{:S(2)}) collective-permute-start(f32[32,1024]{1,0:T(8,128)S(1)} %shard_map.144.refs_3_), channel_id=1, source_target_pairs={{0,4},{4,0},{8,12},{12,8},{16,20},{20,16},{24,28},{28,24},{1,5},{5... | collective-permute-start | bytes 393224 | tf_op jit(solution)/shard_map/ppermute | solution.py:426
  27.1 0.0 collective-permute-done.8.refs_0_.refs_7_.refs_1_
  27.1 0.5 collective-permute-start.9
  27.6 0.0 collective-permute-done.4.refs_4_.refs_2_
  27.6 1.6 %collective-permute-start.11 = (f32[32,1024]{1,0:T(8,128)S(1)}, f32[32,1024]{1,0:T(8,128)S(1)}, u32[]{:S(2)}, u32[]{:S(2)}) collective-permute-start(f32[32,1024]{1,0:T(8,128)S(1)} %shard_map.146), channel_id=1, source_target_pairs={{0,4},{4,0},{8,12},{12,8},{16,20},{20,16},{24,28},{28,24},{1,5},{5... | collective-permute-start | bytes 393224 | tf_op jit(solution)/shard_map/ppermute | solution.py:426
  29.3 2.5 %collective-permute-done.7.refs_5_ = f32[32,1024]{1,0:T(8,128)S(1)} collective-permute-done((f32[32,1024]{1,0:T(8,128)S(1)}, f32[32,1024]{1,0:T(8,128)S(1)}, u32[]{:S(2)}, u32[]{:S(2)}) %collective-permute-start.7) | collective-permute-done | bytes 131104 | tf_op jit(solution)/shard_map/ppermute | solution.py:426
  31.8 0.1 shard_map.148.refs_11_.refs_9_
  32.0 0.5 copy-done
  32.5 2.2 %collective-permute-done.9.refs_8_.refs_2_ = f32[32,1024]{1,0:T(8,128)S(1)} collective-permute-done((f32[32,1024]{1,0:T(8,128)S(1)}, f32[32,1024]{1,0:T(8,128)S(1)}, u32[]{:S(2)}, u32[]{:S(2)}) %collective-permute-start.9) | collective-permute-done | bytes 131104 | tf_op jit(solution)/shard_map/ppermute | solution.py:426
  34.6 2.4 %collective-permute-done.11.refs_11_.refs_5_ = f32[32,1024]{1,0:T(8,128)S(1)} collective-permute-done((f32[32,1024]{1,0:T(8,128)S(1)}, f32[32,1024]{1,0:T(8,128)S(1)}, u32[]{:S(2)}, u32[]{:S(2)}) %collective-permute-start.11) | collective-permute-done | bytes 131104 | tf_op jit(solution)/shard_map/ppermute | solution.py:426
  37.0 0.2 shard_map.150.refs_11_
  37.2 0.6 broadcast_in_dim.15
  37.8 0.6 copy-done.31
  38.4 3.3 %all-to-all-start.2 = ((f32[8,2,16]{2,1,0:T(2,128)}), f32[8,2,16]{2,1,0:T(2,128)S(1)}, u32[]{:S(2)}, u32[]{:S(2)}) async-start(f32[8,2,16]{2,1,0:T(2,128)} %broadcast_in_dim.15), calls=%async_computation.2 | async-start | bytes 16384 | tf_op jit(solution)/shard_map/all_to_all | solution.py:484
  41.8 0.0 copy-start.1
  41.8 0.9 %copy-done.1 = f32[32,1024]{1,0:T(8,128)S(1)} copy-done((f32[32,1024]{1,0:T(8,128)S(1)}, f32[32,1024]{1,0:T(8,128)}, u32[]{:S(2)}) %copy-start.1) | copy-done | bytes 131096
  42.7 0.9 %copy-done.4 = f32[256,128]{1,0:T(8,128)S(1)} copy-done((f32[256,128]{1,0:T(8,128)S(1)}, f32[256,128]{1,0:T(8,128)}, u32[]{:S(2)}) %copy-start.4) | copy-done | bytes 131096
  43.6 0.9 %copy-done.20 = f32[256,128]{1,0:T(8,128)S(1)} copy-done((f32[256,128]{1,0:T(8,128)S(1)}, f32[256,128]{1,0:T(8,128)}, u32[]{:S(2)}) %copy-start.20) | copy-done | bytes 131096
  44.5 0.9 %shard_map.149 = f32[256,128]{1,0:T(8,128)S(1)} custom-call(f32[32,1024]{1,0:T(8,128)S(1)} %collective-permute-done.refs_0_, f32[32,1024]{1,0:T(8,128)S(1)} %collective-permute-done.1.refs_0_.refs_1_, f32[32,1024]{1,0:T(8,128)S(1)} %collective-permute-done.4.refs_4_.refs_2_, f32[32,1024]{1,0:T(8,128)S(1)} %collective-permute-done.3.refs_0_.refs_3_, ...), custom_call_target="tpu_custom_call" | custom-call | flops 167772160 | bytes 2756608 | tf_op jit(solution)/shard_map/pallas_call | solution.py:399
  45.4 0.6 copy-done.22
  46.0 1.2 %all-to-all-done.2.refs_2_ = f32[8,2,16]{2,1,0:T(2,128)S(1)} async-done(((f32[8,2,16]{2,1,0:T(2,128)}), f32[8,2,16]{2,1,0:T(2,128)S(1)}, u32[]{:S(2)}, u32[]{:S(2)}) %all-to-all-start.2) | async-done | bytes 1056 | tf_op jit(solution)/shard_map/all_to_all | solution.py:484
  47.3 1.7 %broadcast_in_dim.13 = f32[4,256,128]{2,1,0:T(8,128)} broadcast(f32[256,128]{1,0:T(8,128)} %copy-done.22), dimensions={1,2} | broadcast | bytes 655360 | tf_op jit(solution)/shard_map/broadcast_in_dim | solution.py:484
  49.0 4.3 %all-to-all-start = ((f32[4,256,128]{2,1,0:T(8,128)}), f32[4,256,128]{2,1,0:T(8,128)}, u32[]{:S(2)}, u32[]{:S(2)}) async-start(f32[4,256,128]{2,1,0:T(8,128)} %broadcast_in_dim.13), calls=%async_computation | async-start | bytes 1048576 | tf_op jit(solution)/shard_map/all_to_all | solution.py:484
  53.3 0.0 copy-start.5
  53.3 0.9 %copy-done.5 = f32[256,128]{1,0:T(8,128)S(1)} copy-done((f32[256,128]{1,0:T(8,128)S(1)}, f32[256,128]{1,0:T(8,128)}, u32[]{:S(2)}) %copy-start.5) | copy-done | bytes 131096
  54.2 0.9 %copy-done.21 = f32[256,128]{1,0:T(8,128)S(1)} copy-done((f32[256,128]{1,0:T(8,128)S(1)}, f32[256,128]{1,0:T(8,128)}, u32[]{:S(2)}) %copy-start.21) | copy-done | bytes 131096
  55.1 1.0 %shard_map.151 = f32[256,128]{1,0:T(8,128)S(1)} custom-call(f32[32,1024]{1,0:T(8,128)S(1)} %collective-permute-done.2.refs_0_.refs_6_, f32[32,1024]{1,0:T(8,128)S(1)} %collective-permute-done.8.refs_0_.refs_7_.refs_1_, f32[32,1024]{1,0:T(8,128)S(1)} %collective-permute-done.9.refs_8_.refs_2_, f32[32,1024]{1,0:T(8,128)S(1)} %collective-permute-done.6.refs_0_.refs_9_.refs_3_, ...), custom_call_target="tpu_custom_call" | custom-call | flops 167772160 | bytes 2752640 | tf_op jit(solution)/shard_map/pallas_call | solution.py:399
  56.1 0.0 copy-start.18
  56.1 0.6 copy-done.18
  56.8 5.2 %all-to-all-done.refs_0_ = f32[4,256,128]{2,1,0:T(8,128)} async-done(((f32[4,256,128]{2,1,0:T(8,128)}), f32[4,256,128]{2,1,0:T(8,128)}, u32[]{:S(2)}, u32[]{:S(2)}) %all-to-all-start) | async-done | bytes 524320 | tf_op jit(solution)/shard_map/all_to_all | solution.py:484
  61.9 1.7 %broadcast_in_dim.14 = f32[4,256,128]{2,1,0:T(8,128)} broadcast(f32[256,128]{1,0:T(8,128)} %copy-done.18), dimensions={1,2} | broadcast | bytes 655360 | tf_op jit(solution)/shard_map/broadcast_in_dim | solution.py:484
  63.7 0.0 copy-start.30
  63.7 3.6 %all-to-all-start.1 = ((f32[4,256,128]{2,1,0:T(8,128)}), f32[4,256,128]{2,1,0:T(8,128)S(1)}, u32[]{:S(2)}, u32[]{:S(2)}) async-start(f32[4,256,128]{2,1,0:T(8,128)} %broadcast_in_dim.14), calls=%async_computation.1 | async-start | bytes 1048576 | tf_op jit(solution)/shard_map/all_to_all | solution.py:484
  67.4 1.2 %copy-done.7 = f32[256,1024]{1,0:T(8,128)S(1)} copy-done((f32[256,1024]{1,0:T(8,128)S(1)}, f32[256,1024]{1,0:T(8,128)}, u32[]{:S(2)}) %copy-start.7) | copy-done | bytes 1048600
  68.6 1.2 %copy-done.9 = f32[256,1024]{1,0:T(8,128)S(1)} copy-done((f32[256,1024]{1,0:T(8,128)S(1)}, f32[256,1024]{1,0:T(8,128)}, u32[]{:S(2)}) %copy-start.9) | copy-done | bytes 1048600
  69.8 1.2 %copy-done.11 = f32[256,1024]{1,0:T(8,128)S(1)} copy-done((f32[256,1024]{1,0:T(8,128)S(1)}, f32[256,1024]{1,0:T(8,128)}, u32[]{:S(2)}) %copy-start.11) | copy-done | bytes 1048600
  71.0 1.2 %copy-done.13 = f32[256,1024]{1,0:T(8,128)S(1)} copy-done((f32[256,1024]{1,0:T(8,128)S(1)}, f32[256,1024]{1,0:T(8,128)}, u32[]{:S(2)}) %copy-start.13) | copy-done | bytes 1048600
  72.3 1.2 %copy-done.15 = f32[256,1024]{1,0:T(8,128)S(1)} copy-done((f32[256,1024]{1,0:T(8,128)S(1)}, f32[256,1024]{1,0:T(8,128)}, u32[]{:S(2)}) %copy-start.15) | copy-done | bytes 1048600
  73.5 1.2 %copy-done.17 = f32[256,1024]{1,0:T(8,128)S(1)} copy-done((f32[256,1024]{1,0:T(8,128)S(1)}, f32[256,1024]{1,0:T(8,128)}, u32[]{:S(2)}) %copy-start.17) | copy-done | bytes 1048600
  74.7 2.4 %shard_map.147 = (bf16[1,256,1024]{2,1,0:T(8,128)(2,1)}, bf16[1,256,1024]{2,1,0:T(8,128)(2,1)}, f32[1,16,256]{2,1,0:T(8,128)}) custom-call(f32[32,1024]{1,0:T(8,128)S(1)} %collective-permute-done.refs_0_, f32[32,1024]{1,0:T(8,128)S(1)} %collective-permute-done.1.refs_0_.refs_1_, f32[32,1024]{1,0:T(8,128)S(1)} %collective-permute-done.4.refs_4_.refs_2_, ...), custom_call_target="tpu_custom_call" | custom-call | flops 335544320 | bytes 9621504 | tf_op jit(solution)/shard_map/pallas_call | solution.py:399
  77.1 1.9 %shard_map.152 = (f32[1,256,128]{2,1,0:T(8,128)}, f32[1,256,128]{2,1,0:T(8,128)}, f32[1,16]{1,0:T(1,128)}, f32[1,16]{1,0:T(1,128)}) custom-call(f32[4,256,128]{2,1,0:T(8,128)} %all-to-all-done.refs_0_, f32[4,256,128]{2,1,0:T(8,128)S(1)} %all-to-all-done.1.refs_1_, f32[8,2,16]{2,1,0:T(2,128)S(1)} %all-to-all-done.2.refs_2_), custom_call_target="tpu_custom_call" | custom-call | bytes 1311872 | tf_op jit(solution)/shard_map/pallas_call | solution.py:399
  (54 shorter events, 0.2 us)
Async XLA Ops:
  3.4 7.6 %copy-start.27 = (f32[16,256]{1,0:T(8,128)}, f32[16,256]{1,0:T(8,128)S(1)}, u32[]{:S(2)}) copy-start(f32[16,256]{1,0:T(8,128)S(1)} %get-tuple-element.77.refs_23_) | copy-start | bytes 49156
  3.4 12.1 %copy-start.23 = (bf16[256,128]{1,0:T(8,128)(2,1)}, bf16[256,128]{1,0:T(8,128)(2,1)S(1)}, u32[]{:S(2)}) copy-start(bf16[256,128]{1,0:T(8,128)(2,1)S(1)} %get-tuple-element.54.b_ref.refs_13_) | copy-start | bytes 196612
  3.4 12.0 %copy-start.25 = (bf16[256,128]{1,0:T(8,128)(2,1)}, bf16[256,128]{1,0:T(8,128)(2,1)S(1)}, u32[]{:S(2)}) copy-start(bf16[256,128]{1,0:T(8,128)(2,1)S(1)} %get-tuple-element.55.c_ref.refs_14_) | copy-start | bytes 196612
  3.4 8.2 %collective-permute-start = (f32[32,1024]{1,0:T(8,128)S(1)}, f32[32,1024]{1,0:T(8,128)S(1)}, u32[]{:S(2)}, u32[]{:S(2)}) collective-permute-start(f32[32,1024]{1,0:T(8,128)S(1)} %get-tuple-element.49.refs_1_), channel_id=1, source_target_pairs={{0,4},{4,0},{8,12},{12,8},{16,20},{20,16},{24,28},{28,24},{1,5},{5... | collective-permute-start | bytes 393224 | tf_op jit(solution)/shard_map/ppermute | solution.py:426
  6.5 10.2 %collective-permute-start.3 = (f32[32,1024]{1,0:T(8,128)S(1)}, f32[32,1024]{1,0:T(8,128)S(1)}, u32[]{:S(2)}, u32[]{:S(2)}) collective-permute-start(f32[32,1024]{1,0:T(8,128)S(1)} %get-tuple-element.60.refs_1_), channel_id=1, source_target_pairs={{0,4},{4,0},{8,12},{12,8},{16,20},{20,16},{24,28},{28,24},{1,5},{5... | collective-permute-start | bytes 393224 | tf_op jit(solution)/shard_map/ppermute | solution.py:426
  6.6 10.3 %collective-permute-start.2 = (f32[32,1024]{1,0:T(8,128)S(1)}, f32[32,1024]{1,0:T(8,128)S(1)}, u32[]{:S(2)}, u32[]{:S(2)}) collective-permute-start(f32[32,1024]{1,0:T(8,128)S(1)} %get-tuple-element.59.refs_1_), channel_id=1, source_target_pairs={{0,4},{4,0},{8,12},{12,8},{16,20},{20,16},{24,28},{28,24},{1,5},{5... | collective-permute-start | bytes 393224 | tf_op jit(solution)/shard_map/ppermute | solution.py:426
  11.0 0.7 copy-start.19
  11.7 0.7 copy-start.3
  12.3 5.1 %collective-permute-start.1 = (f32[32,1024]{1,0:T(8,128)S(1)}, f32[32,1024]{1,0:T(8,128)S(1)}, u32[]{:S(2)}, u32[]{:S(2)}) collective-permute-start(f32[32,1024]{1,0:T(8,128)S(1)} %shard_map.137.after_ref), channel_id=1, source_target_pairs={{0,16},{4,8},{8,4},{12,28},{16,0},{20,24},{24,20},{28,12},{1,17},{... | collective-permute-start | bytes 393224 | tf_op jit(solution)/shard_map/ppermute | solution.py:426
  12.3 8.0 %collective-permute-start.6 = (f32[32,1024]{1,0:T(8,128)S(1)}, f32[32,1024]{1,0:T(8,128)S(1)}, u32[]{:S(2)}, u32[]{:S(2)}) collective-permute-start(f32[32,1024]{1,0:T(8,128)S(1)} %get-tuple-element.66.refs_1_), channel_id=1, source_target_pairs={{0,4},{4,0},{8,12},{12,8},{16,20},{20,16},{24,28},{28,24},{1,5},{5... | collective-permute-start | bytes 393224 | tf_op jit(solution)/shard_map/ppermute | solution.py:426
  16.8 8.6 %collective-permute-start.5 = (f32[32,1024]{1,0:T(8,128)S(1)}, f32[32,1024]{1,0:T(8,128)S(1)}, u32[]{:S(2)}, u32[]{:S(2)}) collective-permute-start(f32[32,1024]{1,0:T(8,128)S(1)} %shard_map.139.refs_3_), channel_id=1, source_target_pairs={{0,16},{4,8},{8,4},{12,28},{16,0},{20,24},{24,20},{28,12},{1,17},{... | collective-permute-start | bytes 393224 | tf_op jit(solution)/shard_map/ppermute | solution.py:426
  16.9 10.2 %collective-permute-start.8 = (f32[32,1024]{1,0:T(8,128)S(1)}, f32[32,1024]{1,0:T(8,128)S(1)}, u32[]{:S(2)}, u32[]{:S(2)}) collective-permute-start(f32[32,1024]{1,0:T(8,128)S(1)} %shard_map.140.refs_3_), channel_id=1, source_target_pairs={{0,16},{4,8},{8,4},{12,28},{16,0},{20,24},{24,20},{28,12},{1,17},{... | collective-permute-start | bytes 393224 | tf_op jit(solution)/shard_map/ppermute | solution.py:426
  17.5 10.1 %collective-permute-start.4 = (f32[32,1024]{1,0:T(8,128)S(1)}, f32[32,1024]{1,0:T(8,128)S(1)}, u32[]{:S(2)}, u32[]{:S(2)}) collective-permute-start(f32[32,1024]{1,0:T(8,128)S(1)} %shard_map.141.refs_3_), channel_id=1, source_target_pairs={{0,4},{4,0},{8,12},{12,8},{16,20},{20,16},{24,28},{28,24},{1,5},{5... | collective-permute-start | bytes 393224 | tf_op jit(solution)/shard_map/ppermute | solution.py:426
  20.3 7.3 %collective-permute-start.10 = (f32[32,1024]{1,0:T(8,128)S(1)}, f32[32,1024]{1,0:T(8,128)S(1)}, u32[]{:S(2)}, u32[]{:S(2)}) collective-permute-start(f32[32,1024]{1,0:T(8,128)S(1)} %shard_map.142.after_ref), channel_id=1, source_target_pairs={{0,16},{4,8},{8,4},{12,28},{16,0},{20,24},{24,20},{28,12},{1,17},{... | collective-permute-start | bytes 393224 | tf_op jit(solution)/shard_map/ppermute | solution.py:426
  21.8 1.0 %copy-start.12 = (f32[256,1024]{1,0:T(8,128)}, f32[256,1024]{1,0:T(8,128)S(1)}, u32[]{:S(2)}) copy-start(f32[256,1024]{1,0:T(8,128)S(1)} %get-tuple-element.73.refs_18_) | copy-start | bytes 3145732
  22.8 1.0 %copy-start.14 = (f32[256,1024]{1,0:T(8,128)}, f32[256,1024]{1,0:T(8,128)S(1)}, u32[]{:S(2)}) copy-start(f32[256,1024]{1,0:T(8,128)S(1)} %get-tuple-element.74.refs_19_) | copy-start | bytes 3145732
  23.8 1.0 %copy-start.16 = (f32[256,1024]{1,0:T(8,128)}, f32[256,1024]{1,0:T(8,128)S(1)}, u32[]{:S(2)}) copy-start(f32[256,1024]{1,0:T(8,128)S(1)} %get-tuple-element.75.refs_20_) | copy-start | bytes 3145732
  24.8 0.6 copy-start.29
  25.4 6.5 %copy-start.6 = (f32[256,1024]{1,0:T(8,128)}, f32[256,1024]{1,0:T(8,128)S(1)}, u32[]{:S(2)}) copy-start(f32[256,1024]{1,0:T(8,128)S(1)} %get-tuple-element.70.refs_15_) | copy-start | bytes 3145732
  25.4 6.5 %copy-start.8 = (f32[256,1024]{1,0:T(8,128)}, f32[256,1024]{1,0:T(8,128)S(1)}, u32[]{:S(2)}) copy-start(f32[256,1024]{1,0:T(8,128)S(1)} %get-tuple-element.71.refs_16_) | copy-start | bytes 3145732
  25.4 6.5 %copy-start.10 = (f32[256,1024]{1,0:T(8,128)}, f32[256,1024]{1,0:T(8,128)S(1)}, u32[]{:S(2)}) copy-start(f32[256,1024]{1,0:T(8,128)S(1)} %get-tuple-element.72.refs_17_) | copy-start | bytes 3145732
  25.4 6.4 %collective-permute-start.7 = (f32[32,1024]{1,0:T(8,128)S(1)}, f32[32,1024]{1,0:T(8,128)S(1)}, u32[]{:S(2)}, u32[]{:S(2)}) collective-permute-start(f32[32,1024]{1,0:T(8,128)S(1)} %shard_map.144.refs_3_), channel_id=1, source_target_pairs={{0,4},{4,0},{8,12},{12,8},{16,20},{20,16},{24,28},{28,24},{1,5},{5... | collective-permute-start | bytes 393224 | tf_op jit(solution)/shard_map/ppermute | solution.py:426
  27.1 7.5 %collective-permute-start.9 = (f32[32,1024]{1,0:T(8,128)S(1)}, f32[32,1024]{1,0:T(8,128)S(1)}, u32[]{:S(2)}, u32[]{:S(2)}) collective-permute-start(f32[32,1024]{1,0:T(8,128)S(1)} %shard_map.145.refs_3_), channel_id=1, source_target_pairs={{0,4},{4,0},{8,12},{12,8},{16,20},{20,16},{24,28},{28,24},{1,5},{5... | collective-permute-start | bytes 393224 | tf_op jit(solution)/shard_map/ppermute | solution.py:426
  27.6 9.4 %collective-permute-start.11 = (f32[32,1024]{1,0:T(8,128)S(1)}, f32[32,1024]{1,0:T(8,128)S(1)}, u32[]{:S(2)}, u32[]{:S(2)}) collective-permute-start(f32[32,1024]{1,0:T(8,128)S(1)} %shard_map.146), channel_id=1, source_target_pairs={{0,4},{4,0},{8,12},{12,8},{16,20},{20,16},{24,28},{28,24},{1,5},{5... | collective-permute-start | bytes 393224 | tf_op jit(solution)/shard_map/ppermute | solution.py:426
  31.8 0.7 copy-start
  37.8 0.6 copy-start.31
  38.4 8.9 %all-to-all-start.2 = ((f32[8,2,16]{2,1,0:T(2,128)}), f32[8,2,16]{2,1,0:T(2,128)S(1)}, u32[]{:S(2)}, u32[]{:S(2)}) async-start(f32[8,2,16]{2,1,0:T(2,128)} %broadcast_in_dim.15), calls=%async_computation.2 | async-start | bytes 16384 | tf_op jit(solution)/shard_map/all_to_all | solution.py:484
  41.8 0.9 %copy-start.1 = (f32[32,1024]{1,0:T(8,128)S(1)}, f32[32,1024]{1,0:T(8,128)}, u32[]{:S(2)}) copy-start(f32[32,1024]{1,0:T(8,128)} %copy-done) | copy-start | bytes 393220
  42.7 0.9 %copy-start.4 = (f32[256,128]{1,0:T(8,128)S(1)}, f32[256,128]{1,0:T(8,128)}, u32[]{:S(2)}) copy-start(f32[256,128]{1,0:T(8,128)} %copy-done.3) | copy-start | bytes 393220
  43.6 0.9 %copy-start.20 = (f32[256,128]{1,0:T(8,128)S(1)}, f32[256,128]{1,0:T(8,128)}, u32[]{:S(2)}) copy-start(f32[256,128]{1,0:T(8,128)} %copy-done.19) | copy-start | bytes 393220
  45.4 0.7 copy-start.22
  49.0 4.3 %copy-start.32 = (f32[2,16]{1,0:T(2,128)S(1)}, f32[2,16]{1,0:T(2,128)}, u32[]{:S(2)}) copy-start(f32[2,16]{1,0:T(2,128)} %copy-done.31) | copy-start | bytes 388
  49.0 12.9 %all-to-all-start = ((f32[4,256,128]{2,1,0:T(8,128)}), f32[4,256,128]{2,1,0:T(8,128)}, u32[]{:S(2)}, u32[]{:S(2)}) async-start(f32[4,256,128]{2,1,0:T(8,128)} %broadcast_in_dim.13), calls=%async_computation | async-start | bytes 1048576 | tf_op jit(solution)/shard_map/all_to_all | solution.py:484
  53.3 0.9 %copy-start.5 = (f32[256,128]{1,0:T(8,128)S(1)}, f32[256,128]{1,0:T(8,128)}, u32[]{:S(2)}) copy-start(f32[256,128]{1,0:T(8,128)} %copy-done.3) | copy-start | bytes 393220
  54.2 0.9 %copy-start.21 = (f32[256,128]{1,0:T(8,128)S(1)}, f32[256,128]{1,0:T(8,128)}, u32[]{:S(2)}) copy-start(f32[256,128]{1,0:T(8,128)} %copy-done.19) | copy-start | bytes 393220
  56.1 0.7 copy-start.18
  63.7 3.6 %copy-start.2 = (f32[32,1024]{1,0:T(8,128)S(1)}, f32[32,1024]{1,0:T(8,128)}, u32[]{:S(2)}) copy-start(f32[32,1024]{1,0:T(8,128)} %copy-done) | copy-start | bytes 393220
  63.7 3.7 %copy-start.24 = (bf16[256,128]{1,0:T(8,128)(2,1)S(1)}, bf16[256,128]{1,0:T(8,128)(2,1)}, u32[]{:S(2)}) copy-start(bf16[256,128]{1,0:T(8,128)(2,1)} %copy-done.23) | copy-start | bytes 196612
  63.7 3.7 %copy-start.26 = (bf16[256,128]{1,0:T(8,128)(2,1)S(1)}, bf16[256,128]{1,0:T(8,128)(2,1)}, u32[]{:S(2)}) copy-start(bf16[256,128]{1,0:T(8,128)(2,1)} %copy-done.25) | copy-start | bytes 196612
  63.7 3.7 %copy-start.28 = (f32[16,256]{1,0:T(8,128)S(1)}, f32[16,256]{1,0:T(8,128)}, u32[]{:S(2)}) copy-start(f32[16,256]{1,0:T(8,128)} %copy-done.27) | copy-start | bytes 49156
  63.7 3.7 %copy-start.30 = (f32[16,256]{1,0:T(8,128)S(1)}, f32[16,256]{1,0:T(8,128)}, u32[]{:S(2)}) copy-start(f32[16,256]{1,0:T(8,128)} %copy-done.29) | copy-start | bytes 49156
  63.7 13.4 %all-to-all-start.1 = ((f32[4,256,128]{2,1,0:T(8,128)}), f32[4,256,128]{2,1,0:T(8,128)S(1)}, u32[]{:S(2)}, u32[]{:S(2)}) async-start(f32[4,256,128]{2,1,0:T(8,128)} %broadcast_in_dim.14), calls=%async_computation.1 | async-start | bytes 1048576 | tf_op jit(solution)/shard_map/all_to_all | solution.py:484
  67.4 1.2 %copy-start.7 = (f32[256,1024]{1,0:T(8,128)S(1)}, f32[256,1024]{1,0:T(8,128)}, u32[]{:S(2)}) copy-start(f32[256,1024]{1,0:T(8,128)} %copy-done.6) | copy-start | bytes 3145732
  68.6 1.2 %copy-start.9 = (f32[256,1024]{1,0:T(8,128)S(1)}, f32[256,1024]{1,0:T(8,128)}, u32[]{:S(2)}) copy-start(f32[256,1024]{1,0:T(8,128)} %copy-done.8) | copy-start | bytes 3145732
  69.8 1.2 %copy-start.11 = (f32[256,1024]{1,0:T(8,128)S(1)}, f32[256,1024]{1,0:T(8,128)}, u32[]{:S(2)}) copy-start(f32[256,1024]{1,0:T(8,128)} %copy-done.10) | copy-start | bytes 3145732
  71.0 1.2 %copy-start.13 = (f32[256,1024]{1,0:T(8,128)S(1)}, f32[256,1024]{1,0:T(8,128)}, u32[]{:S(2)}) copy-start(f32[256,1024]{1,0:T(8,128)} %copy-done.12) | copy-start | bytes 3145732
  72.3 1.2 %copy-start.15 = (f32[256,1024]{1,0:T(8,128)S(1)}, f32[256,1024]{1,0:T(8,128)}, u32[]{:S(2)}) copy-start(f32[256,1024]{1,0:T(8,128)} %copy-done.14) | copy-start | bytes 3145732
  73.5 1.2 %copy-start.17 = (f32[256,1024]{1,0:T(8,128)S(1)}, f32[256,1024]{1,0:T(8,128)}, u32[]{:S(2)}) copy-start(f32[256,1024]{1,0:T(8,128)} %copy-done.16) | copy-start | bytes 3145732

commit v5 on v2

--- a/solution.py
+++ b/solution.py
@@ -13,7 +13,7 @@
 LANES = 256
 CHUNKS = 4
 PARTS = 2
-LAG = 1
+WEIGHTS = {'pass4': 30, 'pass5': 10, 'pass6': 300, 'pass7': 30, 'rate0': 30, 'rate1': 10, 'later': 30, 'sum': 100, 'add1': 100, 'rest': 30}
 
 
 def split(x, parts):
@@ -99,11 +99,19 @@
     return wide, sigmoid, grad.astype(F32) * (wide * sigmoid)
 
 
-def states_kernel(chunks, size, *refs):
+def put_rows(refs, here, value):
+    start = 0
+    for ref in refs:
+        rows = ref.shape[0]
+        ref[:, here] = value[start : start + rows]
+        start += rows
+
+
+def states_kernel(size, *refs):
     sources, outs, (steps_ref, lr_ref, sems) = refs[:8], refs[8:-3], refs[-3:]
     v_ref, gate_ref, go_ref, b_ref, c_ref = outs[:5]
     cum_ref, neg_ref, decay_ref, slope_ref, skip_ref = outs[5:10]
-    mine_refs, other_refs = outs[10 : 10 + chunks], outs[10 + chunks :]
+    mine_refs = outs[10:]
     targets = (v_ref, gate_ref, go_ref, b_ref, c_ref, steps_ref, lr_ref, skip_ref)
     copies = [
         pltpu.make_async_copy(source, target, sems.at[i])
@@ -116,36 +124,49 @@
     length, channels = v_ref.shape
     heads = steps_ref.shape[0]
     width = channels // heads
-    lower = lax.axis_index("seq") < size // 2 if size > 1 else True
     rates = jnp.exp(to_column(lr_ref[...]))
     cumulative = scan_tokens(-rates * steps_ref[...], False)
     total = cumulative[:, -1:]
     decay = jnp.exp(total)
     cum_ref[...] = cumulative
     neg_ref[...] = jnp.broadcast_to(-rates, (heads, length))
-    growth = rows_of_three(jnp.exp(cumulative))
-    fall = rows_of_three(jnp.exp(total - cumulative))
-    copies[3].wait()
-    copies[4].wait()
-    b_t = b_ref[...].astype(F32).T.astype(BF16)
-    c_t = c_ref[...].astype(F32).T.astype(BF16)
-    for i in (0, 1, 2, 7):
-        copies[i].wait()
-    rows = b_t.shape[0] // chunks
     for first in range(0, channels, LANES):
         here = pl.ds(first, LANES)
-        _, _, grad_y = gate_parts(gate_ref[:, here], go_ref[:, here])
-        high, low = split(spread(growth, first, LANES, width) * grad_y, 2)
-        pulled = mm(c_t, high) + mm(c_t, low)
-        scaled = (spread(fall, first, LANES, width) * v_ref[:, here].astype(F32)).astype(BF16)
-        local = mm(b_t, scaled)
-        mine = jnp.where(lower, local, pulled)
-        other = jnp.where(lower, pulled, local)
-        for i in range(chunks):
-            mine_refs[i][:, here] = mine[i * rows : (i + 1) * rows]
-            other_refs[i][:, here] = other[i * rows : (i + 1) * rows]
         decay_ref[:, here] = channel_row(decay, heads, width, first)
         slope_ref[:, here] = channel_row(total * decay, heads, width, first)
+
+    def local():
+        copies[3].wait()
+        b_t = b_ref[...].astype(F32).T.astype(BF16)
+        fall = rows_of_three(jnp.exp(total - cumulative))
+        copies[0].wait()
+        for first in range(0, channels, LANES):
+            here = pl.ds(first, LANES)
+            scaled = spread(fall, first, LANES, width) * v_ref[:, here].astype(F32)
+            put_rows(mine_refs, here, mm(b_t, scaled.astype(BF16)))
+        for i in (1, 2, 4, 7):
+            copies[i].wait()
+
+    def pulled():
+        copies[4].wait()
+        c_t = c_ref[...].astype(F32).T.astype(BF16)
+        growth = rows_of_three(jnp.exp(cumulative))
+        copies[1].wait()
+        copies[2].wait()
+        for first in range(0, channels, LANES):
+            here = pl.ds(first, LANES)
+            _, _, grad_y = gate_parts(gate_ref[:, here], go_ref[:, here])
+            high, low = split(spread(growth, first, LANES, width) * grad_y, 2)
+            put_rows(mine_refs, here, mm(c_t, high) + mm(c_t, low))
+        for i in (0, 3, 7):
+            copies[i].wait()
+
+    if size == 1:
+        local()
+    else:
+        lower = lax.axis_index("seq") < size // 2
+        pl.when(lower)(local)
+        pl.when(jnp.logical_not(lower))(pulled)
 
 
 def intra_kernel(
@@ -210,8 +231,8 @@
 
 
 def factors_kernel(
-    v_ref, gate_ref, go_ref, b_ref, c_ref, cum_ref, after_ref,
-    high_ref, low_ref, scaled_ref, q_ref, r_ref,
+    size, v_ref, gate_ref, go_ref, b_ref, c_ref, cum_ref, after_ref,
+    high_ref, low_ref, scaled_ref, q_ref, r_ref, *other_refs,
 ):
     length, channels = v_ref.shape
     heads = cum_ref.shape[0]
@@ -236,6 +257,19 @@
         q_ref[:, here] = mm(c_t, high) + mm(c_t, low)
         high, low = split(spread(fall_slope, first, LANES, width) * vals, 2)
         r_ref[:, here] = mm(b_t, high) + mm(b_t, low)
+
+    def pulled():
+        put_rows(other_refs, slice(None), mm(c_t, high_ref[...]) + mm(c_t, low_ref[...]))
+
+    def local():
+        put_rows(other_refs, slice(None), mm(b_t, scaled_ref[...]))
+
+    if size == 1:
+        pulled()
+    else:
+        lower = lax.axis_index("seq") < size // 2
+        pl.when(lower)(pulled)
+        pl.when(jnp.logical_not(lower))(local)
 
 
 def prepare_kernel(
@@ -370,6 +404,10 @@
     return values[0]
 
 
+def copy_kernel(x_ref, *refs):
+    refs[-1][...] = x_ref[...]
+
+
 def add_kernel(x_ref, y_ref, *refs):
     refs[-1][...] = x_ref[...] + y_ref[...]
 
@@ -395,14 +433,13 @@
     skip_ref[...] = small[1:]
 
 
-def call(kernel, outs, scratch=(), flops=0, space=pltpu.VMEM, after=()):
+def call(kernel, outs, scratch=(), name="", space=pltpu.VMEM, after=()):
     def run(*args):
         if space == pltpu.HBM:
             args = [pltpu.with_memory_space_constraint(a, space) for a in args]
         specs = [pl.BlockSpec(memory_space=space)] * len(args)
         specs += [pl.BlockSpec(memory_space=pl.ANY)] * len(after)
         args = (*args, *after)
-        size = sum(a.size * a.dtype.itemsize for a in (*args, *outs))
         return pl.pallas_call(
             kernel,
             out_shape=tuple(outs),
@@ -410,7 +447,9 @@
             out_specs=tuple(pl.BlockSpec(memory_space=pltpu.VMEM) for _ in outs),
             scratch_shapes=list(scratch),
             compiler_params=pltpu.CompilerParams(vmem_limit_bytes=VMEM_LIMIT),
-            cost_estimate=pl.CostEstimate(flops=flops, bytes_accessed=size, transcendentals=0),
+            cost_estimate=pl.CostEstimate(
+                flops=WEIGHTS.get(name, 0) * 10**7, bytes_accessed=0, transcendentals=0
+            ),
         )(*args)
 
     return run
@@ -438,13 +477,13 @@
     refs[-1][...] = decay_ref[...] * got_ref[...] + base_ref[...]
 
 
-def pass_on(got, base, decay, after):
-    return call(pass_kernel, [jax.ShapeDtypeStruct(base.shape, F32)], flops=2 * base.size, after=after)(
+def pass_on(got, base, decay, after, name):
+    return call(pass_kernel, [jax.ShapeDtypeStruct(base.shape, F32)], name=name, after=after)(
         got, base, decay
     )[0]
 
 
-def chain(sizes, mine, other, decay, work):
+def chain(sizes, mine, made, decay, work):
     chunks = len(mine)
     size = sizes["seq"]
     if size == 1:
@@ -458,16 +497,18 @@
     middle = size // 2 - 1
     got = {(0, c): hop(mine[c], sizes, 0) for c in range(chunks)}
     steps = [
-        (at + c + (LAG if at > middle else 0), at, c) for at in range(1, size - 1) for c in range(chunks)
+        (at + c + (1 if at > middle else 0), at, c)
+        for at in range(1, size - 1)
+        for c in range(chunks)
     ]
     token = ()
     for count, (_, at, c) in enumerate(sorted(steps)):
         if count in work:
             token = work[count](token)
         if at > middle and c > 2:
-            token = (*token, got[at, c - 3])
-        base = mine[c] if at <= middle else other[c]
-        pay = pass_on(got[at - 1, c], base, decay, token)
+            token = (*token, got[at, c - 2 - 1])
+        base = mine[c] if at <= middle else made["factors"][5 + c]
+        pay = pass_on(got[at - 1, c], base, decay, token, f"pass{min(count, 7)}")
         got[at, c] = hop(pay, sizes, at)
         token = (pay,)
     for k in sorted(work):
@@ -484,11 +525,11 @@
     return states
 
 
-def sum_terms(x, axis, size):
+def sum_terms(x, later, axis, size):
     if size == 1:
         return [x]
     if size == 4:
-        return [x] + [swap(x, axis, size, bit) for bit in (1, 2, 3)]
+        return [x, swap(x, axis, size, 1)] + [swap(later, axis, size, bit) for bit in (2, 3)]
     if size & (size - 1):
         return [lax.psum(x, axis)]
     bit = 1
@@ -498,18 +539,19 @@
     return [x, swap(x, axis, size, bit)]
 
 
-def small_terms(x, axes, sizes, between):
+def small_terms(x, axes, sizes, hooks):
     bits = [(axis, 1 << k) for axis in axes for k in range(sizes[axis].bit_length() - 1)]
     if any(sizes[axis] & (sizes[axis] - 1) for axis in axes):
-        x = lax.psum(x, tuple(axes))
-        between((x,))
-        return [x]
+        x, bits = lax.psum(x, tuple(axes)), []
     for count, (axis, bit) in enumerate(bits):
         theirs = swap(x, axis, sizes[axis], bit)
         if count == len(bits) - 1:
             break
-        x = call(add_kernel, [jax.ShapeDtypeStruct(x.shape, F32)])(x, theirs)[0]
-    between((x,))
+        x = call(add_kernel, [jax.ShapeDtypeStruct(x.shape, F32)], name=f"add{count}")(x, theirs)[0]
+        if count < len(hooks):
+            hooks[count]((x,))
+    for hook in hooks[max(len(bits) - 1, 0) :]:
+        hook((x,))
     return [x, theirs] if bits else [x]
 
 
@@ -529,22 +571,21 @@
     maps = like((length, state), BF16)
 
     out = call(
-        functools.partial(states_kernel, CHUNKS, seq),
+        functools.partial(states_kernel, seq),
         [wide_b, wide_b, wide_b, maps, maps, small, small, row, row, like((1, heads), F32)]
-        + [piece] * (2 * CHUNKS),
+        + [piece] * CHUNKS,
         [
             pltpu.VMEM((heads, length), F32),
             pltpu.VMEM((1, heads), F32),
             pltpu.SemaphoreType.DMA((8,)),
         ],
-        flops=8 * length * channels * state,
         space=pltpu.HBM,
     )(
         values[0], gate_in[0], grad_out[0], in_b[0], in_c[0], step_sizes[0],
         log_rates.reshape(1, heads), skip_gain.reshape(1, heads),
     )
     vals, gate, grad, block_b, block_c, cumulative, negative, decay, slope, skip = out[:10]
-    mine, other = out[10 : 10 + CHUNKS], out[10 + CHUNKS :]
+    mine = out[10:]
 
     made = {}
 
@@ -557,37 +598,37 @@
                 pltpu.VMEM((channels, length), F32),
                 pltpu.VMEM((length, length), F32),
             ],
-            flops=16 * length * length * channels,
+            name="intra",
         )(vals, gate, grad, block_b, block_c, cumulative)
         return (made["intra"][2],)
 
     def factors(after):
         made["factors"] = call(
-            factors_kernel,
-            [wide_b] * 3 + [like((state, channels), F32)] * 2,
-            flops=8 * length * state * channels,
+            functools.partial(factors_kernel, seq),
+            [wide_b] * 3 + [like((state, channels), F32)] * 2 + [piece] * CHUNKS,
+            name="factors",
         )(vals, gate, grad, block_b, block_c, cumulative, *(after if after else made["intra"][2:3]))
-        return (made["factors"][-1],)
+        return made["factors"][5:6]
 
     def prepare(after):
         made["prepare"] = call(
             prepare_kernel,
             [wide] * 6 + [small, like((2, heads), F32)],
-            flops=8 * length * state * channels,
+            name="prepare",
         )(
             vals, gate, grad, cumulative, skip,
             *made["intra"][:2], *(after if after else made["intra"][2:3]),
         )
         return (made["prepare"][-1],)
 
-    last_middle = (max(seq // 2 - 1, 1) - 1) * CHUNKS + CHUNKS
-    states = chain(sizes, mine, other, decay, {0: intra, 1: factors, last_middle + LAG: prepare})
+    sums = max(seq - 2, 0) * CHUNKS
+    states = chain(sizes, mine, made, decay, {0: intra, 1: factors, max(sums - 2, 2): prepare})
     sum_b, sum_c = made["intra"][2:]
-    high, low, scaled, q, r = made["factors"]
+    high, low, scaled, q, r = made["factors"][:5]
     coef, mamba, inner, growth, fall, grad_y, grad_cum, parts = made["prepare"]
 
     rate_row = jnp.zeros((1, channels), F32)
-    terms, counts, done = [], [], []
+    terms, counts = [], []
     for i in range(PARTS):
         final = i == PARTS - 1
         count = CHUNKS // PARTS
@@ -595,34 +636,38 @@
         rate_row = call(
             functools.partial(rate_kernel, seq, count, i * rows * count, heads, final),
             [like((2, heads), F32) if final else row],
+            name=f"rate{i}",
         )(*own, q, r, slope, rate_row, parts)[0]
         share_of = call(
             functools.partial(share_kernel, seq, count, i * rows * count),
             [like((length, 2 * rows * count), F32)],
-            flops=10 * length * channels * rows * count,
+            name=f"share{i}",
             after=(rate_row,),
         )(*own, high, low, scaled, sum_b, sum_c)[0]
-        own = sum_terms(share_of, "tensor", sizes["tensor"])
         if not final:
-            own = [call(sum_kernel, [like(share_of.shape, F32)])(*own)[0]]
-            done += own
-        terms += own
-        counts.append(len(own))
+            own = sum_terms(share_of, share_of, "tensor", sizes["tensor"])
+            terms += call(sum_kernel, [like(share_of.shape, F32)], name="sum")(*own)
+            counts.append(1)
+
+    def exchange(after):
+        later = call(copy_kernel, [like(share_of.shape, F32)], name="later", after=after)(share_of)[0]
+        made["share"] = sum_terms(share_of, later, "tensor", sizes["tensor"])
 
     def rest(after):
         made["rest"] = call(
             functools.partial(rest_kernel, seq, CHUNKS),
             [like((1, length, channels), BF16)] * 2 + [like((1, heads, length), F32)],
-            flops=10 * length * channels * state,
-            after=(*after, *done),
+            name="rest",
+            after=(*after, *terms),
         )(
             *(x for group in states for x in group),
             vals, block_b, block_c, coef, mamba, inner, growth, fall, grad_y, grad_cum, decay, negative,
         )
 
-    own = small_terms(rate_row, ("replica", "seq"), sizes, rest)
-    terms += own
-    counts.append(len(own))
+    own = small_terms(rate_row, ("replica", "seq"), sizes, (exchange, rest))
+    for group in (made["share"], own):
+        terms += group
+        counts.append(len(group))
     grad_values, grad_gate, grad_steps = made["rest"]
     grad_b, grad_c, rate_sum, skip_sum = call(
         functools.partial(last_kernel, tuple(counts)),

time: 47.6 us -> 46.2 us (0.971)
  waiting for transfers between devices: 6.55 us -> 3.69 us
  starting transfers between devices: 26.3 us -> 28 us
    ppermute x12, waiting for transfers between devices: 2.16 us -> 0.16 us  [hop(): return lax.ppermute(x, ('replica', 'seq'), pairs)]
    ppermute x9, starting transfers between devices: 8.63 us -> 9.97 us  [swap(): return lax.ppermute(x, axis, [(i, i ^ bit) for i in range(size)])]
    ppermute x9, waiting for transfers between devices: 4.39 us -> 3.52 us  [swap(): return lax.ppermute(x, axis, [(i, i ^ bit) for i in range(size)])]
    pallas_call x21 -> x22, Pallas kernels: 13.7 us -> 13.6 us  [run(): pl.pallas_call(kernel, out_shape=tuple(outs), in_specs=specs, out_specs=t...]
  transfers between devices with their start and end apart: 21 -> 21, of which waited for: 6 -> 4; matrix products, arithmetic and copies ran while one was open for 0% -> 0% of each run, Pallas kernels for 21% -> 23%
where the time goes in v5:
time: 46.2 us; the launch traced here: 46 us
  starting transfers between devices  28 us (61%)
  Pallas kernels  13.6 us (29%)
  waiting for transfers between devices  3.69 us (8%)
  between operations  0.81 us (2%)
    ppermute x12, starting transfers between devices, hop(): return lax.ppermute(x, ('replica', 'seq'), pairs)  18 us
    pallas_call x22, Pallas kernels, run(): pl.pallas_call(kernel, out_shape=tuple(outs), in_specs=specs, out_specs=t...  13.6 us
    ppermute x9, starting transfers between devices, swap(): return lax.ppermute(x, axis, [(i, i ^ bit) for i in range(size)])  9.97 us
    ppermute x9, waiting for transfers between devices, swap(): return lax.ppermute(x, axis, [(i, i ^ bit) for i in range(size)])  3.52 us
  transfers between devices with their start and end apart: 21, of which 4 were waited for; matrix products, arithmetic and copies ran while one was open for 0% of the time, Pallas kernels for 23%

profile of v5, /device:TPU:0, one launch (start us, length us, event | category | flops | bytes accessed | tf_op | source)
XLA Modules:
  0.0 46.0 jit_solution(2941496599662199048)
XLA Ops:
  0.6 2.3 %shard_map.135 = (bf16[256,1024]{1,0:T(8,128)(2,1)S(1)}, bf16[256,1024]{1,0:T(8,128)(2,1)S(1)}, bf16[256,1024]{1,0:T(8,128)(2,1)S(1)}, bf16[256,128]{1,0:T(8,128...) custom-call(bf16[256,1024]{1,0:T(8,128)(2,1)} %bitcast.10, ...), custom_call_target="tpu_custom_call" | custom-call | tf_op jit(solution)/shard_map/pallas_call | solution.py:443
  2.9 3.1 %collective-permute-start = (f32[32,1024]{1,0:T(8,128)S(1)}, f32[32,1024]{1,0:T(8,128)S(1)}, u32[]{:S(2)}, u32[]{:S(2)}) collective-permute-start(f32[32,1024]{1,0:T(8,128)S(1)} %get-tuple-element.49.refs_1_), channel_id=1, source_target_pairs={{0,4},{4,0},{8,12},{12,8},{16,20},{20,16},{24,28},{28,24},{1,5},{5... | collective-permute-start | bytes 393224 | tf_op jit(solution)/shard_map/ppermute | solution.py:472
  6.0 0.1 collective-permute-start.3
  6.1 1.9 %collective-permute-start.2 = (f32[32,1024]{1,0:T(8,128)S(1)}, f32[32,1024]{1,0:T(8,128)S(1)}, u32[]{:S(2)}, u32[]{:S(2)}) collective-permute-start(f32[32,1024]{1,0:T(8,128)S(1)} %get-tuple-element.59.refs_1_), channel_id=1, source_target_pairs={{0,4},{4,0},{8,12},{12,8},{16,20},{20,16},{24,28},{28,24},{1,5},{5... | collective-permute-start | bytes 393224 | tf_op jit(solution)/shard_map/ppermute | solution.py:472
  8.0 2.5 %shard_map.136 = (f32[256,1024]{1,0:T(8,128)S(1)}, f32[256,1024]{1,0:T(8,128)S(1)}, f32[256,128]{1,0:T(8,128)S(1)}, f32[256,128]{1,0:T(8,128)S(1)}) custom-call(bf16[256,1024]{1,0:T(8,128)(2,1)S(1)} %get-tuple-element.51.v_ref.refs_12_, bf16[256,1024]{1,0:T(8,128)(2,1)S(1)} %get-tuple-element.52.gate_ref, bf16[256,1024]{1,0:T(8,128)(2,1)S(1)} %get-tuple-element.53.go_ref, ...), custom_call_target="tpu_custom_call" | custom-call | tf_op jit(solution)/shard_map/pallas_call | solution.py:443
  10.6 0.0 collective-permute-done.refs_0_
  10.6 0.1 collective-permute-start.1
  10.7 3.4 %collective-permute-start.6 = (f32[32,1024]{1,0:T(8,128)S(1)}, f32[32,1024]{1,0:T(8,128)S(1)}, u32[]{:S(2)}, u32[]{:S(2)}) collective-permute-start(f32[32,1024]{1,0:T(8,128)S(1)} %get-tuple-element.62.refs_1_), channel_id=1, source_target_pairs={{0,4},{4,0},{8,12},{12,8},{16,20},{20,16},{24,28},{28,24},{1,5},{5... | collective-permute-start | bytes 393224 | tf_op jit(solution)/shard_map/ppermute | solution.py:472
  14.1 1.6 %shard_map.138 = (bf16[256,1024]{1,0:T(8,128)(2,1)S(1)}, bf16[256,1024]{1,0:T(8,128)(2,1)S(1)}, bf16[256,1024]{1,0:T(8,128)(2,1)S(1)}, f32[128,1024]{1,0:T(8,128...) custom-call(bf16[256,1024]{1,0:T(8,128)(2,1)S(1)} %get-tuple-element, ...), custom_call_target="tpu_custom_call" | custom-call | tf_op jit(solution)/shard_map/pallas_call | solution.py:443
  15.7 0.0 collective-permute-done.3.refs_0_.refs_3_
  15.7 0.1 collective-permute-start.5
  15.8 0.1 collective-permute-done.2.refs_0_.refs_6_
  16.0 0.4 collective-permute-start.8
  16.4 0.0 collective-permute-done.1.refs_0_.refs_1_
  16.4 3.4 %collective-permute-start.4 = (f32[32,1024]{1,0:T(8,128)S(1)}, f32[32,1024]{1,0:T(8,128)S(1)}, u32[]{:S(2)}, u32[]{:S(2)}) collective-permute-start(f32[32,1024]{1,0:T(8,128)S(1)} %shard_map.141.refs_3_), channel_id=1, source_target_pairs={{0,4},{4,0},{8,12},{12,8},{16,20},{20,16},{24,28},{28,24},{1,5},{5... | collective-permute-start | bytes 393224 | tf_op jit(solution)/shard_map/ppermute | solution.py:472
  19.8 0.0 collective-permute-done.6.refs_0_.refs_3_.refs_9_
  19.8 0.1 collective-permute-start.10
  19.9 0.0 collective-permute-done.5.refs_0_.refs_4_
  19.9 2.3 %collective-permute-start.7 = (f32[32,1024]{1,0:T(8,128)S(1)}, f32[32,1024]{1,0:T(8,128)S(1)}, u32[]{:S(2)}, u32[]{:S(2)}) collective-permute-start(f32[32,1024]{1,0:T(8,128)S(1)} %shard_map.143.after_ref), channel_id=1, source_target_pairs={{0,4},{4,0},{8,12},{12,8},{16,20},{20,16},{24,28},{28,24},{1,5},{5... | collective-permute-start | bytes 393224 | tf_op jit(solution)/shard_map/ppermute | solution.py:472
  22.3 1.4 %shard_map.144 = (f32[256,1024]{1,0:T(8,128)S(1)}, f32[256,1024]{1,0:T(8,128)S(1)}, f32[256,1024]{1,0:T(8,128)S(1)}, f32[256,1024]{1,0:T(8,128)S(1)}, f32[256,10...) custom-call(bf16[256,1024]{1,0:T(8,128)(2,1)S(1)} %get-tuple-element.51.v_ref.refs_12_, ...), custom_call_target="tpu_custom_call" | custom-call | tf_op jit(solution)/shard_map/pallas_call | solution.py:443
  23.7 0.0 collective-permute-done.8.refs_0_.refs_1_.refs_7_
  23.7 1.3 %collective-permute-start.9 = (f32[32,1024]{1,0:T(8,128)S(1)}, f32[32,1024]{1,0:T(8,128)S(1)}, u32[]{:S(2)}, u32[]{:S(2)}) collective-permute-start(f32[32,1024]{1,0:T(8,128)S(1)} %shard_map.145.refs_3_), channel_id=1, source_target_pairs={{0,4},{4,0},{8,12},{12,8},{16,20},{20,16},{24,28},{28,24},{1,5},{5... | collective-permute-start | bytes 393224 | tf_op jit(solution)/shard_map/ppermute | solution.py:472
  25.1 0.0 collective-permute-done.4.refs_4_.refs_2_
  25.1 0.0 collective-permute-done.10.refs_0_.refs_4_.refs_10_
  25.1 1.8 %collective-permute-start.11 = (f32[32,1024]{1,0:T(8,128)S(1)}, f32[32,1024]{1,0:T(8,128)S(1)}, u32[]{:S(2)}, u32[]{:S(2)}) collective-permute-start(f32[32,1024]{1,0:T(8,128)S(1)} %shard_map.146), channel_id=1, source_target_pairs={{0,4},{4,0},{8,12},{12,8},{16,20},{20,16},{24,28},{28,24},{1,5},{5... | collective-permute-start | bytes 393224 | tf_op jit(solution)/shard_map/ppermute | solution.py:472
  26.9 0.0 collective-permute-done.7.refs_5_
  26.9 0.1 shard_map.147.refs_9_.refs_11_
  27.1 0.9 %shard_map.151.refs_0_ = f32[256,128]{1,0:T(8,128)S(1)} custom-call(f32[32,1024]{1,0:T(8,128)S(1)} %collective-permute-done.refs_0_, f32[32,1024]{1,0:T(8,128)S(1)} %collective-permute-done.1.refs_0_.refs_1_, f32[32,1024]{1,0:T(8,128)S(1)} %collective-permute-done.4.refs_4_.refs_2_, f32[32,1024]{1,0:T(8,128)S(1)} %collective-permute-done.3.refs_0_.refs_3_, ...), custom_call_target="tpu_custom_call" | custom-call | tf_op jit(solution)/shard_map/pallas_call | solution.py:443
  28.0 1.6 %collective-permute-start.14 = (f32[256,128]{1,0:T(8,128)S(1)}, f32[256,128]{1,0:T(8,128)S(1)}, u32[]{:S(2)}, u32[]{:S(2)}) collective-permute-start(f32[256,128]{1,0:T(8,128)S(1)} %shard_map.151.refs_0_), channel_id=1, source_target_pairs={{0,1},{1,0},{2,3},{3,2},{4,5},{5,4},{6,7},{7,6},{8,9},{9,8},{10,11... | collective-permute-start | bytes 393224 | tf_op jit(solution)/shard_map/ppermute | solution.py:459
  29.5 1.5 %collective-permute-start.15 = (f32[256,128]{1,0:T(8,128)S(1)}, f32[256,128]{1,0:T(8,128)S(1)}, u32[]{:S(2)}, u32[]{:S(2)}) collective-permute-start(f32[256,128]{1,0:T(8,128)S(1)} %shard_map.151.refs_0_), channel_id=1, source_target_pairs={{0,2},{1,3},{2,0},{3,1},{4,6},{5,7},{6,4},{7,5},{8,10},{9,11},{10,... | collective-permute-start | bytes 393224 | tf_op jit(solution)/shard_map/ppermute | solution.py:459
  31.0 0.5 %collective-permute-start.16 = (f32[256,128]{1,0:T(8,128)S(1)}, f32[256,128]{1,0:T(8,128)S(1)}, u32[]{:S(2)}, u32[]{:S(2)}) collective-permute-start(f32[256,128]{1,0:T(8,128)S(1)} %shard_map.151.refs_0_), channel_id=1, source_target_pairs={{0,3},{1,2},{2,1},{3,0},{4,7},{5,6},{6,5},{7,4},{8,11},{9,10},{10,... | collective-permute-start | bytes 393224 | tf_op jit(solution)/shard_map/ppermute | solution.py:459
  31.5 0.0 collective-permute-done.9.refs_2_.refs_8_
  31.5 0.0 collective-permute-done.11.refs_5_.refs_11_
  31.5 0.2 shard_map.148.x_ref.refs_11_
  31.8 0.0 collective-permute-start.12
  31.8 1.0 %shard_map.154.x_ref.refs_1_ = f32[256,128]{1,0:T(8,128)S(1)} custom-call(f32[32,1024]{1,0:T(8,128)S(1)} %collective-permute-done.2.refs_0_.refs_6_, f32[32,1024]{1,0:T(8,128)S(1)} %collective-permute-done.8.refs_0_.refs_1_.refs_7_, f32[32,1024]{1,0:T(8,128)S(1)} %collective-permute-done.9.refs_2_.refs_8_, ...), custom_call_target="tpu_custom_call" | custom-call | tf_op jit(solution)/shard_map/pallas_call | solution.py:443
  32.8 1.6 %collective-permute-start.17 = (f32[256,128]{1,0:T(8,128)S(1)}, f32[256,128]{1,0:T(8,128)S(1)}, u32[]{:S(2)}, u32[]{:S(2)}) collective-permute-start(f32[256,128]{1,0:T(8,128)S(1)} %shard_map.154.x_ref.refs_1_), channel_id=1, source_target_pairs={{0,1},{1,0},{2,3},{3,2},{4,5},{5,4},{6,7},{7,6},{8,9},{9,8},{10,11... | collective-permute-start | bytes 393224 | tf_op jit(solution)/shard_map/ppermute | solution.py:459
  34.4 0.0 collective-permute-done.12.y_ref
  34.4 1.6 %collective-permute-start.18 = (f32[256,128]{1,0:T(8,128)S(1)}, f32[256,128]{1,0:T(8,128)S(1)}, u32[]{:S(2)}, u32[]{:S(2)}) collective-permute-start(f32[256,128]{1,0:T(8,128)S(1)} %shard_map.155), channel_id=1, source_target_pairs={{0,2},{1,3},{2,0},{3,1},{4,6},{5,7},{6,4},{7,5},{8,10},{9,11},{10,... | collective-permute-start | bytes 393224 | tf_op jit(solution)/shard_map/ppermute | solution.py:459
  36.0 0.0 collective-permute-done.14.refs_1_
  36.0 0.5 %collective-permute-start.19 = (f32[256,128]{1,0:T(8,128)S(1)}, f32[256,128]{1,0:T(8,128)S(1)}, u32[]{:S(2)}, u32[]{:S(2)}) collective-permute-start(f32[256,128]{1,0:T(8,128)S(1)} %shard_map.155), channel_id=1, source_target_pairs={{0,3},{1,2},{2,1},{3,0},{4,7},{5,6},{6,5},{7,4},{8,11},{9,10},{10,... | collective-permute-start | bytes 393224 | tf_op jit(solution)/shard_map/ppermute | solution.py:459
  36.5 0.7 %collective-permute-done.15.refs_2_ = f32[256,128]{1,0:T(8,128)S(1)} collective-permute-done((f32[256,128]{1,0:T(8,128)S(1)}, f32[256,128]{1,0:T(8,128)S(1)}, u32[]{:S(2)}, u32[]{:S(2)}) %collective-permute-start.15) | collective-permute-done | bytes 131104 | tf_op jit(solution)/shard_map/ppermute | solution.py:459
  37.2 1.1 %collective-permute-start.13 = (f32[2,16]{1,0:T(2,128)S(1)}, f32[2,16]{1,0:T(2,128)S(1)}, u32[]{:S(2)}, u32[]{:S(2)}) collective-permute-start(f32[2,16]{1,0:T(2,128)S(1)} %shard_map.149.x_ref.refs_0_), channel_id=1, source_target_pairs={{0,4},{4,0},{8,12},{12,8},{1,5},{5,1},{9,13},{13,9},{2,6},{6,2},{1... | collective-permute-start | bytes 392 | tf_op jit(solution)/shard_map/ppermute | solution.py:459
  38.3 0.0 collective-permute-done.16.refs_3_
  38.3 2.4 %collective-permute-done.13.y_ref = f32[2,16]{1,0:T(2,128)S(1)} collective-permute-done((f32[2,16]{1,0:T(2,128)S(1)}, f32[2,16]{1,0:T(2,128)S(1)}, u32[]{:S(2)}, u32[]{:S(2)}) %collective-permute-start.13) | collective-permute-done | bytes 160 | tf_op jit(solution)/shard_map/ppermute | solution.py:459
  40.8 1.7 %collective-permute-start.20 = (f32[2,16]{1,0:T(2,128)S(1)}, f32[2,16]{1,0:T(2,128)S(1)}, u32[]{:S(2)}, u32[]{:S(2)}) collective-permute-start(f32[2,16]{1,0:T(2,128)S(1)} %shard_map.150.refs_24_.refs_5_), channel_id=1, source_target_pairs={{0,8},{4,12},{8,0},{12,4},{1,9},{5,13},{9,1},{13,5},{2,10},{6,14},... | collective-permute-start | bytes 392 | tf_op jit(solution)/shard_map/ppermute | solution.py:459
  42.4 2.4 %shard_map.153 = (bf16[1,256,1024]{2,1,0:T(8,128)(2,1)}, bf16[1,256,1024]{2,1,0:T(8,128)(2,1)}, f32[1,16,256]{2,1,0:T(8,128)}) custom-call(f32[32,1024]{1,0:T(8,128)S(1)} %collective-permute-done.refs_0_, f32[32,1024]{1,0:T(8,128)S(1)} %collective-permute-done.1.refs_0_.refs_1_, f32[32,1024]{1,0:T(8,128)S(1)} %collective-permute-done.4.refs_4_.refs_2_, ...), custom_call_target="tpu_custom_call" | custom-call | flops 300000000 | tf_op jit(solution)/shard_map/pallas_call | solution.py:443
  44.9 0.3 collective-permute-done.20.refs_6_
  45.2 0.0 collective-permute-done.17.refs_2_
  45.2 0.0 collective-permute-done.18.refs_3_
  45.2 0.0 collective-permute-done.19.refs_4_
  45.2 0.8 %shard_map.156 = (f32[1,256,128]{2,1,0:T(8,128)}, f32[1,256,128]{2,1,0:T(8,128)}, f32[1,16]{1,0:T(1,128)}, f32[1,16]{1,0:T(1,128)}) custom-call(f32[256,128]{1,0:T(8,128)S(1)} %shard_map.152.refs_25_.refs_0_, f32[256,128]{1,0:T(8,128)S(1)} %shard_map.154.x_ref.refs_1_, f32[256,128]{1,0:T(8,128)S(1)} %collective-permute-done.17.refs_2_, ...), custom_call_target="tpu_custom_call" | custom-call | tf_op jit(solution)/shard_map/pallas_call | solution.py:443
  (13 shorter events, 0.2 us)
Async XLA Ops:
  2.9 7.7 %collective-permute-start = (f32[32,1024]{1,0:T(8,128)S(1)}, f32[32,1024]{1,0:T(8,128)S(1)}, u32[]{:S(2)}, u32[]{:S(2)}) collective-permute-start(f32[32,1024]{1,0:T(8,128)S(1)} %get-tuple-element.49.refs_1_), channel_id=1, source_target_pairs={{0,4},{4,0},{8,12},{12,8},{16,20},{20,16},{24,28},{28,24},{1,5},{5... | collective-permute-start | bytes 393224 | tf_op jit(solution)/shard_map/ppermute | solution.py:472
  6.0 9.7 %collective-permute-start.3 = (f32[32,1024]{1,0:T(8,128)S(1)}, f32[32,1024]{1,0:T(8,128)S(1)}, u32[]{:S(2)}, u32[]{:S(2)}) collective-permute-start(f32[32,1024]{1,0:T(8,128)S(1)} %get-tuple-element.60.refs_1_), channel_id=1, source_target_pairs={{0,4},{4,0},{8,12},{12,8},{16,20},{20,16},{24,28},{28,24},{1,5},{5... | collective-permute-start | bytes 393224 | tf_op jit(solution)/shard_map/ppermute | solution.py:472
  6.1 9.9 %collective-permute-start.2 = (f32[32,1024]{1,0:T(8,128)S(1)}, f32[32,1024]{1,0:T(8,128)S(1)}, u32[]{:S(2)}, u32[]{:S(2)}) collective-permute-start(f32[32,1024]{1,0:T(8,128)S(1)} %get-tuple-element.59.refs_1_), channel_id=1, source_target_pairs={{0,4},{4,0},{8,12},{12,8},{16,20},{20,16},{24,28},{28,24},{1,5},{5... | collective-permute-start | bytes 393224 | tf_op jit(solution)/shard_map/ppermute | solution.py:472
  10.6 5.8 %collective-permute-start.1 = (f32[32,1024]{1,0:T(8,128)S(1)}, f32[32,1024]{1,0:T(8,128)S(1)}, u32[]{:S(2)}, u32[]{:S(2)}) collective-permute-start(f32[32,1024]{1,0:T(8,128)S(1)} %shard_map.137.after_ref), channel_id=1, source_target_pairs={{0,16},{4,8},{8,4},{12,28},{16,0},{20,24},{24,20},{28,12},{1,17},{... | collective-permute-start | bytes 393224 | tf_op jit(solution)/shard_map/ppermute | solution.py:472
  10.7 9.1 %collective-permute-start.6 = (f32[32,1024]{1,0:T(8,128)S(1)}, f32[32,1024]{1,0:T(8,128)S(1)}, u32[]{:S(2)}, u32[]{:S(2)}) collective-permute-start(f32[32,1024]{1,0:T(8,128)S(1)} %get-tuple-element.62.refs_1_), channel_id=1, source_target_pairs={{0,4},{4,0},{8,12},{12,8},{16,20},{20,16},{24,28},{28,24},{1,5},{5... | collective-permute-start | bytes 393224 | tf_op jit(solution)/shard_map/ppermute | solution.py:472
  15.7 4.2 %collective-permute-start.5 = (f32[32,1024]{1,0:T(8,128)S(1)}, f32[32,1024]{1,0:T(8,128)S(1)}, u32[]{:S(2)}, u32[]{:S(2)}) collective-permute-start(f32[32,1024]{1,0:T(8,128)S(1)} %shard_map.139.refs_3_), channel_id=1, source_target_pairs={{0,16},{4,8},{8,4},{12,28},{16,0},{20,24},{24,20},{28,12},{1,17},{... | collective-permute-start | bytes 393224 | tf_op jit(solution)/shard_map/ppermute | solution.py:472
  16.0 7.7 %collective-permute-start.8 = (f32[32,1024]{1,0:T(8,128)S(1)}, f32[32,1024]{1,0:T(8,128)S(1)}, u32[]{:S(2)}, u32[]{:S(2)}) collective-permute-start(f32[32,1024]{1,0:T(8,128)S(1)} %shard_map.140.refs_3_), channel_id=1, source_target_pairs={{0,16},{4,8},{8,4},{12,28},{16,0},{20,24},{24,20},{28,12},{1,17},{... | collective-permute-start | bytes 393224 | tf_op jit(solution)/shard_map/ppermute | solution.py:472
  16.4 8.6 %collective-permute-start.4 = (f32[32,1024]{1,0:T(8,128)S(1)}, f32[32,1024]{1,0:T(8,128)S(1)}, u32[]{:S(2)}, u32[]{:S(2)}) collective-permute-start(f32[32,1024]{1,0:T(8,128)S(1)} %shard_map.141.refs_3_), channel_id=1, source_target_pairs={{0,4},{4,0},{8,12},{12,8},{16,20},{20,16},{24,28},{28,24},{1,5},{5... | collective-permute-start | bytes 393224 | tf_op jit(solution)/shard_map/ppermute | solution.py:472
  19.8 5.2 %collective-permute-start.10 = (f32[32,1024]{1,0:T(8,128)S(1)}, f32[32,1024]{1,0:T(8,128)S(1)}, u32[]{:S(2)}, u32[]{:S(2)}) collective-permute-start(f32[32,1024]{1,0:T(8,128)S(1)} %shard_map.142.refs_3_), channel_id=1, source_target_pairs={{0,16},{4,8},{8,4},{12,28},{16,0},{20,24},{24,20},{28,12},{1,17},{... | collective-permute-start | bytes 393224 | tf_op jit(solution)/shard_map/ppermute | solution.py:472
  19.9 7.0 %collective-permute-start.7 = (f32[32,1024]{1,0:T(8,128)S(1)}, f32[32,1024]{1,0:T(8,128)S(1)}, u32[]{:S(2)}, u32[]{:S(2)}) collective-permute-start(f32[32,1024]{1,0:T(8,128)S(1)} %shard_map.143.after_ref), channel_id=1, source_target_pairs={{0,4},{4,0},{8,12},{12,8},{16,20},{20,16},{24,28},{28,24},{1,5},{5... | collective-permute-start | bytes 393224 | tf_op jit(solution)/shard_map/ppermute | solution.py:472
  23.7 7.8 %collective-permute-start.9 = (f32[32,1024]{1,0:T(8,128)S(1)}, f32[32,1024]{1,0:T(8,128)S(1)}, u32[]{:S(2)}, u32[]{:S(2)}) collective-permute-start(f32[32,1024]{1,0:T(8,128)S(1)} %shard_map.145.refs_3_), channel_id=1, source_target_pairs={{0,4},{4,0},{8,12},{12,8},{16,20},{20,16},{24,28},{28,24},{1,5},{5... | collective-permute-start | bytes 393224 | tf_op jit(solution)/shard_map/ppermute | solution.py:472
  25.1 6.4 %collective-permute-start.11 = (f32[32,1024]{1,0:T(8,128)S(1)}, f32[32,1024]{1,0:T(8,128)S(1)}, u32[]{:S(2)}, u32[]{:S(2)}) collective-permute-start(f32[32,1024]{1,0:T(8,128)S(1)} %shard_map.146), channel_id=1, source_target_pairs={{0,4},{4,0},{8,12},{12,8},{16,20},{20,16},{24,28},{28,24},{1,5},{5... | collective-permute-start | bytes 393224 | tf_op jit(solution)/shard_map/ppermute | solution.py:472
  28.0 8.0 %collective-permute-start.14 = (f32[256,128]{1,0:T(8,128)S(1)}, f32[256,128]{1,0:T(8,128)S(1)}, u32[]{:S(2)}, u32[]{:S(2)}) collective-permute-start(f32[256,128]{1,0:T(8,128)S(1)} %shard_map.151.refs_0_), channel_id=1, source_target_pairs={{0,1},{1,0},{2,3},{3,2},{4,5},{5,4},{6,7},{7,6},{8,9},{9,8},{10,11... | collective-permute-start | bytes 393224 | tf_op jit(solution)/shard_map/ppermute | solution.py:459
  29.5 7.7 %collective-permute-start.15 = (f32[256,128]{1,0:T(8,128)S(1)}, f32[256,128]{1,0:T(8,128)S(1)}, u32[]{:S(2)}, u32[]{:S(2)}) collective-permute-start(f32[256,128]{1,0:T(8,128)S(1)} %shard_map.151.refs_0_), channel_id=1, source_target_pairs={{0,2},{1,3},{2,0},{3,1},{4,6},{5,7},{6,4},{7,5},{8,10},{9,11},{10,... | collective-permute-start | bytes 393224 | tf_op jit(solution)/shard_map/ppermute | solution.py:459
  31.0 7.2 %collective-permute-start.16 = (f32[256,128]{1,0:T(8,128)S(1)}, f32[256,128]{1,0:T(8,128)S(1)}, u32[]{:S(2)}, u32[]{:S(2)}) collective-permute-start(f32[256,128]{1,0:T(8,128)S(1)} %shard_map.151.refs_0_), channel_id=1, source_target_pairs={{0,3},{1,2},{2,1},{3,0},{4,7},{5,6},{6,5},{7,4},{8,11},{9,10},{10,... | collective-permute-start | bytes 393224 | tf_op jit(solution)/shard_map/ppermute | solution.py:459
  31.8 2.6 %collective-permute-start.12 = (f32[2,16]{1,0:T(2,128)S(1)}, f32[2,16]{1,0:T(2,128)S(1)}, u32[]{:S(2)}, u32[]{:S(2)}) collective-permute-start(f32[2,16]{1,0:T(2,128)S(1)} %shard_map.148.x_ref.refs_11_), channel_id=1, source_target_pairs={{0,16},{16,0},{1,17},{17,1},{2,18},{18,2},{3,19},{19,3},{4,20},{20... | collective-permute-start | bytes 392 | tf_op jit(solution)/shard_map/ppermute | solution.py:459
  32.8 12.4 %collective-permute-start.17 = (f32[256,128]{1,0:T(8,128)S(1)}, f32[256,128]{1,0:T(8,128)S(1)}, u32[]{:S(2)}, u32[]{:S(2)}) collective-permute-start(f32[256,128]{1,0:T(8,128)S(1)} %shard_map.154.x_ref.refs_1_), channel_id=1, source_target_pairs={{0,1},{1,0},{2,3},{3,2},{4,5},{5,4},{6,7},{7,6},{8,9},{9,8},{10,11... | collective-permute-start | bytes 393224 | tf_op jit(solution)/shard_map/ppermute | solution.py:459
  34.4 10.8 %collective-permute-start.18 = (f32[256,128]{1,0:T(8,128)S(1)}, f32[256,128]{1,0:T(8,128)S(1)}, u32[]{:S(2)}, u32[]{:S(2)}) collective-permute-start(f32[256,128]{1,0:T(8,128)S(1)} %shard_map.155), channel_id=1, source_target_pairs={{0,2},{1,3},{2,0},{3,1},{4,6},{5,7},{6,4},{7,5},{8,10},{9,11},{10,... | collective-permute-start | bytes 393224 | tf_op jit(solution)/shard_map/ppermute | solution.py:459
  36.0 9.2 %collective-permute-start.19 = (f32[256,128]{1,0:T(8,128)S(1)}, f32[256,128]{1,0:T(8,128)S(1)}, u32[]{:S(2)}, u32[]{:S(2)}) collective-permute-start(f32[256,128]{1,0:T(8,128)S(1)} %shard_map.155), channel_id=1, source_target_pairs={{0,3},{1,2},{2,1},{3,0},{4,7},{5,6},{6,5},{7,4},{8,11},{9,10},{10,... | collective-permute-start | bytes 393224 | tf_op jit(solution)/shard_map/ppermute | solution.py:459
  37.2 3.6 %collective-permute-start.13 = (f32[2,16]{1,0:T(2,128)S(1)}, f32[2,16]{1,0:T(2,128)S(1)}, u32[]{:S(2)}, u32[]{:S(2)}) collective-permute-start(f32[2,16]{1,0:T(2,128)S(1)} %shard_map.149.x_ref.refs_0_), channel_id=1, source_target_pairs={{0,4},{4,0},{8,12},{12,8},{1,5},{5,1},{9,13},{13,9},{2,6},{6,2},{1... | collective-permute-start | bytes 392 | tf_op jit(solution)/shard_map/ppermute | solution.py:459
  40.8 4.5 %collective-permute-start.20 = (f32[2,16]{1,0:T(2,128)S(1)}, f32[2,16]{1,0:T(2,128)S(1)}, u32[]{:S(2)}, u32[]{:S(2)}) collective-permute-start(f32[2,16]{1,0:T(2,128)S(1)} %shard_map.150.refs_24_.refs_5_), channel_id=1, source_target_pairs={{0,8},{4,12},{8,0},{12,4},{1,9},{5,13},{9,1},{13,5},{2,10},{6,14},... | collective-permute-start | bytes 392 | tf_op jit(solution)/shard_map/ppermute | solution.py:459

commit v6 on v5

--- a/solution.py
+++ b/solution.py
@@ -355,14 +355,18 @@
     here = slice(start, start + rows)
     grad_b = sum_b_ref[:, here]
     grad_c = sum_c_ref[:, here]
+    pairs_b = pairs_c = jnp.zeros((scaled_ref.shape[0], 2 * rows), F32)
     for begin in range(0, channels, LANES):
         lanes = pl.ds(begin, LANES)
         entering, after = picked(size, states, lanes)
         enter_high, enter_low = split(entering, 2)
         after_high, after_low = split(after, 2)
         high, low, scaled = high_ref[:, lanes], low_ref[:, lanes], scaled_ref[:, lanes]
-        grad_c = grad_c + mm_nt(high, enter_high) + (mm_nt(high, enter_low) + mm_nt(low, enter_high))
-        grad_b = grad_b + mm_nt(scaled, after_high) + mm_nt(scaled, after_low)
+        pairs_c = pairs_c + mm_nt(high, jnp.concatenate([enter_low, enter_high], axis=0))
+        pairs_b = pairs_b + mm_nt(scaled, jnp.concatenate([after_low, after_high], axis=0))
+        grad_c = grad_c + mm_nt(low, enter_high)
+    grad_b = grad_b + (pairs_b[:, :rows] + pairs_b[:, rows:])
+    grad_c = grad_c + (pairs_c[:, :rows] + pairs_c[:, rows:])
     refs[-1][...] = jnp.concatenate([grad_b, grad_c], axis=1)
 
 
@@ -375,16 +379,14 @@
     length, channels = v_ref.shape
     heads = gcum_ref.shape[0]
     width = channels // heads
-    block_b, block_c = b_ref[...], c_ref[...]
+    twice_b, twice_c = (jnp.concatenate([ref[...], ref[...]], axis=1) for ref in (b_ref, c_ref))
     grad_cum = gcum_ref[...]
     grad_total = jnp.zeros((heads, 1), F32)
     for first in range(0, channels, LANES):
         here = pl.ds(first, LANES)
         entering, after = picked(size, states, here)
-        enter_high, enter_low = split(entering, 2)
-        after_high, after_low = split(after, 2)
-        inter = growth_ref[:, here] * (mm(block_c, enter_high) + mm(block_c, enter_low))
-        outer = fall_ref[:, here] * (mm(block_b, after_high) + mm(block_b, after_low))
+        inter = growth_ref[:, here] * mm(twice_c, jnp.concatenate(split(entering, 2), axis=0))
+        outer = fall_ref[:, here] * mm(twice_b, jnp.concatenate(split(after, 2), axis=0))
         gg_ref[0, :, here] = (coef_ref[:, here] * (mamba_ref[:, here] + inter)).astype(BF16)
         gv_ref[0, :, here] = (inner_ref[:, here] + outer).astype(BF16)
         pulled = v_ref[:, here].astype(F32) * outer
@@ -600,7 +602,7 @@
             ],
             name="intra",
         )(vals, gate, grad, block_b, block_c, cumulative)
-        return (made["intra"][2],)
+        return factors((made["intra"][2],))
 
     def factors(after):
         made["factors"] = call(
@@ -622,7 +624,7 @@
         return (made["prepare"][-1],)
 
     sums = max(seq - 2, 0) * CHUNKS
-    states = chain(sizes, mine, made, decay, {0: intra, 1: factors, max(sums - 2, 2): prepare})
+    states = chain(sizes, mine, made, decay, {0: intra, max(sums - 2, 2): prepare})
     sum_b, sum_c = made["intra"][2:]
     high, low, scaled, q, r = made["factors"][:5]
     coef, mamba, inner, growth, fall, grad_y, grad_cum, parts = made["prepare"]

time: 46.2 us -> 46.3 us (level)
  starting transfers between devices: 28 us -> 29 us
  Pallas kernels: 13.6 us -> 13 us
    ppermute x9, starting transfers between devices: 9.97 us -> 10.9 us  [swap(): return lax.ppermute(x, axis, [(i, i ^ bit) for i in range(size)])]
    pallas_call x22, Pallas kernels: 13.6 us -> 13 us  [run(): pl.pallas_call(kernel, out_shape=tuple(outs), in_specs=specs, out_specs=t...]
    ppermute x9, waiting for transfers between devices: 3.52 us -> 3.04 us  [swap(): return lax.ppermute(x, axis, [(i, i ^ bit) for i in range(size)])]
  transfers between devices with their start and end apart: 21 -> 21, of which waited for: 4 -> 3; matrix products, arithmetic and copies ran while one was open for 0% -> 0% of each run, Pallas kernels for 23% -> 22%
where the time goes in v6:
time: 46.3 us; the launch traced here: 46.1 us
  starting transfers between devices  29 us (63%)
  Pallas kernels  13 us (28%)
  waiting for transfers between devices  3.35 us (7%)
  between operations  0.8 us (2%)
    ppermute x12, starting transfers between devices, hop(): return lax.ppermute(x, ('replica', 'seq'), pairs)  18.1 us
    pallas_call x22, Pallas kernels, run(): pl.pallas_call(kernel, out_shape=tuple(outs), in_specs=specs, out_specs=t...  13 us
    ppermute x9, starting transfers between devices, swap(): return lax.ppermute(x, axis, [(i, i ^ bit) for i in range(size)])  10.9 us
    ppermute x9, waiting for transfers between devices, swap(): return lax.ppermute(x, axis, [(i, i ^ bit) for i in range(size)])  3.04 us
  transfers between devices with their start and end apart: 21, of which 3 were waited for; matrix products, arithmetic and copies ran while one was open for 0% of the time, Pallas kernels for 22%

profile of v6, /device:TPU:0, one launch (start us, length us, event | category | flops | bytes accessed | tf_op | source)
XLA Modules:
  0.0 46.1 jit_solution(11449595319490794324)
XLA Ops:
  0.6 2.3 %shard_map.135 = (bf16[256,1024]{1,0:T(8,128)(2,1)S(1)}, bf16[256,1024]{1,0:T(8,128)(2,1)S(1)}, bf16[256,1024]{1,0:T(8,128)(2,1)S(1)}, bf16[256,128]{1,0:T(8,128...) custom-call(bf16[256,1024]{1,0:T(8,128)(2,1)} %bitcast.10, ...), custom_call_target="tpu_custom_call" | custom-call | tf_op jit(solution)/shard_map/pallas_call | solution.py:445
  2.9 3.1 %collective-permute-start = (f32[32,1024]{1,0:T(8,128)S(1)}, f32[32,1024]{1,0:T(8,128)S(1)}, u32[]{:S(2)}, u32[]{:S(2)}) collective-permute-start(f32[32,1024]{1,0:T(8,128)S(1)} %get-tuple-element.49.refs_1_), channel_id=1, source_target_pairs={{0,4},{4,0},{8,12},{12,8},{16,20},{20,16},{24,28},{28,24},{1,5},{5... | collective-permute-start | bytes 393224 | tf_op jit(solution)/shard_map/ppermute | solution.py:474
  6.0 0.1 collective-permute-start.3
  6.1 1.9 %collective-permute-start.2 = (f32[32,1024]{1,0:T(8,128)S(1)}, f32[32,1024]{1,0:T(8,128)S(1)}, u32[]{:S(2)}, u32[]{:S(2)}) collective-permute-start(f32[32,1024]{1,0:T(8,128)S(1)} %get-tuple-element.59.refs_1_), channel_id=1, source_target_pairs={{0,4},{4,0},{8,12},{12,8},{16,20},{20,16},{24,28},{28,24},{1,5},{5... | collective-permute-start | bytes 393224 | tf_op jit(solution)/shard_map/ppermute | solution.py:474
  8.0 2.5 %shard_map.136 = (f32[256,1024]{1,0:T(8,128)S(1)}, f32[256,1024]{1,0:T(8,128)S(1)}, f32[256,128]{1,0:T(8,128)S(1)}, f32[256,128]{1,0:T(8,128)S(1)}) custom-call(bf16[256,1024]{1,0:T(8,128)(2,1)S(1)} %get-tuple-element.51.v_ref.refs_12_, bf16[256,1024]{1,0:T(8,128)(2,1)S(1)} %get-tuple-element.52.gate_ref, bf16[256,1024]{1,0:T(8,128)(2,1)S(1)} %get-tuple-element.53.go_ref, ...), custom_call_target="tpu_custom_call" | custom-call | tf_op jit(solution)/shard_map/pallas_call | solution.py:445
  10.6 1.6 %shard_map.137 = (bf16[256,1024]{1,0:T(8,128)(2,1)S(1)}, bf16[256,1024]{1,0:T(8,128)(2,1)S(1)}, bf16[256,1024]{1,0:T(8,128)(2,1)S(1)}, f32[128,1024]{1,0:T(8,128...) custom-call(bf16[256,1024]{1,0:T(8,128)(2,1)S(1)} %get-tuple-element, ...), custom_call_target="tpu_custom_call" | custom-call | tf_op jit(solution)/shard_map/pallas_call | solution.py:445
  12.2 0.0 collective-permute-done.refs_0_
  12.2 0.1 collective-permute-start.1
  12.3 3.1 %collective-permute-start.6 = (f32[32,1024]{1,0:T(8,128)S(1)}, f32[32,1024]{1,0:T(8,128)S(1)}, u32[]{:S(2)}, u32[]{:S(2)}) collective-permute-start(f32[32,1024]{1,0:T(8,128)S(1)} %get-tuple-element.62.refs_1_), channel_id=1, source_target_pairs={{0,4},{4,0},{8,12},{12,8},{16,20},{20,16},{24,28},{28,24},{1,5},{5... | collective-permute-start | bytes 393224 | tf_op jit(solution)/shard_map/ppermute | solution.py:474
  15.4 0.0 collective-permute-done.3.refs_0_.refs_3_
  15.4 0.1 collective-permute-start.5
  15.5 0.0 collective-permute-done.2.refs_0_.refs_6_
  15.6 0.5 %collective-permute-start.8 = (f32[32,1024]{1,0:T(8,128)S(1)}, f32[32,1024]{1,0:T(8,128)S(1)}, u32[]{:S(2)}, u32[]{:S(2)}) collective-permute-start(f32[32,1024]{1,0:T(8,128)S(1)} %shard_map.140.refs_3_), channel_id=1, source_target_pairs={{0,16},{4,8},{8,4},{12,28},{16,0},{20,24},{24,20},{28,12},{1,17},{... | collective-permute-start | bytes 393224 | tf_op jit(solution)/shard_map/ppermute | solution.py:474
  16.1 0.0 collective-permute-done.1.refs_0_.refs_1_
  16.1 3.7 %collective-permute-start.4 = (f32[32,1024]{1,0:T(8,128)S(1)}, f32[32,1024]{1,0:T(8,128)S(1)}, u32[]{:S(2)}, u32[]{:S(2)}) collective-permute-start(f32[32,1024]{1,0:T(8,128)S(1)} %shard_map.141.refs_3_), channel_id=1, source_target_pairs={{0,4},{4,0},{8,12},{12,8},{16,20},{20,16},{24,28},{28,24},{1,5},{5... | collective-permute-start | bytes 393224 | tf_op jit(solution)/shard_map/ppermute | solution.py:474
  19.8 0.0 collective-permute-done.6.refs_0_.refs_3_.refs_9_
  19.8 0.1 collective-permute-start.10
  19.9 0.0 collective-permute-done.5.refs_0_.refs_4_
  19.9 2.4 %collective-permute-start.7 = (f32[32,1024]{1,0:T(8,128)S(1)}, f32[32,1024]{1,0:T(8,128)S(1)}, u32[]{:S(2)}, u32[]{:S(2)}) collective-permute-start(f32[32,1024]{1,0:T(8,128)S(1)} %shard_map.143.after_ref), channel_id=1, source_target_pairs={{0,4},{4,0},{8,12},{12,8},{16,20},{20,16},{24,28},{28,24},{1,5},{5... | collective-permute-start | bytes 393224 | tf_op jit(solution)/shard_map/ppermute | solution.py:474
  22.4 1.4 %shard_map.144 = (f32[256,1024]{1,0:T(8,128)S(1)}, f32[256,1024]{1,0:T(8,128)S(1)}, f32[256,1024]{1,0:T(8,128)S(1)}, f32[256,1024]{1,0:T(8,128)S(1)}, f32[256,10...) custom-call(bf16[256,1024]{1,0:T(8,128)(2,1)S(1)} %get-tuple-element.51.v_ref.refs_12_, ...), custom_call_target="tpu_custom_call" | custom-call | tf_op jit(solution)/shard_map/pallas_call | solution.py:445
  23.8 0.0 collective-permute-done.8.refs_0_.refs_1_.refs_7_
  23.8 1.3 %collective-permute-start.9 = (f32[32,1024]{1,0:T(8,128)S(1)}, f32[32,1024]{1,0:T(8,128)S(1)}, u32[]{:S(2)}, u32[]{:S(2)}) collective-permute-start(f32[32,1024]{1,0:T(8,128)S(1)} %shard_map.145.refs_3_), channel_id=1, source_target_pairs={{0,4},{4,0},{8,12},{12,8},{16,20},{20,16},{24,28},{28,24},{1,5},{5... | collective-permute-start | bytes 393224 | tf_op jit(solution)/shard_map/ppermute | solution.py:474
  25.2 0.0 collective-permute-done.4.refs_4_.refs_2_
  25.2 0.0 collective-permute-done.10.refs_0_.refs_4_.refs_10_
  25.2 1.7 %collective-permute-start.11 = (f32[32,1024]{1,0:T(8,128)S(1)}, f32[32,1024]{1,0:T(8,128)S(1)}, u32[]{:S(2)}, u32[]{:S(2)}) collective-permute-start(f32[32,1024]{1,0:T(8,128)S(1)} %shard_map.146), channel_id=1, source_target_pairs={{0,4},{4,0},{8,12},{12,8},{16,20},{20,16},{24,28},{28,24},{1,5},{5... | collective-permute-start | bytes 393224 | tf_op jit(solution)/shard_map/ppermute | solution.py:474
  26.9 0.0 collective-permute-done.7.refs_5_
  26.9 0.1 shard_map.147.refs_9_.refs_11_
  27.0 0.7 %shard_map.151.refs_0_ = f32[256,128]{1,0:T(8,128)S(1)} custom-call(f32[32,1024]{1,0:T(8,128)S(1)} %collective-permute-done.refs_0_, f32[32,1024]{1,0:T(8,128)S(1)} %collective-permute-done.1.refs_0_.refs_1_, f32[32,1024]{1,0:T(8,128)S(1)} %collective-permute-done.4.refs_4_.refs_2_, f32[32,1024]{1,0:T(8,128)S(1)} %collective-permute-done.3.refs_0_.refs_3_, ...), custom_call_target="tpu_custom_call" | custom-call | tf_op jit(solution)/shard_map/pallas_call | solution.py:445
  27.7 1.6 %collective-permute-start.14 = (f32[256,128]{1,0:T(8,128)S(1)}, f32[256,128]{1,0:T(8,128)S(1)}, u32[]{:S(2)}, u32[]{:S(2)}) collective-permute-start(f32[256,128]{1,0:T(8,128)S(1)} %shard_map.151.refs_0_), channel_id=1, source_target_pairs={{0,1},{1,0},{2,3},{3,2},{4,5},{5,4},{6,7},{7,6},{8,9},{9,8},{10,11... | collective-permute-start | bytes 393224 | tf_op jit(solution)/shard_map/ppermute | solution.py:461
  29.2 1.5 %collective-permute-start.15 = (f32[256,128]{1,0:T(8,128)S(1)}, f32[256,128]{1,0:T(8,128)S(1)}, u32[]{:S(2)}, u32[]{:S(2)}) collective-permute-start(f32[256,128]{1,0:T(8,128)S(1)} %shard_map.151.refs_0_), channel_id=1, source_target_pairs={{0,2},{1,3},{2,0},{3,1},{4,6},{5,7},{6,4},{7,5},{8,10},{9,11},{10,... | collective-permute-start | bytes 393224 | tf_op jit(solution)/shard_map/ppermute | solution.py:461
  30.8 0.5 %collective-permute-start.16 = (f32[256,128]{1,0:T(8,128)S(1)}, f32[256,128]{1,0:T(8,128)S(1)}, u32[]{:S(2)}, u32[]{:S(2)}) collective-permute-start(f32[256,128]{1,0:T(8,128)S(1)} %shard_map.151.refs_0_), channel_id=1, source_target_pairs={{0,3},{1,2},{2,1},{3,0},{4,7},{5,6},{6,5},{7,4},{8,11},{9,10},{10,... | collective-permute-start | bytes 393224 | tf_op jit(solution)/shard_map/ppermute | solution.py:461
  31.2 0.0 collective-permute-done.9.refs_2_.refs_8_
  31.2 0.3 collective-permute-done.11.refs_5_.refs_11_
  31.5 0.2 shard_map.148.x_ref.refs_11_
  31.8 0.0 collective-permute-start.12
  31.8 0.8 %shard_map.154.x_ref.refs_1_ = f32[256,128]{1,0:T(8,128)S(1)} custom-call(f32[32,1024]{1,0:T(8,128)S(1)} %collective-permute-done.2.refs_0_.refs_6_, f32[32,1024]{1,0:T(8,128)S(1)} %collective-permute-done.8.refs_0_.refs_1_.refs_7_, f32[32,1024]{1,0:T(8,128)S(1)} %collective-permute-done.9.refs_2_.refs_8_, ...), custom_call_target="tpu_custom_call" | custom-call | tf_op jit(solution)/shard_map/pallas_call | solution.py:445
  32.6 1.5 %collective-permute-start.17 = (f32[256,128]{1,0:T(8,128)S(1)}, f32[256,128]{1,0:T(8,128)S(1)}, u32[]{:S(2)}, u32[]{:S(2)}) collective-permute-start(f32[256,128]{1,0:T(8,128)S(1)} %shard_map.154.x_ref.refs_1_), channel_id=1, source_target_pairs={{0,1},{1,0},{2,3},{3,2},{4,5},{5,4},{6,7},{7,6},{8,9},{9,8},{10,11... | collective-permute-start | bytes 393224 | tf_op jit(solution)/shard_map/ppermute | solution.py:461
  34.1 0.0 collective-permute-done.12.y_ref
  34.2 1.6 %collective-permute-start.18 = (f32[256,128]{1,0:T(8,128)S(1)}, f32[256,128]{1,0:T(8,128)S(1)}, u32[]{:S(2)}, u32[]{:S(2)}) collective-permute-start(f32[256,128]{1,0:T(8,128)S(1)} %shard_map.155), channel_id=1, source_target_pairs={{0,2},{1,3},{2,0},{3,1},{4,6},{5,7},{6,4},{7,5},{8,10},{9,11},{10,... | collective-permute-start | bytes 393224 | tf_op jit(solution)/shard_map/ppermute | solution.py:461
  35.8 0.0 collective-permute-done.14.refs_1_
  35.8 0.5 %collective-permute-start.19 = (f32[256,128]{1,0:T(8,128)S(1)}, f32[256,128]{1,0:T(8,128)S(1)}, u32[]{:S(2)}, u32[]{:S(2)}) collective-permute-start(f32[256,128]{1,0:T(8,128)S(1)} %shard_map.155), channel_id=1, source_target_pairs={{0,3},{1,2},{2,1},{3,0},{4,7},{5,6},{6,5},{7,4},{8,11},{9,10},{10,... | collective-permute-start | bytes 393224 | tf_op jit(solution)/shard_map/ppermute | solution.py:461
  36.2 0.6 %collective-permute-done.15.refs_2_ = f32[256,128]{1,0:T(8,128)S(1)} collective-permute-done((f32[256,128]{1,0:T(8,128)S(1)}, f32[256,128]{1,0:T(8,128)S(1)}, u32[]{:S(2)}, u32[]{:S(2)}) %collective-permute-start.15) | collective-permute-done | bytes 131104 | tf_op jit(solution)/shard_map/ppermute | solution.py:461
  36.8 1.1 %collective-permute-start.13 = (f32[2,16]{1,0:T(2,128)S(1)}, f32[2,16]{1,0:T(2,128)S(1)}, u32[]{:S(2)}, u32[]{:S(2)}) collective-permute-start(f32[2,16]{1,0:T(2,128)S(1)} %shard_map.149.x_ref.refs_0_), channel_id=1, source_target_pairs={{0,4},{4,0},{8,12},{12,8},{1,5},{5,1},{9,13},{13,9},{2,6},{6,2},{1... | collective-permute-start | bytes 392 | tf_op jit(solution)/shard_map/ppermute | solution.py:461
  37.9 0.0 collective-permute-done.16.refs_3_
  38.0 2.4 %collective-permute-done.13.y_ref = f32[2,16]{1,0:T(2,128)S(1)} collective-permute-done((f32[2,16]{1,0:T(2,128)S(1)}, f32[2,16]{1,0:T(2,128)S(1)}, u32[]{:S(2)}, u32[]{:S(2)}) %collective-permute-start.13) | collective-permute-done | bytes 160 | tf_op jit(solution)/shard_map/ppermute | solution.py:461
  40.4 2.6 %collective-permute-start.20 = (f32[2,16]{1,0:T(2,128)S(1)}, f32[2,16]{1,0:T(2,128)S(1)}, u32[]{:S(2)}, u32[]{:S(2)}) collective-permute-start(f32[2,16]{1,0:T(2,128)S(1)} %shard_map.150.refs_24_.refs_5_), channel_id=1, source_target_pairs={{0,8},{4,12},{8,0},{12,4},{1,9},{5,13},{9,1},{13,5},{2,10},{6,14},... | collective-permute-start | bytes 392 | tf_op jit(solution)/shard_map/ppermute | solution.py:461
  43.0 2.3 %shard_map.153 = (bf16[1,256,1024]{2,1,0:T(8,128)(2,1)}, bf16[1,256,1024]{2,1,0:T(8,128)(2,1)}, f32[1,16,256]{2,1,0:T(8,128)}) custom-call(f32[32,1024]{1,0:T(8,128)S(1)} %collective-permute-done.refs_0_, f32[32,1024]{1,0:T(8,128)S(1)} %collective-permute-done.1.refs_0_.refs_1_, f32[32,1024]{1,0:T(8,128)S(1)} %collective-permute-done.4.refs_4_.refs_2_, ...), custom_call_target="tpu_custom_call" | custom-call | flops 300000000 | tf_op jit(solution)/shard_map/pallas_call | solution.py:445
  45.3 0.0 collective-permute-done.20.refs_6_
  45.3 0.0 collective-permute-done.17.refs_2_
  45.3 0.0 collective-permute-done.18.refs_3_
  45.3 0.0 collective-permute-done.19.refs_4_
  45.3 0.8 %shard_map.156 = (f32[1,256,128]{2,1,0:T(8,128)}, f32[1,256,128]{2,1,0:T(8,128)}, f32[1,16]{1,0:T(1,128)}, f32[1,16]{1,0:T(1,128)}) custom-call(f32[256,128]{1,0:T(8,128)S(1)} %shard_map.152.refs_25_.refs_0_, f32[256,128]{1,0:T(8,128)S(1)} %shard_map.154.x_ref.refs_1_, f32[256,128]{1,0:T(8,128)S(1)} %collective-permute-done.17.refs_2_, ...), custom_call_target="tpu_custom_call" | custom-call | tf_op jit(solution)/shard_map/pallas_call | solution.py:445
  (13 shorter events, 0.2 us)
Async XLA Ops:
  2.9 9.3 %collective-permute-start = (f32[32,1024]{1,0:T(8,128)S(1)}, f32[32,1024]{1,0:T(8,128)S(1)}, u32[]{:S(2)}, u32[]{:S(2)}) collective-permute-start(f32[32,1024]{1,0:T(8,128)S(1)} %get-tuple-element.49.refs_1_), channel_id=1, source_target_pairs={{0,4},{4,0},{8,12},{12,8},{16,20},{20,16},{24,28},{28,24},{1,5},{5... | collective-permute-start | bytes 393224 | tf_op jit(solution)/shard_map/ppermute | solution.py:474
  6.0 9.4 %collective-permute-start.3 = (f32[32,1024]{1,0:T(8,128)S(1)}, f32[32,1024]{1,0:T(8,128)S(1)}, u32[]{:S(2)}, u32[]{:S(2)}) collective-permute-start(f32[32,1024]{1,0:T(8,128)S(1)} %get-tuple-element.60.refs_1_), channel_id=1, source_target_pairs={{0,4},{4,0},{8,12},{12,8},{16,20},{20,16},{24,28},{28,24},{1,5},{5... | collective-permute-start | bytes 393224 | tf_op jit(solution)/shard_map/ppermute | solution.py:474
  6.1 9.4 %collective-permute-start.2 = (f32[32,1024]{1,0:T(8,128)S(1)}, f32[32,1024]{1,0:T(8,128)S(1)}, u32[]{:S(2)}, u32[]{:S(2)}) collective-permute-start(f32[32,1024]{1,0:T(8,128)S(1)} %get-tuple-element.59.refs_1_), channel_id=1, source_target_pairs={{0,4},{4,0},{8,12},{12,8},{16,20},{20,16},{24,28},{28,24},{1,5},{5... | collective-permute-start | bytes 393224 | tf_op jit(solution)/shard_map/ppermute | solution.py:474
  12.2 3.9 %collective-permute-start.1 = (f32[32,1024]{1,0:T(8,128)S(1)}, f32[32,1024]{1,0:T(8,128)S(1)}, u32[]{:S(2)}, u32[]{:S(2)}) collective-permute-start(f32[32,1024]{1,0:T(8,128)S(1)} %shard_map.138.refs_3_), channel_id=1, source_target_pairs={{0,16},{4,8},{8,4},{12,28},{16,0},{20,24},{24,20},{28,12},{1,17},{... | collective-permute-start | bytes 393224 | tf_op jit(solution)/shard_map/ppermute | solution.py:474
  12.3 7.5 %collective-permute-start.6 = (f32[32,1024]{1,0:T(8,128)S(1)}, f32[32,1024]{1,0:T(8,128)S(1)}, u32[]{:S(2)}, u32[]{:S(2)}) collective-permute-start(f32[32,1024]{1,0:T(8,128)S(1)} %get-tuple-element.62.refs_1_), channel_id=1, source_target_pairs={{0,4},{4,0},{8,12},{12,8},{16,20},{20,16},{24,28},{28,24},{1,5},{5... | collective-permute-start | bytes 393224 | tf_op jit(solution)/shard_map/ppermute | solution.py:474
  15.4 4.5 %collective-permute-start.5 = (f32[32,1024]{1,0:T(8,128)S(1)}, f32[32,1024]{1,0:T(8,128)S(1)}, u32[]{:S(2)}, u32[]{:S(2)}) collective-permute-start(f32[32,1024]{1,0:T(8,128)S(1)} %shard_map.139.refs_3_), channel_id=1, source_target_pairs={{0,16},{4,8},{8,4},{12,28},{16,0},{20,24},{24,20},{28,12},{1,17},{... | collective-permute-start | bytes 393224 | tf_op jit(solution)/shard_map/ppermute | solution.py:474
  15.6 8.2 %collective-permute-start.8 = (f32[32,1024]{1,0:T(8,128)S(1)}, f32[32,1024]{1,0:T(8,128)S(1)}, u32[]{:S(2)}, u32[]{:S(2)}) collective-permute-start(f32[32,1024]{1,0:T(8,128)S(1)} %shard_map.140.refs_3_), channel_id=1, source_target_pairs={{0,16},{4,8},{8,4},{12,28},{16,0},{20,24},{24,20},{28,12},{1,17},{... | collective-permute-start | bytes 393224 | tf_op jit(solution)/shard_map/ppermute | solution.py:474
  16.1 9.0 %collective-permute-start.4 = (f32[32,1024]{1,0:T(8,128)S(1)}, f32[32,1024]{1,0:T(8,128)S(1)}, u32[]{:S(2)}, u32[]{:S(2)}) collective-permute-start(f32[32,1024]{1,0:T(8,128)S(1)} %shard_map.141.refs_3_), channel_id=1, source_target_pairs={{0,4},{4,0},{8,12},{12,8},{16,20},{20,16},{24,28},{28,24},{1,5},{5... | collective-permute-start | bytes 393224 | tf_op jit(solution)/shard_map/ppermute | solution.py:474
  19.8 5.3 %collective-permute-start.10 = (f32[32,1024]{1,0:T(8,128)S(1)}, f32[32,1024]{1,0:T(8,128)S(1)}, u32[]{:S(2)}, u32[]{:S(2)}) collective-permute-start(f32[32,1024]{1,0:T(8,128)S(1)} %shard_map.142.refs_3_), channel_id=1, source_target_pairs={{0,16},{4,8},{8,4},{12,28},{16,0},{20,24},{24,20},{28,12},{1,17},{... | collective-permute-start | bytes 393224 | tf_op jit(solution)/shard_map/ppermute | solution.py:474
  19.9 6.9 %collective-permute-start.7 = (f32[32,1024]{1,0:T(8,128)S(1)}, f32[32,1024]{1,0:T(8,128)S(1)}, u32[]{:S(2)}, u32[]{:S(2)}) collective-permute-start(f32[32,1024]{1,0:T(8,128)S(1)} %shard_map.143.after_ref), channel_id=1, source_target_pairs={{0,4},{4,0},{8,12},{12,8},{16,20},{20,16},{24,28},{28,24},{1,5},{5... | collective-permute-start | bytes 393224 | tf_op jit(solution)/shard_map/ppermute | solution.py:474
  23.8 7.4 %collective-permute-start.9 = (f32[32,1024]{1,0:T(8,128)S(1)}, f32[32,1024]{1,0:T(8,128)S(1)}, u32[]{:S(2)}, u32[]{:S(2)}) collective-permute-start(f32[32,1024]{1,0:T(8,128)S(1)} %shard_map.145.refs_3_), channel_id=1, source_target_pairs={{0,4},{4,0},{8,12},{12,8},{16,20},{20,16},{24,28},{28,24},{1,5},{5... | collective-permute-start | bytes 393224 | tf_op jit(solution)/shard_map/ppermute | solution.py:474
  25.2 6.3 %collective-permute-start.11 = (f32[32,1024]{1,0:T(8,128)S(1)}, f32[32,1024]{1,0:T(8,128)S(1)}, u32[]{:S(2)}, u32[]{:S(2)}) collective-permute-start(f32[32,1024]{1,0:T(8,128)S(1)} %shard_map.146), channel_id=1, source_target_pairs={{0,4},{4,0},{8,12},{12,8},{16,20},{20,16},{24,28},{28,24},{1,5},{5... | collective-permute-start | bytes 393224 | tf_op jit(solution)/shard_map/ppermute | solution.py:474
  27.7 8.1 %collective-permute-start.14 = (f32[256,128]{1,0:T(8,128)S(1)}, f32[256,128]{1,0:T(8,128)S(1)}, u32[]{:S(2)}, u32[]{:S(2)}) collective-permute-start(f32[256,128]{1,0:T(8,128)S(1)} %shard_map.151.refs_0_), channel_id=1, source_target_pairs={{0,1},{1,0},{2,3},{3,2},{4,5},{5,4},{6,7},{7,6},{8,9},{9,8},{10,11... | collective-permute-start | bytes 393224 | tf_op jit(solution)/shard_map/ppermute | solution.py:461
  29.2 7.6 %collective-permute-start.15 = (f32[256,128]{1,0:T(8,128)S(1)}, f32[256,128]{1,0:T(8,128)S(1)}, u32[]{:S(2)}, u32[]{:S(2)}) collective-permute-start(f32[256,128]{1,0:T(8,128)S(1)} %shard_map.151.refs_0_), channel_id=1, source_target_pairs={{0,2},{1,3},{2,0},{3,1},{4,6},{5,7},{6,4},{7,5},{8,10},{9,11},{10,... | collective-permute-start | bytes 393224 | tf_op jit(solution)/shard_map/ppermute | solution.py:461
  30.8 7.2 %collective-permute-start.16 = (f32[256,128]{1,0:T(8,128)S(1)}, f32[256,128]{1,0:T(8,128)S(1)}, u32[]{:S(2)}, u32[]{:S(2)}) collective-permute-start(f32[256,128]{1,0:T(8,128)S(1)} %shard_map.151.refs_0_), channel_id=1, source_target_pairs={{0,3},{1,2},{2,1},{3,0},{4,7},{5,6},{6,5},{7,4},{8,11},{9,10},{10,... | collective-permute-start | bytes 393224 | tf_op jit(solution)/shard_map/ppermute | solution.py:461
  31.8 2.4 %collective-permute-start.12 = (f32[2,16]{1,0:T(2,128)S(1)}, f32[2,16]{1,0:T(2,128)S(1)}, u32[]{:S(2)}, u32[]{:S(2)}) collective-permute-start(f32[2,16]{1,0:T(2,128)S(1)} %shard_map.148.x_ref.refs_11_), channel_id=1, source_target_pairs={{0,16},{16,0},{1,17},{17,1},{2,18},{18,2},{3,19},{19,3},{4,20},{20... | collective-permute-start | bytes 392 | tf_op jit(solution)/shard_map/ppermute | solution.py:461
  32.6 12.7 %collective-permute-start.17 = (f32[256,128]{1,0:T(8,128)S(1)}, f32[256,128]{1,0:T(8,128)S(1)}, u32[]{:S(2)}, u32[]{:S(2)}) collective-permute-start(f32[256,128]{1,0:T(8,128)S(1)} %shard_map.154.x_ref.refs_1_), channel_id=1, source_target_pairs={{0,1},{1,0},{2,3},{3,2},{4,5},{5,4},{6,7},{7,6},{8,9},{9,8},{10,11... | collective-permute-start | bytes 393224 | tf_op jit(solution)/shard_map/ppermute | solution.py:461
  34.2 11.1 %collective-permute-start.18 = (f32[256,128]{1,0:T(8,128)S(1)}, f32[256,128]{1,0:T(8,128)S(1)}, u32[]{:S(2)}, u32[]{:S(2)}) collective-permute-start(f32[256,128]{1,0:T(8,128)S(1)} %shard_map.155), channel_id=1, source_target_pairs={{0,2},{1,3},{2,0},{3,1},{4,6},{5,7},{6,4},{7,5},{8,10},{9,11},{10,... | collective-permute-start | bytes 393224 | tf_op jit(solution)/shard_map/ppermute | solution.py:461
  35.8 9.6 %collective-permute-start.19 = (f32[256,128]{1,0:T(8,128)S(1)}, f32[256,128]{1,0:T(8,128)S(1)}, u32[]{:S(2)}, u32[]{:S(2)}) collective-permute-start(f32[256,128]{1,0:T(8,128)S(1)} %shard_map.155), channel_id=1, source_target_pairs={{0,3},{1,2},{2,1},{3,0},{4,7},{5,6},{6,5},{7,4},{8,11},{9,10},{10,... | collective-permute-start | bytes 393224 | tf_op jit(solution)/shard_map/ppermute | solution.py:461
  36.8 3.6 %collective-permute-start.13 = (f32[2,16]{1,0:T(2,128)S(1)}, f32[2,16]{1,0:T(2,128)S(1)}, u32[]{:S(2)}, u32[]{:S(2)}) collective-permute-start(f32[2,16]{1,0:T(2,128)S(1)} %shard_map.149.x_ref.refs_0_), channel_id=1, source_target_pairs={{0,4},{4,0},{8,12},{12,8},{1,5},{5,1},{9,13},{13,9},{2,6},{6,2},{1... | collective-permute-start | bytes 392 | tf_op jit(solution)/shard_map/ppermute | solution.py:461
  40.4 4.9 %collective-permute-start.20 = (f32[2,16]{1,0:T(2,128)S(1)}, f32[2,16]{1,0:T(2,128)S(1)}, u32[]{:S(2)}, u32[]{:S(2)}) collective-permute-start(f32[2,16]{1,0:T(2,128)S(1)} %shard_map.150.refs_24_.refs_5_), channel_id=1, source_target_pairs={{0,8},{4,12},{8,0},{12,4},{1,9},{5,13},{9,1},{13,5},{2,10},{6,14},... | collective-permute-start | bytes 392 | tf_op jit(solution)/shard_map/ppermute | solution.py:461

commit v7 on v6

--- a/solution.py
+++ b/solution.py
@@ -374,7 +374,7 @@
     states, refs = [refs[3 * i : 3 * i + 3] for i in range(pieces)], refs[3 * pieces :]
     (
         v_ref, b_ref, c_ref, coef_ref, mamba_ref, inner_ref, growth_ref, fall_ref, gy_ref,
-        gcum_ref, decay_ref, neg_ref, *_, gv_ref, gg_ref, gs_ref,
+        gcum_ref, decay_ref, neg_ref, *_, gv_ref, gg_ref, gs_ref, total_ref,
     ) = refs
     length, channels = v_ref.shape
     heads = gcum_ref.shape[0]
@@ -398,6 +398,7 @@
         )
         grad_total = grad_total + head_column(total_row, heads, width, first)
     gs_ref[0] = neg_ref[...] * (scan_tokens(grad_cum, True) + grad_total)
+    total_ref[...] = to_row(grad_total)
 
 
 def tree(values):
@@ -541,19 +542,19 @@
     return [x, swap(x, axis, size, bit)]
 
 
-def small_terms(x, axes, sizes, hooks):
+def small_terms(x, axes, sizes, between):
     bits = [(axis, 1 << k) for axis in axes for k in range(sizes[axis].bit_length() - 1)]
     if any(sizes[axis] & (sizes[axis] - 1) for axis in axes):
         x, bits = lax.psum(x, tuple(axes)), []
+    after = ()
     for count, (axis, bit) in enumerate(bits):
         theirs = swap(x, axis, sizes[axis], bit)
         if count == len(bits) - 1:
             break
-        x = call(add_kernel, [jax.ShapeDtypeStruct(x.shape, F32)], name=f"add{count}")(x, theirs)[0]
-        if count < len(hooks):
-            hooks[count]((x,))
-    for hook in hooks[max(len(bits) - 1, 0) :]:
-        hook((x,))
+        x = call(add_kernel, [jax.ShapeDtypeStruct(x.shape, F32)], name=f"add{count}", after=after)(x, theirs)[0]
+        after = between((x,)) if count == 0 else ()
+    if len(bits) < 2:
+        between((x,))
     return [x, theirs] if bits else [x]
 
 
@@ -602,7 +603,7 @@
             ],
             name="intra",
         )(vals, gate, grad, block_b, block_c, cumulative)
-        return factors((made["intra"][2],))
+        return (made["intra"][2],)
 
     def factors(after):
         made["factors"] = call(
@@ -624,7 +625,7 @@
         return (made["prepare"][-1],)
 
     sums = max(seq - 2, 0) * CHUNKS
-    states = chain(sizes, mine, made, decay, {0: intra, max(sums - 2, 2): prepare})
+    states = chain(sizes, mine, made, decay, {0: intra, 1: factors, max(sums - 2, 2): prepare})
     sum_b, sum_c = made["intra"][2:]
     high, low, scaled, q, r = made["factors"][:5]
     coef, mamba, inner, growth, fall, grad_y, grad_cum, parts = made["prepare"]
@@ -651,26 +652,29 @@
             terms += call(sum_kernel, [like(share_of.shape, F32)], name="sum")(*own)
             counts.append(1)
 
-    def exchange(after):
+    def between(after):
         later = call(copy_kernel, [like(share_of.shape, F32)], name="later", after=after)(share_of)[0]
         made["share"] = sum_terms(share_of, later, "tensor", sizes["tensor"])
+        return rest(after)
 
     def rest(after):
         made["rest"] = call(
             functools.partial(rest_kernel, seq, CHUNKS),
-            [like((1, length, channels), BF16)] * 2 + [like((1, heads, length), F32)],
+            [like((1, length, channels), BF16)] * 2
+            + [like((1, heads, length), F32), like((1, heads), F32)],
             name="rest",
             after=(*after, *terms),
         )(
             *(x for group in states for x in group),
             vals, block_b, block_c, coef, mamba, inner, growth, fall, grad_y, grad_cum, decay, negative,
         )
-
-    own = small_terms(rate_row, ("replica", "seq"), sizes, (exchange, rest))
+        return (made["rest"][3],)
+
+    own = small_terms(rate_row, ("seq", "replica"), sizes, between)
     for group in (made["share"], own):
         terms += group
         counts.append(len(group))
-    grad_values, grad_gate, grad_steps = made["rest"]
+    grad_values, grad_gate, grad_steps, _ = made["rest"]
     grad_b, grad_c, rate_sum, skip_sum = call(
         functools.partial(last_kernel, tuple(counts)),
         [like((1, length, state), F32)] * 2 + [like((1, heads), F32)] * 2,

time: 46.3 us -> 45.3 us (0.978)
  waiting for transfers between devices: 3.35 us -> 1.54 us
  starting transfers between devices: 29 us -> 29.8 us
    ppermute x9, waiting for transfers between devices: 3.04 us -> 1.15 us  [swap(): return lax.ppermute(x, axis, [(i, i ^ bit) for i in range(size)])]
    ppermute x9, starting transfers between devices: 10.9 us -> 11.8 us  [swap(): return lax.ppermute(x, axis, [(i, i ^ bit) for i in range(size)])]
where the time goes in v7:
time: 45.3 us; the launch traced here: 45.1 us
  starting transfers between devices  29.8 us (66%)
  Pallas kernels  13 us (29%)
  waiting for transfers between devices  1.54 us (3%)
  between operations  0.79 us (2%)
    ppermute x12, starting transfers between devices, hop(): return lax.ppermute(x, ('replica', 'seq'), pairs)  18 us
    pallas_call x22, Pallas kernels, run(): pl.pallas_call(kernel, out_shape=tuple(outs), in_specs=specs, out_specs=t...  13 us
    ppermute x9, starting transfers between devices, swap(): return lax.ppermute(x, axis, [(i, i ^ bit) for i in range(size)])  11.8 us
    ppermute x9, waiting for transfers between devices, swap(): return lax.ppermute(x, axis, [(i, i ^ bit) for i in range(size)])  1.15 us
  transfers between devices with their start and end apart: 21, of which 3 were waited for; matrix products, arithmetic and copies ran while one was open for 0% of the time, Pallas kernels for 22%

profile of v7, /device:TPU:0, one launch (start us, length us, event | category | flops | bytes accessed | tf_op | source)
XLA Modules:
  0.0 45.1 jit_solution(18122897925004585053)
XLA Ops:
  0.6 2.3 %shard_map.135 = (bf16[256,1024]{1,0:T(8,128)(2,1)S(1)}, bf16[256,1024]{1,0:T(8,128)(2,1)S(1)}, bf16[256,1024]{1,0:T(8,128)(2,1)S(1)}, bf16[256,128]{1,0:T(8,128...) custom-call(bf16[256,1024]{1,0:T(8,128)(2,1)} %bitcast.10, ...), custom_call_target="tpu_custom_call" | custom-call | tf_op jit(solution)/shard_map/pallas_call | solution.py:446
  2.9 3.1 %collective-permute-start = (f32[32,1024]{1,0:T(8,128)S(1)}, f32[32,1024]{1,0:T(8,128)S(1)}, u32[]{:S(2)}, u32[]{:S(2)}) collective-permute-start(f32[32,1024]{1,0:T(8,128)S(1)} %get-tuple-element.50.refs_1_), channel_id=1, source_target_pairs={{0,4},{4,0},{8,12},{12,8},{16,20},{20,16},{24,28},{28,24},{1,5},{5... | collective-permute-start | bytes 393224 | tf_op jit(solution)/shard_map/ppermute | solution.py:475
  6.0 0.1 collective-permute-start.3
  6.1 1.9 %collective-permute-start.2 = (f32[32,1024]{1,0:T(8,128)S(1)}, f32[32,1024]{1,0:T(8,128)S(1)}, u32[]{:S(2)}, u32[]{:S(2)}) collective-permute-start(f32[32,1024]{1,0:T(8,128)S(1)} %get-tuple-element.60.refs_1_), channel_id=1, source_target_pairs={{0,4},{4,0},{8,12},{12,8},{16,20},{20,16},{24,28},{28,24},{1,5},{5... | collective-permute-start | bytes 393224 | tf_op jit(solution)/shard_map/ppermute | solution.py:475
  8.0 2.5 %shard_map.136 = (f32[256,1024]{1,0:T(8,128)S(1)}, f32[256,1024]{1,0:T(8,128)S(1)}, f32[256,128]{1,0:T(8,128)S(1)}, f32[256,128]{1,0:T(8,128)S(1)}) custom-call(bf16[256,1024]{1,0:T(8,128)(2,1)S(1)} %get-tuple-element.52.v_ref.refs_12_, bf16[256,1024]{1,0:T(8,128)(2,1)S(1)} %get-tuple-element.53.gate_ref, bf16[256,1024]{1,0:T(8,128)(2,1)S(1)} %get-tuple-element.54.go_ref, ...), custom_call_target="tpu_custom_call" | custom-call | tf_op jit(solution)/shard_map/pallas_call | solution.py:446
  10.6 0.0 collective-permute-done.refs_0_
  10.6 0.1 collective-permute-start.1
  10.7 3.4 %collective-permute-start.6 = (f32[32,1024]{1,0:T(8,128)S(1)}, f32[32,1024]{1,0:T(8,128)S(1)}, u32[]{:S(2)}, u32[]{:S(2)}) collective-permute-start(f32[32,1024]{1,0:T(8,128)S(1)} %get-tuple-element.63.refs_1_), channel_id=1, source_target_pairs={{0,4},{4,0},{8,12},{12,8},{16,20},{20,16},{24,28},{28,24},{1,5},{5... | collective-permute-start | bytes 393224 | tf_op jit(solution)/shard_map/ppermute | solution.py:475
  14.1 1.6 %shard_map.138 = (bf16[256,1024]{1,0:T(8,128)(2,1)S(1)}, bf16[256,1024]{1,0:T(8,128)(2,1)S(1)}, bf16[256,1024]{1,0:T(8,128)(2,1)S(1)}, f32[128,1024]{1,0:T(8,128...) custom-call(bf16[256,1024]{1,0:T(8,128)(2,1)S(1)} %get-tuple-element, ...), custom_call_target="tpu_custom_call" | custom-call | tf_op jit(solution)/shard_map/pallas_call | solution.py:446
  15.7 0.0 collective-permute-done.3.refs_0_.refs_3_
  15.7 0.1 collective-permute-start.5
  15.8 0.1 collective-permute-done.2.refs_0_.refs_6_
  16.0 0.4 collective-permute-start.8
  16.4 0.0 collective-permute-done.1.refs_0_.refs_1_
  16.4 3.4 %collective-permute-start.4 = (f32[32,1024]{1,0:T(8,128)S(1)}, f32[32,1024]{1,0:T(8,128)S(1)}, u32[]{:S(2)}, u32[]{:S(2)}) collective-permute-start(f32[32,1024]{1,0:T(8,128)S(1)} %shard_map.141.refs_3_), channel_id=1, source_target_pairs={{0,4},{4,0},{8,12},{12,8},{16,20},{20,16},{24,28},{28,24},{1,5},{5... | collective-permute-start | bytes 393224 | tf_op jit(solution)/shard_map/ppermute | solution.py:475
  19.8 0.0 collective-permute-done.6.refs_0_.refs_3_.refs_9_
  19.8 0.1 collective-permute-start.10
  19.9 0.0 collective-permute-done.5.refs_0_.refs_4_
  19.9 2.3 %collective-permute-start.7 = (f32[32,1024]{1,0:T(8,128)S(1)}, f32[32,1024]{1,0:T(8,128)S(1)}, u32[]{:S(2)}, u32[]{:S(2)}) collective-permute-start(f32[32,1024]{1,0:T(8,128)S(1)} %shard_map.143.after_ref), channel_id=1, source_target_pairs={{0,4},{4,0},{8,12},{12,8},{16,20},{20,16},{24,28},{28,24},{1,5},{5... | collective-permute-start | bytes 393224 | tf_op jit(solution)/shard_map/ppermute | solution.py:475
  22.3 1.4 %shard_map.144 = (f32[256,1024]{1,0:T(8,128)S(1)}, f32[256,1024]{1,0:T(8,128)S(1)}, f32[256,1024]{1,0:T(8,128)S(1)}, f32[256,1024]{1,0:T(8,128)S(1)}, f32[256,10...) custom-call(bf16[256,1024]{1,0:T(8,128)(2,1)S(1)} %get-tuple-element.52.v_ref.refs_12_, ...), custom_call_target="tpu_custom_call" | custom-call | tf_op jit(solution)/shard_map/pallas_call | solution.py:446
  23.7 0.0 collective-permute-done.8.refs_0_.refs_1_.refs_7_
  23.7 1.3 %collective-permute-start.9 = (f32[32,1024]{1,0:T(8,128)S(1)}, f32[32,1024]{1,0:T(8,128)S(1)}, u32[]{:S(2)}, u32[]{:S(2)}) collective-permute-start(f32[32,1024]{1,0:T(8,128)S(1)} %shard_map.145.refs_3_), channel_id=1, source_target_pairs={{0,4},{4,0},{8,12},{12,8},{16,20},{20,16},{24,28},{28,24},{1,5},{5... | collective-permute-start | bytes 393224 | tf_op jit(solution)/shard_map/ppermute | solution.py:475
  25.1 0.0 collective-permute-done.4.refs_4_.refs_2_
  25.1 0.0 collective-permute-done.10.refs_0_.refs_4_.refs_10_
  25.1 1.8 %collective-permute-start.11 = (f32[32,1024]{1,0:T(8,128)S(1)}, f32[32,1024]{1,0:T(8,128)S(1)}, u32[]{:S(2)}, u32[]{:S(2)}) collective-permute-start(f32[32,1024]{1,0:T(8,128)S(1)} %shard_map.146), channel_id=1, source_target_pairs={{0,4},{4,0},{8,12},{12,8},{16,20},{20,16},{24,28},{28,24},{1,5},{5... | collective-permute-start | bytes 393224 | tf_op jit(solution)/shard_map/ppermute | solution.py:475
  26.9 0.0 collective-permute-done.7.refs_5_
  26.9 0.1 shard_map.147.refs_9_.refs_11_
  27.1 0.7 %shard_map.150.refs_0_ = f32[256,128]{1,0:T(8,128)S(1)} custom-call(f32[32,1024]{1,0:T(8,128)S(1)} %collective-permute-done.refs_0_, f32[32,1024]{1,0:T(8,128)S(1)} %collective-permute-done.1.refs_0_.refs_1_, f32[32,1024]{1,0:T(8,128)S(1)} %collective-permute-done.4.refs_4_.refs_2_, f32[32,1024]{1,0:T(8,128)S(1)} %collective-permute-done.3.refs_0_.refs_3_, ...), custom_call_target="tpu_custom_call" | custom-call | tf_op jit(solution)/shard_map/pallas_call | solution.py:446
  27.7 1.6 %collective-permute-start.13 = (f32[256,128]{1,0:T(8,128)S(1)}, f32[256,128]{1,0:T(8,128)S(1)}, u32[]{:S(2)}, u32[]{:S(2)}) collective-permute-start(f32[256,128]{1,0:T(8,128)S(1)} %shard_map.150.refs_0_), channel_id=1, source_target_pairs={{0,1},{1,0},{2,3},{3,2},{4,5},{5,4},{6,7},{7,6},{8,9},{9,8},{10,11... | collective-permute-start | bytes 393224 | tf_op jit(solution)/shard_map/ppermute | solution.py:462
  29.3 1.5 %collective-permute-start.14 = (f32[256,128]{1,0:T(8,128)S(1)}, f32[256,128]{1,0:T(8,128)S(1)}, u32[]{:S(2)}, u32[]{:S(2)}) collective-permute-start(f32[256,128]{1,0:T(8,128)S(1)} %shard_map.150.refs_0_), channel_id=1, source_target_pairs={{0,2},{1,3},{2,0},{3,1},{4,6},{5,7},{6,4},{7,5},{8,10},{9,11},{10,... | collective-permute-start | bytes 393224 | tf_op jit(solution)/shard_map/ppermute | solution.py:462
  30.8 0.5 %collective-permute-start.15 = (f32[256,128]{1,0:T(8,128)S(1)}, f32[256,128]{1,0:T(8,128)S(1)}, u32[]{:S(2)}, u32[]{:S(2)}) collective-permute-start(f32[256,128]{1,0:T(8,128)S(1)} %shard_map.150.refs_0_), channel_id=1, source_target_pairs={{0,3},{1,2},{2,1},{3,0},{4,7},{5,6},{6,5},{7,4},{8,11},{9,10},{10,... | collective-permute-start | bytes 393224 | tf_op jit(solution)/shard_map/ppermute | solution.py:462
  31.3 0.0 collective-permute-done.9.refs_2_.refs_8_
  31.3 0.2 collective-permute-done.11.refs_5_.refs_11_
  31.5 0.2 shard_map.148.x_ref.refs_11_
  31.8 1.7 %collective-permute-start.12 = (f32[2,16]{1,0:T(2,128)S(1)}, f32[2,16]{1,0:T(2,128)S(1)}, u32[]{:S(2)}, u32[]{:S(2)}) collective-permute-start(f32[2,16]{1,0:T(2,128)S(1)} %shard_map.148.x_ref.refs_11_), channel_id=1, source_target_pairs={{0,4},{4,0},{8,12},{12,8},{1,5},{5,1},{9,13},{13,9},{2,6},{6,2},{1... | collective-permute-start | bytes 392 | tf_op jit(solution)/shard_map/ppermute | solution.py:462
  33.5 0.8 %shard_map.153.x_ref.refs_1_ = f32[256,128]{1,0:T(8,128)S(1)} custom-call(f32[32,1024]{1,0:T(8,128)S(1)} %collective-permute-done.2.refs_0_.refs_6_, f32[32,1024]{1,0:T(8,128)S(1)} %collective-permute-done.8.refs_0_.refs_1_.refs_7_, f32[32,1024]{1,0:T(8,128)S(1)} %collective-permute-done.9.refs_2_.refs_8_, ...), custom_call_target="tpu_custom_call" | custom-call | tf_op jit(solution)/shard_map/pallas_call | solution.py:446
  34.3 1.5 %collective-permute-start.16 = (f32[256,128]{1,0:T(8,128)S(1)}, f32[256,128]{1,0:T(8,128)S(1)}, u32[]{:S(2)}, u32[]{:S(2)}) collective-permute-start(f32[256,128]{1,0:T(8,128)S(1)} %shard_map.153.x_ref.refs_1_), channel_id=1, source_target_pairs={{0,1},{1,0},{2,3},{3,2},{4,5},{5,4},{6,7},{7,6},{8,9},{9,8},{10,11... | collective-permute-start | bytes 393224 | tf_op jit(solution)/shard_map/ppermute | solution.py:462
  35.8 0.0 collective-permute-done.12.y_ref
  35.8 1.6 %collective-permute-start.17 = (f32[256,128]{1,0:T(8,128)S(1)}, f32[256,128]{1,0:T(8,128)S(1)}, u32[]{:S(2)}, u32[]{:S(2)}) collective-permute-start(f32[256,128]{1,0:T(8,128)S(1)} %shard_map.154), channel_id=1, source_target_pairs={{0,2},{1,3},{2,0},{3,1},{4,6},{5,7},{6,4},{7,5},{8,10},{9,11},{10,... | collective-permute-start | bytes 393224 | tf_op jit(solution)/shard_map/ppermute | solution.py:462
  37.4 0.0 collective-permute-done.13.refs_1_
  37.4 1.0 %collective-permute-start.18 = (f32[256,128]{1,0:T(8,128)S(1)}, f32[256,128]{1,0:T(8,128)S(1)}, u32[]{:S(2)}, u32[]{:S(2)}) collective-permute-start(f32[256,128]{1,0:T(8,128)S(1)} %shard_map.154), channel_id=1, source_target_pairs={{0,3},{1,2},{2,1},{3,0},{4,7},{5,6},{6,5},{7,4},{8,11},{9,10},{10,... | collective-permute-start | bytes 393224 | tf_op jit(solution)/shard_map/ppermute | solution.py:462
  38.4 0.0 collective-permute-done.14.refs_2_
  38.4 0.0 collective-permute-done.15.refs_3_
  38.4 2.4 %collective-permute-start.19 = (f32[2,16]{1,0:T(2,128)S(1)}, f32[2,16]{1,0:T(2,128)S(1)}, u32[]{:S(2)}, u32[]{:S(2)}) collective-permute-start(f32[2,16]{1,0:T(2,128)S(1)} %shard_map.149.refs_24_.refs_0_.x_ref), channel_id=1, source_target_pairs={{0,8},{4,12},{8,0},{12,4},{1,9},{5,13},{9,1},{13,5},{2,10},{6,14},... | collective-permute-start | bytes 392 | tf_op jit(solution)/shard_map/ppermute | solution.py:462
  40.8 2.3 %shard_map.152 = (bf16[1,256,1024]{2,1,0:T(8,128)(2,1)}, bf16[1,256,1024]{2,1,0:T(8,128)(2,1)}, f32[1,16,256]{2,1,0:T(8,128)}, f32[1,16]{1,0:T(1,128)S(1)}) custom-call(f32[32,1024]{1,0:T(8,128)S(1)} %collective-permute-done.refs_0_, f32[32,1024]{1,0:T(8,128)S(1)} %collective-permute-done.1.refs_0_.refs_1_, ...), custom_call_target="tpu_custom_call" | custom-call | flops 300000000 | tf_op jit(solution)/shard_map/pallas_call | solution.py:446
  43.1 0.0 collective-permute-done.19.y_ref
  43.1 0.0 collective-permute-start.20
  43.2 1.1 %collective-permute-done.20.refs_6_ = f32[2,16]{1,0:T(2,128)S(1)} collective-permute-done((f32[2,16]{1,0:T(2,128)S(1)}, f32[2,16]{1,0:T(2,128)S(1)}, u32[]{:S(2)}, u32[]{:S(2)}) %collective-permute-start.20) | collective-permute-done | bytes 160 | tf_op jit(solution)/shard_map/ppermute | solution.py:462
  44.3 0.0 collective-permute-done.16.refs_2_
  44.3 0.0 collective-permute-done.17.refs_3_
  44.3 0.0 collective-permute-done.18.refs_4_
  44.3 0.8 %shard_map.156 = (f32[1,256,128]{2,1,0:T(8,128)}, f32[1,256,128]{2,1,0:T(8,128)}, f32[1,16]{1,0:T(1,128)}, f32[1,16]{1,0:T(1,128)}) custom-call(f32[256,128]{1,0:T(8,128)S(1)} %shard_map.151.refs_25_.refs_0_, f32[256,128]{1,0:T(8,128)S(1)} %shard_map.153.x_ref.refs_1_, f32[256,128]{1,0:T(8,128)S(1)} %collective-permute-done.16.refs_2_, ...), custom_call_target="tpu_custom_call" | custom-call | tf_op jit(solution)/shard_map/pallas_call | solution.py:446
  (13 shorter events, 0.2 us)
Async XLA Ops:
  2.9 7.7 %collective-permute-start = (f32[32,1024]{1,0:T(8,128)S(1)}, f32[32,1024]{1,0:T(8,128)S(1)}, u32[]{:S(2)}, u32[]{:S(2)}) collective-permute-start(f32[32,1024]{1,0:T(8,128)S(1)} %get-tuple-element.50.refs_1_), channel_id=1, source_target_pairs={{0,4},{4,0},{8,12},{12,8},{16,20},{20,16},{24,28},{28,24},{1,5},{5... | collective-permute-start | bytes 393224 | tf_op jit(solution)/shard_map/ppermute | solution.py:475
  6.0 9.7 %collective-permute-start.3 = (f32[32,1024]{1,0:T(8,128)S(1)}, f32[32,1024]{1,0:T(8,128)S(1)}, u32[]{:S(2)}, u32[]{:S(2)}) collective-permute-start(f32[32,1024]{1,0:T(8,128)S(1)} %get-tuple-element.61.refs_1_), channel_id=1, source_target_pairs={{0,4},{4,0},{8,12},{12,8},{16,20},{20,16},{24,28},{28,24},{1,5},{5... | collective-permute-start | bytes 393224 | tf_op jit(solution)/shard_map/ppermute | solution.py:475
  6.1 9.9 %collective-permute-start.2 = (f32[32,1024]{1,0:T(8,128)S(1)}, f32[32,1024]{1,0:T(8,128)S(1)}, u32[]{:S(2)}, u32[]{:S(2)}) collective-permute-start(f32[32,1024]{1,0:T(8,128)S(1)} %get-tuple-element.60.refs_1_), channel_id=1, source_target_pairs={{0,4},{4,0},{8,12},{12,8},{16,20},{20,16},{24,28},{28,24},{1,5},{5... | collective-permute-start | bytes 393224 | tf_op jit(solution)/shard_map/ppermute | solution.py:475
  10.6 5.8 %collective-permute-start.1 = (f32[32,1024]{1,0:T(8,128)S(1)}, f32[32,1024]{1,0:T(8,128)S(1)}, u32[]{:S(2)}, u32[]{:S(2)}) collective-permute-start(f32[32,1024]{1,0:T(8,128)S(1)} %shard_map.137.after_ref), channel_id=1, source_target_pairs={{0,16},{4,8},{8,4},{12,28},{16,0},{20,24},{24,20},{28,12},{1,17},{... | collective-permute-start | bytes 393224 | tf_op jit(solution)/shard_map/ppermute | solution.py:475
  10.7 9.1 %collective-permute-start.6 = (f32[32,1024]{1,0:T(8,128)S(1)}, f32[32,1024]{1,0:T(8,128)S(1)}, u32[]{:S(2)}, u32[]{:S(2)}) collective-permute-start(f32[32,1024]{1,0:T(8,128)S(1)} %get-tuple-element.63.refs_1_), channel_id=1, source_target_pairs={{0,4},{4,0},{8,12},{12,8},{16,20},{20,16},{24,28},{28,24},{1,5},{5... | collective-permute-start | bytes 393224 | tf_op jit(solution)/shard_map/ppermute | solution.py:475
  15.7 4.2 %collective-permute-start.5 = (f32[32,1024]{1,0:T(8,128)S(1)}, f32[32,1024]{1,0:T(8,128)S(1)}, u32[]{:S(2)}, u32[]{:S(2)}) collective-permute-start(f32[32,1024]{1,0:T(8,128)S(1)} %shard_map.139.refs_3_), channel_id=1, source_target_pairs={{0,16},{4,8},{8,4},{12,28},{16,0},{20,24},{24,20},{28,12},{1,17},{... | collective-permute-start | bytes 393224 | tf_op jit(solution)/shard_map/ppermute | solution.py:475
  16.0 7.7 %collective-permute-start.8 = (f32[32,1024]{1,0:T(8,128)S(1)}, f32[32,1024]{1,0:T(8,128)S(1)}, u32[]{:S(2)}, u32[]{:S(2)}) collective-permute-start(f32[32,1024]{1,0:T(8,128)S(1)} %shard_map.140.refs_3_), channel_id=1, source_target_pairs={{0,16},{4,8},{8,4},{12,28},{16,0},{20,24},{24,20},{28,12},{1,17},{... | collective-permute-start | bytes 393224 | tf_op jit(solution)/shard_map/ppermute | solution.py:475
  16.4 8.6 %collective-permute-start.4 = (f32[32,1024]{1,0:T(8,128)S(1)}, f32[32,1024]{1,0:T(8,128)S(1)}, u32[]{:S(2)}, u32[]{:S(2)}) collective-permute-start(f32[32,1024]{1,0:T(8,128)S(1)} %shard_map.141.refs_3_), channel_id=1, source_target_pairs={{0,4},{4,0},{8,12},{12,8},{16,20},{20,16},{24,28},{28,24},{1,5},{5... | collective-permute-start | bytes 393224 | tf_op jit(solution)/shard_map/ppermute | solution.py:475
  19.8 5.2 %collective-permute-start.10 = (f32[32,1024]{1,0:T(8,128)S(1)}, f32[32,1024]{1,0:T(8,128)S(1)}, u32[]{:S(2)}, u32[]{:S(2)}) collective-permute-start(f32[32,1024]{1,0:T(8,128)S(1)} %shard_map.142.refs_3_), channel_id=1, source_target_pairs={{0,16},{4,8},{8,4},{12,28},{16,0},{20,24},{24,20},{28,12},{1,17},{... | collective-permute-start | bytes 393224 | tf_op jit(solution)/shard_map/ppermute | solution.py:475
  19.9 7.0 %collective-permute-start.7 = (f32[32,1024]{1,0:T(8,128)S(1)}, f32[32,1024]{1,0:T(8,128)S(1)}, u32[]{:S(2)}, u32[]{:S(2)}) collective-permute-start(f32[32,1024]{1,0:T(8,128)S(1)} %shard_map.143.after_ref), channel_id=1, source_target_pairs={{0,4},{4,0},{8,12},{12,8},{16,20},{20,16},{24,28},{28,24},{1,5},{5... | collective-permute-start | bytes 393224 | tf_op jit(solution)/shard_map/ppermute | solution.py:475
  23.7 7.6 %collective-permute-start.9 = (f32[32,1024]{1,0:T(8,128)S(1)}, f32[32,1024]{1,0:T(8,128)S(1)}, u32[]{:S(2)}, u32[]{:S(2)}) collective-permute-start(f32[32,1024]{1,0:T(8,128)S(1)} %shard_map.145.refs_3_), channel_id=1, source_target_pairs={{0,4},{4,0},{8,12},{12,8},{16,20},{20,16},{24,28},{28,24},{1,5},{5... | collective-permute-start | bytes 393224 | tf_op jit(solution)/shard_map/ppermute | solution.py:475
  25.1 6.4 %collective-permute-start.11 = (f32[32,1024]{1,0:T(8,128)S(1)}, f32[32,1024]{1,0:T(8,128)S(1)}, u32[]{:S(2)}, u32[]{:S(2)}) collective-permute-start(f32[32,1024]{1,0:T(8,128)S(1)} %shard_map.146), channel_id=1, source_target_pairs={{0,4},{4,0},{8,12},{12,8},{16,20},{20,16},{24,28},{28,24},{1,5},{5... | collective-permute-start | bytes 393224 | tf_op jit(solution)/shard_map/ppermute | solution.py:475
  27.7 9.7 %collective-permute-start.13 = (f32[256,128]{1,0:T(8,128)S(1)}, f32[256,128]{1,0:T(8,128)S(1)}, u32[]{:S(2)}, u32[]{:S(2)}) collective-permute-start(f32[256,128]{1,0:T(8,128)S(1)} %shard_map.150.refs_0_), channel_id=1, source_target_pairs={{0,1},{1,0},{2,3},{3,2},{4,5},{5,4},{6,7},{7,6},{8,9},{9,8},{10,11... | collective-permute-start | bytes 393224 | tf_op jit(solution)/shard_map/ppermute | solution.py:462
  29.3 9.1 %collective-permute-start.14 = (f32[256,128]{1,0:T(8,128)S(1)}, f32[256,128]{1,0:T(8,128)S(1)}, u32[]{:S(2)}, u32[]{:S(2)}) collective-permute-start(f32[256,128]{1,0:T(8,128)S(1)} %shard_map.150.refs_0_), channel_id=1, source_target_pairs={{0,2},{1,3},{2,0},{3,1},{4,6},{5,7},{6,4},{7,5},{8,10},{9,11},{10,... | collective-permute-start | bytes 393224 | tf_op jit(solution)/shard_map/ppermute | solution.py:462
  30.8 7.6 %collective-permute-start.15 = (f32[256,128]{1,0:T(8,128)S(1)}, f32[256,128]{1,0:T(8,128)S(1)}, u32[]{:S(2)}, u32[]{:S(2)}) collective-permute-start(f32[256,128]{1,0:T(8,128)S(1)} %shard_map.150.refs_0_), channel_id=1, source_target_pairs={{0,3},{1,2},{2,1},{3,0},{4,7},{5,6},{6,5},{7,4},{8,11},{9,10},{10,... | collective-permute-start | bytes 393224 | tf_op jit(solution)/shard_map/ppermute | solution.py:462
  31.8 4.1 %collective-permute-start.12 = (f32[2,16]{1,0:T(2,128)S(1)}, f32[2,16]{1,0:T(2,128)S(1)}, u32[]{:S(2)}, u32[]{:S(2)}) collective-permute-start(f32[2,16]{1,0:T(2,128)S(1)} %shard_map.148.x_ref.refs_11_), channel_id=1, source_target_pairs={{0,4},{4,0},{8,12},{12,8},{1,5},{5,1},{9,13},{13,9},{2,6},{6,2},{1... | collective-permute-start | bytes 392 | tf_op jit(solution)/shard_map/ppermute | solution.py:462
  34.3 10.0 %collective-permute-start.16 = (f32[256,128]{1,0:T(8,128)S(1)}, f32[256,128]{1,0:T(8,128)S(1)}, u32[]{:S(2)}, u32[]{:S(2)}) collective-permute-start(f32[256,128]{1,0:T(8,128)S(1)} %shard_map.153.x_ref.refs_1_), channel_id=1, source_target_pairs={{0,1},{1,0},{2,3},{3,2},{4,5},{5,4},{6,7},{7,6},{8,9},{9,8},{10,11... | collective-permute-start | bytes 393224 | tf_op jit(solution)/shard_map/ppermute | solution.py:462
  35.8 8.5 %collective-permute-start.17 = (f32[256,128]{1,0:T(8,128)S(1)}, f32[256,128]{1,0:T(8,128)S(1)}, u32[]{:S(2)}, u32[]{:S(2)}) collective-permute-start(f32[256,128]{1,0:T(8,128)S(1)} %shard_map.154), channel_id=1, source_target_pairs={{0,2},{1,3},{2,0},{3,1},{4,6},{5,7},{6,4},{7,5},{8,10},{9,11},{10,... | collective-permute-start | bytes 393224 | tf_op jit(solution)/shard_map/ppermute | solution.py:462
  37.4 6.9 %collective-permute-start.18 = (f32[256,128]{1,0:T(8,128)S(1)}, f32[256,128]{1,0:T(8,128)S(1)}, u32[]{:S(2)}, u32[]{:S(2)}) collective-permute-start(f32[256,128]{1,0:T(8,128)S(1)} %shard_map.154), channel_id=1, source_target_pairs={{0,3},{1,2},{2,1},{3,0},{4,7},{5,6},{6,5},{7,4},{8,11},{9,10},{10,... | collective-permute-start | bytes 393224 | tf_op jit(solution)/shard_map/ppermute | solution.py:462
  38.4 4.7 %collective-permute-start.19 = (f32[2,16]{1,0:T(2,128)S(1)}, f32[2,16]{1,0:T(2,128)S(1)}, u32[]{:S(2)}, u32[]{:S(2)}) collective-permute-start(f32[2,16]{1,0:T(2,128)S(1)} %shard_map.149.refs_24_.refs_0_.x_ref), channel_id=1, source_target_pairs={{0,8},{4,12},{8,0},{12,4},{1,9},{5,13},{9,1},{13,5},{2,10},{6,14},... | collective-permute-start | bytes 392 | tf_op jit(solution)/shard_map/ppermute | solution.py:462
  43.1 1.2 %collective-permute-start.20 = (f32[2,16]{1,0:T(2,128)S(1)}, f32[2,16]{1,0:T(2,128)S(1)}, u32[]{:S(2)}, u32[]{:S(2)}) collective-permute-start(f32[2,16]{1,0:T(2,128)S(1)} %shard_map.155.refs_5_), channel_id=1, source_target_pairs={{0,16},{16,0},{1,17},{17,1},{2,18},{18,2},{3,19},{19,3},{4,20},{20... | collective-permute-start | bytes 392 | tf_op jit(solution)/shard_map/ppermute | solution.py:462

commit v8 on v7

--- a/solution.py
+++ b/solution.py
@@ -119,47 +119,52 @@
     ]
     for i in (6, 5, 3, 4, 0, 1, 2, 7):
         copies[i].start()
-    copies[6].wait()
-    copies[5].wait()
     length, channels = v_ref.shape
     heads = steps_ref.shape[0]
     width = channels // heads
-    rates = jnp.exp(to_column(lr_ref[...]))
-    cumulative = scan_tokens(-rates * steps_ref[...], False)
-    total = cumulative[:, -1:]
-    decay = jnp.exp(total)
-    cum_ref[...] = cumulative
-    neg_ref[...] = jnp.broadcast_to(-rates, (heads, length))
-    for first in range(0, channels, LANES):
-        here = pl.ds(first, LANES)
-        decay_ref[:, here] = channel_row(decay, heads, width, first)
-        slope_ref[:, here] = channel_row(total * decay, heads, width, first)
+
+    def wait(*which):
+        for i in which:
+            copies[i].wait()
+
+    def scan():
+        rates = jnp.exp(to_column(lr_ref[...]))
+        cumulative = scan_tokens(-rates * steps_ref[...], False)
+        return rates, cumulative, cumulative[:, -1:]
+
+    def keep(rates, cumulative, total):
+        decay = jnp.exp(total)
+        cum_ref[...] = cumulative
+        neg_ref[...] = jnp.broadcast_to(-rates, (heads, length))
+        for first in range(0, channels, LANES):
+            here = pl.ds(first, LANES)
+            decay_ref[:, here] = channel_row(decay, heads, width, first)
+            slope_ref[:, here] = channel_row(total * decay, heads, width, first)
 
     def local():
-        copies[3].wait()
+        wait(6, 5, 3, 0)
+        rates, cumulative, total = scan()
         b_t = b_ref[...].astype(F32).T.astype(BF16)
         fall = rows_of_three(jnp.exp(total - cumulative))
-        copies[0].wait()
         for first in range(0, channels, LANES):
             here = pl.ds(first, LANES)
             scaled = spread(fall, first, LANES, width) * v_ref[:, here].astype(F32)
             put_rows(mine_refs, here, mm(b_t, scaled.astype(BF16)))
-        for i in (1, 2, 4, 7):
-            copies[i].wait()
+        keep(rates, cumulative, total)
+        wait(1, 2, 4, 7)
 
     def pulled():
-        copies[4].wait()
+        wait(6, 5, 4, 1, 2)
+        rates, cumulative, total = scan()
         c_t = c_ref[...].astype(F32).T.astype(BF16)
         growth = rows_of_three(jnp.exp(cumulative))
-        copies[1].wait()
-        copies[2].wait()
         for first in range(0, channels, LANES):
             here = pl.ds(first, LANES)
             _, _, grad_y = gate_parts(gate_ref[:, here], go_ref[:, here])
             high, low = split(spread(growth, first, LANES, width) * grad_y, 2)
             put_rows(mine_refs, here, mm(c_t, high) + mm(c_t, low))
-        for i in (0, 3, 7):
-            copies[i].wait()
+        keep(rates, cumulative, total)
+        wait(0, 3, 7)
 
     if size == 1:
         local()

time: 45.3 us -> 45.6 us (level)
  transfers between devices with their start and end apart: 21 -> 21, of which waited for: 3 -> 2; matrix products, arithmetic and copies ran while one was open for 0% -> 0% of each run, Pallas kernels for 22% -> 22%
where the time goes in v8:
time: 45.6 us; the launch traced here: 45.4 us
  starting transfers between devices  30 us (66%)
  Pallas kernels  13.2 us (29%)
  waiting for transfers between devices  1.41 us (3%)
  between operations  0.8 us (2%)
    ppermute x12, starting transfers between devices, hop(): return lax.ppermute(x, ('replica', 'seq'), pairs)  18.2 us
    pallas_call x22, Pallas kernels, run(): pl.pallas_call(kernel, out_shape=tuple(outs), in_specs=specs, out_specs=t...  13.2 us
    ppermute x9, starting transfers between devices, swap(): return lax.ppermute(x, axis, [(i, i ^ bit) for i in range(size)])  11.8 us
    ppermute x9, waiting for transfers between devices, swap(): return lax.ppermute(x, axis, [(i, i ^ bit) for i in range(size)])  1.15 us
  transfers between devices with their start and end apart: 21, of which 2 were waited for; matrix products, arithmetic and copies ran while one was open for 0% of the time, Pallas kernels for 22%

profile of v8, /device:TPU:0, one launch (start us, length us, event | category | flops | bytes accessed | tf_op | source)
XLA Modules:
  0.0 45.4 jit_solution(14589809609425173911)
XLA Ops:
  0.6 2.4 %shard_map.135 = (bf16[256,1024]{1,0:T(8,128)(2,1)S(1)}, bf16[256,1024]{1,0:T(8,128)(2,1)S(1)}, bf16[256,1024]{1,0:T(8,128)(2,1)S(1)}, bf16[256,128]{1,0:T(8,128...) custom-call(bf16[256,1024]{1,0:T(8,128)(2,1)} %bitcast.10, ...), custom_call_target="tpu_custom_call" | custom-call | tf_op jit(solution)/shard_map/pallas_call | solution.py:451
  3.1 3.1 %collective-permute-start = (f32[32,1024]{1,0:T(8,128)S(1)}, f32[32,1024]{1,0:T(8,128)S(1)}, u32[]{:S(2)}, u32[]{:S(2)}) collective-permute-start(f32[32,1024]{1,0:T(8,128)S(1)} %get-tuple-element.50.refs_1_), channel_id=1, source_target_pairs={{0,4},{4,0},{8,12},{12,8},{16,20},{20,16},{24,28},{28,24},{1,5},{5... | collective-permute-start | bytes 393224 | tf_op jit(solution)/shard_map/ppermute | solution.py:480
  6.2 0.1 collective-permute-start.3
  6.2 1.9 %collective-permute-start.2 = (f32[32,1024]{1,0:T(8,128)S(1)}, f32[32,1024]{1,0:T(8,128)S(1)}, u32[]{:S(2)}, u32[]{:S(2)}) collective-permute-start(f32[32,1024]{1,0:T(8,128)S(1)} %get-tuple-element.60.refs_1_), channel_id=1, source_target_pairs={{0,4},{4,0},{8,12},{12,8},{16,20},{20,16},{24,28},{28,24},{1,5},{5... | collective-permute-start | bytes 393224 | tf_op jit(solution)/shard_map/ppermute | solution.py:480
  8.2 2.5 %shard_map.136 = (f32[256,1024]{1,0:T(8,128)S(1)}, f32[256,1024]{1,0:T(8,128)S(1)}, f32[256,128]{1,0:T(8,128)S(1)}, f32[256,128]{1,0:T(8,128)S(1)}) custom-call(bf16[256,1024]{1,0:T(8,128)(2,1)S(1)} %get-tuple-element.52.v_ref.refs_12_, bf16[256,1024]{1,0:T(8,128)(2,1)S(1)} %get-tuple-element.53.gate_ref, bf16[256,1024]{1,0:T(8,128)(2,1)S(1)} %get-tuple-element.54.go_ref, ...), custom_call_target="tpu_custom_call" | custom-call | tf_op jit(solution)/shard_map/pallas_call | solution.py:451
  10.7 0.0 collective-permute-done.refs_0_
  10.8 0.1 collective-permute-start.1
  10.8 3.5 %collective-permute-start.6 = (f32[32,1024]{1,0:T(8,128)S(1)}, f32[32,1024]{1,0:T(8,128)S(1)}, u32[]{:S(2)}, u32[]{:S(2)}) collective-permute-start(f32[32,1024]{1,0:T(8,128)S(1)} %get-tuple-element.63.refs_1_), channel_id=1, source_target_pairs={{0,4},{4,0},{8,12},{12,8},{16,20},{20,16},{24,28},{28,24},{1,5},{5... | collective-permute-start | bytes 393224 | tf_op jit(solution)/shard_map/ppermute | solution.py:480
  14.4 1.6 %shard_map.138 = (bf16[256,1024]{1,0:T(8,128)(2,1)S(1)}, bf16[256,1024]{1,0:T(8,128)(2,1)S(1)}, bf16[256,1024]{1,0:T(8,128)(2,1)S(1)}, f32[128,1024]{1,0:T(8,128...) custom-call(bf16[256,1024]{1,0:T(8,128)(2,1)S(1)} %get-tuple-element, ...), custom_call_target="tpu_custom_call" | custom-call | tf_op jit(solution)/shard_map/pallas_call | solution.py:451
  16.0 0.0 collective-permute-done.3.refs_0_.refs_3_
  16.0 0.1 collective-permute-start.5
  16.1 0.0 collective-permute-done.2.refs_0_.refs_6_
  16.1 0.5 %collective-permute-start.8 = (f32[32,1024]{1,0:T(8,128)S(1)}, f32[32,1024]{1,0:T(8,128)S(1)}, u32[]{:S(2)}, u32[]{:S(2)}) collective-permute-start(f32[32,1024]{1,0:T(8,128)S(1)} %shard_map.140.refs_3_), channel_id=1, source_target_pairs={{0,16},{4,8},{8,4},{12,28},{16,0},{20,24},{24,20},{28,12},{1,17},{... | collective-permute-start | bytes 393224 | tf_op jit(solution)/shard_map/ppermute | solution.py:480
  16.7 0.0 collective-permute-done.1.refs_0_.refs_1_
  16.7 3.4 %collective-permute-start.4 = (f32[32,1024]{1,0:T(8,128)S(1)}, f32[32,1024]{1,0:T(8,128)S(1)}, u32[]{:S(2)}, u32[]{:S(2)}) collective-permute-start(f32[32,1024]{1,0:T(8,128)S(1)} %shard_map.141.refs_3_), channel_id=1, source_target_pairs={{0,4},{4,0},{8,12},{12,8},{16,20},{20,16},{24,28},{28,24},{1,5},{5... | collective-permute-start | bytes 393224 | tf_op jit(solution)/shard_map/ppermute | solution.py:480
  20.1 0.0 collective-permute-done.6.refs_0_.refs_3_.refs_9_
  20.1 0.1 collective-permute-start.10
  20.2 0.0 collective-permute-done.5.refs_0_.refs_4_
  20.2 2.3 %collective-permute-start.7 = (f32[32,1024]{1,0:T(8,128)S(1)}, f32[32,1024]{1,0:T(8,128)S(1)}, u32[]{:S(2)}, u32[]{:S(2)}) collective-permute-start(f32[32,1024]{1,0:T(8,128)S(1)} %shard_map.143.after_ref), channel_id=1, source_target_pairs={{0,4},{4,0},{8,12},{12,8},{16,20},{20,16},{24,28},{28,24},{1,5},{5... | collective-permute-start | bytes 393224 | tf_op jit(solution)/shard_map/ppermute | solution.py:480
  22.5 1.4 %shard_map.144 = (f32[256,1024]{1,0:T(8,128)S(1)}, f32[256,1024]{1,0:T(8,128)S(1)}, f32[256,1024]{1,0:T(8,128)S(1)}, f32[256,1024]{1,0:T(8,128)S(1)}, f32[256,10...) custom-call(bf16[256,1024]{1,0:T(8,128)(2,1)S(1)} %get-tuple-element.52.v_ref.refs_12_, ...), custom_call_target="tpu_custom_call" | custom-call | tf_op jit(solution)/shard_map/pallas_call | solution.py:451
  24.0 0.0 collective-permute-done.8.refs_0_.refs_1_.refs_7_
  24.0 1.3 %collective-permute-start.9 = (f32[32,1024]{1,0:T(8,128)S(1)}, f32[32,1024]{1,0:T(8,128)S(1)}, u32[]{:S(2)}, u32[]{:S(2)}) collective-permute-start(f32[32,1024]{1,0:T(8,128)S(1)} %shard_map.145.refs_3_), channel_id=1, source_target_pairs={{0,4},{4,0},{8,12},{12,8},{16,20},{20,16},{24,28},{28,24},{1,5},{5... | collective-permute-start | bytes 393224 | tf_op jit(solution)/shard_map/ppermute | solution.py:480
  25.3 0.0 collective-permute-done.4.refs_4_.refs_2_
  25.3 0.0 collective-permute-done.10.refs_0_.refs_4_.refs_10_
  25.4 1.8 %collective-permute-start.11 = (f32[32,1024]{1,0:T(8,128)S(1)}, f32[32,1024]{1,0:T(8,128)S(1)}, u32[]{:S(2)}, u32[]{:S(2)}) collective-permute-start(f32[32,1024]{1,0:T(8,128)S(1)} %shard_map.146), channel_id=1, source_target_pairs={{0,4},{4,0},{8,12},{12,8},{16,20},{20,16},{24,28},{28,24},{1,5},{5... | collective-permute-start | bytes 393224 | tf_op jit(solution)/shard_map/ppermute | solution.py:480
  27.2 0.0 collective-permute-done.7.refs_5_
  27.2 0.1 shard_map.147.refs_9_.refs_11_
  27.3 0.7 %shard_map.150.refs_0_ = f32[256,128]{1,0:T(8,128)S(1)} custom-call(f32[32,1024]{1,0:T(8,128)S(1)} %collective-permute-done.refs_0_, f32[32,1024]{1,0:T(8,128)S(1)} %collective-permute-done.1.refs_0_.refs_1_, f32[32,1024]{1,0:T(8,128)S(1)} %collective-permute-done.4.refs_4_.refs_2_, f32[32,1024]{1,0:T(8,128)S(1)} %collective-permute-done.3.refs_0_.refs_3_, ...), custom_call_target="tpu_custom_call" | custom-call | tf_op jit(solution)/shard_map/pallas_call | solution.py:451
  28.0 1.6 %collective-permute-start.13 = (f32[256,128]{1,0:T(8,128)S(1)}, f32[256,128]{1,0:T(8,128)S(1)}, u32[]{:S(2)}, u32[]{:S(2)}) collective-permute-start(f32[256,128]{1,0:T(8,128)S(1)} %shard_map.150.refs_0_), channel_id=1, source_target_pairs={{0,1},{1,0},{2,3},{3,2},{4,5},{5,4},{6,7},{7,6},{8,9},{9,8},{10,11... | collective-permute-start | bytes 393224 | tf_op jit(solution)/shard_map/ppermute | solution.py:467
  29.6 1.5 %collective-permute-start.14 = (f32[256,128]{1,0:T(8,128)S(1)}, f32[256,128]{1,0:T(8,128)S(1)}, u32[]{:S(2)}, u32[]{:S(2)}) collective-permute-start(f32[256,128]{1,0:T(8,128)S(1)} %shard_map.150.refs_0_), channel_id=1, source_target_pairs={{0,2},{1,3},{2,0},{3,1},{4,6},{5,7},{6,4},{7,5},{8,10},{9,11},{10,... | collective-permute-start | bytes 393224 | tf_op jit(solution)/shard_map/ppermute | solution.py:467
  31.1 0.5 %collective-permute-start.15 = (f32[256,128]{1,0:T(8,128)S(1)}, f32[256,128]{1,0:T(8,128)S(1)}, u32[]{:S(2)}, u32[]{:S(2)}) collective-permute-start(f32[256,128]{1,0:T(8,128)S(1)} %shard_map.150.refs_0_), channel_id=1, source_target_pairs={{0,3},{1,2},{2,1},{3,0},{4,7},{5,6},{6,5},{7,4},{8,11},{9,10},{10,... | collective-permute-start | bytes 393224 | tf_op jit(solution)/shard_map/ppermute | solution.py:467
  31.6 0.0 collective-permute-done.9.refs_2_.refs_8_
  31.6 0.2 collective-permute-done.11.refs_5_.refs_11_
  31.8 0.2 shard_map.148.x_ref.refs_11_
  32.0 1.7 %collective-permute-start.12 = (f32[2,16]{1,0:T(2,128)S(1)}, f32[2,16]{1,0:T(2,128)S(1)}, u32[]{:S(2)}, u32[]{:S(2)}) collective-permute-start(f32[2,16]{1,0:T(2,128)S(1)} %shard_map.148.x_ref.refs_11_), channel_id=1, source_target_pairs={{0,4},{4,0},{8,12},{12,8},{1,5},{5,1},{9,13},{13,9},{2,6},{6,2},{1... | collective-permute-start | bytes 392 | tf_op jit(solution)/shard_map/ppermute | solution.py:467
  33.7 0.8 %shard_map.153.x_ref.refs_1_ = f32[256,128]{1,0:T(8,128)S(1)} custom-call(f32[32,1024]{1,0:T(8,128)S(1)} %collective-permute-done.2.refs_0_.refs_6_, f32[32,1024]{1,0:T(8,128)S(1)} %collective-permute-done.8.refs_0_.refs_1_.refs_7_, f32[32,1024]{1,0:T(8,128)S(1)} %collective-permute-done.9.refs_2_.refs_8_, ...), custom_call_target="tpu_custom_call" | custom-call | tf_op jit(solution)/shard_map/pallas_call | solution.py:451
  34.5 1.6 %collective-permute-start.16 = (f32[256,128]{1,0:T(8,128)S(1)}, f32[256,128]{1,0:T(8,128)S(1)}, u32[]{:S(2)}, u32[]{:S(2)}) collective-permute-start(f32[256,128]{1,0:T(8,128)S(1)} %shard_map.153.x_ref.refs_1_), channel_id=1, source_target_pairs={{0,1},{1,0},{2,3},{3,2},{4,5},{5,4},{6,7},{7,6},{8,9},{9,8},{10,11... | collective-permute-start | bytes 393224 | tf_op jit(solution)/shard_map/ppermute | solution.py:467
  36.1 0.0 collective-permute-done.12.y_ref
  36.1 1.6 %collective-permute-start.17 = (f32[256,128]{1,0:T(8,128)S(1)}, f32[256,128]{1,0:T(8,128)S(1)}, u32[]{:S(2)}, u32[]{:S(2)}) collective-permute-start(f32[256,128]{1,0:T(8,128)S(1)} %shard_map.154), channel_id=1, source_target_pairs={{0,2},{1,3},{2,0},{3,1},{4,6},{5,7},{6,4},{7,5},{8,10},{9,11},{10,... | collective-permute-start | bytes 393224 | tf_op jit(solution)/shard_map/ppermute | solution.py:467
  37.7 0.0 collective-permute-done.13.refs_1_
  37.7 1.0 %collective-permute-start.18 = (f32[256,128]{1,0:T(8,128)S(1)}, f32[256,128]{1,0:T(8,128)S(1)}, u32[]{:S(2)}, u32[]{:S(2)}) collective-permute-start(f32[256,128]{1,0:T(8,128)S(1)} %shard_map.154), channel_id=1, source_target_pairs={{0,3},{1,2},{2,1},{3,0},{4,7},{5,6},{6,5},{7,4},{8,11},{9,10},{10,... | collective-permute-start | bytes 393224 | tf_op jit(solution)/shard_map/ppermute | solution.py:467
  38.7 0.0 collective-permute-done.14.refs_2_
  38.7 0.0 collective-permute-done.15.refs_3_
  38.7 2.4 %collective-permute-start.19 = (f32[2,16]{1,0:T(2,128)S(1)}, f32[2,16]{1,0:T(2,128)S(1)}, u32[]{:S(2)}, u32[]{:S(2)}) collective-permute-start(f32[2,16]{1,0:T(2,128)S(1)} %shard_map.149.refs_24_.refs_0_.x_ref), channel_id=1, source_target_pairs={{0,8},{4,12},{8,0},{12,4},{1,9},{5,13},{9,1},{13,5},{2,10},{6,14},... | collective-permute-start | bytes 392 | tf_op jit(solution)/shard_map/ppermute | solution.py:467
  41.1 2.3 %shard_map.152 = (bf16[1,256,1024]{2,1,0:T(8,128)(2,1)}, bf16[1,256,1024]{2,1,0:T(8,128)(2,1)}, f32[1,16,256]{2,1,0:T(8,128)}, f32[1,16]{1,0:T(1,128)S(1)}) custom-call(f32[32,1024]{1,0:T(8,128)S(1)} %collective-permute-done.refs_0_, f32[32,1024]{1,0:T(8,128)S(1)} %collective-permute-done.1.refs_0_.refs_1_, ...), custom_call_target="tpu_custom_call" | custom-call | flops 300000000 | tf_op jit(solution)/shard_map/pallas_call | solution.py:451
  43.4 0.0 collective-permute-done.19.y_ref
  43.4 0.0 collective-permute-start.20
  43.4 1.1 %collective-permute-done.20.refs_6_ = f32[2,16]{1,0:T(2,128)S(1)} collective-permute-done((f32[2,16]{1,0:T(2,128)S(1)}, f32[2,16]{1,0:T(2,128)S(1)}, u32[]{:S(2)}, u32[]{:S(2)}) %collective-permute-start.20) | collective-permute-done | bytes 160 | tf_op jit(solution)/shard_map/ppermute | solution.py:467
  44.6 0.0 collective-permute-done.16.refs_2_
  44.6 0.0 collective-permute-done.17.refs_3_
  44.6 0.0 collective-permute-done.18.refs_4_
  44.6 0.8 %shard_map.156 = (f32[1,256,128]{2,1,0:T(8,128)}, f32[1,256,128]{2,1,0:T(8,128)}, f32[1,16]{1,0:T(1,128)}, f32[1,16]{1,0:T(1,128)}) custom-call(f32[256,128]{1,0:T(8,128)S(1)} %shard_map.151.refs_25_.refs_0_, f32[256,128]{1,0:T(8,128)S(1)} %shard_map.153.x_ref.refs_1_, f32[256,128]{1,0:T(8,128)S(1)} %collective-permute-done.16.refs_2_, ...), custom_call_target="tpu_custom_call" | custom-call | tf_op jit(solution)/shard_map/pallas_call | solution.py:451
  (13 shorter events, 0.2 us)
Async XLA Ops:
  3.1 7.7 %collective-permute-start = (f32[32,1024]{1,0:T(8,128)S(1)}, f32[32,1024]{1,0:T(8,128)S(1)}, u32[]{:S(2)}, u32[]{:S(2)}) collective-permute-start(f32[32,1024]{1,0:T(8,128)S(1)} %get-tuple-element.50.refs_1_), channel_id=1, source_target_pairs={{0,4},{4,0},{8,12},{12,8},{16,20},{20,16},{24,28},{28,24},{1,5},{5... | collective-permute-start | bytes 393224 | tf_op jit(solution)/shard_map/ppermute | solution.py:480
  6.2 9.8 %collective-permute-start.3 = (f32[32,1024]{1,0:T(8,128)S(1)}, f32[32,1024]{1,0:T(8,128)S(1)}, u32[]{:S(2)}, u32[]{:S(2)}) collective-permute-start(f32[32,1024]{1,0:T(8,128)S(1)} %get-tuple-element.61.refs_1_), channel_id=1, source_target_pairs={{0,4},{4,0},{8,12},{12,8},{16,20},{20,16},{24,28},{28,24},{1,5},{5... | collective-permute-start | bytes 393224 | tf_op jit(solution)/shard_map/ppermute | solution.py:480
  6.2 9.9 %collective-permute-start.2 = (f32[32,1024]{1,0:T(8,128)S(1)}, f32[32,1024]{1,0:T(8,128)S(1)}, u32[]{:S(2)}, u32[]{:S(2)}) collective-permute-start(f32[32,1024]{1,0:T(8,128)S(1)} %get-tuple-element.60.refs_1_), channel_id=1, source_target_pairs={{0,4},{4,0},{8,12},{12,8},{16,20},{20,16},{24,28},{28,24},{1,5},{5... | collective-permute-start | bytes 393224 | tf_op jit(solution)/shard_map/ppermute | solution.py:480
  10.8 5.9 %collective-permute-start.1 = (f32[32,1024]{1,0:T(8,128)S(1)}, f32[32,1024]{1,0:T(8,128)S(1)}, u32[]{:S(2)}, u32[]{:S(2)}) collective-permute-start(f32[32,1024]{1,0:T(8,128)S(1)} %shard_map.137.after_ref), channel_id=1, source_target_pairs={{0,16},{4,8},{8,4},{12,28},{16,0},{20,24},{24,20},{28,12},{1,17},{... | collective-permute-start | bytes 393224 | tf_op jit(solution)/shard_map/ppermute | solution.py:480
  10.8 9.2 %collective-permute-start.6 = (f32[32,1024]{1,0:T(8,128)S(1)}, f32[32,1024]{1,0:T(8,128)S(1)}, u32[]{:S(2)}, u32[]{:S(2)}) collective-permute-start(f32[32,1024]{1,0:T(8,128)S(1)} %get-tuple-element.63.refs_1_), channel_id=1, source_target_pairs={{0,4},{4,0},{8,12},{12,8},{16,20},{20,16},{24,28},{28,24},{1,5},{5... | collective-permute-start | bytes 393224 | tf_op jit(solution)/shard_map/ppermute | solution.py:480
  16.0 4.2 %collective-permute-start.5 = (f32[32,1024]{1,0:T(8,128)S(1)}, f32[32,1024]{1,0:T(8,128)S(1)}, u32[]{:S(2)}, u32[]{:S(2)}) collective-permute-start(f32[32,1024]{1,0:T(8,128)S(1)} %shard_map.139.refs_3_), channel_id=1, source_target_pairs={{0,16},{4,8},{8,4},{12,28},{16,0},{20,24},{24,20},{28,12},{1,17},{... | collective-permute-start | bytes 393224 | tf_op jit(solution)/shard_map/ppermute | solution.py:480
  16.1 7.8 %collective-permute-start.8 = (f32[32,1024]{1,0:T(8,128)S(1)}, f32[32,1024]{1,0:T(8,128)S(1)}, u32[]{:S(2)}, u32[]{:S(2)}) collective-permute-start(f32[32,1024]{1,0:T(8,128)S(1)} %shard_map.140.refs_3_), channel_id=1, source_target_pairs={{0,16},{4,8},{8,4},{12,28},{16,0},{20,24},{24,20},{28,12},{1,17},{... | collective-permute-start | bytes 393224 | tf_op jit(solution)/shard_map/ppermute | solution.py:480
  16.7 8.6 %collective-permute-start.4 = (f32[32,1024]{1,0:T(8,128)S(1)}, f32[32,1024]{1,0:T(8,128)S(1)}, u32[]{:S(2)}, u32[]{:S(2)}) collective-permute-start(f32[32,1024]{1,0:T(8,128)S(1)} %shard_map.141.refs_3_), channel_id=1, source_target_pairs={{0,4},{4,0},{8,12},{12,8},{16,20},{20,16},{24,28},{28,24},{1,5},{5... | collective-permute-start | bytes 393224 | tf_op jit(solution)/shard_map/ppermute | solution.py:480
  20.1 5.2 %collective-permute-start.10 = (f32[32,1024]{1,0:T(8,128)S(1)}, f32[32,1024]{1,0:T(8,128)S(1)}, u32[]{:S(2)}, u32[]{:S(2)}) collective-permute-start(f32[32,1024]{1,0:T(8,128)S(1)} %shard_map.142.refs_3_), channel_id=1, source_target_pairs={{0,16},{4,8},{8,4},{12,28},{16,0},{20,24},{24,20},{28,12},{1,17},{... | collective-permute-start | bytes 393224 | tf_op jit(solution)/shard_map/ppermute | solution.py:480
  20.2 7.0 %collective-permute-start.7 = (f32[32,1024]{1,0:T(8,128)S(1)}, f32[32,1024]{1,0:T(8,128)S(1)}, u32[]{:S(2)}, u32[]{:S(2)}) collective-permute-start(f32[32,1024]{1,0:T(8,128)S(1)} %shard_map.143.after_ref), channel_id=1, source_target_pairs={{0,4},{4,0},{8,12},{12,8},{16,20},{20,16},{24,28},{28,24},{1,5},{5... | collective-permute-start | bytes 393224 | tf_op jit(solution)/shard_map/ppermute | solution.py:480
  24.0 7.6 %collective-permute-start.9 = (f32[32,1024]{1,0:T(8,128)S(1)}, f32[32,1024]{1,0:T(8,128)S(1)}, u32[]{:S(2)}, u32[]{:S(2)}) collective-permute-start(f32[32,1024]{1,0:T(8,128)S(1)} %shard_map.145.refs_3_), channel_id=1, source_target_pairs={{0,4},{4,0},{8,12},{12,8},{16,20},{20,16},{24,28},{28,24},{1,5},{5... | collective-permute-start | bytes 393224 | tf_op jit(solution)/shard_map/ppermute | solution.py:480
  25.4 6.4 %collective-permute-start.11 = (f32[32,1024]{1,0:T(8,128)S(1)}, f32[32,1024]{1,0:T(8,128)S(1)}, u32[]{:S(2)}, u32[]{:S(2)}) collective-permute-start(f32[32,1024]{1,0:T(8,128)S(1)} %shard_map.146), channel_id=1, source_target_pairs={{0,4},{4,0},{8,12},{12,8},{16,20},{20,16},{24,28},{28,24},{1,5},{5... | collective-permute-start | bytes 393224 | tf_op jit(solution)/shard_map/ppermute | solution.py:480
  28.0 9.7 %collective-permute-start.13 = (f32[256,128]{1,0:T(8,128)S(1)}, f32[256,128]{1,0:T(8,128)S(1)}, u32[]{:S(2)}, u32[]{:S(2)}) collective-permute-start(f32[256,128]{1,0:T(8,128)S(1)} %shard_map.150.refs_0_), channel_id=1, source_target_pairs={{0,1},{1,0},{2,3},{3,2},{4,5},{5,4},{6,7},{7,6},{8,9},{9,8},{10,11... | collective-permute-start | bytes 393224 | tf_op jit(solution)/shard_map/ppermute | solution.py:467
  29.6 9.1 %collective-permute-start.14 = (f32[256,128]{1,0:T(8,128)S(1)}, f32[256,128]{1,0:T(8,128)S(1)}, u32[]{:S(2)}, u32[]{:S(2)}) collective-permute-start(f32[256,128]{1,0:T(8,128)S(1)} %shard_map.150.refs_0_), channel_id=1, source_target_pairs={{0,2},{1,3},{2,0},{3,1},{4,6},{5,7},{6,4},{7,5},{8,10},{9,11},{10,... | collective-permute-start | bytes 393224 | tf_op jit(solution)/shard_map/ppermute | solution.py:467
  31.1 7.6 %collective-permute-start.15 = (f32[256,128]{1,0:T(8,128)S(1)}, f32[256,128]{1,0:T(8,128)S(1)}, u32[]{:S(2)}, u32[]{:S(2)}) collective-permute-start(f32[256,128]{1,0:T(8,128)S(1)} %shard_map.150.refs_0_), channel_id=1, source_target_pairs={{0,3},{1,2},{2,1},{3,0},{4,7},{5,6},{6,5},{7,4},{8,11},{9,10},{10,... | collective-permute-start | bytes 393224 | tf_op jit(solution)/shard_map/ppermute | solution.py:467
  32.0 4.1 %collective-permute-start.12 = (f32[2,16]{1,0:T(2,128)S(1)}, f32[2,16]{1,0:T(2,128)S(1)}, u32[]{:S(2)}, u32[]{:S(2)}) collective-permute-start(f32[2,16]{1,0:T(2,128)S(1)} %shard_map.148.x_ref.refs_11_), channel_id=1, source_target_pairs={{0,4},{4,0},{8,12},{12,8},{1,5},{5,1},{9,13},{13,9},{2,6},{6,2},{1... | collective-permute-start | bytes 392 | tf_op jit(solution)/shard_map/ppermute | solution.py:467
  34.5 10.0 %collective-permute-start.16 = (f32[256,128]{1,0:T(8,128)S(1)}, f32[256,128]{1,0:T(8,128)S(1)}, u32[]{:S(2)}, u32[]{:S(2)}) collective-permute-start(f32[256,128]{1,0:T(8,128)S(1)} %shard_map.153.x_ref.refs_1_), channel_id=1, source_target_pairs={{0,1},{1,0},{2,3},{3,2},{4,5},{5,4},{6,7},{7,6},{8,9},{9,8},{10,11... | collective-permute-start | bytes 393224 | tf_op jit(solution)/shard_map/ppermute | solution.py:467
  36.1 8.5 %collective-permute-start.17 = (f32[256,128]{1,0:T(8,128)S(1)}, f32[256,128]{1,0:T(8,128)S(1)}, u32[]{:S(2)}, u32[]{:S(2)}) collective-permute-start(f32[256,128]{1,0:T(8,128)S(1)} %shard_map.154), channel_id=1, source_target_pairs={{0,2},{1,3},{2,0},{3,1},{4,6},{5,7},{6,4},{7,5},{8,10},{9,11},{10,... | collective-permute-start | bytes 393224 | tf_op jit(solution)/shard_map/ppermute | solution.py:467
  37.7 6.9 %collective-permute-start.18 = (f32[256,128]{1,0:T(8,128)S(1)}, f32[256,128]{1,0:T(8,128)S(1)}, u32[]{:S(2)}, u32[]{:S(2)}) collective-permute-start(f32[256,128]{1,0:T(8,128)S(1)} %shard_map.154), channel_id=1, source_target_pairs={{0,3},{1,2},{2,1},{3,0},{4,7},{5,6},{6,5},{7,4},{8,11},{9,10},{10,... | collective-permute-start | bytes 393224 | tf_op jit(solution)/shard_map/ppermute | solution.py:467
  38.7 4.7 %collective-permute-start.19 = (f32[2,16]{1,0:T(2,128)S(1)}, f32[2,16]{1,0:T(2,128)S(1)}, u32[]{:S(2)}, u32[]{:S(2)}) collective-permute-start(f32[2,16]{1,0:T(2,128)S(1)} %shard_map.149.refs_24_.refs_0_.x_ref), channel_id=1, source_target_pairs={{0,8},{4,12},{8,0},{12,4},{1,9},{5,13},{9,1},{13,5},{2,10},{6,14},... | collective-permute-start | bytes 392 | tf_op jit(solution)/shard_map/ppermute | solution.py:467
  43.4 1.2 %collective-permute-start.20 = (f32[2,16]{1,0:T(2,128)S(1)}, f32[2,16]{1,0:T(2,128)S(1)}, u32[]{:S(2)}, u32[]{:S(2)}) collective-permute-start(f32[2,16]{1,0:T(2,128)S(1)} %shard_map.155.refs_5_), channel_id=1, source_target_pairs={{0,16},{16,0},{1,17},{17,1},{2,18},{18,2},{3,19},{19,3},{4,20},{20... | collective-permute-start | bytes 392 | tf_op jit(solution)/shard_map/ppermute | solution.py:467

commit v9 on v6

--- a/solution.py
+++ b/solution.py
@@ -117,8 +117,18 @@
         pltpu.make_async_copy(source, target, sems.at[i])
         for i, (source, target) in enumerate(zip(sources, targets))
     ]
-    for i in (6, 5, 3, 4, 0, 1, 2, 7):
-        copies[i].start()
+
+    def start(*which):
+        for i in which:
+            copies[i].start()
+
+    start(6, 5)
+    if size == 1:
+        start(3, 0, 4, 1, 2, 7)
+    else:
+        lower = lax.axis_index("seq") < size // 2
+        pl.when(lower)(lambda: start(3, 0, 4, 1, 2, 7))
+        pl.when(jnp.logical_not(lower))(lambda: start(4, 1, 2, 3, 0, 7))
     copies[6].wait()
     copies[5].wait()
     length, channels = v_ref.shape
@@ -164,7 +174,6 @@
     if size == 1:
         local()
     else:
-        lower = lax.axis_index("seq") < size // 2
         pl.when(lower)(local)
         pl.when(jnp.logical_not(lower))(pulled)
 
@@ -541,10 +550,12 @@
     return [x, swap(x, axis, size, bit)]
 
 
-def small_terms(x, axes, sizes, hooks):
-    bits = [(axis, 1 << k) for axis in axes for k in range(sizes[axis].bit_length() - 1)]
+def small_terms(x, sizes, hooks):
+    axes = ("seq", "replica")
+    along, across = ([(axis, 1 << k) for k in range(sizes[axis].bit_length() - 1)] for axis in axes)
+    bits = along[:1] + across + along[1:]
     if any(sizes[axis] & (sizes[axis] - 1) for axis in axes):
-        x, bits = lax.psum(x, tuple(axes)), []
+        x, bits = lax.psum(x, axes), []
     for count, (axis, bit) in enumerate(bits):
         theirs = swap(x, axis, sizes[axis], bit)
         if count == len(bits) - 1:
@@ -602,7 +613,7 @@
             ],
             name="intra",
         )(vals, gate, grad, block_b, block_c, cumulative)
-        return factors((made["intra"][2],))
+        return (made["intra"][2],)
 
     def factors(after):
         made["factors"] = call(
@@ -624,7 +635,7 @@
         return (made["prepare"][-1],)
 
     sums = max(seq - 2, 0) * CHUNKS
-    states = chain(sizes, mine, made, decay, {0: intra, max(sums - 2, 2): prepare})
+    states = chain(sizes, mine, made, decay, {0: intra, 1: factors, max(sums - 2, 2): prepare})
     sum_b, sum_c = made["intra"][2:]
     high, low, scaled, q, r = made["factors"][:5]
     coef, mamba, inner, growth, fall, grad_y, grad_cum, parts = made["prepare"]
@@ -666,7 +677,7 @@
             vals, block_b, block_c, coef, mamba, inner, growth, fall, grad_y, grad_cum, decay, negative,
         )
 
-    own = small_terms(rate_row, ("replica", "seq"), sizes, (exchange, rest))
+    own = small_terms(rate_row, sizes, (exchange, rest))
     for group in (made["share"], own):
         terms += group
         counts.append(len(group))

time: 46.3 us -> 45 us (0.972)
  waiting for transfers between devices: 3.35 us -> 1.7 us
    ppermute x9, waiting for transfers between devices: 3.04 us -> 1.12 us  [swap(): return lax.ppermute(x, axis, [(i, i ^ bit) for i in range(size)])]
    ppermute x9, starting transfers between devices: 10.9 us -> 11.7 us  [swap(): return lax.ppermute(x, axis, [(i, i ^ bit) for i in range(size)])]
where the time goes in v9:
time: 45 us; the launch traced here: 44.8 us
  starting transfers between devices  29.3 us (65%)
  Pallas kernels  13 us (29%)
  waiting for transfers between devices  1.7 us (4%)
  between operations  0.8 us (2%)
    ppermute x12, starting transfers between devices, hop(): return lax.ppermute(x, ('replica', 'seq'), pairs)  17.6 us
    pallas_call x22, Pallas kernels, run(): pl.pallas_call(kernel, out_shape=tuple(outs), in_specs=specs, out_specs=t...  13 us
    ppermute x9, starting transfers between devices, swap(): return lax.ppermute(x, axis, [(i, i ^ bit) for i in range(size)])  11.7 us
    ppermute x9, waiting for transfers between devices, swap(): return lax.ppermute(x, axis, [(i, i ^ bit) for i in range(size)])  1.12 us
  transfers between devices with their start and end apart: 21, of which 3 were waited for; matrix products, arithmetic and copies ran while one was open for 0% of the time, Pallas kernels for 22%

profile of v9, /device:TPU:0, one launch (start us, length us, event | category | flops | bytes accessed | tf_op | source)
XLA Modules:
  0.0 44.8 jit_solution(6347804719562908428)
XLA Ops:
  0.6 2.3 %shard_map.135 = (bf16[256,1024]{1,0:T(8,128)(2,1)S(1)}, bf16[256,1024]{1,0:T(8,128)(2,1)S(1)}, bf16[256,1024]{1,0:T(8,128)(2,1)S(1)}, bf16[256,128]{1,0:T(8,128...) custom-call(bf16[256,1024]{1,0:T(8,128)(2,1)} %bitcast.10, ...), custom_call_target="tpu_custom_call" | custom-call | tf_op jit(solution)/shard_map/pallas_call | solution.py:454
  2.9 3.1 %collective-permute-start = (f32[32,1024]{1,0:T(8,128)S(1)}, f32[32,1024]{1,0:T(8,128)S(1)}, u32[]{:S(2)}, u32[]{:S(2)}) collective-permute-start(f32[32,1024]{1,0:T(8,128)S(1)} %get-tuple-element.49.refs_1_), channel_id=1, source_target_pairs={{0,4},{4,0},{8,12},{12,8},{16,20},{20,16},{24,28},{28,24},{1,5},{5... | collective-permute-start | bytes 393224 | tf_op jit(solution)/shard_map/ppermute | solution.py:483
  6.0 0.1 collective-permute-start.3
  6.1 1.9 %collective-permute-start.2 = (f32[32,1024]{1,0:T(8,128)S(1)}, f32[32,1024]{1,0:T(8,128)S(1)}, u32[]{:S(2)}, u32[]{:S(2)}) collective-permute-start(f32[32,1024]{1,0:T(8,128)S(1)} %get-tuple-element.59.refs_1_), channel_id=1, source_target_pairs={{0,4},{4,0},{8,12},{12,8},{16,20},{20,16},{24,28},{28,24},{1,5},{5... | collective-permute-start | bytes 393224 | tf_op jit(solution)/shard_map/ppermute | solution.py:483
  8.0 2.5 %shard_map.136 = (f32[256,1024]{1,0:T(8,128)S(1)}, f32[256,1024]{1,0:T(8,128)S(1)}, f32[256,128]{1,0:T(8,128)S(1)}, f32[256,128]{1,0:T(8,128)S(1)}) custom-call(bf16[256,1024]{1,0:T(8,128)(2,1)S(1)} %get-tuple-element.51.v_ref.refs_12_, bf16[256,1024]{1,0:T(8,128)(2,1)S(1)} %get-tuple-element.52.gate_ref, bf16[256,1024]{1,0:T(8,128)(2,1)S(1)} %get-tuple-element.53.go_ref, ...), custom_call_target="tpu_custom_call" | custom-call | tf_op jit(solution)/shard_map/pallas_call | solution.py:454
  10.6 0.0 collective-permute-done.refs_0_
  10.6 0.1 collective-permute-start.1
  10.7 3.2 %collective-permute-start.6 = (f32[32,1024]{1,0:T(8,128)S(1)}, f32[32,1024]{1,0:T(8,128)S(1)}, u32[]{:S(2)}, u32[]{:S(2)}) collective-permute-start(f32[32,1024]{1,0:T(8,128)S(1)} %get-tuple-element.62.refs_1_), channel_id=1, source_target_pairs={{0,4},{4,0},{8,12},{12,8},{16,20},{20,16},{24,28},{28,24},{1,5},{5... | collective-permute-start | bytes 393224 | tf_op jit(solution)/shard_map/ppermute | solution.py:483
  13.9 1.6 %shard_map.138 = (bf16[256,1024]{1,0:T(8,128)(2,1)S(1)}, bf16[256,1024]{1,0:T(8,128)(2,1)S(1)}, bf16[256,1024]{1,0:T(8,128)(2,1)S(1)}, f32[128,1024]{1,0:T(8,128...) custom-call(bf16[256,1024]{1,0:T(8,128)(2,1)S(1)} %get-tuple-element, ...), custom_call_target="tpu_custom_call" | custom-call | tf_op jit(solution)/shard_map/pallas_call | solution.py:454
  15.5 0.0 collective-permute-done.3.refs_0_.refs_3_
  15.6 0.1 collective-permute-start.5
  15.6 0.3 collective-permute-done.2.refs_0_.refs_6_
  16.0 0.2 collective-permute-start.8
  16.2 0.0 collective-permute-done.1.refs_0_.refs_1_
  16.2 3.4 %collective-permute-start.4 = (f32[32,1024]{1,0:T(8,128)S(1)}, f32[32,1024]{1,0:T(8,128)S(1)}, u32[]{:S(2)}, u32[]{:S(2)}) collective-permute-start(f32[32,1024]{1,0:T(8,128)S(1)} %shard_map.141.refs_3_), channel_id=1, source_target_pairs={{0,4},{4,0},{8,12},{12,8},{16,20},{20,16},{24,28},{28,24},{1,5},{5... | collective-permute-start | bytes 393224 | tf_op jit(solution)/shard_map/ppermute | solution.py:483
  19.6 0.0 collective-permute-done.6.refs_0_.refs_3_.refs_9_
  19.6 0.1 collective-permute-start.10
  19.7 0.0 collective-permute-done.5.refs_0_.refs_4_
  19.8 2.3 %collective-permute-start.7 = (f32[32,1024]{1,0:T(8,128)S(1)}, f32[32,1024]{1,0:T(8,128)S(1)}, u32[]{:S(2)}, u32[]{:S(2)}) collective-permute-start(f32[32,1024]{1,0:T(8,128)S(1)} %shard_map.143.after_ref), channel_id=1, source_target_pairs={{0,4},{4,0},{8,12},{12,8},{16,20},{20,16},{24,28},{28,24},{1,5},{5... | collective-permute-start | bytes 393224 | tf_op jit(solution)/shard_map/ppermute | solution.py:483
  22.1 1.4 %shard_map.144 = (f32[256,1024]{1,0:T(8,128)S(1)}, f32[256,1024]{1,0:T(8,128)S(1)}, f32[256,1024]{1,0:T(8,128)S(1)}, f32[256,1024]{1,0:T(8,128)S(1)}, f32[256,10...) custom-call(bf16[256,1024]{1,0:T(8,128)(2,1)S(1)} %get-tuple-element.51.v_ref.refs_12_, ...), custom_call_target="tpu_custom_call" | custom-call | tf_op jit(solution)/shard_map/pallas_call | solution.py:454
  23.5 0.0 collective-permute-done.8.refs_0_.refs_1_.refs_7_
  23.5 1.3 %collective-permute-start.9 = (f32[32,1024]{1,0:T(8,128)S(1)}, f32[32,1024]{1,0:T(8,128)S(1)}, u32[]{:S(2)}, u32[]{:S(2)}) collective-permute-start(f32[32,1024]{1,0:T(8,128)S(1)} %shard_map.145.refs_3_), channel_id=1, source_target_pairs={{0,4},{4,0},{8,12},{12,8},{16,20},{20,16},{24,28},{28,24},{1,5},{5... | collective-permute-start | bytes 393224 | tf_op jit(solution)/shard_map/ppermute | solution.py:483
  24.9 0.0 collective-permute-done.4.refs_4_.refs_2_
  24.9 0.0 collective-permute-done.10.refs_0_.refs_4_.refs_10_
  24.9 1.8 %collective-permute-start.11 = (f32[32,1024]{1,0:T(8,128)S(1)}, f32[32,1024]{1,0:T(8,128)S(1)}, u32[]{:S(2)}, u32[]{:S(2)}) collective-permute-start(f32[32,1024]{1,0:T(8,128)S(1)} %shard_map.146), channel_id=1, source_target_pairs={{0,4},{4,0},{8,12},{12,8},{16,20},{20,16},{24,28},{28,24},{1,5},{5... | collective-permute-start | bytes 393224 | tf_op jit(solution)/shard_map/ppermute | solution.py:483
  26.7 0.0 collective-permute-done.7.refs_5_
  26.7 0.1 shard_map.147.refs_9_.refs_11_
  26.9 0.7 %shard_map.151.refs_0_ = f32[256,128]{1,0:T(8,128)S(1)} custom-call(f32[32,1024]{1,0:T(8,128)S(1)} %collective-permute-done.refs_0_, f32[32,1024]{1,0:T(8,128)S(1)} %collective-permute-done.1.refs_0_.refs_1_, f32[32,1024]{1,0:T(8,128)S(1)} %collective-permute-done.4.refs_4_.refs_2_, f32[32,1024]{1,0:T(8,128)S(1)} %collective-permute-done.3.refs_0_.refs_3_, ...), custom_call_target="tpu_custom_call" | custom-call | tf_op jit(solution)/shard_map/pallas_call | solution.py:454
  27.5 1.6 %collective-permute-start.14 = (f32[256,128]{1,0:T(8,128)S(1)}, f32[256,128]{1,0:T(8,128)S(1)}, u32[]{:S(2)}, u32[]{:S(2)}) collective-permute-start(f32[256,128]{1,0:T(8,128)S(1)} %shard_map.151.refs_0_), channel_id=1, source_target_pairs={{0,1},{1,0},{2,3},{3,2},{4,5},{5,4},{6,7},{7,6},{8,9},{9,8},{10,11... | collective-permute-start | bytes 393224 | tf_op jit(solution)/shard_map/ppermute | solution.py:470
  29.1 1.5 %collective-permute-start.15 = (f32[256,128]{1,0:T(8,128)S(1)}, f32[256,128]{1,0:T(8,128)S(1)}, u32[]{:S(2)}, u32[]{:S(2)}) collective-permute-start(f32[256,128]{1,0:T(8,128)S(1)} %shard_map.151.refs_0_), channel_id=1, source_target_pairs={{0,2},{1,3},{2,0},{3,1},{4,6},{5,7},{6,4},{7,5},{8,10},{9,11},{10,... | collective-permute-start | bytes 393224 | tf_op jit(solution)/shard_map/ppermute | solution.py:470
  30.6 0.5 %collective-permute-start.16 = (f32[256,128]{1,0:T(8,128)S(1)}, f32[256,128]{1,0:T(8,128)S(1)}, u32[]{:S(2)}, u32[]{:S(2)}) collective-permute-start(f32[256,128]{1,0:T(8,128)S(1)} %shard_map.151.refs_0_), channel_id=1, source_target_pairs={{0,3},{1,2},{2,1},{3,0},{4,7},{5,6},{6,5},{7,4},{8,11},{9,10},{10,... | collective-permute-start | bytes 393224 | tf_op jit(solution)/shard_map/ppermute | solution.py:470
  31.1 0.0 collective-permute-done.9.refs_2_.refs_8_
  31.1 0.2 collective-permute-done.11.refs_5_.refs_11_
  31.3 0.2 shard_map.148.x_ref.refs_11_
  31.6 1.7 %collective-permute-start.12 = (f32[2,16]{1,0:T(2,128)S(1)}, f32[2,16]{1,0:T(2,128)S(1)}, u32[]{:S(2)}, u32[]{:S(2)}) collective-permute-start(f32[2,16]{1,0:T(2,128)S(1)} %shard_map.148.x_ref.refs_11_), channel_id=1, source_target_pairs={{0,4},{4,0},{8,12},{12,8},{1,5},{5,1},{9,13},{13,9},{2,6},{6,2},{1... | collective-permute-start | bytes 392 | tf_op jit(solution)/shard_map/ppermute | solution.py:470
  33.3 0.8 %shard_map.154.x_ref.refs_1_ = f32[256,128]{1,0:T(8,128)S(1)} custom-call(f32[32,1024]{1,0:T(8,128)S(1)} %collective-permute-done.2.refs_0_.refs_6_, f32[32,1024]{1,0:T(8,128)S(1)} %collective-permute-done.8.refs_0_.refs_1_.refs_7_, f32[32,1024]{1,0:T(8,128)S(1)} %collective-permute-done.9.refs_2_.refs_8_, ...), custom_call_target="tpu_custom_call" | custom-call | tf_op jit(solution)/shard_map/pallas_call | solution.py:454
  34.1 1.5 %collective-permute-start.17 = (f32[256,128]{1,0:T(8,128)S(1)}, f32[256,128]{1,0:T(8,128)S(1)}, u32[]{:S(2)}, u32[]{:S(2)}) collective-permute-start(f32[256,128]{1,0:T(8,128)S(1)} %shard_map.154.x_ref.refs_1_), channel_id=1, source_target_pairs={{0,1},{1,0},{2,3},{3,2},{4,5},{5,4},{6,7},{7,6},{8,9},{9,8},{10,11... | collective-permute-start | bytes 393224 | tf_op jit(solution)/shard_map/ppermute | solution.py:470
  35.6 0.0 collective-permute-done.12.y_ref
  35.6 1.6 %collective-permute-start.18 = (f32[256,128]{1,0:T(8,128)S(1)}, f32[256,128]{1,0:T(8,128)S(1)}, u32[]{:S(2)}, u32[]{:S(2)}) collective-permute-start(f32[256,128]{1,0:T(8,128)S(1)} %shard_map.155), channel_id=1, source_target_pairs={{0,2},{1,3},{2,0},{3,1},{4,6},{5,7},{6,4},{7,5},{8,10},{9,11},{10,... | collective-permute-start | bytes 393224 | tf_op jit(solution)/shard_map/ppermute | solution.py:470
  37.2 0.0 collective-permute-done.14.refs_1_
  37.2 1.0 %collective-permute-start.19 = (f32[256,128]{1,0:T(8,128)S(1)}, f32[256,128]{1,0:T(8,128)S(1)}, u32[]{:S(2)}, u32[]{:S(2)}) collective-permute-start(f32[256,128]{1,0:T(8,128)S(1)} %shard_map.155), channel_id=1, source_target_pairs={{0,3},{1,2},{2,1},{3,0},{4,7},{5,6},{6,5},{7,4},{8,11},{9,10},{10,... | collective-permute-start | bytes 393224 | tf_op jit(solution)/shard_map/ppermute | solution.py:470
  38.2 0.0 collective-permute-done.15.refs_2_
  38.2 0.0 collective-permute-start.13
  38.2 0.0 collective-permute-done.16.refs_3_
  38.2 1.1 %collective-permute-done.13.y_ref = f32[2,16]{1,0:T(2,128)S(1)} collective-permute-done((f32[2,16]{1,0:T(2,128)S(1)}, f32[2,16]{1,0:T(2,128)S(1)}, u32[]{:S(2)}, u32[]{:S(2)}) %collective-permute-start.13) | collective-permute-done | bytes 160 | tf_op jit(solution)/shard_map/ppermute | solution.py:470
  39.3 2.3 %collective-permute-start.20 = (f32[2,16]{1,0:T(2,128)S(1)}, f32[2,16]{1,0:T(2,128)S(1)}, u32[]{:S(2)}, u32[]{:S(2)}) collective-permute-start(f32[2,16]{1,0:T(2,128)S(1)} %shard_map.150.refs_24_.refs_5_), channel_id=1, source_target_pairs={{0,8},{4,12},{8,0},{12,4},{1,9},{5,13},{9,1},{13,5},{2,10},{6,14},... | collective-permute-start | bytes 392 | tf_op jit(solution)/shard_map/ppermute | solution.py:470
  41.7 2.3 %shard_map.153 = (bf16[1,256,1024]{2,1,0:T(8,128)(2,1)}, bf16[1,256,1024]{2,1,0:T(8,128)(2,1)}, f32[1,16,256]{2,1,0:T(8,128)}) custom-call(f32[32,1024]{1,0:T(8,128)S(1)} %collective-permute-done.refs_0_, f32[32,1024]{1,0:T(8,128)S(1)} %collective-permute-done.1.refs_0_.refs_1_, f32[32,1024]{1,0:T(8,128)S(1)} %collective-permute-done.4.refs_4_.refs_2_, ...), custom_call_target="tpu_custom_call" | custom-call | flops 300000000 | tf_op jit(solution)/shard_map/pallas_call | solution.py:454
  44.0 0.0 collective-permute-done.20.refs_6_
  44.0 0.0 collective-permute-done.17.refs_2_
  44.0 0.0 collective-permute-done.18.refs_3_
  44.0 0.0 collective-permute-done.19.refs_4_
  44.0 0.8 %shard_map.156 = (f32[1,256,128]{2,1,0:T(8,128)}, f32[1,256,128]{2,1,0:T(8,128)}, f32[1,16]{1,0:T(1,128)}, f32[1,16]{1,0:T(1,128)}) custom-call(f32[256,128]{1,0:T(8,128)S(1)} %shard_map.152.refs_25_.refs_0_, f32[256,128]{1,0:T(8,128)S(1)} %shard_map.154.x_ref.refs_1_, f32[256,128]{1,0:T(8,128)S(1)} %collective-permute-done.17.refs_2_, ...), custom_call_target="tpu_custom_call" | custom-call | tf_op jit(solution)/shard_map/pallas_call | solution.py:454
  (13 shorter events, 0.2 us)
Async XLA Ops:
  2.9 7.7 %collective-permute-start = (f32[32,1024]{1,0:T(8,128)S(1)}, f32[32,1024]{1,0:T(8,128)S(1)}, u32[]{:S(2)}, u32[]{:S(2)}) collective-permute-start(f32[32,1024]{1,0:T(8,128)S(1)} %get-tuple-element.49.refs_1_), channel_id=1, source_target_pairs={{0,4},{4,0},{8,12},{12,8},{16,20},{20,16},{24,28},{28,24},{1,5},{5... | collective-permute-start | bytes 393224 | tf_op jit(solution)/shard_map/ppermute | solution.py:483
  6.0 9.5 %collective-permute-start.3 = (f32[32,1024]{1,0:T(8,128)S(1)}, f32[32,1024]{1,0:T(8,128)S(1)}, u32[]{:S(2)}, u32[]{:S(2)}) collective-permute-start(f32[32,1024]{1,0:T(8,128)S(1)} %get-tuple-element.60.refs_1_), channel_id=1, source_target_pairs={{0,4},{4,0},{8,12},{12,8},{16,20},{20,16},{24,28},{28,24},{1,5},{5... | collective-permute-start | bytes 393224 | tf_op jit(solution)/shard_map/ppermute | solution.py:483
  6.1 9.9 %collective-permute-start.2 = (f32[32,1024]{1,0:T(8,128)S(1)}, f32[32,1024]{1,0:T(8,128)S(1)}, u32[]{:S(2)}, u32[]{:S(2)}) collective-permute-start(f32[32,1024]{1,0:T(8,128)S(1)} %get-tuple-element.59.refs_1_), channel_id=1, source_target_pairs={{0,4},{4,0},{8,12},{12,8},{16,20},{20,16},{24,28},{28,24},{1,5},{5... | collective-permute-start | bytes 393224 | tf_op jit(solution)/shard_map/ppermute | solution.py:483
  10.6 5.6 %collective-permute-start.1 = (f32[32,1024]{1,0:T(8,128)S(1)}, f32[32,1024]{1,0:T(8,128)S(1)}, u32[]{:S(2)}, u32[]{:S(2)}) collective-permute-start(f32[32,1024]{1,0:T(8,128)S(1)} %shard_map.137.after_ref), channel_id=1, source_target_pairs={{0,16},{4,8},{8,4},{12,28},{16,0},{20,24},{24,20},{28,12},{1,17},{... | collective-permute-start | bytes 393224 | tf_op jit(solution)/shard_map/ppermute | solution.py:483
  10.7 8.9 %collective-permute-start.6 = (f32[32,1024]{1,0:T(8,128)S(1)}, f32[32,1024]{1,0:T(8,128)S(1)}, u32[]{:S(2)}, u32[]{:S(2)}) collective-permute-start(f32[32,1024]{1,0:T(8,128)S(1)} %get-tuple-element.62.refs_1_), channel_id=1, source_target_pairs={{0,4},{4,0},{8,12},{12,8},{16,20},{20,16},{24,28},{28,24},{1,5},{5... | collective-permute-start | bytes 393224 | tf_op jit(solution)/shard_map/ppermute | solution.py:483
  15.6 4.2 %collective-permute-start.5 = (f32[32,1024]{1,0:T(8,128)S(1)}, f32[32,1024]{1,0:T(8,128)S(1)}, u32[]{:S(2)}, u32[]{:S(2)}) collective-permute-start(f32[32,1024]{1,0:T(8,128)S(1)} %shard_map.139.refs_3_), channel_id=1, source_target_pairs={{0,16},{4,8},{8,4},{12,28},{16,0},{20,24},{24,20},{28,12},{1,17},{... | collective-permute-start | bytes 393224 | tf_op jit(solution)/shard_map/ppermute | solution.py:483
  16.0 7.5 %collective-permute-start.8 = (f32[32,1024]{1,0:T(8,128)S(1)}, f32[32,1024]{1,0:T(8,128)S(1)}, u32[]{:S(2)}, u32[]{:S(2)}) collective-permute-start(f32[32,1024]{1,0:T(8,128)S(1)} %shard_map.140.refs_3_), channel_id=1, source_target_pairs={{0,16},{4,8},{8,4},{12,28},{16,0},{20,24},{24,20},{28,12},{1,17},{... | collective-permute-start | bytes 393224 | tf_op jit(solution)/shard_map/ppermute | solution.py:483
  16.2 8.6 %collective-permute-start.4 = (f32[32,1024]{1,0:T(8,128)S(1)}, f32[32,1024]{1,0:T(8,128)S(1)}, u32[]{:S(2)}, u32[]{:S(2)}) collective-permute-start(f32[32,1024]{1,0:T(8,128)S(1)} %shard_map.141.refs_3_), channel_id=1, source_target_pairs={{0,4},{4,0},{8,12},{12,8},{16,20},{20,16},{24,28},{28,24},{1,5},{5... | collective-permute-start | bytes 393224 | tf_op jit(solution)/shard_map/ppermute | solution.py:483
  19.6 5.2 %collective-permute-start.10 = (f32[32,1024]{1,0:T(8,128)S(1)}, f32[32,1024]{1,0:T(8,128)S(1)}, u32[]{:S(2)}, u32[]{:S(2)}) collective-permute-start(f32[32,1024]{1,0:T(8,128)S(1)} %shard_map.142.refs_3_), channel_id=1, source_target_pairs={{0,16},{4,8},{8,4},{12,28},{16,0},{20,24},{24,20},{28,12},{1,17},{... | collective-permute-start | bytes 393224 | tf_op jit(solution)/shard_map/ppermute | solution.py:483
  19.8 7.0 %collective-permute-start.7 = (f32[32,1024]{1,0:T(8,128)S(1)}, f32[32,1024]{1,0:T(8,128)S(1)}, u32[]{:S(2)}, u32[]{:S(2)}) collective-permute-start(f32[32,1024]{1,0:T(8,128)S(1)} %shard_map.143.after_ref), channel_id=1, source_target_pairs={{0,4},{4,0},{8,12},{12,8},{16,20},{20,16},{24,28},{28,24},{1,5},{5... | collective-permute-start | bytes 393224 | tf_op jit(solution)/shard_map/ppermute | solution.py:483
  23.5 7.6 %collective-permute-start.9 = (f32[32,1024]{1,0:T(8,128)S(1)}, f32[32,1024]{1,0:T(8,128)S(1)}, u32[]{:S(2)}, u32[]{:S(2)}) collective-permute-start(f32[32,1024]{1,0:T(8,128)S(1)} %shard_map.145.refs_3_), channel_id=1, source_target_pairs={{0,4},{4,0},{8,12},{12,8},{16,20},{20,16},{24,28},{28,24},{1,5},{5... | collective-permute-start | bytes 393224 | tf_op jit(solution)/shard_map/ppermute | solution.py:483
  24.9 6.4 %collective-permute-start.11 = (f32[32,1024]{1,0:T(8,128)S(1)}, f32[32,1024]{1,0:T(8,128)S(1)}, u32[]{:S(2)}, u32[]{:S(2)}) collective-permute-start(f32[32,1024]{1,0:T(8,128)S(1)} %shard_map.146), channel_id=1, source_target_pairs={{0,4},{4,0},{8,12},{12,8},{16,20},{20,16},{24,28},{28,24},{1,5},{5... | collective-permute-start | bytes 393224 | tf_op jit(solution)/shard_map/ppermute | solution.py:483
  27.5 9.7 %collective-permute-start.14 = (f32[256,128]{1,0:T(8,128)S(1)}, f32[256,128]{1,0:T(8,128)S(1)}, u32[]{:S(2)}, u32[]{:S(2)}) collective-permute-start(f32[256,128]{1,0:T(8,128)S(1)} %shard_map.151.refs_0_), channel_id=1, source_target_pairs={{0,1},{1,0},{2,3},{3,2},{4,5},{5,4},{6,7},{7,6},{8,9},{9,8},{10,11... | collective-permute-start | bytes 393224 | tf_op jit(solution)/shard_map/ppermute | solution.py:470
  29.1 9.1 %collective-permute-start.15 = (f32[256,128]{1,0:T(8,128)S(1)}, f32[256,128]{1,0:T(8,128)S(1)}, u32[]{:S(2)}, u32[]{:S(2)}) collective-permute-start(f32[256,128]{1,0:T(8,128)S(1)} %shard_map.151.refs_0_), channel_id=1, source_target_pairs={{0,2},{1,3},{2,0},{3,1},{4,6},{5,7},{6,4},{7,5},{8,10},{9,11},{10,... | collective-permute-start | bytes 393224 | tf_op jit(solution)/shard_map/ppermute | solution.py:470
  30.6 7.6 %collective-permute-start.16 = (f32[256,128]{1,0:T(8,128)S(1)}, f32[256,128]{1,0:T(8,128)S(1)}, u32[]{:S(2)}, u32[]{:S(2)}) collective-permute-start(f32[256,128]{1,0:T(8,128)S(1)} %shard_map.151.refs_0_), channel_id=1, source_target_pairs={{0,3},{1,2},{2,1},{3,0},{4,7},{5,6},{6,5},{7,4},{8,11},{9,10},{10,... | collective-permute-start | bytes 393224 | tf_op jit(solution)/shard_map/ppermute | solution.py:470
  31.6 4.1 %collective-permute-start.12 = (f32[2,16]{1,0:T(2,128)S(1)}, f32[2,16]{1,0:T(2,128)S(1)}, u32[]{:S(2)}, u32[]{:S(2)}) collective-permute-start(f32[2,16]{1,0:T(2,128)S(1)} %shard_map.148.x_ref.refs_11_), channel_id=1, source_target_pairs={{0,4},{4,0},{8,12},{12,8},{1,5},{5,1},{9,13},{13,9},{2,6},{6,2},{1... | collective-permute-start | bytes 392 | tf_op jit(solution)/shard_map/ppermute | solution.py:470
  34.1 9.9 %collective-permute-start.17 = (f32[256,128]{1,0:T(8,128)S(1)}, f32[256,128]{1,0:T(8,128)S(1)}, u32[]{:S(2)}, u32[]{:S(2)}) collective-permute-start(f32[256,128]{1,0:T(8,128)S(1)} %shard_map.154.x_ref.refs_1_), channel_id=1, source_target_pairs={{0,1},{1,0},{2,3},{3,2},{4,5},{5,4},{6,7},{7,6},{8,9},{9,8},{10,11... | collective-permute-start | bytes 393224 | tf_op jit(solution)/shard_map/ppermute | solution.py:470
  35.6 8.3 %collective-permute-start.18 = (f32[256,128]{1,0:T(8,128)S(1)}, f32[256,128]{1,0:T(8,128)S(1)}, u32[]{:S(2)}, u32[]{:S(2)}) collective-permute-start(f32[256,128]{1,0:T(8,128)S(1)} %shard_map.155), channel_id=1, source_target_pairs={{0,2},{1,3},{2,0},{3,1},{4,6},{5,7},{6,4},{7,5},{8,10},{9,11},{10,... | collective-permute-start | bytes 393224 | tf_op jit(solution)/shard_map/ppermute | solution.py:470
  37.2 6.8 %collective-permute-start.19 = (f32[256,128]{1,0:T(8,128)S(1)}, f32[256,128]{1,0:T(8,128)S(1)}, u32[]{:S(2)}, u32[]{:S(2)}) collective-permute-start(f32[256,128]{1,0:T(8,128)S(1)} %shard_map.155), channel_id=1, source_target_pairs={{0,3},{1,2},{2,1},{3,0},{4,7},{5,6},{6,5},{7,4},{8,11},{9,10},{10,... | collective-permute-start | bytes 393224 | tf_op jit(solution)/shard_map/ppermute | solution.py:470
  38.2 1.1 %collective-permute-start.13 = (f32[2,16]{1,0:T(2,128)S(1)}, f32[2,16]{1,0:T(2,128)S(1)}, u32[]{:S(2)}, u32[]{:S(2)}) collective-permute-start(f32[2,16]{1,0:T(2,128)S(1)} %shard_map.149.x_ref.refs_0_), channel_id=1, source_target_pairs={{0,16},{16,0},{1,17},{17,1},{2,18},{18,2},{3,19},{19,3},{4,20},{20... | collective-permute-start | bytes 392 | tf_op jit(solution)/shard_map/ppermute | solution.py:470
  39.3 4.6 %collective-permute-start.20 = (f32[2,16]{1,0:T(2,128)S(1)}, f32[2,16]{1,0:T(2,128)S(1)}, u32[]{:S(2)}, u32[]{:S(2)}) collective-permute-start(f32[2,16]{1,0:T(2,128)S(1)} %shard_map.150.refs_24_.refs_5_), channel_id=1, source_target_pairs={{0,8},{4,12},{8,0},{12,4},{1,9},{5,13},{9,1},{13,5},{2,10},{6,14},... | collective-permute-start | bytes 392 | tf_op jit(solution)/shard_map/ppermute | solution.py:470

commit v10 on v9

--- a/solution.py
+++ b/solution.py
@@ -241,7 +241,7 @@
 
 def factors_kernel(
     size, v_ref, gate_ref, go_ref, b_ref, c_ref, cum_ref, after_ref,
-    high_ref, low_ref, scaled_ref, q_ref, r_ref, *other_refs,
+    high_ref, low_ref, scaled_ref, *other_refs,
 ):
     length, channels = v_ref.shape
     heads = cum_ref.shape[0]
@@ -250,8 +250,6 @@
     left_over = cumulative[:, -1:] - cumulative
     growth = rows_of_three(jnp.exp(cumulative))
     fall = rows_of_three(jnp.exp(left_over))
-    growth_slope = rows_of_three(cumulative * jnp.exp(cumulative))
-    fall_slope = rows_of_three(left_over * jnp.exp(left_over))
     b_t = b_ref[...].astype(F32).T.astype(BF16)
     c_t = c_ref[...].astype(F32).T.astype(BF16)
     for first in range(0, channels, LANES):
@@ -262,10 +260,6 @@
         high_ref[:, here] = high
         low_ref[:, here] = low
         scaled_ref[:, here] = (spread(fall, first, LANES, width) * vals).astype(BF16)
-        high, low = split(spread(growth_slope, first, LANES, width) * grad_y, 2)
-        q_ref[:, here] = mm(c_t, high) + mm(c_t, low)
-        high, low = split(spread(fall_slope, first, LANES, width) * vals, 2)
-        r_ref[:, here] = mm(b_t, high) + mm(b_t, low)
 
     def pulled():
         put_rows(other_refs, slice(None), mm(c_t, high_ref[...]) + mm(c_t, low_ref[...]))
@@ -279,6 +273,24 @@
         lower = lax.axis_index("seq") < size // 2
         pl.when(lower)(pulled)
         pl.when(jnp.logical_not(lower))(local)
+
+
+def slopes_kernel(v_ref, gate_ref, go_ref, b_ref, c_ref, cum_ref, after_ref, q_ref, r_ref):
+    length, channels = v_ref.shape
+    width = channels // cum_ref.shape[0]
+    cumulative = cum_ref[...]
+    left_over = cumulative[:, -1:] - cumulative
+    growth_slope = rows_of_three(cumulative * jnp.exp(cumulative))
+    fall_slope = rows_of_three(left_over * jnp.exp(left_over))
+    b_t = b_ref[...].astype(F32).T.astype(BF16)
+    c_t = c_ref[...].astype(F32).T.astype(BF16)
+    for first in range(0, channels, LANES):
+        here = pl.ds(first, LANES)
+        _, _, grad_y = gate_parts(gate_ref[:, here], go_ref[:, here])
+        high, low = split(spread(growth_slope, first, LANES, width) * grad_y, 2)
+        q_ref[:, here] = mm(c_t, high) + mm(c_t, low)
+        high, low = split(spread(fall_slope, first, LANES, width) * v_ref[:, here].astype(F32), 2)
+        r_ref[:, here] = mm(b_t, high) + mm(b_t, low)
 
 
 def prepare_kernel(
@@ -518,7 +530,7 @@
             token = work[count](token)
         if at > middle and c > 2:
             token = (*token, got[at, c - 2 - 1])
-        base = mine[c] if at <= middle else made["factors"][5 + c]
+        base = mine[c] if at <= middle else made["factors"][3 + c]
         pay = pass_on(got[at - 1, c], base, decay, token, f"pass{min(count, 7)}")
         got[at, c] = hop(pay, sizes, at)
         token = (pay,)
@@ -618,10 +630,16 @@
     def factors(after):
         made["factors"] = call(
             functools.partial(factors_kernel, seq),
-            [wide_b] * 3 + [like((state, channels), F32)] * 2 + [piece] * CHUNKS,
+            [wide_b] * 3 + [piece] * CHUNKS,
             name="factors",
         )(vals, gate, grad, block_b, block_c, cumulative, *(after if after else made["intra"][2:3]))
-        return made["factors"][5:6]
+        return made["factors"][3:4]
+
+    def slopes(after):
+        made["slopes"] = call(slopes_kernel, [like((state, channels), F32)] * 2, name="slopes")(
+            vals, gate, grad, block_b, block_c, cumulative, *(after if after else made["intra"][2:3])
+        )
+        return made["slopes"][:1]
 
     def prepare(after):
         made["prepare"] = call(
@@ -635,9 +653,10 @@
         return (made["prepare"][-1],)
 
     sums = max(seq - 2, 0) * CHUNKS
-    states = chain(sizes, mine, made, decay, {0: intra, 1: factors, max(sums - 2, 2): prepare})
+    states = chain(sizes, mine, made, decay, {0: intra, 1: factors, 2: slopes, max(sums - 2, 3): prepare})
     sum_b, sum_c = made["intra"][2:]
-    high, low, scaled, q, r = made["factors"][:5]
+    high, low, scaled = made["factors"][:3]
+    q, r = made["slopes"]
     coef, mamba, inner, growth, fall, grad_y, grad_cum, parts = made["prepare"]
 
     rate_row = jnp.zeros((1, channels), F32)

time: 45 us -> 44.8 us (level)
  starting transfers between devices: 29.3 us -> 28.2 us
  Pallas kernels: 13 us -> 13.5 us
    ppermute x12, starting transfers between devices: 17.6 us -> 16.9 us  [hop(): return lax.ppermute(x, ('replica', 'seq'), pairs)]
    pallas_call x22 -> x23, Pallas kernels: 13 us -> 13.5 us  [run(): pl.pallas_call(kernel, out_shape=tuple(outs), in_specs=specs, out_specs=t...]
  transfers between devices with their start and end apart: 21 -> 21, of which waited for: 3 -> 3; matrix products, arithmetic and copies ran while one was open for 0% -> 0% of each run, Pallas kernels for 22% -> 23%
where the time goes in v10:
time: 44.8 us; the launch traced here: 44.6 us
  starting transfers between devices  28.2 us (63%)
  Pallas kernels  13.5 us (30%)
  waiting for transfers between devices  2.13 us (5%)
  between operations  0.81 us (2%)
    ppermute x12, starting transfers between devices, hop(): return lax.ppermute(x, ('replica', 'seq'), pairs)  16.9 us
    pallas_call x23, Pallas kernels, run(): pl.pallas_call(kernel, out_shape=tuple(outs), in_specs=specs, out_specs=t...  13.5 us
    ppermute x9, starting transfers between devices, swap(): return lax.ppermute(x, axis, [(i, i ^ bit) for i in range(size)])  11.3 us
    ppermute x9, waiting for transfers between devices, swap(): return lax.ppermute(x, axis, [(i, i ^ bit) for i in range(size)])  1.37 us
  transfers between devices with their start and end apart: 21, of which 3 were waited for; matrix products, arithmetic and copies ran while one was open for 0% of the time, Pallas kernels for 23%

profile of v10, /device:TPU:0, one launch (start us, length us, event | category | flops | bytes accessed | tf_op | source)
XLA Modules:
  0.0 44.6 jit_solution(7284501936084778576)
XLA Ops:
  0.6 2.3 %shard_map.135 = (bf16[256,1024]{1,0:T(8,128)(2,1)S(1)}, bf16[256,1024]{1,0:T(8,128)(2,1)S(1)}, bf16[256,1024]{1,0:T(8,128)(2,1)S(1)}, bf16[256,128]{1,0:T(8,128...) custom-call(bf16[256,1024]{1,0:T(8,128)(2,1)} %bitcast.10, ...), custom_call_target="tpu_custom_call" | custom-call | tf_op jit(solution)/shard_map/pallas_call | solution.py:466
  2.9 3.1 %collective-permute-start = (f32[32,1024]{1,0:T(8,128)S(1)}, f32[32,1024]{1,0:T(8,128)S(1)}, u32[]{:S(2)}, u32[]{:S(2)}) collective-permute-start(f32[32,1024]{1,0:T(8,128)S(1)} %get-tuple-element.49.refs_1_), channel_id=1, source_target_pairs={{0,4},{4,0},{8,12},{12,8},{16,20},{20,16},{24,28},{28,24},{1,5},{5... | collective-permute-start | bytes 393224 | tf_op jit(solution)/shard_map/ppermute | solution.py:495
  6.0 0.1 collective-permute-start.3
  6.1 1.9 %collective-permute-start.2 = (f32[32,1024]{1,0:T(8,128)S(1)}, f32[32,1024]{1,0:T(8,128)S(1)}, u32[]{:S(2)}, u32[]{:S(2)}) collective-permute-start(f32[32,1024]{1,0:T(8,128)S(1)} %get-tuple-element.59.refs_1_), channel_id=1, source_target_pairs={{0,4},{4,0},{8,12},{12,8},{16,20},{20,16},{24,28},{28,24},{1,5},{5... | collective-permute-start | bytes 393224 | tf_op jit(solution)/shard_map/ppermute | solution.py:495
  8.0 2.5 %shard_map.136 = (f32[256,1024]{1,0:T(8,128)S(1)}, f32[256,1024]{1,0:T(8,128)S(1)}, f32[256,128]{1,0:T(8,128)S(1)}, f32[256,128]{1,0:T(8,128)S(1)}) custom-call(bf16[256,1024]{1,0:T(8,128)(2,1)S(1)} %get-tuple-element.51.v_ref.refs_12_, bf16[256,1024]{1,0:T(8,128)(2,1)S(1)} %get-tuple-element.52.gate_ref, bf16[256,1024]{1,0:T(8,128)(2,1)S(1)} %get-tuple-element.53.go_ref, ...), custom_call_target="tpu_custom_call" | custom-call | tf_op jit(solution)/shard_map/pallas_call | solution.py:466
  10.6 0.0 collective-permute-done.refs_0_
  10.6 0.1 collective-permute-start.1
  10.7 3.2 %collective-permute-start.6 = (f32[32,1024]{1,0:T(8,128)S(1)}, f32[32,1024]{1,0:T(8,128)S(1)}, u32[]{:S(2)}, u32[]{:S(2)}) collective-permute-start(f32[32,1024]{1,0:T(8,128)S(1)} %get-tuple-element.63.refs_1_), channel_id=1, source_target_pairs={{0,4},{4,0},{8,12},{12,8},{16,20},{20,16},{24,28},{28,24},{1,5},{5... | collective-permute-start | bytes 393224 | tf_op jit(solution)/shard_map/ppermute | solution.py:495
  13.9 1.1 %shard_map.138 = (bf16[256,1024]{1,0:T(8,128)(2,1)S(1)}, bf16[256,1024]{1,0:T(8,128)(2,1)S(1)}, bf16[256,1024]{1,0:T(8,128)(2,1)S(1)}, f32[32,1024]{1,0:T(8,128)...) custom-call(bf16[256,1024]{1,0:T(8,128)(2,1)S(1)} %get-tuple-element.51.v_ref.refs_12_, ...), custom_call_target="tpu_custom_call" | custom-call | tf_op jit(solution)/shard_map/pallas_call | solution.py:466
  15.0 0.0 collective-permute-done.3.refs_0_.refs_3_
  15.1 0.1 collective-permute-start.5
  15.1 1.1 %shard_map.140 = (f32[128,1024]{1,0:T(8,128)S(1)}, f32[128,1024]{1,0:T(8,128)S(1)}) custom-call(bf16[256,1024]{1,0:T(8,128)(2,1)S(1)} %get-tuple-element.51.v_ref.refs_12_, bf16[256,1024]{1,0:T(8,128)(2,1)S(1)} %get-tuple-element.52.gate_ref, bf16[256,1024]{1,0:T(8,128)(2,1)S(1)} %get-tuple-element.53.go_ref, ...), custom_call_target="tpu_custom_call" | custom-call | tf_op jit(solution)/shard_map/pallas_call | solution.py:466
  16.2 0.0 collective-permute-done.2.refs_0_.refs_6_
  16.2 0.6 %collective-permute-start.8 = (f32[32,1024]{1,0:T(8,128)S(1)}, f32[32,1024]{1,0:T(8,128)S(1)}, u32[]{:S(2)}, u32[]{:S(2)}) collective-permute-start(f32[32,1024]{1,0:T(8,128)S(1)} %shard_map.141.refs_3_), channel_id=1, source_target_pairs={{0,16},{4,8},{8,4},{12,28},{16,0},{20,24},{24,20},{28,12},{1,17},{... | collective-permute-start | bytes 393224 | tf_op jit(solution)/shard_map/ppermute | solution.py:495
  16.8 0.0 collective-permute-done.1.refs_0_.refs_1_
  16.8 2.8 %collective-permute-start.4 = (f32[32,1024]{1,0:T(8,128)S(1)}, f32[32,1024]{1,0:T(8,128)S(1)}, u32[]{:S(2)}, u32[]{:S(2)}) collective-permute-start(f32[32,1024]{1,0:T(8,128)S(1)} %shard_map.142.refs_3_), channel_id=1, source_target_pairs={{0,4},{4,0},{8,12},{12,8},{16,20},{20,16},{24,28},{28,24},{1,5},{5... | collective-permute-start | bytes 393224 | tf_op jit(solution)/shard_map/ppermute | solution.py:495
  19.6 0.0 collective-permute-done.6.refs_0_.refs_3_.refs_9_
  19.6 0.1 collective-permute-start.10
  19.7 0.0 collective-permute-done.5.refs_0_.refs_4_
  19.8 1.6 %collective-permute-start.7 = (f32[32,1024]{1,0:T(8,128)S(1)}, f32[32,1024]{1,0:T(8,128)S(1)}, u32[]{:S(2)}, u32[]{:S(2)}) collective-permute-start(f32[32,1024]{1,0:T(8,128)S(1)} %shard_map.144.after_ref), channel_id=1, source_target_pairs={{0,4},{4,0},{8,12},{12,8},{16,20},{20,16},{24,28},{28,24},{1,5},{5... | collective-permute-start | bytes 393224 | tf_op jit(solution)/shard_map/ppermute | solution.py:495
  21.4 1.4 %shard_map.145 = (f32[256,1024]{1,0:T(8,128)S(1)}, f32[256,1024]{1,0:T(8,128)S(1)}, f32[256,1024]{1,0:T(8,128)S(1)}, f32[256,1024]{1,0:T(8,128)S(1)}, f32[256,10...) custom-call(bf16[256,1024]{1,0:T(8,128)(2,1)S(1)} %get-tuple-element.51.v_ref.refs_12_, ...), custom_call_target="tpu_custom_call" | custom-call | tf_op jit(solution)/shard_map/pallas_call | solution.py:466
  22.8 0.0 collective-permute-done.8.refs_0_.refs_1_.refs_7_
  22.9 1.6 %collective-permute-start.9 = (f32[32,1024]{1,0:T(8,128)S(1)}, f32[32,1024]{1,0:T(8,128)S(1)}, u32[]{:S(2)}, u32[]{:S(2)}) collective-permute-start(f32[32,1024]{1,0:T(8,128)S(1)} %shard_map.146.refs_3_), channel_id=1, source_target_pairs={{0,4},{4,0},{8,12},{12,8},{16,20},{20,16},{24,28},{28,24},{1,5},{5... | collective-permute-start | bytes 393224 | tf_op jit(solution)/shard_map/ppermute | solution.py:495
  24.4 0.0 collective-permute-done.4.refs_4_.refs_2_
  24.4 0.0 collective-permute-done.10.refs_0_.refs_4_.refs_10_
  24.5 1.8 %collective-permute-start.11 = (f32[32,1024]{1,0:T(8,128)S(1)}, f32[32,1024]{1,0:T(8,128)S(1)}, u32[]{:S(2)}, u32[]{:S(2)}) collective-permute-start(f32[32,1024]{1,0:T(8,128)S(1)} %shard_map.147), channel_id=1, source_target_pairs={{0,4},{4,0},{8,12},{12,8},{16,20},{20,16},{24,28},{28,24},{1,5},{5... | collective-permute-start | bytes 393224 | tf_op jit(solution)/shard_map/ppermute | solution.py:495
  26.2 0.0 collective-permute-done.7.refs_5_
  26.2 0.1 shard_map.148.refs_9_.refs_11_
  26.4 0.7 %shard_map.152.refs_0_ = f32[256,128]{1,0:T(8,128)S(1)} custom-call(f32[32,1024]{1,0:T(8,128)S(1)} %collective-permute-done.refs_0_, f32[32,1024]{1,0:T(8,128)S(1)} %collective-permute-done.1.refs_0_.refs_1_, f32[32,1024]{1,0:T(8,128)S(1)} %collective-permute-done.4.refs_4_.refs_2_, f32[32,1024]{1,0:T(8,128)S(1)} %collective-permute-done.3.refs_0_.refs_3_, ...), custom_call_target="tpu_custom_call" | custom-call | tf_op jit(solution)/shard_map/pallas_call | solution.py:466
  27.0 1.6 %collective-permute-start.14 = (f32[256,128]{1,0:T(8,128)S(1)}, f32[256,128]{1,0:T(8,128)S(1)}, u32[]{:S(2)}, u32[]{:S(2)}) collective-permute-start(f32[256,128]{1,0:T(8,128)S(1)} %shard_map.152.refs_0_), channel_id=1, source_target_pairs={{0,1},{1,0},{2,3},{3,2},{4,5},{5,4},{6,7},{7,6},{8,9},{9,8},{10,11... | collective-permute-start | bytes 393224 | tf_op jit(solution)/shard_map/ppermute | solution.py:482
  28.6 1.5 %collective-permute-start.15 = (f32[256,128]{1,0:T(8,128)S(1)}, f32[256,128]{1,0:T(8,128)S(1)}, u32[]{:S(2)}, u32[]{:S(2)}) collective-permute-start(f32[256,128]{1,0:T(8,128)S(1)} %shard_map.152.refs_0_), channel_id=1, source_target_pairs={{0,2},{1,3},{2,0},{3,1},{4,6},{5,7},{6,4},{7,5},{8,10},{9,11},{10,... | collective-permute-start | bytes 393224 | tf_op jit(solution)/shard_map/ppermute | solution.py:482
  30.1 0.5 %collective-permute-start.16 = (f32[256,128]{1,0:T(8,128)S(1)}, f32[256,128]{1,0:T(8,128)S(1)}, u32[]{:S(2)}, u32[]{:S(2)}) collective-permute-start(f32[256,128]{1,0:T(8,128)S(1)} %shard_map.152.refs_0_), channel_id=1, source_target_pairs={{0,3},{1,2},{2,1},{3,0},{4,7},{5,6},{6,5},{7,4},{8,11},{9,10},{10,... | collective-permute-start | bytes 393224 | tf_op jit(solution)/shard_map/ppermute | solution.py:482
  30.6 0.0 collective-permute-done.9.refs_2_.refs_8_
  30.6 0.7 %collective-permute-done.11.refs_5_.refs_11_ = f32[32,1024]{1,0:T(8,128)S(1)} collective-permute-done((f32[32,1024]{1,0:T(8,128)S(1)}, f32[32,1024]{1,0:T(8,128)S(1)}, u32[]{:S(2)}, u32[]{:S(2)}) %collective-permute-start.11) | collective-permute-done | bytes 131104 | tf_op jit(solution)/shard_map/ppermute | solution.py:495
  31.3 0.2 shard_map.149.x_ref.refs_11_
  31.6 1.7 %collective-permute-start.12 = (f32[2,16]{1,0:T(2,128)S(1)}, f32[2,16]{1,0:T(2,128)S(1)}, u32[]{:S(2)}, u32[]{:S(2)}) collective-permute-start(f32[2,16]{1,0:T(2,128)S(1)} %shard_map.149.x_ref.refs_11_), channel_id=1, source_target_pairs={{0,4},{4,0},{8,12},{12,8},{1,5},{5,1},{9,13},{13,9},{2,6},{6,2},{1... | collective-permute-start | bytes 392 | tf_op jit(solution)/shard_map/ppermute | solution.py:482
  33.3 0.8 %shard_map.155.x_ref.refs_1_ = f32[256,128]{1,0:T(8,128)S(1)} custom-call(f32[32,1024]{1,0:T(8,128)S(1)} %collective-permute-done.2.refs_0_.refs_6_, f32[32,1024]{1,0:T(8,128)S(1)} %collective-permute-done.8.refs_0_.refs_1_.refs_7_, f32[32,1024]{1,0:T(8,128)S(1)} %collective-permute-done.9.refs_2_.refs_8_, ...), custom_call_target="tpu_custom_call" | custom-call | tf_op jit(solution)/shard_map/pallas_call | solution.py:466
  34.1 1.5 %collective-permute-start.17 = (f32[256,128]{1,0:T(8,128)S(1)}, f32[256,128]{1,0:T(8,128)S(1)}, u32[]{:S(2)}, u32[]{:S(2)}) collective-permute-start(f32[256,128]{1,0:T(8,128)S(1)} %shard_map.155.x_ref.refs_1_), channel_id=1, source_target_pairs={{0,1},{1,0},{2,3},{3,2},{4,5},{5,4},{6,7},{7,6},{8,9},{9,8},{10,11... | collective-permute-start | bytes 393224 | tf_op jit(solution)/shard_map/ppermute | solution.py:482
  35.6 0.0 collective-permute-done.12.y_ref
  35.6 1.6 %collective-permute-start.18 = (f32[256,128]{1,0:T(8,128)S(1)}, f32[256,128]{1,0:T(8,128)S(1)}, u32[]{:S(2)}, u32[]{:S(2)}) collective-permute-start(f32[256,128]{1,0:T(8,128)S(1)} %shard_map.156), channel_id=1, source_target_pairs={{0,2},{1,3},{2,0},{3,1},{4,6},{5,7},{6,4},{7,5},{8,10},{9,11},{10,... | collective-permute-start | bytes 393224 | tf_op jit(solution)/shard_map/ppermute | solution.py:482
  37.2 0.0 collective-permute-done.14.refs_1_
  37.2 1.0 %collective-permute-start.19 = (f32[256,128]{1,0:T(8,128)S(1)}, f32[256,128]{1,0:T(8,128)S(1)}, u32[]{:S(2)}, u32[]{:S(2)}) collective-permute-start(f32[256,128]{1,0:T(8,128)S(1)} %shard_map.156), channel_id=1, source_target_pairs={{0,3},{1,2},{2,1},{3,0},{4,7},{5,6},{6,5},{7,4},{8,11},{9,10},{10,... | collective-permute-start | bytes 393224 | tf_op jit(solution)/shard_map/ppermute | solution.py:482
  38.2 0.0 collective-permute-done.15.refs_2_
  38.2 0.0 collective-permute-start.13
  38.2 0.0 collective-permute-done.16.refs_3_
  38.2 1.1 %collective-permute-done.13.y_ref = f32[2,16]{1,0:T(2,128)S(1)} collective-permute-done((f32[2,16]{1,0:T(2,128)S(1)}, f32[2,16]{1,0:T(2,128)S(1)}, u32[]{:S(2)}, u32[]{:S(2)}) %collective-permute-start.13) | collective-permute-done | bytes 160 | tf_op jit(solution)/shard_map/ppermute | solution.py:482
  39.3 1.9 %collective-permute-start.20 = (f32[2,16]{1,0:T(2,128)S(1)}, f32[2,16]{1,0:T(2,128)S(1)}, u32[]{:S(2)}, u32[]{:S(2)}) collective-permute-start(f32[2,16]{1,0:T(2,128)S(1)} %shard_map.151.refs_24_.refs_5_), channel_id=1, source_target_pairs={{0,8},{4,12},{8,0},{12,4},{1,9},{5,13},{9,1},{13,5},{2,10},{6,14},... | collective-permute-start | bytes 392 | tf_op jit(solution)/shard_map/ppermute | solution.py:482
  41.3 2.3 %shard_map.154 = (bf16[1,256,1024]{2,1,0:T(8,128)(2,1)}, bf16[1,256,1024]{2,1,0:T(8,128)(2,1)}, f32[1,16,256]{2,1,0:T(8,128)}) custom-call(f32[32,1024]{1,0:T(8,128)S(1)} %collective-permute-done.refs_0_, f32[32,1024]{1,0:T(8,128)S(1)} %collective-permute-done.1.refs_0_.refs_1_, f32[32,1024]{1,0:T(8,128)S(1)} %collective-permute-done.4.refs_4_.refs_2_, ...), custom_call_target="tpu_custom_call" | custom-call | flops 300000000 | tf_op jit(solution)/shard_map/pallas_call | solution.py:466
  43.6 0.3 collective-permute-done.20.refs_6_
  43.8 0.0 collective-permute-done.17.refs_2_
  43.8 0.0 collective-permute-done.18.refs_3_
  43.8 0.0 collective-permute-done.19.refs_4_
  43.8 0.8 %shard_map.157 = (f32[1,256,128]{2,1,0:T(8,128)}, f32[1,256,128]{2,1,0:T(8,128)}, f32[1,16]{1,0:T(1,128)}, f32[1,16]{1,0:T(1,128)}) custom-call(f32[256,128]{1,0:T(8,128)S(1)} %shard_map.153.refs_25_.refs_0_, f32[256,128]{1,0:T(8,128)S(1)} %shard_map.155.x_ref.refs_1_, f32[256,128]{1,0:T(8,128)S(1)} %collective-permute-done.17.refs_2_, ...), custom_call_target="tpu_custom_call" | custom-call | tf_op jit(solution)/shard_map/pallas_call | solution.py:466
  (13 shorter events, 0.2 us)
Async XLA Ops:
  2.9 7.7 %collective-permute-start = (f32[32,1024]{1,0:T(8,128)S(1)}, f32[32,1024]{1,0:T(8,128)S(1)}, u32[]{:S(2)}, u32[]{:S(2)}) collective-permute-start(f32[32,1024]{1,0:T(8,128)S(1)} %get-tuple-element.49.refs_1_), channel_id=1, source_target_pairs={{0,4},{4,0},{8,12},{12,8},{16,20},{20,16},{24,28},{28,24},{1,5},{5... | collective-permute-start | bytes 393224 | tf_op jit(solution)/shard_map/ppermute | solution.py:495
  6.0 9.0 %collective-permute-start.3 = (f32[32,1024]{1,0:T(8,128)S(1)}, f32[32,1024]{1,0:T(8,128)S(1)}, u32[]{:S(2)}, u32[]{:S(2)}) collective-permute-start(f32[32,1024]{1,0:T(8,128)S(1)} %get-tuple-element.60.refs_1_), channel_id=1, source_target_pairs={{0,4},{4,0},{8,12},{12,8},{16,20},{20,16},{24,28},{28,24},{1,5},{5... | collective-permute-start | bytes 393224 | tf_op jit(solution)/shard_map/ppermute | solution.py:495
  6.1 10.1 %collective-permute-start.2 = (f32[32,1024]{1,0:T(8,128)S(1)}, f32[32,1024]{1,0:T(8,128)S(1)}, u32[]{:S(2)}, u32[]{:S(2)}) collective-permute-start(f32[32,1024]{1,0:T(8,128)S(1)} %get-tuple-element.59.refs_1_), channel_id=1, source_target_pairs={{0,4},{4,0},{8,12},{12,8},{16,20},{20,16},{24,28},{28,24},{1,5},{5... | collective-permute-start | bytes 393224 | tf_op jit(solution)/shard_map/ppermute | solution.py:495
  10.6 6.2 %collective-permute-start.1 = (f32[32,1024]{1,0:T(8,128)S(1)}, f32[32,1024]{1,0:T(8,128)S(1)}, u32[]{:S(2)}, u32[]{:S(2)}) collective-permute-start(f32[32,1024]{1,0:T(8,128)S(1)} %shard_map.137.after_ref), channel_id=1, source_target_pairs={{0,16},{4,8},{8,4},{12,28},{16,0},{20,24},{24,20},{28,12},{1,17},{... | collective-permute-start | bytes 393224 | tf_op jit(solution)/shard_map/ppermute | solution.py:495
  10.7 8.9 %collective-permute-start.6 = (f32[32,1024]{1,0:T(8,128)S(1)}, f32[32,1024]{1,0:T(8,128)S(1)}, u32[]{:S(2)}, u32[]{:S(2)}) collective-permute-start(f32[32,1024]{1,0:T(8,128)S(1)} %get-tuple-element.63.refs_1_), channel_id=1, source_target_pairs={{0,4},{4,0},{8,12},{12,8},{16,20},{20,16},{24,28},{28,24},{1,5},{5... | collective-permute-start | bytes 393224 | tf_op jit(solution)/shard_map/ppermute | solution.py:495
  15.1 4.7 %collective-permute-start.5 = (f32[32,1024]{1,0:T(8,128)S(1)}, f32[32,1024]{1,0:T(8,128)S(1)}, u32[]{:S(2)}, u32[]{:S(2)}) collective-permute-start(f32[32,1024]{1,0:T(8,128)S(1)} %shard_map.139.after_ref), channel_id=1, source_target_pairs={{0,16},{4,8},{8,4},{12,28},{16,0},{20,24},{24,20},{28,12},{1,17},{... | collective-permute-start | bytes 393224 | tf_op jit(solution)/shard_map/ppermute | solution.py:495
  16.2 6.6 %collective-permute-start.8 = (f32[32,1024]{1,0:T(8,128)S(1)}, f32[32,1024]{1,0:T(8,128)S(1)}, u32[]{:S(2)}, u32[]{:S(2)}) collective-permute-start(f32[32,1024]{1,0:T(8,128)S(1)} %shard_map.141.refs_3_), channel_id=1, source_target_pairs={{0,16},{4,8},{8,4},{12,28},{16,0},{20,24},{24,20},{28,12},{1,17},{... | collective-permute-start | bytes 393224 | tf_op jit(solution)/shard_map/ppermute | solution.py:495
  16.8 7.6 %collective-permute-start.4 = (f32[32,1024]{1,0:T(8,128)S(1)}, f32[32,1024]{1,0:T(8,128)S(1)}, u32[]{:S(2)}, u32[]{:S(2)}) collective-permute-start(f32[32,1024]{1,0:T(8,128)S(1)} %shard_map.142.refs_3_), channel_id=1, source_target_pairs={{0,4},{4,0},{8,12},{12,8},{16,20},{20,16},{24,28},{28,24},{1,5},{5... | collective-permute-start | bytes 393224 | tf_op jit(solution)/shard_map/ppermute | solution.py:495
  19.6 4.8 %collective-permute-start.10 = (f32[32,1024]{1,0:T(8,128)S(1)}, f32[32,1024]{1,0:T(8,128)S(1)}, u32[]{:S(2)}, u32[]{:S(2)}) collective-permute-start(f32[32,1024]{1,0:T(8,128)S(1)} %shard_map.143.refs_3_), channel_id=1, source_target_pairs={{0,16},{4,8},{8,4},{12,28},{16,0},{20,24},{24,20},{28,12},{1,17},{... | collective-permute-start | bytes 393224 | tf_op jit(solution)/shard_map/ppermute | solution.py:495
  19.8 6.5 %collective-permute-start.7 = (f32[32,1024]{1,0:T(8,128)S(1)}, f32[32,1024]{1,0:T(8,128)S(1)}, u32[]{:S(2)}, u32[]{:S(2)}) collective-permute-start(f32[32,1024]{1,0:T(8,128)S(1)} %shard_map.144.after_ref), channel_id=1, source_target_pairs={{0,4},{4,0},{8,12},{12,8},{16,20},{20,16},{24,28},{28,24},{1,5},{5... | collective-permute-start | bytes 393224 | tf_op jit(solution)/shard_map/ppermute | solution.py:495
  22.9 7.7 %collective-permute-start.9 = (f32[32,1024]{1,0:T(8,128)S(1)}, f32[32,1024]{1,0:T(8,128)S(1)}, u32[]{:S(2)}, u32[]{:S(2)}) collective-permute-start(f32[32,1024]{1,0:T(8,128)S(1)} %shard_map.146.refs_3_), channel_id=1, source_target_pairs={{0,4},{4,0},{8,12},{12,8},{16,20},{20,16},{24,28},{28,24},{1,5},{5... | collective-permute-start | bytes 393224 | tf_op jit(solution)/shard_map/ppermute | solution.py:495
  24.5 6.9 %collective-permute-start.11 = (f32[32,1024]{1,0:T(8,128)S(1)}, f32[32,1024]{1,0:T(8,128)S(1)}, u32[]{:S(2)}, u32[]{:S(2)}) collective-permute-start(f32[32,1024]{1,0:T(8,128)S(1)} %shard_map.147), channel_id=1, source_target_pairs={{0,4},{4,0},{8,12},{12,8},{16,20},{20,16},{24,28},{28,24},{1,5},{5... | collective-permute-start | bytes 393224 | tf_op jit(solution)/shard_map/ppermute | solution.py:495
  27.0 10.2 %collective-permute-start.14 = (f32[256,128]{1,0:T(8,128)S(1)}, f32[256,128]{1,0:T(8,128)S(1)}, u32[]{:S(2)}, u32[]{:S(2)}) collective-permute-start(f32[256,128]{1,0:T(8,128)S(1)} %shard_map.152.refs_0_), channel_id=1, source_target_pairs={{0,1},{1,0},{2,3},{3,2},{4,5},{5,4},{6,7},{7,6},{8,9},{9,8},{10,11... | collective-permute-start | bytes 393224 | tf_op jit(solution)/shard_map/ppermute | solution.py:482
  28.6 9.6 %collective-permute-start.15 = (f32[256,128]{1,0:T(8,128)S(1)}, f32[256,128]{1,0:T(8,128)S(1)}, u32[]{:S(2)}, u32[]{:S(2)}) collective-permute-start(f32[256,128]{1,0:T(8,128)S(1)} %shard_map.152.refs_0_), channel_id=1, source_target_pairs={{0,2},{1,3},{2,0},{3,1},{4,6},{5,7},{6,4},{7,5},{8,10},{9,11},{10,... | collective-permute-start | bytes 393224 | tf_op jit(solution)/shard_map/ppermute | solution.py:482
  30.1 8.1 %collective-permute-start.16 = (f32[256,128]{1,0:T(8,128)S(1)}, f32[256,128]{1,0:T(8,128)S(1)}, u32[]{:S(2)}, u32[]{:S(2)}) collective-permute-start(f32[256,128]{1,0:T(8,128)S(1)} %shard_map.152.refs_0_), channel_id=1, source_target_pairs={{0,3},{1,2},{2,1},{3,0},{4,7},{5,6},{6,5},{7,4},{8,11},{9,10},{10,... | collective-permute-start | bytes 393224 | tf_op jit(solution)/shard_map/ppermute | solution.py:482
  31.6 4.1 %collective-permute-start.12 = (f32[2,16]{1,0:T(2,128)S(1)}, f32[2,16]{1,0:T(2,128)S(1)}, u32[]{:S(2)}, u32[]{:S(2)}) collective-permute-start(f32[2,16]{1,0:T(2,128)S(1)} %shard_map.149.x_ref.refs_11_), channel_id=1, source_target_pairs={{0,4},{4,0},{8,12},{12,8},{1,5},{5,1},{9,13},{13,9},{2,6},{6,2},{1... | collective-permute-start | bytes 392 | tf_op jit(solution)/shard_map/ppermute | solution.py:482
  34.1 9.7 %collective-permute-start.17 = (f32[256,128]{1,0:T(8,128)S(1)}, f32[256,128]{1,0:T(8,128)S(1)}, u32[]{:S(2)}, u32[]{:S(2)}) collective-permute-start(f32[256,128]{1,0:T(8,128)S(1)} %shard_map.155.x_ref.refs_1_), channel_id=1, source_target_pairs={{0,1},{1,0},{2,3},{3,2},{4,5},{5,4},{6,7},{7,6},{8,9},{9,8},{10,11... | collective-permute-start | bytes 393224 | tf_op jit(solution)/shard_map/ppermute | solution.py:482
  35.6 8.2 %collective-permute-start.18 = (f32[256,128]{1,0:T(8,128)S(1)}, f32[256,128]{1,0:T(8,128)S(1)}, u32[]{:S(2)}, u32[]{:S(2)}) collective-permute-start(f32[256,128]{1,0:T(8,128)S(1)} %shard_map.156), channel_id=1, source_target_pairs={{0,2},{1,3},{2,0},{3,1},{4,6},{5,7},{6,4},{7,5},{8,10},{9,11},{10,... | collective-permute-start | bytes 393224 | tf_op jit(solution)/shard_map/ppermute | solution.py:482
  37.2 6.6 %collective-permute-start.19 = (f32[256,128]{1,0:T(8,128)S(1)}, f32[256,128]{1,0:T(8,128)S(1)}, u32[]{:S(2)}, u32[]{:S(2)}) collective-permute-start(f32[256,128]{1,0:T(8,128)S(1)} %shard_map.156), channel_id=1, source_target_pairs={{0,3},{1,2},{2,1},{3,0},{4,7},{5,6},{6,5},{7,4},{8,11},{9,10},{10,... | collective-permute-start | bytes 393224 | tf_op jit(solution)/shard_map/ppermute | solution.py:482
  38.2 1.1 %collective-permute-start.13 = (f32[2,16]{1,0:T(2,128)S(1)}, f32[2,16]{1,0:T(2,128)S(1)}, u32[]{:S(2)}, u32[]{:S(2)}) collective-permute-start(f32[2,16]{1,0:T(2,128)S(1)} %shard_map.150.x_ref.refs_0_), channel_id=1, source_target_pairs={{0,16},{16,0},{1,17},{17,1},{2,18},{18,2},{3,19},{19,3},{4,20},{20... | collective-permute-start | bytes 392 | tf_op jit(solution)/shard_map/ppermute | solution.py:482
  39.3 4.5 %collective-permute-start.20 = (f32[2,16]{1,0:T(2,128)S(1)}, f32[2,16]{1,0:T(2,128)S(1)}, u32[]{:S(2)}, u32[]{:S(2)}) collective-permute-start(f32[2,16]{1,0:T(2,128)S(1)} %shard_map.151.refs_24_.refs_5_), channel_id=1, source_target_pairs={{0,8},{4,12},{8,0},{12,4},{1,9},{5,13},{9,1},{13,5},{2,10},{6,14},... | collective-permute-start | bytes 392 | tf_op jit(solution)/shard_map/ppermute | solution.py:482

commit v11 on v10

--- a/solution.py
+++ b/solution.py
@@ -13,7 +13,7 @@
 LANES = 256
 CHUNKS = 4
 PARTS = 2
-WEIGHTS = {'pass4': 30, 'pass5': 10, 'pass6': 300, 'pass7': 30, 'rate0': 30, 'rate1': 10, 'later': 30, 'sum': 100, 'add1': 100, 'rest': 30}
+WEIGHTS = {'pass4': 30, 'pass5': 10, 'pass6': 300, 'pass7': 30, 'rate0': 30, 'rate1': 10, 'later': 30, 'sum': 100, 'add1': 100, 'rest': 30, 'share1': 0}
 
 
 def split(x, parts):
@@ -552,7 +552,7 @@
     if size == 1:
         return [x]
     if size == 4:
-        return [x, swap(x, axis, size, 1)] + [swap(later, axis, size, bit) for bit in (2, 3)]
+        return [x, swap(x, axis, size, 1), swap(x, axis, size, 2), swap(later, axis, size, 3)]
     if size & (size - 1):
         return [lax.psum(x, axis)]
     bit = 1

time: 44.8 us -> 45 us (level)
  no operation moved by 1% of the time
where the time goes in v11:
time: 45 us; the launch traced here: 44.9 us
  starting transfers between devices  28.3 us (63%)
  Pallas kernels  13.5 us (30%)
  waiting for transfers between devices  2.25 us (5%)
  between operations  0.83 us (2%)
    ppermute x12, starting transfers between devices, hop(): return lax.ppermute(x, ('replica', 'seq'), pairs)  16.9 us
    pallas_call x23, Pallas kernels, run(): pl.pallas_call(kernel, out_shape=tuple(outs), in_specs=specs, out_specs=t...  13.5 us
    ppermute x9, starting transfers between devices, swap(): return lax.ppermute(x, axis, [(i, i ^ bit) for i in range(size)])  11.4 us
    ppermute x9, waiting for transfers between devices, swap(): return lax.ppermute(x, axis, [(i, i ^ bit) for i in range(size)])  1.48 us
  transfers between devices with their start and end apart: 21, of which 3 were waited for; matrix products, arithmetic and copies ran while one was open for 0% of the time, Pallas kernels for 23%

profile of v11, /device:TPU:0, one launch (start us, length us, event | category | flops | bytes accessed | tf_op | source)
XLA Modules:
  0.0 44.9 jit_solution(18089213103229204312)
XLA Ops:
  0.6 2.3 %shard_map.135 = (bf16[256,1024]{1,0:T(8,128)(2,1)S(1)}, bf16[256,1024]{1,0:T(8,128)(2,1)S(1)}, bf16[256,1024]{1,0:T(8,128)(2,1)S(1)}, bf16[256,128]{1,0:T(8,128...) custom-call(bf16[256,1024]{1,0:T(8,128)(2,1)} %bitcast.10, ...), custom_call_target="tpu_custom_call" | custom-call | tf_op jit(solution)/shard_map/pallas_call | solution.py:466
  2.9 3.1 %collective-permute-start = (f32[32,1024]{1,0:T(8,128)S(1)}, f32[32,1024]{1,0:T(8,128)S(1)}, u32[]{:S(2)}, u32[]{:S(2)}) collective-permute-start(f32[32,1024]{1,0:T(8,128)S(1)} %get-tuple-element.49.refs_1_), channel_id=1, source_target_pairs={{0,4},{4,0},{8,12},{12,8},{16,20},{20,16},{24,28},{28,24},{1,5},{5... | collective-permute-start | bytes 393224 | tf_op jit(solution)/shard_map/ppermute | solution.py:495
  6.0 0.1 collective-permute-start.3
  6.1 1.9 %collective-permute-start.2 = (f32[32,1024]{1,0:T(8,128)S(1)}, f32[32,1024]{1,0:T(8,128)S(1)}, u32[]{:S(2)}, u32[]{:S(2)}) collective-permute-start(f32[32,1024]{1,0:T(8,128)S(1)} %get-tuple-element.59.refs_1_), channel_id=1, source_target_pairs={{0,4},{4,0},{8,12},{12,8},{16,20},{20,16},{24,28},{28,24},{1,5},{5... | collective-permute-start | bytes 393224 | tf_op jit(solution)/shard_map/ppermute | solution.py:495
  8.0 2.5 %shard_map.136 = (f32[256,1024]{1,0:T(8,128)S(1)}, f32[256,1024]{1,0:T(8,128)S(1)}, f32[256,128]{1,0:T(8,128)S(1)}, f32[256,128]{1,0:T(8,128)S(1)}) custom-call(bf16[256,1024]{1,0:T(8,128)(2,1)S(1)} %get-tuple-element.51.v_ref.refs_12_, bf16[256,1024]{1,0:T(8,128)(2,1)S(1)} %get-tuple-element.52.gate_ref, bf16[256,1024]{1,0:T(8,128)(2,1)S(1)} %get-tuple-element.53.go_ref, ...), custom_call_target="tpu_custom_call" | custom-call | tf_op jit(solution)/shard_map/pallas_call | solution.py:466
  10.6 0.0 collective-permute-done.refs_0_
  10.6 0.1 collective-permute-start.1
  10.7 3.2 %collective-permute-start.6 = (f32[32,1024]{1,0:T(8,128)S(1)}, f32[32,1024]{1,0:T(8,128)S(1)}, u32[]{:S(2)}, u32[]{:S(2)}) collective-permute-start(f32[32,1024]{1,0:T(8,128)S(1)} %get-tuple-element.63.refs_1_), channel_id=1, source_target_pairs={{0,4},{4,0},{8,12},{12,8},{16,20},{20,16},{24,28},{28,24},{1,5},{5... | collective-permute-start | bytes 393224 | tf_op jit(solution)/shard_map/ppermute | solution.py:495
  13.9 1.1 %shard_map.138 = (bf16[256,1024]{1,0:T(8,128)(2,1)S(1)}, bf16[256,1024]{1,0:T(8,128)(2,1)S(1)}, bf16[256,1024]{1,0:T(8,128)(2,1)S(1)}, f32[32,1024]{1,0:T(8,128)...) custom-call(bf16[256,1024]{1,0:T(8,128)(2,1)S(1)} %get-tuple-element.51.v_ref.refs_12_, ...), custom_call_target="tpu_custom_call" | custom-call | tf_op jit(solution)/shard_map/pallas_call | solution.py:466
  15.0 0.0 collective-permute-done.3.refs_0_.refs_3_
  15.1 0.1 collective-permute-start.5
  15.1 1.1 %shard_map.140 = (f32[128,1024]{1,0:T(8,128)S(1)}, f32[128,1024]{1,0:T(8,128)S(1)}) custom-call(bf16[256,1024]{1,0:T(8,128)(2,1)S(1)} %get-tuple-element.51.v_ref.refs_12_, bf16[256,1024]{1,0:T(8,128)(2,1)S(1)} %get-tuple-element.52.gate_ref, bf16[256,1024]{1,0:T(8,128)(2,1)S(1)} %get-tuple-element.53.go_ref, ...), custom_call_target="tpu_custom_call" | custom-call | tf_op jit(solution)/shard_map/pallas_call | solution.py:466
  16.2 0.0 collective-permute-done.2.refs_0_.refs_6_
  16.2 0.6 %collective-permute-start.8 = (f32[32,1024]{1,0:T(8,128)S(1)}, f32[32,1024]{1,0:T(8,128)S(1)}, u32[]{:S(2)}, u32[]{:S(2)}) collective-permute-start(f32[32,1024]{1,0:T(8,128)S(1)} %shard_map.141.refs_3_), channel_id=1, source_target_pairs={{0,16},{4,8},{8,4},{12,28},{16,0},{20,24},{24,20},{28,12},{1,17},{... | collective-permute-start | bytes 393224 | tf_op jit(solution)/shard_map/ppermute | solution.py:495
  16.8 0.0 collective-permute-done.1.refs_0_.refs_1_
  16.8 2.8 %collective-permute-start.4 = (f32[32,1024]{1,0:T(8,128)S(1)}, f32[32,1024]{1,0:T(8,128)S(1)}, u32[]{:S(2)}, u32[]{:S(2)}) collective-permute-start(f32[32,1024]{1,0:T(8,128)S(1)} %shard_map.142.refs_3_), channel_id=1, source_target_pairs={{0,4},{4,0},{8,12},{12,8},{16,20},{20,16},{24,28},{28,24},{1,5},{5... | collective-permute-start | bytes 393224 | tf_op jit(solution)/shard_map/ppermute | solution.py:495
  19.6 0.0 collective-permute-done.6.refs_0_.refs_3_.refs_9_
  19.6 0.1 collective-permute-start.10
  19.7 0.0 collective-permute-done.5.refs_0_.refs_4_
  19.8 1.6 %collective-permute-start.7 = (f32[32,1024]{1,0:T(8,128)S(1)}, f32[32,1024]{1,0:T(8,128)S(1)}, u32[]{:S(2)}, u32[]{:S(2)}) collective-permute-start(f32[32,1024]{1,0:T(8,128)S(1)} %shard_map.144.after_ref), channel_id=1, source_target_pairs={{0,4},{4,0},{8,12},{12,8},{16,20},{20,16},{24,28},{28,24},{1,5},{5... | collective-permute-start | bytes 393224 | tf_op jit(solution)/shard_map/ppermute | solution.py:495
  21.4 1.4 %shard_map.145 = (f32[256,1024]{1,0:T(8,128)S(1)}, f32[256,1024]{1,0:T(8,128)S(1)}, f32[256,1024]{1,0:T(8,128)S(1)}, f32[256,1024]{1,0:T(8,128)S(1)}, f32[256,10...) custom-call(bf16[256,1024]{1,0:T(8,128)(2,1)S(1)} %get-tuple-element.51.v_ref.refs_12_, ...), custom_call_target="tpu_custom_call" | custom-call | tf_op jit(solution)/shard_map/pallas_call | solution.py:466
  22.8 0.0 collective-permute-done.8.refs_0_.refs_1_.refs_7_
  22.9 1.6 %collective-permute-start.9 = (f32[32,1024]{1,0:T(8,128)S(1)}, f32[32,1024]{1,0:T(8,128)S(1)}, u32[]{:S(2)}, u32[]{:S(2)}) collective-permute-start(f32[32,1024]{1,0:T(8,128)S(1)} %shard_map.146.refs_3_), channel_id=1, source_target_pairs={{0,4},{4,0},{8,12},{12,8},{16,20},{20,16},{24,28},{28,24},{1,5},{5... | collective-permute-start | bytes 393224 | tf_op jit(solution)/shard_map/ppermute | solution.py:495
  24.4 0.0 collective-permute-done.4.refs_4_.refs_2_
  24.4 0.0 collective-permute-done.10.refs_0_.refs_4_.refs_10_
  24.5 1.8 %collective-permute-start.11 = (f32[32,1024]{1,0:T(8,128)S(1)}, f32[32,1024]{1,0:T(8,128)S(1)}, u32[]{:S(2)}, u32[]{:S(2)}) collective-permute-start(f32[32,1024]{1,0:T(8,128)S(1)} %shard_map.147), channel_id=1, source_target_pairs={{0,4},{4,0},{8,12},{12,8},{16,20},{20,16},{24,28},{28,24},{1,5},{5... | collective-permute-start | bytes 393224 | tf_op jit(solution)/shard_map/ppermute | solution.py:495
  26.2 0.0 collective-permute-done.7.refs_5_
  26.2 0.1 shard_map.148.refs_9_.refs_11_
  26.4 0.7 %shard_map.152.refs_0_ = f32[256,128]{1,0:T(8,128)S(1)} custom-call(f32[32,1024]{1,0:T(8,128)S(1)} %collective-permute-done.refs_0_, f32[32,1024]{1,0:T(8,128)S(1)} %collective-permute-done.1.refs_0_.refs_1_, f32[32,1024]{1,0:T(8,128)S(1)} %collective-permute-done.4.refs_4_.refs_2_, f32[32,1024]{1,0:T(8,128)S(1)} %collective-permute-done.3.refs_0_.refs_3_, ...), custom_call_target="tpu_custom_call" | custom-call | tf_op jit(solution)/shard_map/pallas_call | solution.py:466
  27.0 1.6 %collective-permute-start.14 = (f32[256,128]{1,0:T(8,128)S(1)}, f32[256,128]{1,0:T(8,128)S(1)}, u32[]{:S(2)}, u32[]{:S(2)}) collective-permute-start(f32[256,128]{1,0:T(8,128)S(1)} %shard_map.152.refs_0_), channel_id=1, source_target_pairs={{0,1},{1,0},{2,3},{3,2},{4,5},{5,4},{6,7},{7,6},{8,9},{9,8},{10,11... | collective-permute-start | bytes 393224 | tf_op jit(solution)/shard_map/ppermute | solution.py:482
  28.6 1.5 %collective-permute-start.15 = (f32[256,128]{1,0:T(8,128)S(1)}, f32[256,128]{1,0:T(8,128)S(1)}, u32[]{:S(2)}, u32[]{:S(2)}) collective-permute-start(f32[256,128]{1,0:T(8,128)S(1)} %shard_map.152.refs_0_), channel_id=1, source_target_pairs={{0,2},{1,3},{2,0},{3,1},{4,6},{5,7},{6,4},{7,5},{8,10},{9,11},{10,... | collective-permute-start | bytes 393224 | tf_op jit(solution)/shard_map/ppermute | solution.py:482
  30.1 0.5 %collective-permute-start.16 = (f32[256,128]{1,0:T(8,128)S(1)}, f32[256,128]{1,0:T(8,128)S(1)}, u32[]{:S(2)}, u32[]{:S(2)}) collective-permute-start(f32[256,128]{1,0:T(8,128)S(1)} %shard_map.152.refs_0_), channel_id=1, source_target_pairs={{0,3},{1,2},{2,1},{3,0},{4,7},{5,6},{6,5},{7,4},{8,11},{9,10},{10,... | collective-permute-start | bytes 393224 | tf_op jit(solution)/shard_map/ppermute | solution.py:482
  30.6 0.0 collective-permute-done.9.refs_2_.refs_8_
  30.6 0.7 %collective-permute-done.11.refs_5_.refs_11_ = f32[32,1024]{1,0:T(8,128)S(1)} collective-permute-done((f32[32,1024]{1,0:T(8,128)S(1)}, f32[32,1024]{1,0:T(8,128)S(1)}, u32[]{:S(2)}, u32[]{:S(2)}) %collective-permute-start.11) | collective-permute-done | bytes 131104 | tf_op jit(solution)/shard_map/ppermute | solution.py:495
  31.3 0.2 shard_map.149.x_ref.refs_11_
  31.6 1.7 %collective-permute-start.12 = (f32[2,16]{1,0:T(2,128)S(1)}, f32[2,16]{1,0:T(2,128)S(1)}, u32[]{:S(2)}, u32[]{:S(2)}) collective-permute-start(f32[2,16]{1,0:T(2,128)S(1)} %shard_map.149.x_ref.refs_11_), channel_id=1, source_target_pairs={{0,4},{4,0},{8,12},{12,8},{1,5},{5,1},{9,13},{13,9},{2,6},{6,2},{1... | collective-permute-start | bytes 392 | tf_op jit(solution)/shard_map/ppermute | solution.py:482
  33.3 0.8 %shard_map.155.x_ref.refs_1_ = f32[256,128]{1,0:T(8,128)S(1)} custom-call(f32[32,1024]{1,0:T(8,128)S(1)} %collective-permute-done.2.refs_0_.refs_6_, f32[32,1024]{1,0:T(8,128)S(1)} %collective-permute-done.8.refs_0_.refs_1_.refs_7_, f32[32,1024]{1,0:T(8,128)S(1)} %collective-permute-done.9.refs_2_.refs_8_, ...), custom_call_target="tpu_custom_call" | custom-call | tf_op jit(solution)/shard_map/pallas_call | solution.py:466
  34.1 1.5 %collective-permute-start.17 = (f32[256,128]{1,0:T(8,128)S(1)}, f32[256,128]{1,0:T(8,128)S(1)}, u32[]{:S(2)}, u32[]{:S(2)}) collective-permute-start(f32[256,128]{1,0:T(8,128)S(1)} %shard_map.155.x_ref.refs_1_), channel_id=1, source_target_pairs={{0,1},{1,0},{2,3},{3,2},{4,5},{5,4},{6,7},{7,6},{8,9},{9,8},{10,11... | collective-permute-start | bytes 393224 | tf_op jit(solution)/shard_map/ppermute | solution.py:482
  35.6 0.0 collective-permute-done.12.y_ref
  35.6 1.5 %collective-permute-start.18 = (f32[256,128]{1,0:T(8,128)S(1)}, f32[256,128]{1,0:T(8,128)S(1)}, u32[]{:S(2)}, u32[]{:S(2)}) collective-permute-start(f32[256,128]{1,0:T(8,128)S(1)} %shard_map.155.x_ref.refs_1_), channel_id=1, source_target_pairs={{0,2},{1,3},{2,0},{3,1},{4,6},{5,7},{6,4},{7,5},{8,10},{9,11},{10,... | collective-permute-start | bytes 393224 | tf_op jit(solution)/shard_map/ppermute | solution.py:482
  37.2 0.0 collective-permute-done.14.refs_1_
  37.2 0.1 collective-permute-start.13
  37.2 0.0 collective-permute-done.15.refs_2_
  37.3 1.0 %collective-permute-start.19 = (f32[256,128]{1,0:T(8,128)S(1)}, f32[256,128]{1,0:T(8,128)S(1)}, u32[]{:S(2)}, u32[]{:S(2)}) collective-permute-start(f32[256,128]{1,0:T(8,128)S(1)} %shard_map.156), channel_id=1, source_target_pairs={{0,3},{1,2},{2,1},{3,0},{4,7},{5,6},{6,5},{7,4},{8,11},{9,10},{10,... | collective-permute-start | bytes 393224 | tf_op jit(solution)/shard_map/ppermute | solution.py:482
  38.3 0.0 collective-permute-done.16.refs_3_
  38.3 0.0 collective-permute-done.13.y_ref
  38.4 2.0 %collective-permute-start.20 = (f32[2,16]{1,0:T(2,128)S(1)}, f32[2,16]{1,0:T(2,128)S(1)}, u32[]{:S(2)}, u32[]{:S(2)}) collective-permute-start(f32[2,16]{1,0:T(2,128)S(1)} %shard_map.151.refs_24_.refs_5_), channel_id=1, source_target_pairs={{0,8},{4,12},{8,0},{12,4},{1,9},{5,13},{9,1},{13,5},{2,10},{6,14},... | collective-permute-start | bytes 392 | tf_op jit(solution)/shard_map/ppermute | solution.py:482
  40.4 2.3 %shard_map.154 = (bf16[1,256,1024]{2,1,0:T(8,128)(2,1)}, bf16[1,256,1024]{2,1,0:T(8,128)(2,1)}, f32[1,16,256]{2,1,0:T(8,128)}) custom-call(f32[32,1024]{1,0:T(8,128)S(1)} %collective-permute-done.refs_0_, f32[32,1024]{1,0:T(8,128)S(1)} %collective-permute-done.1.refs_0_.refs_1_, f32[32,1024]{1,0:T(8,128)S(1)} %collective-permute-done.4.refs_4_.refs_2_, ...), custom_call_target="tpu_custom_call" | custom-call | flops 300000000 | tf_op jit(solution)/shard_map/pallas_call | solution.py:466
  42.6 0.3 collective-permute-done.20.refs_6_
  42.9 0.0 collective-permute-done.17.refs_2_
  42.9 0.0 collective-permute-done.18.refs_3_
  42.9 1.2 %collective-permute-done.19.refs_4_ = f32[256,128]{1,0:T(8,128)S(1)} collective-permute-done((f32[256,128]{1,0:T(8,128)S(1)}, f32[256,128]{1,0:T(8,128)S(1)}, u32[]{:S(2)}, u32[]{:S(2)}) %collective-permute-start.19) | collective-permute-done | bytes 131104 | tf_op jit(solution)/shard_map/ppermute | solution.py:482
  44.1 0.8 %shard_map.157 = (f32[1,256,128]{2,1,0:T(8,128)}, f32[1,256,128]{2,1,0:T(8,128)}, f32[1,16]{1,0:T(1,128)}, f32[1,16]{1,0:T(1,128)}) custom-call(f32[256,128]{1,0:T(8,128)S(1)} %shard_map.153.refs_25_.refs_0_, f32[256,128]{1,0:T(8,128)S(1)} %shard_map.155.x_ref.refs_1_, f32[256,128]{1,0:T(8,128)S(1)} %collective-permute-done.17.refs_2_, ...), custom_call_target="tpu_custom_call" | custom-call | tf_op jit(solution)/shard_map/pallas_call | solution.py:466
  (13 shorter events, 0.2 us)
Async XLA Ops:
  2.9 7.7 %collective-permute-start = (f32[32,1024]{1,0:T(8,128)S(1)}, f32[32,1024]{1,0:T(8,128)S(1)}, u32[]{:S(2)}, u32[]{:S(2)}) collective-permute-start(f32[32,1024]{1,0:T(8,128)S(1)} %get-tuple-element.49.refs_1_), channel_id=1, source_target_pairs={{0,4},{4,0},{8,12},{12,8},{16,20},{20,16},{24,28},{28,24},{1,5},{5... | collective-permute-start | bytes 393224 | tf_op jit(solution)/shard_map/ppermute | solution.py:495
  6.0 9.0 %collective-permute-start.3 = (f32[32,1024]{1,0:T(8,128)S(1)}, f32[32,1024]{1,0:T(8,128)S(1)}, u32[]{:S(2)}, u32[]{:S(2)}) collective-permute-start(f32[32,1024]{1,0:T(8,128)S(1)} %get-tuple-element.60.refs_1_), channel_id=1, source_target_pairs={{0,4},{4,0},{8,12},{12,8},{16,20},{20,16},{24,28},{28,24},{1,5},{5... | collective-permute-start | bytes 393224 | tf_op jit(solution)/shard_map/ppermute | solution.py:495
  6.1 10.1 %collective-permute-start.2 = (f32[32,1024]{1,0:T(8,128)S(1)}, f32[32,1024]{1,0:T(8,128)S(1)}, u32[]{:S(2)}, u32[]{:S(2)}) collective-permute-start(f32[32,1024]{1,0:T(8,128)S(1)} %get-tuple-element.59.refs_1_), channel_id=1, source_target_pairs={{0,4},{4,0},{8,12},{12,8},{16,20},{20,16},{24,28},{28,24},{1,5},{5... | collective-permute-start | bytes 393224 | tf_op jit(solution)/shard_map/ppermute | solution.py:495
  10.6 6.2 %collective-permute-start.1 = (f32[32,1024]{1,0:T(8,128)S(1)}, f32[32,1024]{1,0:T(8,128)S(1)}, u32[]{:S(2)}, u32[]{:S(2)}) collective-permute-start(f32[32,1024]{1,0:T(8,128)S(1)} %shard_map.137.after_ref), channel_id=1, source_target_pairs={{0,16},{4,8},{8,4},{12,28},{16,0},{20,24},{24,20},{28,12},{1,17},{... | collective-permute-start | bytes 393224 | tf_op jit(solution)/shard_map/ppermute | solution.py:495
  10.7 8.9 %collective-permute-start.6 = (f32[32,1024]{1,0:T(8,128)S(1)}, f32[32,1024]{1,0:T(8,128)S(1)}, u32[]{:S(2)}, u32[]{:S(2)}) collective-permute-start(f32[32,1024]{1,0:T(8,128)S(1)} %get-tuple-element.63.refs_1_), channel_id=1, source_target_pairs={{0,4},{4,0},{8,12},{12,8},{16,20},{20,16},{24,28},{28,24},{1,5},{5... | collective-permute-start | bytes 393224 | tf_op jit(solution)/shard_map/ppermute | solution.py:495
  15.1 4.7 %collective-permute-start.5 = (f32[32,1024]{1,0:T(8,128)S(1)}, f32[32,1024]{1,0:T(8,128)S(1)}, u32[]{:S(2)}, u32[]{:S(2)}) collective-permute-start(f32[32,1024]{1,0:T(8,128)S(1)} %shard_map.139.after_ref), channel_id=1, source_target_pairs={{0,16},{4,8},{8,4},{12,28},{16,0},{20,24},{24,20},{28,12},{1,17},{... | collective-permute-start | bytes 393224 | tf_op jit(solution)/shard_map/ppermute | solution.py:495
  16.2 6.6 %collective-permute-start.8 = (f32[32,1024]{1,0:T(8,128)S(1)}, f32[32,1024]{1,0:T(8,128)S(1)}, u32[]{:S(2)}, u32[]{:S(2)}) collective-permute-start(f32[32,1024]{1,0:T(8,128)S(1)} %shard_map.141.refs_3_), channel_id=1, source_target_pairs={{0,16},{4,8},{8,4},{12,28},{16,0},{20,24},{24,20},{28,12},{1,17},{... | collective-permute-start | bytes 393224 | tf_op jit(solution)/shard_map/ppermute | solution.py:495
  16.8 7.6 %collective-permute-start.4 = (f32[32,1024]{1,0:T(8,128)S(1)}, f32[32,1024]{1,0:T(8,128)S(1)}, u32[]{:S(2)}, u32[]{:S(2)}) collective-permute-start(f32[32,1024]{1,0:T(8,128)S(1)} %shard_map.142.refs_3_), channel_id=1, source_target_pairs={{0,4},{4,0},{8,12},{12,8},{16,20},{20,16},{24,28},{28,24},{1,5},{5... | collective-permute-start | bytes 393224 | tf_op jit(solution)/shard_map/ppermute | solution.py:495
  19.6 4.8 %collective-permute-start.10 = (f32[32,1024]{1,0:T(8,128)S(1)}, f32[32,1024]{1,0:T(8,128)S(1)}, u32[]{:S(2)}, u32[]{:S(2)}) collective-permute-start(f32[32,1024]{1,0:T(8,128)S(1)} %shard_map.143.refs_3_), channel_id=1, source_target_pairs={{0,16},{4,8},{8,4},{12,28},{16,0},{20,24},{24,20},{28,12},{1,17},{... | collective-permute-start | bytes 393224 | tf_op jit(solution)/shard_map/ppermute | solution.py:495
  19.8 6.5 %collective-permute-start.7 = (f32[32,1024]{1,0:T(8,128)S(1)}, f32[32,1024]{1,0:T(8,128)S(1)}, u32[]{:S(2)}, u32[]{:S(2)}) collective-permute-start(f32[32,1024]{1,0:T(8,128)S(1)} %shard_map.144.after_ref), channel_id=1, source_target_pairs={{0,4},{4,0},{8,12},{12,8},{16,20},{20,16},{24,28},{28,24},{1,5},{5... | collective-permute-start | bytes 393224 | tf_op jit(solution)/shard_map/ppermute | solution.py:495
  22.9 7.7 %collective-permute-start.9 = (f32[32,1024]{1,0:T(8,128)S(1)}, f32[32,1024]{1,0:T(8,128)S(1)}, u32[]{:S(2)}, u32[]{:S(2)}) collective-permute-start(f32[32,1024]{1,0:T(8,128)S(1)} %shard_map.146.refs_3_), channel_id=1, source_target_pairs={{0,4},{4,0},{8,12},{12,8},{16,20},{20,16},{24,28},{28,24},{1,5},{5... | collective-permute-start | bytes 393224 | tf_op jit(solution)/shard_map/ppermute | solution.py:495
  24.5 6.9 %collective-permute-start.11 = (f32[32,1024]{1,0:T(8,128)S(1)}, f32[32,1024]{1,0:T(8,128)S(1)}, u32[]{:S(2)}, u32[]{:S(2)}) collective-permute-start(f32[32,1024]{1,0:T(8,128)S(1)} %shard_map.147), channel_id=1, source_target_pairs={{0,4},{4,0},{8,12},{12,8},{16,20},{20,16},{24,28},{28,24},{1,5},{5... | collective-permute-start | bytes 393224 | tf_op jit(solution)/shard_map/ppermute | solution.py:495
  27.0 10.1 %collective-permute-start.14 = (f32[256,128]{1,0:T(8,128)S(1)}, f32[256,128]{1,0:T(8,128)S(1)}, u32[]{:S(2)}, u32[]{:S(2)}) collective-permute-start(f32[256,128]{1,0:T(8,128)S(1)} %shard_map.152.refs_0_), channel_id=1, source_target_pairs={{0,1},{1,0},{2,3},{3,2},{4,5},{5,4},{6,7},{7,6},{8,9},{9,8},{10,11... | collective-permute-start | bytes 393224 | tf_op jit(solution)/shard_map/ppermute | solution.py:482
  28.6 8.7 %collective-permute-start.15 = (f32[256,128]{1,0:T(8,128)S(1)}, f32[256,128]{1,0:T(8,128)S(1)}, u32[]{:S(2)}, u32[]{:S(2)}) collective-permute-start(f32[256,128]{1,0:T(8,128)S(1)} %shard_map.152.refs_0_), channel_id=1, source_target_pairs={{0,2},{1,3},{2,0},{3,1},{4,6},{5,7},{6,4},{7,5},{8,10},{9,11},{10,... | collective-permute-start | bytes 393224 | tf_op jit(solution)/shard_map/ppermute | solution.py:482
  30.1 8.2 %collective-permute-start.16 = (f32[256,128]{1,0:T(8,128)S(1)}, f32[256,128]{1,0:T(8,128)S(1)}, u32[]{:S(2)}, u32[]{:S(2)}) collective-permute-start(f32[256,128]{1,0:T(8,128)S(1)} %shard_map.152.refs_0_), channel_id=1, source_target_pairs={{0,3},{1,2},{2,1},{3,0},{4,7},{5,6},{6,5},{7,4},{8,11},{9,10},{10,... | collective-permute-start | bytes 393224 | tf_op jit(solution)/shard_map/ppermute | solution.py:482
  31.6 4.1 %collective-permute-start.12 = (f32[2,16]{1,0:T(2,128)S(1)}, f32[2,16]{1,0:T(2,128)S(1)}, u32[]{:S(2)}, u32[]{:S(2)}) collective-permute-start(f32[2,16]{1,0:T(2,128)S(1)} %shard_map.149.x_ref.refs_11_), channel_id=1, source_target_pairs={{0,4},{4,0},{8,12},{12,8},{1,5},{5,1},{9,13},{13,9},{2,6},{6,2},{1... | collective-permute-start | bytes 392 | tf_op jit(solution)/shard_map/ppermute | solution.py:482
  34.1 8.8 %collective-permute-start.17 = (f32[256,128]{1,0:T(8,128)S(1)}, f32[256,128]{1,0:T(8,128)S(1)}, u32[]{:S(2)}, u32[]{:S(2)}) collective-permute-start(f32[256,128]{1,0:T(8,128)S(1)} %shard_map.155.x_ref.refs_1_), channel_id=1, source_target_pairs={{0,1},{1,0},{2,3},{3,2},{4,5},{5,4},{6,7},{7,6},{8,9},{9,8},{10,11... | collective-permute-start | bytes 393224 | tf_op jit(solution)/shard_map/ppermute | solution.py:482
  35.6 7.3 %collective-permute-start.18 = (f32[256,128]{1,0:T(8,128)S(1)}, f32[256,128]{1,0:T(8,128)S(1)}, u32[]{:S(2)}, u32[]{:S(2)}) collective-permute-start(f32[256,128]{1,0:T(8,128)S(1)} %shard_map.155.x_ref.refs_1_), channel_id=1, source_target_pairs={{0,2},{1,3},{2,0},{3,1},{4,6},{5,7},{6,4},{7,5},{8,10},{9,11},{10,... | collective-permute-start | bytes 393224 | tf_op jit(solution)/shard_map/ppermute | solution.py:482
  37.2 1.2 %collective-permute-start.13 = (f32[2,16]{1,0:T(2,128)S(1)}, f32[2,16]{1,0:T(2,128)S(1)}, u32[]{:S(2)}, u32[]{:S(2)}) collective-permute-start(f32[2,16]{1,0:T(2,128)S(1)} %shard_map.150.x_ref.refs_0_), channel_id=1, source_target_pairs={{0,16},{16,0},{1,17},{17,1},{2,18},{18,2},{3,19},{19,3},{4,20},{20... | collective-permute-start | bytes 392 | tf_op jit(solution)/shard_map/ppermute | solution.py:482
  37.3 6.8 %collective-permute-start.19 = (f32[256,128]{1,0:T(8,128)S(1)}, f32[256,128]{1,0:T(8,128)S(1)}, u32[]{:S(2)}, u32[]{:S(2)}) collective-permute-start(f32[256,128]{1,0:T(8,128)S(1)} %shard_map.156), channel_id=1, source_target_pairs={{0,3},{1,2},{2,1},{3,0},{4,7},{5,6},{6,5},{7,4},{8,11},{9,10},{10,... | collective-permute-start | bytes 393224 | tf_op jit(solution)/shard_map/ppermute | solution.py:482
  38.4 4.5 %collective-permute-start.20 = (f32[2,16]{1,0:T(2,128)S(1)}, f32[2,16]{1,0:T(2,128)S(1)}, u32[]{:S(2)}, u32[]{:S(2)}) collective-permute-start(f32[2,16]{1,0:T(2,128)S(1)} %shard_map.151.refs_24_.refs_5_), channel_id=1, source_target_pairs={{0,8},{4,12},{8,0},{12,4},{1,9},{5,13},{9,1},{13,5},{2,10},{6,14},... | collective-permute-start | bytes 392 | tf_op jit(solution)/shard_map/ppermute | solution.py:482
